TPU v7x, 32 devices: a whole 2x2x4 slice. The times are simulated.
32 devices in a mesh: dp: 8 (over y, x, core), tensor: 4 (over z).
Axes of the slice: x: 2, y: 2, z: 4, core: 2. Of those that a mesh axis runs over, the one named last changes fastest.
Arguments:
- inputs: bfloat16 [8, 1024, 2048], P('dp', 'tensor'), may hold values from -6 to 6
- cotangent: bfloat16 [8, 1024, 2048], P('dp', 'tensor'), may hold values from -6 to 6
- seg_ids: int32 [8, 1024], P('dp'), may hold values from 0 to 127, as said below
- norm_gains: bfloat16 [1, 2, 2048], P(None, None, ('dp', 'tensor')), may hold values from 0.5 to 1.5
- w_q: bfloat16 [1, 2048, 1024], P(None, 'dp', 'tensor'), may hold values from -0.125 to 0.125
- key_value_weight: bfloat16 [1, 2048, 512], P(None, ('dp', 'tensor')), may hold values from -0.125 to 0.125
- w_zx: bfloat16 [1, 2048, 2, 3072], P(None, 'dp', None, 'tensor'), may hold values from -0.125 to 0.125
- w_bc: bfloat16 [1, 2048, 512], P(None, ('dp', 'tensor')), may hold values from -0.125 to 0.125
- w_dt: bfloat16 [1, 2048, 48], P(None, 'dp', 'tensor'), may hold values from -0.125 to 0.125
- a_log: float32 [1, 48], P(None, 'tensor'), may hold values from 0 to 2.5
- dt_bias: float32 [1, 48], P(None, 'tensor'), may hold values from -9 to -3
- d_skip: float32 [1, 48], P(None, 'tensor'), may hold values from 0.5 to 1.5
- conv_x: float32 [1, 4, 3072], P(None, None, 'tensor'), may hold values from -3 to 3
- conv_bc: bfloat16 [1, 4, 512], P(None, None, ('dp', 'tensor')), may hold values from -3 to 3
- m_gain: float32 [1, 3072], P(None, 'tensor'), may hold values from 0.5 to 1.5
- w_ao: bfloat16 [1, 1024, 2048], P(None, 'tensor', 'dp'), may hold values from -0.75 to 0.75
- w_mo: bfloat16 [1, 3072, 2048], P(None, 'tensor', 'dp'), may hold values from -0.109375 to 0.109375
- w_gu: bfloat16 [1, 2048, 2, 4096], P(None, 'dp', None, 'tensor'), may hold values from -0.125 to 0.125
- w_down: bfloat16 [1, 4096, 2048], P(None, 'tensor', 'dp'), may hold values from -0.09375 to 0.09375
Outputs:
- hidden_out: bfloat16 [8, 1024, 2048], P('dp', 'tensor')
- input_grad: float32 [8, 1024, 2048], P('dp', 'tensor')
- grad_norm_gains: float32 [1, 2, 2048], P(None, None, ('dp', 'tensor'))
- grad_w_q: float32 [1, 2048, 1024], P(None, 'dp', 'tensor')
- grad_w_kv: float32 [1, 2048, 512], P(None, ('dp', 'tensor'))
- grad_w_zx: float32 [1, 2048, 2, 3072], P(None, 'dp', None, 'tensor')
- grad_w_bc: float32 [1, 2048, 512], P(None, ('dp', 'tensor'))
- grad_w_dt: float32 [1, 2048, 48], P(None, 'dp', 'tensor')
- grad_a_log: float32 [1, 48], P(None, 'tensor')
- grad_dt_bias: float32 [1, 48], P(None, 'tensor')
- grad_d_skip: float32 [1, 48], P(None, 'tensor')
- grad_conv_x: float32 [1, 4, 3072], P(None, None, 'tensor')
- grad_conv_bc: float32 [1, 4, 512], P(None, None, ('dp', 'tensor'))
- grad_m_gain: float32 [1, 3072], P(None, 'tensor')
- grad_w_ao: float32 [1, 1024, 2048], P(None, 'tensor', 'dp')
- grad_w_mo: float32 [1, 3072, 2048], P(None, 'tensor', 'dp')
- grad_w_gu: float32 [1, 2048, 2, 4096], P(None, 'dp', None, 'tensor')
- grad_w_down: float32 [1, 4096, 2048], P(None, 'tensor', 'dp')
Inputs may be any that keep to these rules, and one draw needn't show every extreme that they name: `seg_ids`: in each sequence the ids start at 0, never fall and rise by at most one from a position to the next. One document of each sequence begins at position 64 or earlier and ends at position 960 or later.
All inputs are finite; a program needn't handle non-finite values.
Results may differ from a plain program's by a relative error of at most 0.017.
Values may be sent and summed in bfloat16 or wider, within the bound.
No kernel may reach another device: no remote copies, remote signals or barrier semaphores. Data moves between devices by JAX's collectives and lax.ppermute only.
A program may use at most 320 MiB of HBM per device.

v0:
```python
from functools import partial

import jax
import jax.numpy as jnp
from jax import lax
from jax.sharding import PartitionSpec as P

QUERY_HEADS = 8
KEY_VALUE_HEADS = 2
HEAD_SIZE = 128
HM = 48
P_SIZE = 64


NORM_EPS = 1e-05
ROPE_BASE = 100000000000.0
MASK_FILL = -1e30
HIGHEST = lax.Precision.HIGHEST


def rms_factor(hidden):
    return lax.rsqrt(jnp.mean(hidden * hidden, axis=-1, keepdims=True) + NORM_EPS)


def norm_backward(hidden, gain_vec, d_normed, grad_h):
    factor = rms_factor(hidden)
    weighted = gain_vec * d_normed
    inner_mean = jnp.mean(weighted * hidden, axis=-1, keepdims=True)
    grad_h = grad_h + factor * weighted - hidden * factor**3 * inner_mean
    d_gain = jnp.sum(d_normed * hidden * factor, axis=(0, 1))
    return (grad_h, d_gain)


def rotary_tables(length_total, head_dim):
    positions = jnp.arange(length_total).astype(jnp.float32)
    freqs = ROPE_BASE ** (-jnp.arange(0, head_dim // 2).astype(jnp.float32) * 2.0 / head_dim)
    angles = positions[:, None] * freqs[None, :]
    return (jnp.cos(angles)[:, None, :], jnp.sin(angles)[:, None, :])


def apply_rotation(values, cosine_table, sine_table):
    half_dim = values.shape[-1] // 2
    front_half = values[..., :half_dim]
    back_half = values[..., half_dim:]
    return jnp.concatenate(
        [
            front_half * cosine_table - back_half * sine_table,
            back_half * cosine_table + front_half * sine_table,
        ],
        axis=-1,
    )


def doc_conv(signal, kernel, segment):
    length_total = signal.shape[0]
    taps = kernel.shape[0]
    summed = jnp.zeros(signal.shape, jnp.float32)
    for tap_index in range(taps):
        offset = taps - 1 - tap_index
        shifted = jnp.pad(signal, ((offset, 0), (0, 0)))[:length_total]
        seg_shift = jnp.pad(segment, (offset, 0), constant_values=-1)[:length_total]
        summed = summed + kernel[tap_index] * shifted * (seg_shift == segment)[:, None]
    return jax.nn.silu(summed)


def ssd_block(carried, pieces):
    inputs_x, keys_b, query_c, log_decay, step_size, segment, prior_seg = pieces
    block_len = segment.shape[0]
    cumulative = jnp.cumsum(log_decay, axis=0)
    order_idx = jnp.arange(block_len)
    within = (segment[:, None] == segment[None, :]) & (order_idx[:, None] >= order_idx[None, :])
    mask_three = within[:, :, None]
    gap_logs = cumulative[:, None, :] - cumulative[None, :, :]
    decays = jnp.where(mask_three, jnp.exp(jnp.where(mask_three, gap_logs, 0.0)), 0.0)
    c_dot_b = jnp.dot(query_c, keys_b.T, precision=HIGHEST)
    scaled_x = inputs_x * step_size[:, :, None]
    local_y = jnp.einsum("ijh,jhp->ihp", decays * c_dot_b[:, :, None], scaled_x, precision=HIGHEST)
    entering = jnp.exp(cumulative) * (segment == prior_seg)[:, None]
    carried_y = (
        jnp.einsum("in,hpn->ihp", query_c, carried, precision=HIGHEST) * entering[:, :, None]
    )
    last_seg = segment[-1]
    leaving = jnp.exp(cumulative[-1][None, :] - cumulative) * (segment == last_seg)[:, None]
    keep_scale = jnp.exp(cumulative[-1]) * (last_seg == prior_seg)
    updated = carried * keep_scale[:, None, None] + jnp.einsum(
        "jh,jhp,jn->hpn", leaving, scaled_x, keys_b, precision=HIGHEST
    )
    return (updated, local_y + carried_y)


def ssd_scan(x_conv, keys_b, query_c, log_decay, step_size, segment):
    length_total, head_count, head_dim = x_conv.shape
    block_len = min(128, length_total)
    blocks = length_total // block_len
    prior_seg = jnp.concatenate(
        [jnp.full((1,), -1, jnp.int32), segment[block_len - 1 : length_total - 1 : block_len]]
    )

    def by_blocks(array_in):
        return array_in.reshape((blocks, block_len) + array_in.shape[1:])

    initial = jnp.zeros((head_count, head_dim, keys_b.shape[1]), jnp.float32)
    _, outputs = lax.scan(
        jax.checkpoint(ssd_block),
        initial,
        (
            by_blocks(x_conv),
            by_blocks(keys_b),
            by_blocks(query_c),
            by_blocks(log_decay),
            by_blocks(step_size),
            by_blocks(segment),
            prior_seg,
        ),
    )
    return outputs.reshape(length_total, head_count, head_dim)


def mamba_core(x_raw, bc_raw, dt_raw, a_log, dt_bias, d_skip, conv_x, conv_bc, segment):
    length_total, head_count = dt_raw.shape
    x_conv = doc_conv(x_raw, conv_x, segment).reshape(length_total, head_count, -1)
    bc_conv = doc_conv(bc_raw, conv_bc, segment)
    states = bc_conv.shape[1] // 2
    step_size = jax.nn.softplus(dt_raw + dt_bias)
    log_decay = -step_size * jnp.exp(a_log)
    output = ssd_scan(
        x_conv, bc_conv[:, :states], bc_conv[:, states:], log_decay, step_size, segment
    )
    return (output + d_skip[None, :, None] * x_conv).reshape(length_total, -1)


def core_batch(x_raw, bc_raw, dt_raw, a_log, dt_bias, d_skip, conv_x, conv_bc, seg_ids):
    return jax.vmap(mamba_core, in_axes=(0, 0, 0, None, None, None, None, None, 0))(
        x_raw, bc_raw, dt_raw, a_log, dt_bias, d_skip, conv_x, conv_bc, seg_ids
    )


def block_mask(seg_ids, row_start, row_count, key_end):
    row_pos = row_start + jnp.arange(row_count)
    key_pos = jnp.arange(key_end)
    causal = row_pos[:, None] >= key_pos[None, :]
    same_doc = seg_ids[:, row_start : row_start + row_count, None] == seg_ids[:, None, :key_end]
    return causal[None] & same_doc


def split_pair(values):
    high_part = values.astype(jnp.bfloat16)
    rest_part = (values - high_part.astype(jnp.float32)).astype(jnp.bfloat16)
    return (high_part, rest_part)


def project_qkv(normed, wq_g, wkv_sel, cosine_table, sine_table):
    seqs_dev = normed.shape[0]
    length_total = normed.shape[1]
    head_dim = wkv_sel.shape[1] // 2
    q_proj = jnp.einsum("std,dc->stc", normed, wq_g, preferred_element_type=jnp.float32).reshape(
        seqs_dev, length_total, -1, head_dim
    )
    queries = apply_rotation(q_proj, cosine_table, sine_table).astype(jnp.bfloat16)
    key_value_projected = jnp.einsum(
        "std,dc->stc", normed, wkv_sel, preferred_element_type=jnp.float32
    )
    rotated_keys = apply_rotation(
        key_value_projected[..., :head_dim], cosine_table[:, 0], sine_table[:, 0]
    ).astype(jnp.bfloat16)
    value_rows = key_value_projected[..., head_dim:].astype(jnp.bfloat16)
    return (queries, rotated_keys, value_rows)


def attention_forward(normed, wq_g, wkv_sel, seg_ids, cosine_table, sine_table):
    seqs_dev = normed.shape[0]
    length_total = normed.shape[1]
    queries, rotated_keys, value_rows = project_qkv(normed, wq_g, wkv_sel, cosine_table, sine_table)
    scale_qk = rotated_keys.shape[2] ** (-0.5)
    block_rows = min(512, length_total)
    attended_parts = []
    lse_parts = []
    for row_start in range(0, length_total, block_rows):
        key_end = row_start + block_rows
        scores = (
            jnp.einsum(
                "sqhd,skd->shqk",
                queries[:, row_start:key_end],
                rotated_keys[:, :key_end],
                preferred_element_type=jnp.float32,
            )
            * scale_qk
        )
        allowed = block_mask(seg_ids, row_start, block_rows, key_end)[:, None]
        masked = jnp.where(allowed, scores, MASK_FILL)
        top_score = jnp.max(masked, axis=-1, keepdims=True)
        raised = jnp.exp(masked - top_score)
        totals = jnp.sum(raised, axis=-1, keepdims=True)
        prob_low = (raised / totals).astype(jnp.bfloat16)
        lse_parts.append(top_score + jnp.log(totals))
        attended_parts.append(
            jnp.einsum(
                "shqk,skd->sqhd",
                prob_low,
                value_rows[:, :key_end],
                preferred_element_type=jnp.float32,
            ).astype(jnp.bfloat16)
        )
    attended = jnp.concatenate(attended_parts, axis=1).reshape(seqs_dev, length_total, -1)
    return (attended, jnp.concatenate(lse_parts, axis=2))


def gather_tokens(pieces):
    return lax.all_gather(pieces, "tensor", axis=1, tiled=True)


def scatter_tokens(partial_sum):
    return lax.psum_scatter(partial_sum, "tensor", scatter_dimension=1, tiled=True)


def local(
    inputs,
    cotangent,
    seg_ids,
    norm_gains,
    w_q,
    key_value_weight,
    w_zx,
    w_bc,
    w_dt,
    a_log,
    dt_bias,
    d_skip,
    conv_x,
    conv_bc,
    m_gain,
    w_ao,
    w_mo,
    w_gu,
    w_down,
):
    layers = w_q.shape[0]
    query_local = w_q.shape[2] // HEAD_SIZE
    key_value_head = lax.axis_index("tensor") * query_local // (QUERY_HEADS // KEY_VALUE_HEADS)
    seqs_dev = seg_ids.shape[0]
    length_total = seg_ids.shape[1]
    cosine_table, sine_table = rotary_tables(length_total, HEAD_SIZE)
    gains_all, key_value_full, bc_all, convbc_all = (
        lax.all_gather(norm_gains, ("dp", "tensor"), axis=2, tiled=True),
        lax.all_gather(key_value_weight, ("dp", "tensor"), axis=1, tiled=True),
        lax.all_gather(w_bc, ("dp", "tensor"), axis=1, tiled=True),
        lax.all_gather(conv_bc, ("dp", "tensor"), axis=2, tiled=True),
    )
    gains_f = gains_all.astype(jnp.float32)
    convbc_f = convbc_all.astype(jnp.float32)
    bc_width = bc_all.shape[2]

    def fetch_layer(layer_index):
        return (
            lax.all_gather(w_q[layer_index], "dp", axis=0, tiled=True),
            lax.all_gather(w_zx[layer_index], "dp", axis=0, tiled=True),
            lax.all_gather(w_dt[layer_index], "dp", axis=0, tiled=True),
            lax.all_gather(w_ao[layer_index], "dp", axis=1, tiled=True),
            lax.all_gather(w_mo[layer_index], "dp", axis=1, tiled=True),
            lax.all_gather(w_gu[layer_index], "dp", axis=0, tiled=True),
            lax.all_gather(w_down[layer_index], "dp", axis=1, tiled=True),
        )

    def select_kv(layer_index):
        wk_sel = lax.dynamic_slice_in_dim(
            key_value_full[layer_index], key_value_head * HEAD_SIZE, HEAD_SIZE, 1
        )
        value_weight_selected = lax.dynamic_slice_in_dim(
            key_value_full[layer_index],
            (KEY_VALUE_HEADS + key_value_head) * HEAD_SIZE,
            HEAD_SIZE,
            1,
        )
        return jnp.concatenate([wk_sel, value_weight_selected], axis=1)

    hidden = inputs.astype(jnp.float32)
    layer_index = 0
    weights = fetch_layer(layer_index)
    wq_g, wzx_g, wdt_g, wao_g, wmo_g, wgu_g, wdown_g = weights
    wkv_sel = select_kv(layer_index)
    h_in = hidden
    normed1 = gather_tokens(
        (hidden * rms_factor(hidden) * gains_f[layer_index, 0]).astype(jnp.bfloat16)
    )
    attended, log_sums = attention_forward(
        normed1, wq_g, wkv_sel, seg_ids, cosine_table, sine_table
    )
    attn_part = jnp.einsum("stc,cd->std", attended, wao_g, preferred_element_type=jnp.float32)
    zx_proj = jnp.einsum("std,dkc->stkc", normed1, wzx_g, preferred_element_type=jnp.float32)
    bc_raw = jnp.einsum(
        "std,dc->stc", normed1, bc_all[layer_index], preferred_element_type=jnp.float32
    )
    dt_raw = jnp.einsum("std,dc->stc", normed1, wdt_g, preferred_element_type=jnp.float32)
    y_out = core_batch(
        zx_proj[:, :, 1],
        bc_raw,
        dt_raw,
        a_log[layer_index],
        dt_bias[layer_index],
        d_skip[layer_index],
        conv_x[layer_index],
        convbc_f[layer_index],
        seg_ids,
    )
    gated = y_out * jax.nn.silu(zx_proj[:, :, 0])
    squares = lax.psum(jnp.sum(gated * gated, axis=-1), "tensor")
    rstd = lax.rsqrt(squares / (HM * P_SIZE) + NORM_EPS)[..., None]
    mixed = (gated * rstd * m_gain[layer_index]).astype(jnp.bfloat16)
    mamba_part = jnp.einsum("stc,cd->std", mixed, wmo_g, preferred_element_type=jnp.float32)
    hidden = hidden + scatter_tokens(attn_part + mamba_part)
    h_mid = hidden
    normed2 = gather_tokens(
        (hidden * rms_factor(hidden) * gains_f[layer_index, 1]).astype(jnp.bfloat16)
    )
    gate_up = jnp.einsum("std,dkf->stkf", normed2, wgu_g, preferred_element_type=jnp.float32)
    act = (jax.nn.silu(gate_up[:, :, 0]) * gate_up[:, :, 1]).astype(jnp.bfloat16)
    hidden = hidden + scatter_tokens(
        jnp.einsum("stf,fd->std", act, wdown_g, preferred_element_type=jnp.float32)
    )
    saved = [(h_in, h_mid, normed1, normed2, attended, log_sums, rstd)]
    hidden_out = hidden.astype(jnp.bfloat16)
    grad_h = cotangent.astype(jnp.float32)
    scale_qk = HEAD_SIZE ** (-0.5)
    block_rows = min(512, length_total)
    layer_store = [None] * layers
    shared_store = [None] * layers
    head_store = [None] * layers
    for layer_index in reversed(range(layers)):
        h_in, h_mid, normed1, normed2, attended, log_sums, rstd = saved[layer_index]
        weights = fetch_layer(layer_index)
        wq_g, wzx_g, wdt_g, wao_g, wmo_g, wgu_g, wdown_g = weights
        wkv_sel = select_kv(layer_index)
        d_out = gather_tokens(grad_h.astype(jnp.bfloat16))
        gate_up = jnp.einsum("std,dkf->stkf", normed2, wgu_g, preferred_element_type=jnp.float32)
        gate_val = gate_up[:, :, 0]
        up_val = gate_up[:, :, 1]
        sig_gate = jax.nn.sigmoid(gate_val)
        silu_gate = gate_val * sig_gate
        act = (silu_gate * up_val).astype(jnp.bfloat16)
        g_down = jnp.einsum("stf,std->fd", act, d_out, preferred_element_type=jnp.float32)
        d_act = jnp.einsum("std,fd->stf", d_out, wdown_g, preferred_element_type=jnp.float32)
        d_gu = jnp.stack(
            [d_act * up_val * sig_gate * (1.0 + gate_val * (1.0 - sig_gate)), d_act * silu_gate],
            axis=2,
        ).astype(jnp.bfloat16)
        g_gu = jnp.einsum("std,stkf->dkf", normed2, d_gu, preferred_element_type=jnp.float32)
        d_norm2 = scatter_tokens(
            jnp.einsum("stkf,dkf->std", d_gu, wgu_g, preferred_element_type=jnp.float32)
        )
        grad_h, g_gain2 = norm_backward(h_mid, gains_f[layer_index, 1], d_norm2, grad_h)
        d_branch = gather_tokens(grad_h.astype(jnp.bfloat16))
        queries, rotated_keys, value_rows = project_qkv(
            normed1, wq_g, wkv_sel, cosine_table, sine_table
        )
        g_ao = jnp.einsum("stc,std->cd", attended, d_branch, preferred_element_type=jnp.float32)
        d_att = (
            jnp.einsum("std,cd->stc", d_branch, wao_g, preferred_element_type=jnp.float32)
            .astype(jnp.bfloat16)
            .reshape(seqs_dev, length_total, query_local, HEAD_SIZE)
        )
        query_parts = []
        d_keys = jnp.zeros((seqs_dev, length_total, HEAD_SIZE), jnp.float32)
        d_vals = jnp.zeros((seqs_dev, length_total, HEAD_SIZE), jnp.float32)
        for row_start in range(0, length_total, block_rows):
            key_end = row_start + block_rows
            q_block = queries[:, row_start:key_end]
            do_block = d_att[:, row_start:key_end]
            scores = (
                jnp.einsum(
                    "sqhd,skd->shqk",
                    q_block,
                    rotated_keys[:, :key_end],
                    preferred_element_type=jnp.float32,
                )
                * scale_qk
            )
            allowed = block_mask(seg_ids, row_start, block_rows, key_end)[:, None]
            prob_f = jnp.where(
                allowed,
                jnp.exp(jnp.where(allowed, scores, MASK_FILL) - log_sums[:, :, row_start:key_end]),
                0.0,
            )
            prob_low = prob_f.astype(jnp.bfloat16)
            d_prob = jnp.einsum(
                "sqhd,skd->shqk",
                do_block,
                value_rows[:, :key_end],
                preferred_element_type=jnp.float32,
            )
            delta_row = jnp.sum(prob_f * d_prob, axis=-1, keepdims=True)
            d_scores = (prob_f * (d_prob - delta_row)).astype(jnp.bfloat16)
            query_parts.append(
                jnp.einsum(
                    "shqk,skd->sqhd",
                    d_scores,
                    rotated_keys[:, :key_end],
                    preferred_element_type=jnp.float32,
                )
                * scale_qk
            )
            padding = ((0, 0), (0, length_total - key_end), (0, 0))
            d_keys = d_keys + jnp.pad(
                jnp.einsum("shqk,sqhd->skd", d_scores, q_block, preferred_element_type=jnp.float32)
                * scale_qk,
                padding,
            )
            d_vals = d_vals + jnp.pad(
                jnp.einsum(
                    "shqk,sqhd->skd", prob_low, do_block, preferred_element_type=jnp.float32
                ),
                padding,
            )
        d_query = (
            apply_rotation(jnp.concatenate(query_parts, axis=1), cosine_table, -sine_table)
            .reshape(seqs_dev, length_total, -1)
            .astype(jnp.bfloat16)
        )
        d_keys = apply_rotation(d_keys, cosine_table[:, 0], -sine_table[:, 0])
        g_q = jnp.einsum("std,stc->dc", normed1, d_query, preferred_element_type=jnp.float32)
        zx_proj = jnp.einsum("std,dkc->stkc", normed1, wzx_g, preferred_element_type=jnp.float32)
        bc_raw = jnp.einsum(
            "std,dc->stc", normed1, bc_all[layer_index], preferred_element_type=jnp.float32
        )
        dt_raw = jnp.einsum("std,dc->stc", normed1, wdt_g, preferred_element_type=jnp.float32)
        gate_z = zx_proj[:, :, 0]
        y_out, core_back = jax.vjp(
            partial(core_batch, seg_ids=seg_ids),
            zx_proj[:, :, 1],
            bc_raw,
            dt_raw,
            a_log[layer_index],
            dt_bias[layer_index],
            d_skip[layer_index],
            conv_x[layer_index],
            convbc_f[layer_index],
        )
        gated = y_out * jax.nn.silu(gate_z)
        unit_norm = gated * rstd
        mixed = (unit_norm * m_gain[layer_index]).astype(jnp.bfloat16)
        g_mo = jnp.einsum("stc,std->cd", mixed, d_branch, preferred_element_type=jnp.float32)
        d_mixed = jnp.einsum("std,cd->stc", d_branch, wmo_g, preferred_element_type=jnp.float32)
        g_mgain = jnp.sum(d_mixed * unit_norm, axis=(0, 1))
        d_unit = d_mixed * m_gain[layer_index]
        gate_dot = lax.psum(jnp.sum(d_unit * gated, axis=-1), "tensor")
        d_gated = rstd * d_unit - gated * rstd**3 * gate_dot[..., None] / (HM * P_SIZE)
        sig_z = jax.nn.sigmoid(gate_z)
        d_y = d_gated * gate_z * sig_z
        d_z = d_gated * y_out * sig_z * (1.0 + gate_z * (1.0 - sig_z))
        d_xraw, d_bc, d_dt, g_alog, g_dtbias, g_dskip, g_convx, g_convbc = core_back(d_y)
        d_zx = jnp.stack([d_z, d_xraw], axis=2).astype(jnp.bfloat16)
        g_zx = jnp.einsum("std,stkc->dkc", normed1, d_zx, preferred_element_type=jnp.float32)
        d_norm1 = jnp.einsum("stkc,dkc->std", d_zx, wzx_g, preferred_element_type=jnp.float32)
        d_norm1 = d_norm1 + jnp.einsum(
            "stc,dc->std", d_query, wq_g, preferred_element_type=jnp.float32
        )
        exact_grads = jnp.concatenate([d_keys, d_vals, d_bc, d_dt], axis=-1)
        wide_weights = jnp.concatenate([wkv_sel, bc_all[layer_index], wdt_g], axis=1)
        grad_high, grad_rest = split_pair(exact_grads)
        exact_gradient = jnp.einsum(
            "std,stc->dc", normed1, grad_high, preferred_element_type=jnp.float32
        ) + jnp.einsum("std,stc->dc", normed1, grad_rest, preferred_element_type=jnp.float32)
        d_norm1 = d_norm1 + jnp.einsum(
            "stc,dc->std", grad_high, wide_weights, preferred_element_type=jnp.float32
        )
        d_norm1 = d_norm1 + jnp.einsum(
            "stc,dc->std", grad_rest, wide_weights, preferred_element_type=jnp.float32
        )
        d_norm1 = scatter_tokens(d_norm1)
        grad_h, g_gain1 = norm_backward(h_in, gains_f[layer_index, 0], d_norm1, grad_h)
        key_value_gradient = jnp.zeros(
            (key_value_full.shape[1], key_value_full.shape[2]), jnp.float32
        )
        key_value_gradient = lax.dynamic_update_slice_in_dim(
            key_value_gradient, exact_gradient[:, :HEAD_SIZE], key_value_head * HEAD_SIZE, 1
        )
        key_value_gradient = lax.dynamic_update_slice_in_dim(
            key_value_gradient,
            exact_gradient[:, HEAD_SIZE : 2 * HEAD_SIZE],
            (KEY_VALUE_HEADS + key_value_head) * HEAD_SIZE,
            1,
        )
        g_bc = exact_gradient[:, 2 * HEAD_SIZE : 2 * HEAD_SIZE + bc_width]
        g_dt = exact_gradient[:, 2 * HEAD_SIZE + bc_width :]
        grads_here = (g_q, g_zx, g_dt, g_ao, g_mo, g_gu, g_down)
        layer_store[layer_index] = (
            lax.psum_scatter(
                grads_here[0].astype(jnp.bfloat16), "dp", scatter_dimension=0, tiled=True
            ).astype(jnp.float32),
            lax.psum_scatter(
                grads_here[1].astype(jnp.bfloat16), "dp", scatter_dimension=0, tiled=True
            ).astype(jnp.float32),
            lax.psum_scatter(
                grads_here[2].astype(jnp.bfloat16), "dp", scatter_dimension=0, tiled=True
            ).astype(jnp.float32),
            lax.psum_scatter(
                grads_here[3].astype(jnp.bfloat16), "dp", scatter_dimension=1, tiled=True
            ).astype(jnp.float32),
            lax.psum_scatter(
                grads_here[4].astype(jnp.bfloat16), "dp", scatter_dimension=1, tiled=True
            ).astype(jnp.float32),
            lax.psum_scatter(
                grads_here[5].astype(jnp.bfloat16), "dp", scatter_dimension=0, tiled=True
            ).astype(jnp.float32),
            lax.psum_scatter(
                grads_here[6].astype(jnp.bfloat16), "dp", scatter_dimension=1, tiled=True
            ).astype(jnp.float32),
        )
        shared_store[layer_index] = (
            jnp.stack([g_gain1, g_gain2]),
            key_value_gradient,
            g_bc,
            g_convbc,
        )
        head_store[layer_index] = (g_alog, g_dtbias, g_dskip, g_convx, g_mgain)
    stacked = tuple((jnp.stack([layer_store[0][member]]) for member in range(7)))
    shared_stack = tuple((jnp.stack([shared_store[0][member]]) for member in range(4)))
    shared_out = (
        lax.psum_scatter(shared_stack[0], ("dp", "tensor"), scatter_dimension=2, tiled=True),
        lax.psum_scatter(shared_stack[1], ("dp", "tensor"), scatter_dimension=1, tiled=True),
        lax.psum_scatter(shared_stack[2], ("dp", "tensor"), scatter_dimension=1, tiled=True),
        lax.psum_scatter(shared_stack[3], ("dp", "tensor"), scatter_dimension=2, tiled=True),
    )
    head_stack = tuple((jnp.stack([head_store[0][member]]) for member in range(5)))
    head_out = lax.psum(head_stack, "dp")
    return (
        hidden_out,
        grad_h,
        shared_out[0],
        stacked[0],
        shared_out[1],
        stacked[1],
        shared_out[2],
        stacked[2],
        head_out[0],
        head_out[1],
        head_out[2],
        head_out[3],
        shared_out[3],
        head_out[4],
        stacked[3],
        stacked[4],
        stacked[5],
        stacked[6],
    )


def solution(mesh):
    return jax.shard_map(
        local,
        mesh=mesh,
        in_specs=(
            P("dp", "tensor", None),
            P("dp", "tensor", None),
            P("dp", None),
            P(None, None, ("dp", "tensor")),
            P(None, "dp", "tensor"),
            P(None, ("dp", "tensor"), None),
            P(None, "dp", None, "tensor"),
            P(None, ("dp", "tensor"), None),
            P(None, "dp", "tensor"),
            P(None, "tensor"),
            P(None, "tensor"),
            P(None, "tensor"),
            P(None, None, "tensor"),
            P(None, None, ("dp", "tensor")),
            P(None, "tensor"),
            P(None, "tensor", "dp"),
            P(None, "tensor", "dp"),
            P(None, "dp", None, "tensor"),
            P(None, "tensor", "dp"),
        ),
        out_specs=(
            P("dp", "tensor", None),
            P("dp", "tensor", None),
            P(None, None, ("dp", "tensor")),
            P(None, "dp", "tensor"),
            P(None, ("dp", "tensor"), None),
            P(None, "dp", None, "tensor"),
            P(None, ("dp", "tensor"), None),
            P(None, "dp", "tensor"),
            P(None, "tensor"),
            P(None, "tensor"),
            P(None, "tensor"),
            P(None, None, "tensor"),
            P(None, None, ("dp", "tensor")),
            P(None, "tensor"),
            P(None, "tensor", "dp"),
            P(None, "tensor", "dp"),
            P(None, "dp", None, "tensor"),
            P(None, "tensor", "dp"),
        ),
        check_vma=False,
    )
```

profile of v0, /device:TPU:0, one launch (start us, length us, event | category | flops | bytes accessed | tf_op | source)
XLA Modules:
  0.0 3002.5 jit_solution(10777192674182425169)
XLA Ops:
  9.5 81.2 %all_gather.52 = bf16[1,2,2048]{1,0,2:T(2,128)(2,1)S(1)} all-gather(bf16[1,2,64]{1,0,2:T(2,128)(2,1)S(1)} %copy.553), channel_id=1, replica_groups=mesh['dp'=8,'tensor'=4] {'dp','tensor'}, dimensions={2}, use_global_device_ids=true | all-gather | bytes 8448 | tf_op jit(solution)/shard_map/all_gather | solution.py:244
  92.7 34.1 %slice_reduce_fusion.1 = (f32[2048]{0:T(1024)}, f32[2048]{0:T(1024)S(1)}) fusion(f32[1,2,2048]{1,0,2:T(1,128)S(1)} %convert_element_type.432), kind=kLoop, calls=%fused_computation.464 | loop fusion | bytes 32768 | tf_op jit(solution)/shard_map/slice | solution.py:313
  144.1 69.3 %all_gather.59 = bf16[1,4,512]{1,0,2:T(2,128)(2,1)S(1)} all-gather(bf16[1,4,16]{1,0,2:T(2,128)(2,1)S(1)} %copy.563), channel_id=1, replica_groups=mesh['dp'=8,'tensor'=4] {'dp','tensor'}, dimensions={2}, use_global_device_ids=true | all-gather | bytes 4224 | tf_op jit(solution)/shard_map/all_gather | solution.py:247
  235.5 33.0 %all-gather.24.cloned.1.call-done = bf16[1,2048,512]{2,1,0:T(8,128)(2,1)} async-done(((bf16[1,64,512]{2,1,0:T(8,128)(2,1)}), bf16[1,2048,512]{2,1,0:T(8,128)(2,1)}) %all-gather.24.cloned.1.call-update) | async-done | bytes 2097168 | tf_op jit(solution)/shard_map/all_gather | solution.py:246
  289.3 25.9 all-gather.36.cloned.1.call-done
  315.2 10.3 fusion.237
  332.4 8.6 copy.562
  345.2 206.8 %while.55 = (s32[]{:T(128)}, f32[1,12,64,256]{3,2,1,0:T(8,128)S(1)}, f32[8,1,128,12,64]{2,0,1,4,3:T(8,128)}, f32[8,1,128,12]{3,2,1,0:T(8,128)}, s32[8,1,128]{2,1...) while((s32[]{:T(128)}, ...), condition=%wide.region_7.8_spmd.clone, body=%wide.region_5.7_spmd.clone.sunk | while | flops 807620096 | bytes 5918713 | solution.py:103
  360.1 11.0 dynamic_update_slice.97
  386.0 11.0 dynamic_update_slice.97
  411.8 11.0 dynamic_update_slice.97
  437.7 11.0 dynamic_update_slice.97
  463.5 11.0 dynamic_update_slice.97
  489.4 11.0 dynamic_update_slice.97
  515.2 11.0 dynamic_update_slice.97
  541.1 11.0 dynamic_update_slice.97
  552.1 8.7 copy.571
  565.8 11.7 psum.49
  577.6 9.7 fusion.230
  598.2 139.4 %reduce-scatter.19.cloned.1.call-done = f32[1,256,2048]{2,1,0:T(8,128)} async-done(((f32[1,1024,2048]{2,1,0:T(8,128)}), f32[1,256,2048]{2,1,0:T(8,128)}) %reduce-scatter.19.cloned.1.call-update) | async-done | bytes 2097168 | tf_op jit(solution)/shard_map/reduce_scatter | solution.py:213
  742.8 52.4 %all-gather.40.cloned.1.call-done = bf16[1,2048,2,1024]{3,1,2,0:T(8,128)(2,1)} async-done(((bf16[1,256,2,1024]{3,1,2,0:T(8,128)(2,1)}), bf16[1,2048,2,1024]{3,1,2,0:T(8,128)(2,1)}) %all-gather.40.cloned.1.call-update) | async-done | bytes 8388624 | tf_op jit(solution)/shard_map/all_gather | solution.py:260
  795.2 82.8 %all-gather.26.cloned.1.call-done = bf16[1,1024,2048]{2,1,0:T(8,128)(2,1)} async-done(((bf16[1,256,2048]{2,1,0:T(8,128)(2,1)}), bf16[1,1024,2048]{2,1,0:T(8,128)(2,1)}) %all-gather.26.cloned.1.call-update) | async-done | bytes 4194320 | tf_op jit(solution)/shard_map/all_gather | solution.py:209
  878.0 14.5 fusion.208
  892.5 66.4 %all-gather.28.cloned.1.call-done = bf16[1,1024,2048]{2,1,0:T(8,128)(2,1)} async-done(((bf16[1,256,2048]{2,1,0:T(8,128)(2,1)}), bf16[1,1024,2048]{2,1,0:T(8,128)(2,1)}) %all-gather.28.cloned.1.call-update) | async-done | bytes 4194320 | tf_op jit(solution)/shard_map/all_gather | solution.py:209
  958.9 37.7 %all-gather.42.cloned.1.call-done = bf16[1,1024,2048]{2,1,0:T(8,128)(2,1)} async-done(((bf16[1,1024,256]{2,1,0:T(8,128)(2,1)}), bf16[1,1024,2048]{2,1,0:T(8,128)(2,1)}) %all-gather.42.cloned.1.call-update) | async-done | bytes 4194320 | tf_op jit(solution)/shard_map/all_gather | solution.py:261
  996.6 11.7 fusion.279
  1010.2 13.3 fusion.152
  1023.8 12.6 convolution_bitcast_fusion.12
  1037.6 130.6 %reduce-scatter.23.cloned.1.call-done = f32[1,256,2048]{2,1,0:T(8,128)} async-done(((f32[1,1024,2048]{2,1,0:T(8,128)}), f32[1,256,2048]{2,1,0:T(8,128)}) %reduce-scatter.23.cloned.1.call-update) | async-done | bytes 2097168 | tf_op jit(solution)/shard_map/reduce_scatter | solution.py:213
  1170.9 144.7 %reduce-scatter.21.cloned.1.call-done = f32[1,256,2048]{2,1,0:T(8,128)} async-done(((f32[1,1024,2048]{2,1,0:T(8,128)}), f32[1,256,2048]{2,1,0:T(8,128)}) %reduce-scatter.21.cloned.1.call-update) | async-done | bytes 2097168 | tf_op jit(solution)/shard_map/reduce_scatter | solution.py:213
  1320.9 134.1 %while.56 = (s32[]{:T(128)}, f32[1,12,64,256]{3,2,1,0:T(8,128)S(1)}, f32[8,1,128,12,64]{2,4,3,1,0:T(8,128)}, f32[8,1,12,64,256]{4,3,2,1,0:T(8,128)}, f32[8,1,128...) while((s32[]{:T(128)}, ...), condition=%wide.region_17.18_spmd.clone, body=%wide.region_15.17_spmd.clone.sunk | while | flops 807816704 | bytes 6706174 | solution.py:103
  1483.6 11.9 multiply_reduce_fusion.3
  1495.6 11.2 psum.50
  1523.9 316.0 %while.57 = (s32[]{:T(128)}, f32[1,12,64,256]{3,2,1,0:T(8,128)S(1)}, f32[8,1,128,12,64]{2,0,4,3,1:T(8,128)}, f32[8,1,128,256]{3,2,0,1:T(8,128)}, f32[8,1,128,256...) while((s32[]{:T(128)}, ...), condition=%wide.region_30.31_spmd.clone, body=%wide.region_20.30_spmd.clone.sunk | while | flops 1968849920 | bytes 20446272 | solution.py:103
  1542.0 11.0 dynamic_update_slice.103
  1581.5 11.0 dynamic_update_slice.103
  1621.0 11.0 dynamic_update_slice.103
  1660.5 11.0 dynamic_update_slice.103
  1700.0 11.0 dynamic_update_slice.103
  1739.4 11.0 dynamic_update_slice.103
  1778.9 11.0 dynamic_update_slice.103
  1818.4 11.0 dynamic_update_slice.103
  1862.2 11.7 fusion.342
  1895.1 8.7 multiply_reduce_fusion.6
  1907.0 11.6 fusion.148
  1918.7 10.6 fusion.143
  1929.5 11.7 fusion.198
  1941.2 14.2 convolution_convert_fusion
  1984.8 11.0 copy.616
  2010.4 10.3 fusion.205
  2022.7 11.1 convolution_convert_fusion.1
  2040.2 32.1 %reduce-scatter.25.cloned.1.call-done = f32[1,256,2048]{2,1,0:T(8,128)} async-done(((f32[1,1024,2048]{2,1,0:T(8,128)}), f32[1,256,2048]{2,1,0:T(8,128)}) %reduce-scatter.25.cloned.1.call-update) | async-done | bytes 2097168 | tf_op jit(solution)/shard_map/reduce_scatter | solution.py:213
  2077.6 50.0 %reduce-scatter.41.cloned.1.call-done = bf16[1024,256]{1,0:T(8,128)(2,1)} async-done(((bf16[1024,2048]{1,0:T(8,128)(2,1)}), bf16[1024,256]{1,0:T(8,128)(2,1)}) %reduce-scatter.41.cloned.1.call-update) | async-done | bytes 524304 | tf_op jit(solution)/shard_map/reduce_scatter | solution.py:504
  2129.7 73.0 %reduce-scatter.39.cloned.1.call-done = bf16[256,2,1024]{2,0,1:T(8,128)(2,1)} async-done(((bf16[2048,2,1024]{2,0,1:T(8,128)(2,1)}), bf16[256,2,1024]{2,0,1:T(8,128)(2,1)}) %reduce-scatter.39.cloned.1.call-update) | async-done | bytes 1048592 | tf_op jit(solution)/shard_map/reduce_scatter | solution.py:501
  2207.4 24.0 all-reduce.30
  2231.4 107.5 %reduce-scatter.45.cloned.1.call-done = f32[16,4]{1,0:T(8,128)} async-done(((f32[512,4]{1,0:T(8,128)}), f32[16,4]{1,0:T(8,128)}) %reduce-scatter.45.cloned.1.call-update) | async-done | bytes 272
  2340.3 30.5 %reduce-scatter.33.cloned.1.call-done = bf16[256,12]{0,1:T(8,128)(2,1)} async-done(((bf16[2048,12]{0,1:T(8,128)(2,1)}), bf16[256,12]{0,1:T(8,128)(2,1)}) %reduce-scatter.33.cloned.1.call-update) | async-done | bytes 6160 | tf_op jit(solution)/shard_map/reduce_scatter | solution.py:492
  2372.1 38.0 %reduce-scatter.27.cloned.1.call-done = bf16[256,256]{1,0:T(8,128)(2,1)} async-done(((bf16[2048,256]{1,0:T(8,128)(2,1)}), bf16[256,256]{1,0:T(8,128)(2,1)}) %reduce-scatter.27.cloned.1.call-update) | async-done | bytes 131088 | tf_op jit(solution)/shard_map/reduce_scatter | solution.py:486
  2411.7 37.6 %reduce-scatter.35.cloned.1.call-done = bf16[256,256]{1,0:T(8,128)(2,1)} async-done(((bf16[256,2048]{1,0:T(8,128)(2,1)}), bf16[256,256]{1,0:T(8,128)(2,1)}) %reduce-scatter.35.cloned.1.call-update) | async-done | bytes 131088 | tf_op jit(solution)/shard_map/reduce_scatter | solution.py:495
  2450.9 145.7 %all-reduce.33.cloned.1.call-done = f32[1,2048,512]{2,0,1:T(1,128)} async-done(((f32[1,2048,512]{2,0,1:T(1,128)}), f32[1,2048,512]{2,0,1:T(1,128)}) %all-reduce.33.cloned.1.call-update) | async-done | bytes 4194320
  2598.1 46.8 %reduce-scatter.37.cloned.1.call-done = bf16[768,256]{1,0:T(8,128)(2,1)} async-done(((bf16[768,2048]{1,0:T(8,128)(2,1)}), bf16[768,256]{1,0:T(8,128)(2,1)}) %reduce-scatter.37.cloned.1.call-update) | async-done | bytes 393232 | tf_op jit(solution)/shard_map/reduce_scatter | solution.py:498
  2646.8 63.6 %reduce-scatter.31.cloned.1.call-done = bf16[256,2,768]{2,0,1:T(8,128)(2,1)} async-done(((bf16[2048,2,768]{2,0,1:T(8,128)(2,1)}), bf16[256,2,768]{2,0,1:T(8,128)(2,1)}) %reduce-scatter.31.cloned.1.call-update) | async-done | bytes 786448 | tf_op jit(solution)/shard_map/reduce_scatter | solution.py:489
  2716.1 132.1 %reduce-scatter.43.cloned.1.call-done = f32[64,2]{1,0:T(8,128)} async-done(((f32[2048,2]{1,0:T(8,128)}), f32[64,2]{1,0:T(8,128)}) %reduce-scatter.43.cloned.1.call-update) | async-done | bytes 528
  2849.7 145.5 %reduce-scatter.29.cloned.1.call-done = f32[1,64,512]{2,1,0:T(8,128)} async-done(((f32[1,2048,512]{2,1,0:T(8,128)}), f32[1,64,512]{2,1,0:T(8,128)}) %reduce-scatter.29.cloned.1.call-update) | async-done | bytes 131088 | tf_op jit(solution)/shard_map/reduce_scatter | solution.py:519
  (1269 shorter events, 737.6 us)
Async XLA Ops:
  7.2 84.6 %copy-start.8 = (bf16[1,256,2048]{2,1,0:T(8,128)(2,1)S(1)}, bf16[1,256,2048]{2,1,0:T(8,128)(2,1)}, u32[]{:S(2)}) copy-start(bf16[1,256,2048]{2,1,0:T(8,128)(2,1)} %param.25) | copy-start | bytes 3145732
  7.2 219.2 %all-gather.32.cloned.1.call-start = ((), (), s32[]{:S(2)}) async-start(), calls=%async_computation.32 | async-start | bytes 1179648 | tf_op jit(solution)/shard_map/all_gather | solution.py:255
  7.9 220.1 %all-gather.22.cloned.1.call-start = ((), (), s32[]{:S(2)}) async-start(), calls=%async_computation.15 | async-start | bytes 2162688 | tf_op jit(solution)/shard_map/all_gather | solution.py:245
  8.7 221.7 %all-gather.20.cloned.1.call-start = ((), (), s32[]{:S(2)}) async-start(), calls=%async_computation.14 | async-start | bytes 5242880 | tf_op jit(solution)/shard_map/all_gather | solution.py:209
  91.8 37.7 %copy-start.55 = (bf16[1,256,2,768]{3,2,1,0:T(2,128)(2,1)S(1)}, bf16[1,256,2,768]{3,2,1,0:T(2,128)(2,1)}, u32[]{:S(2)}) copy-start(bf16[1,256,2,768]{3,2,1,0:T(2,128)(2,1)} %param.31) | copy-start | bytes 2359300
  92.7 34.1 %copy-start.119 = (f32[256]{0:T(256)}, f32[256]{0:T(256)S(1)}, u32[]{:S(2)}) copy-start(f32[256]{0:T(256)S(1)} %get-tuple-element.1240) | copy-start | bytes 3076
  126.8 16.6 copy-start.130
  127.4 16.6 copy-start.142
  128.6 92.8 %copy-start.144 = (f32[1,12]{1,0:T(1,128)S(1)}, f32[1,12]{1,0:T(1,128)}, u32[]{:S(2)}) copy-start(f32[1,12]{1,0:T(1,128)} %param.36) | copy-start | bytes 148
  128.6 93.8 %copy-start.139 = (f32[1,768]{1,0:T(1,128)S(1)}, f32[1,768]{1,0:T(1,128)}, u32[]{:S(2)}) copy-start(f32[1,768]{1,0:T(1,128)} %param.39) | copy-start | bytes 9220
  128.7 139.8 %all-gather.24.cloned.1.call-start = ((), (), s32[]{:S(2)}) async-start(), calls=%async_computation.16 | async-start | bytes 2162688 | tf_op jit(solution)/shard_map/all_gather | solution.py:246
  129.2 186.0 %all-gather.36.cloned.1.call-start = ((), (), s32[]{:S(2)}) async-start(), calls=%async_computation.34 | async-start | bytes 7077888 | tf_op jit(solution)/shard_map/all_gather | solution.py:256
  130.5 447.1 %all-gather.38.cloned.1.call-start = ((), (), s32[]{:S(2)}) async-start(), calls=%async_computation.35 | async-start | bytes 3538944 | tf_op jit(solution)/shard_map/all_gather | solution.py:259
  131.1 456.2 %all-gather.34.cloned.1.call-start = ((), (), s32[]{:S(2)}) async-start(), calls=%async_computation.33 | async-start | bytes 1179648 | tf_op jit(solution)/shard_map/all_gather | solution.py:258
  131.8 605.7 %reduce-scatter.19.cloned.1.call-start = ((), (), s32[]{:S(2)}) async-start(), calls=%async_computation.17 | async-start | bytes 10485760 | tf_op jit(solution)/shard_map/reduce_scatter | solution.py:213
  133.6 194.5 %copy-start.70 = (f32[1,1024]{1,0:T(1,128)}, f32[1,1024]{1,0:T(1,128)S(1)}, u32[]{:S(2)}) copy-start(f32[1,1024]{1,0:T(1,128)S(1)} %get-tuple-element.1236) | copy-start | bytes 12292
  133.6 194.5 %copy-start.72 = (f32[1,1024]{1,0:T(1,128)}, f32[1,1024]{1,0:T(1,128)S(1)}, u32[]{:S(2)}) copy-start(f32[1,1024]{1,0:T(1,128)S(1)} %get-tuple-element.1237) | copy-start | bytes 12292
  133.6 194.5 %copy-start.74 = (f32[1,1024]{1,0:T(1,128)}, f32[1,1024]{1,0:T(1,128)S(1)}, u32[]{:S(2)}) copy-start(f32[1,1024]{1,0:T(1,128)S(1)} %get-tuple-element.1238) | copy-start | bytes 12292
  133.7 96.7 %copy-start.134 = (f32[64]{0:T(128)}, f32[64]{0:T(128)S(1)}, u32[]{:S(2)}) copy-start(f32[64]{0:T(128)S(1)} %multiply_power_fusion) | copy-start | bytes 772
  133.7 147.3 %copy-start.88 = (f32[1024]{0:T(1024)}, f32[1024]{0:T(1024)S(1)}, u32[]{:S(2)}) copy-start(f32[1024]{0:T(1024)S(1)} %iota_convert_fusion) | copy-start | bytes 12292
  134.4 95.9 %copy-start.132 = (f32[12]{0:T(128)}, f32[12]{0:T(128)S(1)}, u32[]{:S(2)}) copy-start(f32[12]{0:T(128)S(1)} %exponential_bitcast_fusion) | copy-start | bytes 148
  221.4 52.3 %copy-start.111 = (f32[512]{0:T(512)}, f32[512]{0:T(512)S(1)}, u32[]{:S(2)}) copy-start(f32[512]{0:T(512)S(1)} %get-tuple-element.1076) | copy-start | bytes 6148
  221.4 52.3 %copy-start.113 = (f32[512]{0:T(512)}, f32[512]{0:T(512)S(1)}, u32[]{:S(2)}) copy-start(f32[512]{0:T(512)S(1)} %get-tuple-element.1078) | copy-start | bytes 6148
  221.4 52.3 %copy-start.115 = (f32[512]{0:T(512)}, f32[512]{0:T(512)S(1)}, u32[]{:S(2)}) copy-start(f32[512]{0:T(512)S(1)} %get-tuple-element.1079) | copy-start | bytes 6148
  221.4 52.3 %copy-start.117 = (f32[512]{0:T(512)}, f32[512]{0:T(512)S(1)}, u32[]{:S(2)}) copy-start(f32[512]{0:T(512)S(1)} %get-tuple-element.1077) | copy-start | bytes 6148
  225.2 58.3 %copy-start.33 = (f32[1024,64]{0,1:T(8,128)}, f32[1024,64]{0,1:T(8,128)S(1)}, u32[]{:S(2)}) copy-start(f32[1024,64]{0,1:T(8,128)S(1)} %get-tuple-element.1233) | copy-start | bytes 786436
  226.3 58.0 %copy-start.25 = (pred[512,1024]{0,1:T(8,128)(4,1)}, pred[512,1024]{0,1:T(8,128)(4,1)S(1)}, u32[]{:S(2)}) copy-start(pred[512,1024]{0,1:T(8,128)(4,1)S(1)} %fusion.277) | copy-start | bytes 1572868
  560.8 16.8 copy-start.107
  577.5 929.3 %copy-start.92 = (f32[1,1024]{1,0:T(1,128)}, f32[1,1024]{1,0:T(1,128)S(1)}, u32[]{:S(2)}) copy-start(f32[1,1024]{1,0:T(1,128)S(1)} %add_rsqrt_fusion) | copy-start | bytes 12292
  595.7 199.5 %all-gather.40.cloned.1.call-start = ((), (), s32[]{:S(2)}) async-start(), calls=%async_computation.36 | async-start | bytes 9437184 | tf_op jit(solution)/shard_map/all_gather | solution.py:260
  598.1 141.7 %copy-start.79 = (f32[2048]{0:T(1024)S(1)}, f32[2048]{0:T(1024)}, u32[]{:S(2)}) copy-start(f32[2048]{0:T(1024)} %get-tuple-element.1074) | copy-start | bytes 24580
  598.2 279.8 %all-gather.26.cloned.1.call-start = ((), (), s32[]{:S(2)}) async-start(), calls=%async_computation.18 | async-start | bytes 5242880 | tf_op jit(solution)/shard_map/all_gather | solution.py:209
  741.0 217.9 %all-gather.28.cloned.1.call-start = ((), (), s32[]{:S(2)}) async-start(), calls=%async_computation.20 | async-start | bytes 5242880 | tf_op jit(solution)/shard_map/all_gather | solution.py:209
  741.8 254.8 %all-gather.42.cloned.1.call-start = ((), (), s32[]{:S(2)}) async-start(), calls=%async_computation.37 | async-start | bytes 4718592 | tf_op jit(solution)/shard_map/all_gather | solution.py:261
  742.3 425.8 %reduce-scatter.23.cloned.1.call-start = ((), (), s32[]{:S(2)}) async-start(), calls=%async_computation.21 | async-start | bytes 10485760 | tf_op jit(solution)/shard_map/reduce_scatter | solution.py:213
  1023.5 292.1 %reduce-scatter.21.cloned.1.call-start = ((), (), s32[]{:S(2)}) async-start(), calls=%async_computation.19 | async-start | bytes 10485760 | tf_op jit(solution)/shard_map/reduce_scatter | solution.py:213
  1036.4 426.3 %all-gather.30.cloned.1.call-start = ((), (), s32[]{:S(2)}) async-start(), calls=%async_computation.22 | async-start | bytes 5242880 | tf_op jit(solution)/shard_map/all_gather | solution.py:209
  1320.9 751.4 %reduce-scatter.25.cloned.1.call-start = ((), (), s32[]{:S(2)}) async-start(), calls=%async_computation.23 | async-start | bytes 10485760 | tf_op jit(solution)/shard_map/reduce_scatter | solution.py:213
  1462.6 44.2 %copy-start.103 = (f32[1024]{0:T(1024)}, f32[1024]{0:T(1024)S(1)}, u32[]{:S(2)}) copy-start(f32[1024]{0:T(1024)S(1)} %multiply_multiply_fusion.7) | copy-start | bytes 12292
  1523.9 316.0 %copy-start.71 = (f32[1,1024]{1,0:T(1,128)S(1)}, f32[1,1024]{1,0:T(1,128)}, u32[]{:S(2)}) copy-start(f32[1,1024]{1,0:T(1,128)} %copy-done.70) | copy-start | bytes 12292
  1523.9 316.0 %copy-start.73 = (f32[1,1024]{1,0:T(1,128)S(1)}, f32[1,1024]{1,0:T(1,128)}, u32[]{:S(2)}) copy-start(f32[1,1024]{1,0:T(1,128)} %copy-done.72) | copy-start | bytes 12292
  1905.4 13.3 copy-start.35
  1929.3 198.3 %reduce-scatter.41.cloned.1.call-start = ((), (), s32[]{:S(2)}) async-start(), calls=%async_computation.31 | async-start | bytes 4718592 | tf_op jit(solution)/shard_map/reduce_scatter | solution.py:504
  1941.2 261.5 %reduce-scatter.39.cloned.1.call-start = ((), (), s32[]{:S(2)}) async-start(), calls=%async_computation.30 | async-start | bytes 9437184 | tf_op jit(solution)/shard_map/reduce_scatter | solution.py:501
  1955.4 383.5 %reduce-scatter.45.cloned.1.call-start = ((), (), s32[]{:S(2)}) async-start(), calls=%async_computation.39 | async-start | bytes 270336
  1956.4 414.4 %reduce-scatter.33.cloned.1.call-start = ((), (), s32[]{:S(2)}) async-start(), calls=%async_computation.27 | async-start | bytes 73728 | tf_op jit(solution)/shard_map/reduce_scatter | solution.py:492
  1970.5 439.5 %reduce-scatter.27.cloned.1.call-start = ((), (), s32[]{:S(2)}) async-start(), calls=%async_computation.24 | async-start | bytes 1179648 | tf_op jit(solution)/shard_map/reduce_scatter | solution.py:486
  1975.3 473.9 %reduce-scatter.35.cloned.1.call-start = ((), (), s32[]{:S(2)}) async-start(), calls=%async_computation.28 | async-start | bytes 1179648 | tf_op jit(solution)/shard_map/reduce_scatter | solution.py:495
  1980.0 616.5 %all-reduce.33.cloned.1.call-start = ((), (), s32[]{:S(2)}) async-start(), calls=%async_computation.40 | async-start | bytes 8388608
  1995.8 649.1 %reduce-scatter.37.cloned.1.call-start = ((), (), s32[]{:S(2)}) async-start(), calls=%async_computation.29 | async-start | bytes 3538944 | tf_op jit(solution)/shard_map/reduce_scatter | solution.py:498
  2020.7 689.7 %reduce-scatter.31.cloned.1.call-start = ((), (), s32[]{:S(2)}) async-start(), calls=%async_computation.26 | async-start | bytes 7077888 | tf_op jit(solution)/shard_map/reduce_scatter | solution.py:489
  2033.8 814.5 %reduce-scatter.43.cloned.1.call-start = ((), (), s32[]{:S(2)}) async-start(), calls=%async_computation.38 | async-start | bytes 1081344
  2036.5 35.8 %copy-start.9 = (bf16[1,256,2048]{2,1,0:T(8,128)(2,1)S(1)}, bf16[1,256,2048]{2,1,0:T(8,128)(2,1)}, u32[]{:S(2)}) copy-start(bf16[1,256,2048]{2,1,0:T(8,128)(2,1)} %param.25) | copy-start | bytes 3145732
  2036.5 35.8 %copy-start.78 = (f32[2048]{0:T(1024)S(1)}, f32[2048]{0:T(1024)}, u32[]{:S(2)}) copy-start(f32[2048]{0:T(1024)} %copy-done.77) | copy-start | bytes 24580
  2036.5 35.8 %copy-start.120 = (f32[256]{0:T(256)S(1)}, f32[256]{0:T(256)}, u32[]{:S(2)}) copy-start(f32[256]{0:T(256)} %copy-done.119) | copy-start | bytes 3076
  2039.1 35.4 %copy-start.110 = (f32[2048]{0:T(1024)S(1)}, f32[2048]{0:T(1024)}, u32[]{:S(2)}) copy-start(f32[2048]{0:T(1024)} %get-tuple-element.1068) | copy-start | bytes 24580
  2076.4 918.7 %reduce-scatter.29.cloned.1.call-start = ((), (), s32[]{:S(2)}) async-start(), calls=%async_computation.25 | async-start | bytes 4325376 | tf_op jit(solution)/shard_map/reduce_scatter | solution.py:519
  2129.7 77.4 %copy-start.121 = (f32[768]{0:T(1024)S(1)}, f32[768]{0:T(1024)}, u32[]{:S(2)}) copy-start(f32[768]{0:T(1024)} %get-tuple-element.1169) | copy-start | bytes 9220
  2129.7 77.6 %copy-start.138 = (f32[768]{0:T(1024)S(1)}, f32[768]{0:T(1024)}, u32[]{:S(2)}) copy-start(f32[768]{0:T(1024)} %get-tuple-element.1060) | copy-start | bytes 9220
  2129.7 77.7 %copy-start.143 = (f32[12]{0:T(128)S(1)}, f32[12]{0:T(128)}, u32[]{:S(2)}) copy-start(f32[12]{0:T(128)} %get-tuple-element.1228) | copy-start | bytes 148
  2129.7 77.7 %copy-start.147 = (f32[1,12]{1,0:T(1,128)S(1)}, f32[1,12]{1,0:T(1,128)}, u32[]{:S(2)}) copy-start(f32[1,12]{1,0:T(1,128)} %param.34) | copy-start | bytes 148
  2129.7 77.7 %copy-start.141 = (f32[12]{0:T(128)S(1)}, f32[12]{0:T(128)}, u32[]{:S(2)}) copy-start(f32[12]{0:T(128)} %get-tuple-element.1171) | copy-start | bytes 148
  2598.1 116.1 %copy-start.20 = (f32[1,256,2048]{2,1,0:T(8,128)S(1)}, f32[1,256,2048]{2,1,0:T(8,128)}, u32[]{:S(2)}) copy-start(f32[1,256,2048]{2,1,0:T(8,128)} %reduce-scatter.25.cloned.1.call-done) | copy-start | bytes 6291460
  2598.1 116.1 %copy-start.137 = (f32[256]{0:T(256)S(1)}, f32[256]{0:T(256)}, u32[]{:S(2)}) copy-start(f32[256]{0:T(256)} %get-tuple-element.1239) | copy-start | bytes 3076
  (193 other events, 932.7 us)
Sparse Core Ops, SparseCore 0:
  9.9 26.5 all-gather.31
  39.4 56.6 all-gather.21
  128.8 81.7 all-gather.19
  213.3 55.0 all-gather.23
  270.8 44.3 all-gather.35
  316.9 32.8 all-gather.37
  351.7 23.5 all-gather.33
  595.8 141.7 reduce-scatter.18
  740.1 55.1 all-gather.39
  797.2 80.7 all-gather.25
  879.6 79.2 all-gather.27
  960.6 35.9 all-gather.41
  1023.7 144.4 reduce-scatter.22
  1170.4 145.1 reduce-scatter.20
  1321.0 81.4 all-gather.29
  1929.4 142.8 reduce-scatter.24
  2075.5 52.0 reduce-scatter.40
  2131.3 71.3 reduce-scatter.38
  2205.5 133.3 reduce-scatter.44
  2342.6 28.0 reduce-scatter.32
  2373.9 36.0 reduce-scatter.26
  2413.2 35.9 reduce-scatter.34
  2454.8 141.7 all-reduce.32
  2599.8 45.0 reduce-scatter.36
  2648.7 61.7 reduce-scatter.30
  2712.5 135.6 reduce-scatter.42
  2851.1 144.0 reduce-scatter.28
where the time goes:
time: 3020 us; the launch traced here: 3000 us
  waiting for transfers between devices  1620 us (54%)
  local copies, waits for them, and re-layouts  490 us (16%)
  matrix products  440 us (15%)
  other arithmetic  205 us (7%)
  blocking collectives  204 us (7%)
    reduce_scatter x4, waiting for transfers between devices, scatter_tokens(): lax.psum_scatter(partial_sum, 'tensor', scatter_dimension=1, tiled=True)  447 us
    unnamed x30, waiting for transfers between devices  390 us
    dynamic_update_slice x56, local copies, waits for them, and re-layouts, ssd_scan(): lax.scan(jax.checkpoint(ssd_block), initial, (by_blocks(x_conv), by_block...  198 us
    all_gather x4, waiting for transfers between devices, gather_tokens(): return lax.all_gather(pieces, 'tensor', axis=1, tiled=True)  149 us
    reduce_scatter x1, waiting for transfers between devices, local(): lax.psum_scatter(shared_stack[1], ('dp', 'tensor'), scatter_dimension=1,...  145 us
    all_gather x1, blocking collectives, local(): lax.all_gather(norm_gains, ('dp', 'tensor'), axis=2, tiled=True)  81.2 us
    dot_general x32, matrix products, ssd_block(): jnp.einsum('ijh,jhp->ihp', decays * c_dot_b[:, :, None], scaled_x, precis...  78.1 us
    reduce_scatter x1, waiting for transfers between devices, local(): lax.psum_scatter(grads_here[5].astype(jnp.bfloat16), 'dp', scatter_dimens...  73 us
  transfers between devices with their start and end apart: 27, of which 21 were waited for; matrix products, arithmetic and copies ran while one was open for 21% of the time, Pallas kernels for 0%

commit v1 on v0

v1 whole, which is shorter than its diff:
```python
from functools import partial

import jax
import jax.numpy as jnp
import numpy as np
from jax import lax
from jax.experimental import pallas as pl
from jax.experimental.pallas import tpu as pltpu
from jax.sharding import PartitionSpec as P

QUERY_HEADS = 8
KEY_VALUE_HEADS = 2
HEAD_SIZE = 128
HM = 48
P_SIZE = 64
LANES = 128
CHUNK = 128
NORM_EPS = 1e-05
ROPE_BASE = 100000000000.0
MASK_FILL = -1e30
F32 = jnp.float32
BF16 = jnp.bfloat16
NN = (((1,), (0,)), ((), ()))
NT = (((1,), (1,)), ((), ()))
TN = (((0,), (0,)), ((), ()))
VMEM_LIMIT = 48 * 1024 * 1024


def dot(left, right, dims=NN):
    return lax.dot_general(left, right, dims, preferred_element_type=F32)


def dot_exact(left, right):
    return lax.dot_general(
        left, right, NN, precision=lax.Precision.HIGHEST, preferred_element_type=F32
    )


def sigmoid(v):
    return 1.0 / (1.0 + jnp.exp(-v))


def send_dp(value, mask):
    size = lax.axis_size("dp")
    return lax.ppermute(value, "dp", [(i, i ^ mask) for i in range(size)])


def dp_gather(rows, *earlier):
    chips = lax.axis_size("dp") // 2
    if earlier:
        rows = after(rows, *earlier)
    mine = [rows] + [send_dp(rows, 2 * k) for k in range(1, chips)]
    mine = jnp.concatenate(mine, axis=0)
    return jnp.concatenate([mine, send_dp(mine, 1)], axis=0), mine


def dp_scatter(grad):
    chips = lax.axis_size("dp") // 2
    half = grad.shape[0] // 2
    block = half // chips
    other = send_dp(grad[half:], 1)
    pair = (grad[:half].astype(F32) + other.astype(F32)).astype(grad.dtype)
    total = pair[:block].astype(F32)
    for k in range(1, chips):
        total = total + send_dp(pair[k * block : (k + 1) * block], 2 * k).astype(F32)
    return total


def dp_sum(value):
    chips = lax.axis_size("dp") // 2
    value = value + send_dp(value, 1)
    total = value
    for k in range(1, chips):
        total = total + send_dp(value, 2 * k)
    return total


def send_z(value, shift):
    size = lax.axis_size("tensor")
    return lax.ppermute(value, "tensor", [(i, (i + shift) % size) for i in range(size)])


def z_gather_direct(rows):
    size = lax.axis_size("tensor")
    me = lax.axis_index("tensor")
    count = rows.shape[0]
    out = jnp.zeros((size * count,) + rows.shape[1:], rows.dtype)
    pieces = [rows] + [send_z(rows, k) for k in range(1, size)]
    for k, piece in enumerate(pieces):
        out = lax.dynamic_update_slice_in_dim(out, piece, lax.rem(me - k + size, size) * count, 0)
    return out


def z_scatter_direct(total):
    size = lax.axis_size("tensor")
    me = lax.axis_index("tensor")
    count = total.shape[0] // size
    mine = lax.dynamic_slice_in_dim(total, me * count, count, 0).astype(F32)
    for k in range(1, size):
        piece = lax.dynamic_slice_in_dim(total, lax.rem(me + k, size) * count, count, 0)
        mine = mine + send_z(piece, k).astype(F32)
    return mine


def z_gather(rows):
    size = lax.axis_size("tensor")
    me = lax.axis_index("tensor")
    count = rows.shape[0]
    from_left, from_right = [], []
    right = left = rows
    for s in range(size - 1):
        right = lax.ppermute(right, "tensor", [(i, i + 1) for i in range(s, size - 1)])
        left = lax.ppermute(left, "tensor", [(i, i - 1) for i in range(1, size - s)])
        from_left.append(right)
        from_right.append(left)
    out = jnp.zeros((size * count,) + rows.shape[1:], rows.dtype)
    out = lax.dynamic_update_slice_in_dim(out, rows, me * count, 0)
    for d in range(1, size):
        piece = from_left[d - 1] + from_right[size - d - 1]
        out = lax.dynamic_update_slice_in_dim(out, piece, lax.rem(me - d + size, size) * count, 0)
    return out


def z_scatter(total):
    size = lax.axis_size("tensor")
    me = lax.axis_index("tensor")
    count = total.shape[0] // size

    def part(offset):
        index = jnp.clip(me + offset, 0, size - 1)
        return lax.dynamic_slice_in_dim(total, index * count, count, 0)

    right = left = None
    for s in range(size - 1):
        d = size - 1 - s
        to_right, to_left = part(d), part(-d)
        if s:
            to_right = (to_right.astype(F32) + right.astype(F32)).astype(total.dtype)
            to_left = (to_left.astype(F32) + left.astype(F32)).astype(total.dtype)
        right = lax.ppermute(to_right, "tensor", [(i, i + 1) for i in range(s + 1)])
        left = lax.ppermute(to_left, "tensor", [(i, i - 1) for i in range(size - 1 - s, size)])
    return part(0).astype(F32) + right.astype(F32) + left.astype(F32)


def z_sum(value):
    size = lax.axis_size("tensor")
    total = value
    for k in range(1, size):
        total = total + send_z(value, k)
    return total


def block_order(j, chips):
    return 2 * lax.rem(j, chips) + lax.div(j, chips)


def place_of(mask, chips):
    return (mask & 1) * chips + lax.shift_right_logical(mask, 1)


def permute_kernel(me_ref, in_ref, out_ref):
    out_ref[...] = in_ref[...]


def permute_blocks(value, me, count, forward):
    chips = count // 2
    rows, width = value.shape
    block = width // count

    def source(j, me_ref):
        if forward:
            return (0, me_ref[0] ^ block_order(j, chips))
        return (0, place_of(me_ref[0] ^ j, chips))

    return pl.pallas_call(
        permute_kernel,
        grid_spec=pltpu.PrefetchScalarGridSpec(
            num_scalar_prefetch=1,
            grid=(count,),
            in_specs=[pl.BlockSpec((rows, block), source)],
            out_specs=pl.BlockSpec((rows, block), lambda j, me_ref: (0, j)),
        ),
        out_shape=jax.ShapeDtypeStruct(value.shape, value.dtype),
        cost_estimate=pl.CostEstimate(
            flops=0, bytes_accessed=2 * value.size * value.dtype.itemsize, transcendentals=0
        ),
        name="permute_blocks",
    )(me, value)


def norm_kernel(count, me_ref, x_ref, gain_ref, out_ref):
    chips = count // 2
    width = x_ref.shape[1]
    block = width // count
    x = x_ref[...].astype(F32)
    factor = lax.rsqrt(jnp.sum(x * x, axis=1, keepdims=True) * (1.0 / width) + NORM_EPS)
    for j in range(count):
        source = me_ref[0] ^ (2 * (j % chips) + j // chips)
        columns = pl.ds(pl.multiple_of(source * block, block), block)
        here = slice(j * block, (j + 1) * block)
        out = x_ref[:, columns].astype(F32) * factor * gain_ref[:, here]
        out_ref[:, here] = out.astype(BF16)


def norm_permuted(value, gain, me, count):
    rows, width = value.shape
    block = min(256, rows)
    return pl.pallas_call(
        partial(norm_kernel, count),
        grid_spec=pltpu.PrefetchScalarGridSpec(
            num_scalar_prefetch=1,
            grid=(rows // block,),
            in_specs=[
                pl.BlockSpec((block, width), lambda i, me_ref: (i, 0)),
                pl.BlockSpec((1, width), lambda i, me_ref: (0, 0)),
            ],
            out_specs=pl.BlockSpec((block, width), lambda i, me_ref: (i, 0)),
        ),
        out_shape=jax.ShapeDtypeStruct(value.shape, BF16),
        compiler_params=pltpu.CompilerParams(vmem_limit_bytes=VMEM_LIMIT),
        cost_estimate=pl.CostEstimate(
            flops=4 * value.size, bytes_accessed=4 * value.size, transcendentals=rows
        ),
        name="norm_permuted",
    )(me, value, gain)


def rotary_rows(length):
    half = HEAD_SIZE // 2
    freqs = np.float32(ROPE_BASE) ** (
        -np.arange(half).astype(np.float32) * np.float32(2.0) / np.float32(HEAD_SIZE)
    )
    angles = np.arange(length).astype(np.float32)[:, None] * freqs.astype(np.float32)[None, :]
    cosine, sine = np.cos(angles), np.sin(angles)
    return (
        np.concatenate([cosine, cosine], axis=1).astype(np.float32),
        np.concatenate([-sine, sine], axis=1).astype(np.float32),
    )


def rotate(value, cosine, sine):
    return value * cosine + pltpu.roll(value, HEAD_SIZE // 2, 1) * sine


def attention_probs(q_ref, keys, cos_ref, sin_ref, allowed, start, stop):
    query = rotate(q_ref[start:stop, :], cos_ref[start:stop, :], sin_ref[start:stop, :])
    query = query.astype(BF16)
    scores = dot(query, keys, NT) * (HEAD_SIZE**-0.5)
    scores = jnp.where(allowed, scores, MASK_FILL)
    raised = jnp.exp(scores - jnp.max(scores, axis=1, keepdims=True))
    return query, raised * (1.0 / jnp.sum(raised, axis=1, keepdims=True))


def attention_mask(aux_ref, segr_ref, start, stop):
    rows = start + lax.broadcasted_iota(jnp.int32, (stop - start, stop), 0)
    cols = lax.broadcasted_iota(jnp.int32, (stop - start, stop), 1)
    return (aux_ref[start:stop, 0:1] == segr_ref[0:1, :stop]) & (rows >= cols)


def attention_forward_kernel(heads, block, *refs):
    q_refs = refs[:heads]
    k_ref, v_ref, cos_ref, sin_ref, aux_ref, segr_ref, out_ref = refs[heads:]
    length = k_ref.shape[0]
    keys = rotate(k_ref[...], cos_ref[...], sin_ref[...]).astype(BF16)
    vals = v_ref[...].astype(BF16)
    for start in range(0, length, block):
        stop = start + block
        allowed = attention_mask(aux_ref, segr_ref, start, stop)
        for h in range(heads):
            _, probs = attention_probs(
                q_refs[h], keys[:stop], cos_ref, sin_ref, allowed, start, stop
            )
            out = dot(probs.astype(BF16), vals[:stop])
            out_ref[start:stop, h * HEAD_SIZE : (h + 1) * HEAD_SIZE] = out.astype(BF16)


def attention_backward_kernel(heads, block, *refs):
    q_refs = refs[:heads]
    k_ref, v_ref, cos_ref, sin_ref, aux_ref, segr_ref, do_ref, out_ref, dk, dv = refs[heads:]
    length = k_ref.shape[0]
    scale = HEAD_SIZE**-0.5
    keys = rotate(k_ref[...], cos_ref[...], sin_ref[...]).astype(BF16)
    vals = v_ref[...].astype(BF16)
    dk[...] = jnp.zeros_like(dk)
    dv[...] = jnp.zeros_like(dv)
    for start in range(0, length, block):
        stop = start + block
        allowed = attention_mask(aux_ref, segr_ref, start, stop)
        for h in range(heads):
            query, probs = attention_probs(
                q_refs[h], keys[:stop], cos_ref, sin_ref, allowed, start, stop
            )
            given = do_ref[start:stop, h * HEAD_SIZE : (h + 1) * HEAD_SIZE].astype(BF16)
            d_probs = dot(given, vals[:stop], NT)
            delta = jnp.sum(probs * d_probs, axis=1, keepdims=True)
            d_scores = (probs * (d_probs - delta)).astype(BF16)
            d_query = dot(d_scores, keys[:stop]) * scale
            d_query = rotate(d_query, cos_ref[start:stop, :], -sin_ref[start:stop, :])
            out_ref[start:stop, h * HEAD_SIZE : (h + 1) * HEAD_SIZE] = d_query.astype(BF16)
            dk[:stop, :] += dot(d_scores, query, TN)
            dv[:stop, :] += dot(probs.astype(BF16), given, TN)
    d_keys = rotate(dk[...] * scale, cos_ref[...], -sin_ref[...])
    out_ref[:, heads * HEAD_SIZE : (heads + 1) * HEAD_SIZE] = d_keys.astype(BF16)
    out_ref[:, (heads + 1) * HEAD_SIZE :] = dv[...].astype(BF16)


def attention_call(kernel, name, panel, first, heads, tables, aux, segr, extra, width, scratch):
    length = panel.shape[0]

    def column(index):
        return pl.BlockSpec((length, HEAD_SIZE), lambda i: (0, index))

    def whole(array):
        return pl.BlockSpec(array.shape, lambda i: (0, 0))

    specs = [column(first // HEAD_SIZE + h) for h in range(heads + 2)]
    operands = [*tables, aux, segr]
    specs += [whole(a) for a in operands]
    if extra is not None:
        specs.append(pl.BlockSpec((length, heads * HEAD_SIZE), lambda i: (0, 0)))
        operands.append(extra)
    return pl.pallas_call(
        partial(kernel, heads, min(256, length)),
        grid=(1,),
        in_specs=specs,
        out_specs=pl.BlockSpec((length, width), lambda i: (0, 0)),
        out_shape=jax.ShapeDtypeStruct((length, width), BF16),
        scratch_shapes=scratch,
        compiler_params=pltpu.CompilerParams(vmem_limit_bytes=VMEM_LIMIT),
        cost_estimate=pl.CostEstimate(
            flops=(16 if extra is not None else 8) * heads * length * length * HEAD_SIZE,
            bytes_accessed=4 * length * 12 * HEAD_SIZE,
            transcendentals=heads * length * length,
        ),
        name=name,
    )(*([panel] * (heads + 2)), *operands)


def split_pair(value):
    high = value.astype(BF16)
    return high, (value - high.astype(F32)).astype(BF16)


def widen(value, expand_ref):
    high, rest = split_pair(value)
    return dot(jnp.concatenate([high, rest], axis=1), expand_ref[...])


def by_head(value, reduce_ref):
    high, rest = split_pair(value)
    return dot(high, reduce_ref[...]) + dot(rest, reduce_ref[...])


def conv_rows(current, halo, pad, taps_ref, aux):
    rows = current.shape[0]
    pad[0:8, :] = halo
    pad[8 : 8 + rows, :] = current
    out = taps_ref[3:4, :] * current
    for k in range(1, 4):
        out = out + taps_ref[3 - k : 4 - k, :] * (pad[8 - k : 8 - k + rows, :] * aux[:, k : k + 1])
    return out


def head_scalars(dt_raw, par_ref, lower):
    biased = dt_raw + par_ref[1:2, :]
    step = jnp.maximum(biased, 0.0) + jnp.log1p(jnp.exp(-jnp.abs(biased)))
    log_decay = -step * jnp.exp(par_ref[0:1, :])
    cumulative = dot_exact(lower, log_decay)
    return biased, step, log_decay, cumulative


def triangle(rows, flip):
    i = lax.broadcasted_iota(jnp.int32, (rows, rows), 0)
    j = lax.broadcasted_iota(jnp.int32, (rows, rows), 1)
    return (i <= j) if flip else (i >= j)


def mamba_forward_kernel(
    cols,
    p_ref,
    halo_ref,
    aux_ref,
    segr_ref,
    cx_ref,
    cbc_ref,
    par_ref,
    dskip_ref,
    mgain_ref,
    expand_ref,
    gm_ref,
    sq_ref,
    y_ref,
    st_ref,
    state,
    pad_x,
    pad_bc,
):
    width, states = cols["width"], cols["states"]
    rows = p_ref.shape[0]
    x0, bc0, dt0 = cols["x"], cols["bc"], cols["dt"]

    @pl.when(pl.program_id(0) == 0)
    def _():
        state[...] = jnp.zeros_like(state)

    aux = aux_ref[...]
    u_x = conv_rows(
        p_ref[:, x0 : x0 + width], halo_ref[:, x0 : x0 + width], pad_x, cx_ref, aux
    )
    x_conv = u_x * sigmoid(u_x)
    u_bc = conv_rows(
        p_ref[:, bc0 : bc0 + 2 * states], halo_ref[:, bc0 : bc0 + 2 * states], pad_bc, cbc_ref, aux
    )
    bc = (u_bc * sigmoid(u_bc)).astype(BF16)
    keys, query = bc[:, :states], bc[:, states:]
    lower = triangle(rows, False)
    _, step, _, cum = head_scalars(p_ref[:, dt0 : dt0 + LANES], par_ref, lower.astype(F32))
    cum_t = cum.T
    last = cum[rows - 1 : rows, :]
    entering = jnp.exp(cum) * aux[:, 7:8]
    leaving = jnp.exp(last - cum) * aux[:, 8:9]
    wide = widen(jnp.concatenate([step, entering, leaving], axis=0), expand_ref)
    step_w, enter_w, leave_w = wide[:rows], wide[rows : 2 * rows], wide[2 * rows :]
    xs = x_conv * step_w
    xs_low = xs.astype(BF16)
    mask = lower & (aux[:, 0:1] == segr_ref[0:1, :])
    c_dot_b = dot(query, keys, NT)
    held = state[...]
    held_low = held.astype(BF16)
    st_ref[0] = held_low
    carried = dot(query, held_low) * enter_w
    lane = lax.broadcasted_iota(jnp.int32, (rows, LANES), 1)
    parts = []
    for pair in range(width // LANES):
        pair_x = xs_low[:, pair * LANES : (pair + 1) * LANES]
        sides = []
        for e in range(2):
            h = 2 * pair + e
            gap = cum[:, h : h + 1] - cum_t[h : h + 1, :]
            decay = jnp.exp(jnp.where(mask, gap, MASK_FILL))
            sides.append(dot((decay * c_dot_b).astype(BF16), pair_x))
        parts.append(jnp.where(lane < P_SIZE, sides[0], sides[1]))
    y = jnp.concatenate(parts, axis=1) + carried + dskip_ref[0:1, :] * x_conv
    state[...] = held * enter_w[rows - 1 : rows, :] + dot(
        keys, (leave_w * xs).astype(BF16), TN
    )
    z = p_ref[:, :width]
    gated = y * (z * sigmoid(z))
    y_ref[...] = y
    gm_ref[...] = (gated * mgain_ref[0:1, :]).astype(BF16)
    sq_ref[...] = jnp.broadcast_to(jnp.sum(gated * gated, axis=1, keepdims=True), sq_ref.shape)


def mamba_backward_kernel(
    cols,
    p_ref,
    halo_ref,
    aux_ref,
    segr_ref,
    cx_ref,
    cbc_ref,
    par_ref,
    dskip_ref,
    mgain_ref,
    expand_ref,
    reduce_ref,
    y_ref,
    st_ref,
    db_ref,
    aux2_ref,
    dqkv_ref,
    dp_ref,
    gw_ref,
    gcx_ref,
    gcbc_ref,
    gh_ref,
    d_state,
    pad_x,
    pad_bc,
    fut_x,
    fut_bc,
):
    width, states = cols["width"], cols["states"]
    rows = p_ref.shape[0]
    x0, q0, bc0, dt0 = cols["x"], cols["q"], cols["bc"], cols["dt"]
    first_step = pl.program_id(0) == 0

    @pl.when(first_step)
    def _():
        d_state[...] = jnp.zeros_like(d_state)
        gw_ref[...] = jnp.zeros_like(gw_ref)
        gcx_ref[...] = jnp.zeros_like(gcx_ref)
        gcbc_ref[...] = jnp.zeros_like(gcbc_ref)
        gh_ref[...] = jnp.zeros_like(gh_ref)
        fut_x[...] = jnp.zeros_like(fut_x)
        fut_bc[...] = jnp.zeros_like(fut_bc)

    aux = aux_ref[...]
    u_x = conv_rows(
        p_ref[:, x0 : x0 + width], halo_ref[:, x0 : x0 + width], pad_x, cx_ref, aux
    )
    sig_x = sigmoid(u_x)
    x_conv = u_x * sig_x
    u_bc = conv_rows(
        p_ref[:, bc0 : bc0 + 2 * states], halo_ref[:, bc0 : bc0 + 2 * states], pad_bc, cbc_ref, aux
    )
    sig_bc = sigmoid(u_bc)
    bc = (u_bc * sig_bc).astype(BF16)
    keys, query = bc[:, :states], bc[:, states:]
    lower = triangle(rows, False).astype(F32)
    biased, step, log_decay, cum = head_scalars(p_ref[:, dt0 : dt0 + LANES], par_ref, lower)
    cum_t = cum.T
    last = cum[rows - 1 : rows, :]
    entering = jnp.exp(cum) * aux[:, 7:8]
    leaving = jnp.exp(last - cum) * aux[:, 8:9]
    wide = widen(jnp.concatenate([step, entering, leaving], axis=0), expand_ref)
    step_w, enter_w, leave_w = wide[:rows], wide[rows : 2 * rows], wide[2 * rows :]
    xs = x_conv * step_w
    xs_low = xs.astype(BF16)

    y = y_ref[...]
    z = p_ref[:, :width]
    sig_z = sigmoid(z)
    silu_z = z * sig_z
    gated = y * silu_z
    rstd = aux2_ref[:, 0:1]
    inner = aux2_ref[:, 1:2]
    d_mixed = db_ref[:, db_ref.shape[1] - width :]
    g_mgain = jnp.sum(d_mixed * (gated * rstd), axis=0, keepdims=True)
    d_gated = rstd * (d_mixed * mgain_ref[0:1, :]) - gated * inner
    d_y = d_gated * silu_z
    dp_ref[:, :width] = (d_gated * y * (sig_z * (1.0 + z * (1.0 - sig_z)))).astype(BF16)
    gw_ref[0:1, :] += g_mgain
    gw_ref[1:2, :] += jnp.sum(d_y * x_conv, axis=0, keepdims=True)

    dy_low = d_y.astype(BF16)
    held_low = st_ref[0]
    d_next = d_state[...]
    d_next_low = d_next.astype(BF16)
    entered_dy = (enter_w * d_y).astype(BF16)
    left_xs = (leave_w * xs).astype(BF16)
    from_next = leave_w * dot(keys, d_next_low)
    mask_t = triangle(rows, True) & (aux[:, 0:1] == segr_ref[0:1, :])
    b_dot_c = dot(keys, query, NT)
    lane = lax.broadcasted_iota(jnp.int32, (rows, LANES), 1)
    d_gram = jnp.zeros((rows, rows), F32)
    parts = []
    for pair in range(width // LANES):
        pair_dy = dy_low[:, pair * LANES : (pair + 1) * LANES]
        pair_x = xs_low[:, pair * LANES : (pair + 1) * LANES]
        sides = []
        for e in range(2):
            h = 2 * pair + e
            gap = cum_t[h : h + 1, :] - cum[:, h : h + 1]
            decay = jnp.exp(jnp.where(mask_t, gap, MASK_FILL))
            sides.append(dot((decay * b_dot_c).astype(BF16), pair_dy))
            inside = (lane < P_SIZE) if e == 0 else (lane >= P_SIZE)
            only = jnp.where(inside, pair_x, jnp.zeros_like(pair_x))
            d_gram = d_gram + decay * dot(only, pair_dy, NT)
        parts.append(jnp.where(lane < P_SIZE, sides[0], sides[1]))
    d_xs_inner = jnp.concatenate(parts, axis=1)
    d_xs = d_xs_inner + from_next
    d_gram = d_gram.astype(BF16)
    d_keys = dot(d_gram, query) + dot(left_xs, d_next_low, NT)
    d_query = dot(d_gram, keys, TN) + dot(entered_dy, held_low, NT)
    keep_w = enter_w[rows - 1 : rows, :]
    d_state[...] = dot(query, entered_dy, TN) + keep_w * d_next

    y_scan = y - dskip_ref[0:1, :] * x_conv
    pairs = dy_low.astype(F32) * y_scan - xs_low.astype(F32) * d_xs_inner
    d_cum = by_head(pairs - xs * from_next, reduce_ref)
    at_last = jnp.sum(xs * from_next, axis=0, keepdims=True) + keep_w * jnp.sum(
        held_low.astype(F32) * d_next, axis=0, keepdims=True
    )
    at_last = by_head(jnp.broadcast_to(at_last, (8, width)), reduce_ref)[0:1, :]
    d_log = dot_exact(triangle(rows, True).astype(F32), d_cum) + at_last
    d_step = by_head(x_conv * d_xs, reduce_ref) - d_log * jnp.exp(par_ref[0:1, :])
    d_dt = d_step * sigmoid(biased)
    dp_ref[:, dt0 : dt0 + LANES] = d_dt.astype(BF16)
    gh_ref[0:1, :] += jnp.sum(d_log * log_decay, axis=0, keepdims=True)
    gh_ref[1:2, :] += jnp.sum(d_dt, axis=0, keepdims=True)

    d_ux = (dskip_ref[0:1, :] * d_y + step_w * d_xs) * (sig_x * (1.0 + u_x * (1.0 - sig_x)))
    d_conv = jnp.concatenate([d_keys, d_query], axis=1)
    d_ubc = d_conv * (sig_bc * (1.0 + u_bc * (1.0 - sig_bc)))
    for grad, pad, fut, taps_ref, g_ref, c0 in (
        (d_ux, pad_x, fut_x, cx_ref, gcx_ref, x0),
        (d_ubc, pad_bc, fut_bc, cbc_ref, gcbc_ref, bc0),
    ):
        size = grad.shape[1]
        g_ref[3:4, :] += jnp.sum(grad * pad[8 : 8 + rows, :], axis=0, keepdims=True)
        for k in range(1, 4):
            shifted = pad[8 - k : 8 - k + rows, :] * aux[:, k : k + 1]
            g_ref[3 - k : 4 - k, :] += jnp.sum(grad * shifted, axis=0, keepdims=True)
        fut[0:rows, :] = grad
        d_in = taps_ref[3:4, :] * grad
        for k in range(1, 4):
            d_in = d_in + taps_ref[3 - k : 4 - k, :] * (
                fut[k : k + rows, :] * aux[:, 3 + k : 4 + k]
            )
        fut[rows : rows + 8, :] = grad[0:8, :]
        dp_ref[:, c0 : c0 + size] = d_in.astype(BF16)
    dp_ref[:, q0 : q0 + dqkv_ref.shape[1]] = dqkv_ref[...]


def head_maps(width):
    expand = (np.arange(width)[None, :] // P_SIZE == np.arange(LANES)[:, None]).astype(np.float32)
    return (
        jnp.asarray(np.concatenate([expand, expand], axis=0), BF16),
        jnp.asarray(expand.T, BF16),
    )


def mamba_specs(panel, chunk, chunk_of):
    length, total = panel.shape

    def rows(array):
        return pl.BlockSpec((chunk, array.shape[1]), lambda i: (chunk_of(i), 0))

    def fixed(array):
        return pl.BlockSpec(array.shape, lambda i: (0, 0))

    halo = pl.BlockSpec(
        (8, total), lambda i: (jnp.maximum(chunk_of(i) * (chunk // 8) - 1, 0), 0)
    )
    seg = pl.BlockSpec((8, chunk), lambda i: (0, chunk_of(i)))
    return rows, fixed, halo, seg


def mamba_forward(cols, panel, aux, segr, cx, cbc, par, dskip, mgain):
    length = panel.shape[0]
    width, states = cols["width"], cols["states"]
    chunk = min(CHUNK, length)
    chunks = length // chunk
    expand, _ = head_maps(width)
    rows, fixed, halo, seg = mamba_specs(panel, chunk, lambda i: i)
    small = [cx, cbc, par, dskip, mgain, expand]
    shapes = [
        jax.ShapeDtypeStruct((length, width), BF16),
        jax.ShapeDtypeStruct((length, LANES), F32),
        jax.ShapeDtypeStruct((length, width), F32),
        jax.ShapeDtypeStruct((chunks, states, width), BF16),
    ]
    return pl.pallas_call(
        partial(mamba_forward_kernel, cols),
        grid=(chunks,),
        in_specs=[rows(panel), halo, rows(aux), seg] + [fixed(a) for a in small],
        out_specs=[
            rows(shapes[0]),
            rows(shapes[1]),
            rows(shapes[2]),
            pl.BlockSpec((1, states, width), lambda i: (i, 0, 0)),
        ],
        out_shape=shapes,
        scratch_shapes=[
            pltpu.VMEM((states, width), F32),
            pltpu.VMEM((chunk + 8, width), F32),
            pltpu.VMEM((chunk + 8, 2 * states), F32),
        ],
        compiler_params=pltpu.CompilerParams(vmem_limit_bytes=VMEM_LIMIT),
        cost_estimate=pl.CostEstimate(
            flops=2 * length * width * (2 * states + 4 * chunk) * 4,
            bytes_accessed=4 * (panel.size + 3 * length * width),
            transcendentals=length * width * 4,
        ),
        name="mamba_forward",
    )(panel, panel, aux, segr, *small)


def mamba_backward(
    cols, panel, aux, segr, cx, cbc, par, dskip, mgain, y, held, d_branch_in, aux2, d_qkv
):
    length = panel.shape[0]
    width, states = cols["width"], cols["states"]
    chunk = min(CHUNK, length)
    chunks = length // chunk
    expand, reduce = head_maps(width)
    rows, fixed, halo, seg = mamba_specs(panel, chunk, lambda i: chunks - 1 - i)
    small = [cx, cbc, par, dskip, mgain, expand, reduce]
    sums = [(8, width), (8, width), (8, 2 * states), (8, LANES)]
    return pl.pallas_call(
        partial(mamba_backward_kernel, cols),
        grid=(chunks,),
        in_specs=[rows(panel), halo, rows(aux), seg]
        + [fixed(a) for a in small]
        + [
            rows(y),
            pl.BlockSpec((1, states, width), lambda i: (chunks - 1 - i, 0, 0)),
            rows(d_branch_in),
            rows(aux2),
            rows(d_qkv),
        ],
        out_specs=[rows(panel)] + [pl.BlockSpec(s, lambda i: (0, 0)) for s in sums],
        out_shape=[jax.ShapeDtypeStruct(panel.shape, BF16)]
        + [jax.ShapeDtypeStruct(s, F32) for s in sums],
        scratch_shapes=[
            pltpu.VMEM((states, width), F32),
            pltpu.VMEM((chunk + 8, width), F32),
            pltpu.VMEM((chunk + 8, 2 * states), F32),
            pltpu.VMEM((chunk + 8, width), F32),
            pltpu.VMEM((chunk + 8, 2 * states), F32),
        ],
        compiler_params=pltpu.CompilerParams(vmem_limit_bytes=VMEM_LIMIT),
        cost_estimate=pl.CostEstimate(
            flops=2 * length * width * (4 * states + 8 * chunk) * 4,
            bytes_accessed=4 * (panel.size + 3 * length * width),
            transcendentals=length * width * 4,
        ),
        name="mamba_backward",
    )(panel, panel, aux, segr, *small, y, held, d_branch_in, aux2, d_qkv)


def pad_rows(value, rows):
    return jnp.pad(value, ((0, rows - value.shape[0]), (0, 0)))


def segment_tables(segment, chunk):
    length = segment.shape[0]
    seg = segment.astype(F32)
    columns = [seg]
    for k in range(1, 4):
        before = jnp.concatenate([jnp.full((k,), -1.0, F32), seg[:-k]])
        columns.append((before == seg).astype(F32))
    for k in range(1, 4):
        after = jnp.concatenate([seg[k:], jnp.full((k,), -1.0, F32)])
        columns.append((after == seg).astype(F32))
    blocks = seg.reshape(-1, chunk)
    ends = blocks[:, -1:]
    prior = jnp.concatenate([jnp.full((1, 1), -1.0, F32), ends[:-1]], axis=0)
    columns.append((blocks == prior).astype(F32).reshape(-1))
    columns.append((blocks == ends).astype(F32).reshape(-1))
    stacked = jnp.stack(columns + [jnp.zeros_like(seg)] * (16 - len(columns)), axis=0)
    return jnp.pad(stacked.T, ((0, 0), (0, LANES - 16))), jnp.broadcast_to(seg, (8, length))


def rms_factor(hidden):
    return lax.rsqrt(jnp.mean(hidden * hidden, axis=-1, keepdims=True) + NORM_EPS)


def norm_backward(hidden, gain, d_normed, grad_h):
    factor = rms_factor(hidden)
    weighted = gain * d_normed
    inner_mean = jnp.mean(weighted * hidden, axis=-1, keepdims=True)
    return grad_h + factor * weighted - hidden * factor**3 * inner_mean, factor


def after(value, *earlier):
    return lax.optimization_barrier((value, *earlier))[0]


def local(
    inputs,
    cotangent,
    seg_ids,
    norm_gains,
    w_q,
    key_value_weight,
    w_zx,
    w_bc,
    w_dt,
    a_log,
    dt_bias,
    d_skip,
    conv_x,
    conv_bc,
    m_gain,
    w_ao,
    w_mo,
    w_gu,
    w_down,
):
    members = lax.axis_size("dp")
    size_z = lax.axis_size("tensor")
    me_z = lax.axis_index("tensor")
    me = lax.axis_index("dp").astype(jnp.int32).reshape(1)
    length = seg_ids.shape[1]
    model = inputs.shape[2]
    block = model // members
    owned = key_value_weight.shape[1]
    heads = w_q.shape[2] // HEAD_SIZE
    kv_head = me_z * heads // (QUERY_HEADS // KEY_VALUE_HEADS)
    width = w_zx.shape[3]
    m_heads = w_dt.shape[2]
    states2 = w_bc.shape[2]
    hidden_units = w_gu.shape[3]
    cols = {"width": width, "states": states2 // 2, "x": width, "q": 2 * width}
    cols["k"] = cols["q"] + heads * HEAD_SIZE
    cols["v"] = cols["k"] + HEAD_SIZE
    cols["bc"] = cols["v"] + HEAD_SIZE
    cols["dt"] = cols["bc"] + states2
    att_width = heads * HEAD_SIZE

    taps = conv_bc.shape[2]
    lane_rows = 2 * KEY_VALUE_HEADS * HEAD_SIZE + states2
    shares = [norm_gains.shape[2], taps]
    tiny = jnp.concatenate(
        [
            jnp.pad(norm_gains[0], ((0, 0), (0, lane_rows - shares[0]))),
            jnp.pad(conv_bc[0], ((0, 10), (0, lane_rows - shares[1]))),
        ],
        axis=0,
    )
    shared = jnp.concatenate([key_value_weight[0], w_bc[0]], axis=1)
    shared = jnp.concatenate([tiny, shared], axis=0)
    shared = z_gather_direct(shared).reshape(size_z, 16 + owned, lane_rows)
    x_all = z_gather(after(inputs[0], shared))
    tiny = shared[:, :16]
    shared = shared[:, 16:].reshape(block, lane_rows)
    gain_blocks = jnp.swapaxes(tiny[:, :2, : shares[0]], 0, 1).reshape(2, block)
    tap_blocks = jnp.swapaxes(tiny[:, 2:6, :taps], 0, 1).reshape(4, size_z * taps)
    tiny = jnp.concatenate(
        [
            jnp.pad(gain_blocks, ((0, 0), (0, max(block, LANES) - block))),
            jnp.pad(tap_blocks, ((0, 10), (0, max(block, LANES) - size_z * taps))),
        ],
        axis=0,
    )
    kv_cols = [
        lax.dynamic_slice_in_dim(shared, (base + kv_head) * HEAD_SIZE, HEAD_SIZE, 1)
        for base in (0, KEY_VALUE_HEADS)
    ]
    panel_rest = jnp.concatenate(
        [w_q[0]]
        + kv_cols
        + [
            shared[:, 2 * KEY_VALUE_HEADS * HEAD_SIZE :],
            jnp.pad(w_dt[0], ((0, 0), (0, LANES - m_heads))),
        ],
        axis=1,
    )
    w_zx_all, sent = dp_gather(w_zx[0].reshape(block, 2 * width))
    w_rest, sent = dp_gather(panel_rest, sent)
    w_a = jnp.concatenate([w_zx_all, w_rest], axis=1)
    tiny, _ = dp_gather(tiny)
    tiny = tiny.astype(F32).reshape(members, 16, -1)
    gains = jnp.swapaxes(tiny[:, :2, :block], 0, 1).reshape(2, model)
    tap_blocks = tiny[:, 2:6, : size_z * taps]
    order = np.array([2 * (j % (members // 2)) + j // (members // 2) for j in range(members)])
    owner = jnp.asarray(order, jnp.int32) ^ me[0]
    hit = (jnp.arange(members)[:, None] == owner[None, :]).astype(F32)
    convbc_all = jnp.sum(hit[:, :, None, None] * tap_blocks[None], axis=1)
    convbc_all = jnp.swapaxes(convbc_all, 0, 1).reshape(4, states2)
    w_b, sent = dp_gather(jnp.concatenate([w_ao[0], w_mo[0]], axis=0).T, sent)
    w_c, sent = dp_gather(w_gu[0].reshape(block, 2 * hidden_units), sent)
    w_d, sent = dp_gather(w_down[0].T, sent)

    x_local = permute_blocks(inputs[0], me, members, True).astype(F32)
    cot_low = permute_blocks(cotangent[0], me, members, True)
    cot = cot_low.astype(F32)
    gain1, gain2 = gains[0:1], gains[1:2]

    chunk = min(CHUNK, length)
    aux, segr = segment_tables(seg_ids[0], chunk)
    tables = [jnp.asarray(t) for t in rotary_rows(length)]
    cx = pad_rows(conv_x[0], 8)
    cbc = pad_rows(convbc_all, 8)
    par = jnp.pad(
        jnp.stack([a_log[0], dt_bias[0]]), ((0, 6), (0, LANES - m_heads))
    )
    dskip = jnp.broadcast_to(jnp.repeat(d_skip[0], P_SIZE)[None, :], (8, width))
    mgain = jnp.broadcast_to(m_gain[0][None, :], (8, width))

    normed1 = norm_permuted(x_all, gain1, me, members)
    panel = dot(normed1, w_a)
    d_out = lax.all_gather(after(cot_low, x_all), "tensor", axis=0, tiled=True)
    attended = attention_call(
        attention_forward_kernel,
        "attention_forward",
        panel,
        cols["q"],
        heads,
        tables,
        aux,
        segr,
        None,
        att_width,
        [],
    )
    gm, squares, y_out, held = mamba_forward(
        cols, panel, aux, segr, cx, cbc, par, dskip, mgain
    )
    squares = z_sum(squares[:, 0].reshape(-1, LANES)).reshape(length, 1)
    rstd = lax.rsqrt(squares / (HM * P_SIZE) + NORM_EPS)
    branch = dot(attended, w_b[:, :att_width], NT) + rstd * dot(gm, w_b[:, att_width:], NT)
    h_mid = x_local + z_scatter(branch.astype(BF16))

    normed2 = z_gather((h_mid * rms_factor(h_mid) * gain2).astype(BF16))
    gate_up = dot(normed2, w_c)
    gate, up = gate_up[:, :hidden_units], gate_up[:, hidden_units:]
    sig_gate = sigmoid(gate)
    silu_gate = gate * sig_gate
    act = (silu_gate * up).astype(BF16)
    d_act = dot(d_out, w_d)
    d_gu = jnp.concatenate(
        [d_act * up * (sig_gate * (1.0 + gate * (1.0 - sig_gate))), d_act * silu_gate], axis=1
    ).astype(BF16)
    d_norm2 = z_scatter(dot(d_gu, w_c, NT).astype(BF16))
    grad_mid, factor2 = norm_backward(h_mid, gain2, d_norm2, cot)
    g_gain2 = jnp.sum(d_norm2 * h_mid * factor2, axis=0)
    d_branch = z_gather(grad_mid.astype(BF16))
    ffn = lax.psum_scatter(
        after(dot(act, w_d, NT).astype(BF16), d_branch), "tensor", scatter_dimension=0, tiled=True
    ).astype(F32)
    hidden_out = permute_blocks((h_mid + ffn).astype(BF16), me, members, False)
    g_c = dp_scatter(dot(normed2, d_gu, TN).astype(BF16))
    g_d = dp_scatter(dot(d_out, act, TN).astype(BF16))

    d_branch = after(d_branch, g_c, g_d)
    d_b = dot(d_branch, w_b)
    mixed = (gm.astype(F32) * rstd).astype(BF16)
    g_b = dp_scatter(
        dot(d_branch, jnp.concatenate([attended, mixed], axis=1), TN).astype(BF16)
    )
    inner = jnp.sum(d_b[:, att_width:] * gm.astype(F32), axis=1)
    inner = z_sum(inner.reshape(-1, LANES)).reshape(length, 1)
    aux2 = jnp.pad(
        jnp.concatenate([rstd, rstd**3 * inner / (HM * P_SIZE)], axis=1),
        ((0, 0), (0, LANES - 2)),
    )
    d_qkv = attention_call(
        attention_backward_kernel,
        "attention_backward",
        panel,
        cols["q"],
        heads,
        tables,
        aux,
        segr,
        d_b,
        att_width + 2 * HEAD_SIZE,
        [pltpu.VMEM((length, HEAD_SIZE), F32), pltpu.VMEM((length, HEAD_SIZE), F32)],
    )
    d_panel, g_wide, g_cx, g_cbc, g_heads = mamba_backward(
        cols, panel, aux, segr, cx, cbc, par, dskip, mgain, y_out, held, d_b, aux2, d_qkv
    )
    d_norm1_part = dot(d_panel, w_a, NT)
    d_norm1 = z_scatter(d_norm1_part.astype(BF16))
    g_gain1 = jnp.sum(d_norm1_part * (normed1.astype(F32) / gain1), axis=0)
    grad_in, _ = norm_backward(x_local, gain1, d_norm1, grad_mid)
    input_grad = permute_blocks(grad_in, me, members, False)

    by_dp = [
        g_heads[0:2],
        jnp.pad(g_wide[1].reshape(m_heads, P_SIZE).sum(axis=1), (0, LANES - m_heads))[None],
        g_cx[:4].reshape(-1, LANES),
        g_wide[0].reshape(-1, LANES),
    ]
    counts = [v.shape[0] for v in by_dp]
    by_dp = jnp.concatenate(by_dp, axis=0)
    g_convbc = z_sum(g_cbc)[:4].reshape(-1, LANES)
    by_dp = jnp.concatenate([by_dp, g_convbc], axis=0)
    by_dp = dp_sum(pad_rows(by_dp, -(-by_dp.shape[0] // 8) * 8))
    ends = np.cumsum(counts)
    g_alog, g_dtbias = by_dp[0:1, :m_heads], by_dp[1:2, :m_heads]
    g_dskip = by_dp[2:3, :m_heads]
    g_convx = by_dp[ends[1] : ends[2]].reshape(1, 4, width)
    g_mgain = by_dp[ends[2] : ends[3]].reshape(1, width)
    g_convbc = by_dp[ends[3] : ends[3] + 4 * states2 // LANES].reshape(4, states2)
    slot = lax.axis_index("dp") * size_z + me_z
    g_convbc = lax.dynamic_slice_in_dim(g_convbc, slot * taps, taps, 1)[None]

    g_a = dp_scatter(dot(normed1, d_panel, TN).astype(BF16))
    g_gain = dp_scatter(jnp.pad(jnp.stack([g_gain1, g_gain2], axis=1), ((0, 0), (0, 6))))
    g_q = g_a[:, cols["q"] : cols["k"]]
    g_zx = g_a[:, : 2 * width].reshape(1, block, 2, width)
    g_dt = g_a[:, cols["dt"] : cols["dt"] + m_heads]
    kv_part = jnp.zeros((block, 2 * KEY_VALUE_HEADS * HEAD_SIZE), F32)
    for base, name in ((0, "k"), (KEY_VALUE_HEADS, "v")):
        kv_part = lax.dynamic_update_slice_in_dim(
            kv_part,
            g_a[:, cols[name] : cols[name] + HEAD_SIZE],
            (base + kv_head) * HEAD_SIZE,
            1,
        )
    shared_grad = z_scatter_direct(
        jnp.concatenate(
            [kv_part, g_a[:, cols["bc"] : cols["dt"]], jnp.pad(g_gain, ((0, 0), (0, LANES - 8)))],
            axis=1,
        )
    )
    kv_total = 2 * KEY_VALUE_HEADS * HEAD_SIZE
    g_kv = shared_grad[:, :kv_total]
    g_bc = shared_grad[:, kv_total : kv_total + states2]
    g_gains = shared_grad[:, kv_total + states2 : kv_total + states2 + 2].T

    return (
        hidden_out[None],
        input_grad[None],
        g_gains[None],
        g_q[None],
        g_kv[None],
        g_zx,
        g_bc[None],
        g_dt[None],
        g_alog,
        g_dtbias,
        g_dskip,
        g_convx,
        g_convbc,
        g_mgain,
        g_b[:, :att_width].T[None],
        g_b[:, att_width:].T[None],
        g_c.reshape(1, block, 2, hidden_units),
        g_d.T[None],
    )


def solution(mesh):
    return jax.shard_map(
        local,
        mesh=mesh,
        in_specs=(
            P("dp", "tensor", None),
            P("dp", "tensor", None),
            P("dp", None),
            P(None, None, ("dp", "tensor")),
            P(None, "dp", "tensor"),
            P(None, ("dp", "tensor"), None),
            P(None, "dp", None, "tensor"),
            P(None, ("dp", "tensor"), None),
            P(None, "dp", "tensor"),
            P(None, "tensor"),
            P(None, "tensor"),
            P(None, "tensor"),
            P(None, None, "tensor"),
            P(None, None, ("dp", "tensor")),
            P(None, "tensor"),
            P(None, "tensor", "dp"),
            P(None, "tensor", "dp"),
            P(None, "dp", None, "tensor"),
            P(None, "tensor", "dp"),
        ),
        out_specs=(
            P("dp", "tensor", None),
            P("dp", "tensor", None),
            P(None, None, ("dp", "tensor")),
            P(None, "dp", "tensor"),
            P(None, ("dp", "tensor"), None),
            P(None, "dp", None, "tensor"),
            P(None, ("dp", "tensor"), None),
            P(None, "dp", "tensor"),
            P(None, "tensor"),
            P(None, "tensor"),
            P(None, "tensor"),
            P(None, None, "tensor"),
            P(None, None, ("dp", "tensor")),
            P(None, "tensor"),
            P(None, "tensor", "dp"),
            P(None, "tensor", "dp"),
            P(None, "dp", None, "tensor"),
            P(None, "tensor", "dp"),
        ),
        check_vma=False,
    )
```

time: 3020 us -> 1090 us (0.36)
  waiting for transfers between devices: 1620 us -> 415 us
  local copies, waits for them, and re-layouts: 490 us -> 119 us
  matrix products: 440 us -> 136 us
  starting transfers between devices: 2.82 us -> 212 us
  blocking collectives: 204 us -> 0 us
  other arithmetic: 205 us -> 94.1 us
  Pallas kernels: 0 us -> 87.4 us
    reduce_scatter x12 -> x1, waiting for transfers between devices: 932 us -> 0.01 us  [local(): lax.psum_scatter(after(dot(act, w_d, NT).astype(BF16), d_branch), 'tensor...]
    ppermute x0 -> x99, waiting for transfers between devices: none -> 415 us  [the longest x48 125 us: send_dp(): return lax.ppermute(value, 'dp', [(i, i ^ mask) for i in range(size)])]
    unnamed x30 -> x2, waiting for transfers between devices: 390 us -> 0.03 us
    dot_general x181 -> x13, matrix products: 440 us -> 136 us  [dot(): return lax.dot_general(left, right, dims, preferred_element_type=F32)]
    all_gather x12 -> x1, waiting for transfers between devices: 298 us -> 0.01 us  [local(): d_out = lax.all_gather(after(cot_low, x_all), 'tensor', axis=0, tiled=True)]
    ppermute x0 -> x99, starting transfers between devices: none -> 212 us  [the longest x15 69.9 us: send_z(): lax.ppermute(value, 'tensor', [(i, (i + shift) % size) for i in range(siz...]
    dynamic_update_slice x58 -> x6, local copies, waits for them, and re-layouts: 200 us -> 1.14 us  [the longest x1 1.06 us: z_gather(): out = lax.dynamic_update_slice_in_dim(out, rows, me * count, 0)]
    all_gather x3 -> x0, blocking collectives: 158 us -> none  [the longest x1 81.2 us: local(): lax.all_gather(norm_gains, ('dp', 'tensor'), axis=2, tiled=True)]
  transfers between devices with their start and end apart: 27 -> 101, of which waited for: 21 -> 37; matrix products, arithmetic and copies ran while one was open for 21% -> 25% of each run, Pallas kernels for 0% -> 8%
where the time goes in v1:
time: 1090 us; the launch traced here: 1080 us
  waiting for transfers between devices  415 us (38%)
  starting transfers between devices  212 us (19%)
  matrix products  136 us (12%)
  local copies, waits for them, and re-layouts  119 us (11%)
  other arithmetic  94.1 us (9%)
  Pallas kernels  87.4 us (8%)
  between operations  16.3 us (1%)
    dot_general x13, matrix products, dot(): return lax.dot_general(left, right, dims, preferred_element_type=F32)  136 us
    ppermute x48, waiting for transfers between devices, send_dp(): return lax.ppermute(value, 'dp', [(i, i ^ mask) for i in range(size)])  125 us
    ppermute x9, waiting for transfers between devices, z_gather(): lax.ppermute(left, 'tensor', [(i, i - 1) for i in range(1, size - s)])  114 us
    ppermute x9, waiting for transfers between devices, z_scatter(): right = lax.ppermute(to_right, 'tensor', [(i, i + 1) for i in range(s + 1)])  107 us
    ppermute x15, starting transfers between devices, send_z(): lax.ppermute(value, 'tensor', [(i, (i + shift) % size) for i in range(siz...  69.9 us
    unnamed x179, local copies, waits for them, and re-layouts  61.3 us
    ppermute x48, starting transfers between devices, send_dp(): return lax.ppermute(value, 'dp', [(i, i ^ mask) for i in range(size)])  55 us
    ppermute x9, starting transfers between devices, z_scatter(): right = lax.ppermute(to_right, 'tensor', [(i, i + 1) for i in range(s + 1)])  44 us
  transfers between devices with their start and end apart: 101, of which 37 were waited for; matrix products, arithmetic and copies ran while one was open for 25% of the time, Pallas kernels for 8%

profile of v1, /device:TPU:0, one launch (start us, length us, event | category | flops | bytes accessed | tf_op | source)
XLA Modules:
  0.0 1080.7 jit_solution(12756993882321130115)
XLA Ops:
  31.0 6.5 collective-permute-done.13
  39.9 13.7 %collective-permute-done.14 = bf16[256,1536]{1,0:T(8,128)(2,1)} collective-permute-done((bf16[256,1536]{1,0:T(8,128)(2,1)S(1)}, bf16[256,1536]{1,0:T(8,128)(2,1)}, u32[]{:S(2)}, u32[]{:S(2)}) %collective-permute-start.14) | collective-permute-done | bytes 786464 | tf_op jit(solution)/shard_map/ppermute | solution.py:45
  75.2 9.7 collective-permute-done.18
  95.6 5.9 collective-permute-done.5
  109.6 8.7 collective-permute-done.23
  121.2 7.2 collective-permute-done.6
  147.2 18.5 %fusion.1.refs_0_.refs_1_.refs_2_.refs_3_.p_ref.halo_ref = f32[1024,2688]{1,0:T(8,128)} fusion(bf16[1024,2048]{1,0:T(8,128)(2,1)S(1)} %norm_permuted.1, bf16[2048,1152]{1,0:T(8,128)(2,1)} %constant_dynamic-update-slice_fusion.16, bf16[2048,1536]{1,0:T(8,128)(2,1)} %constant_dynamic-update-slice_fusion.4), kind=kOutput, calls=%fused_computation.8 | convolution fusion | flops 11296309248 | bytes 26214400 | tf_op jit(solution)/shard_map/dot_general | solution.py:30
  165.8 14.0 %mamba_forward.1 = (bf16[1024,768]{1,0:T(8,128)(2,1)S(1)}, f32[1024,128]{1,0:T(8,128)S(1)}, f32[1024,768]{1,0:T(8,128)}, bf16[8,256,768]{2,1,0:T(8,128)(2,1)}) custom-call(f32[1024,2688]{1,0:T(8,128)} %fusion.1.refs_0_.refs_1_.refs_2_.refs_3_.p_ref.halo_ref, f32[1024,2688]{1,0:T(8,128)} %fusion.1.refs_0_.refs_1_.refs_2_.refs_3_.p_ref.halo_ref, ...), custom_call_target="tpu_custom_call" | custom-call | flops 6442450944 | bytes 20447232 | tf_op jit(solution)/shard_map/mamba_forward/pallas_call | solution.py:644
  180.1 14.1 %collective-permute-start.27 = (f32[8,128]{1,0:T(8,128)S(1)}, f32[8,128]{1,0:T(8,128)S(1)}, u32[]{:S(2)}, u32[]{:S(2)}) collective-permute-start(f32[8,128]{1,0:T(8,128)S(1)} %bitcast.177), channel_id=1, source_target_pairs={{0,3},{1,0},{2,1},{3,2},{4,7},{5,4},{6,5},{7,6},{8,11},{9,8},{10,9... | collective-permute-start | bytes 12296 | tf_op jit(solution)/shard_map/ppermute | solution.py:80
  195.2 6.0 attention_forward.1
  209.8 5.7 collective-permute-start.28
  217.2 17.5 %collective-permute-done.28 = bf16[256,2048]{1,0:T(8,128)(2,1)} collective-permute-done((bf16[256,2048]{1,0:T(8,128)(2,1)S(1)}, bf16[256,2048]{1,0:T(8,128)(2,1)}, u32[]{:S(2)}, u32[]{:S(2)}) %collective-permute-start.28) | collective-permute-done | bytes 1048608 | tf_op jit(solution)/shard_map/ppermute | solution.py:140
  236.6 5.5 collective-permute-start.29
  242.1 18.2 %collective-permute-done.29 = bf16[256,2048]{1,0:T(8,128)(2,1)} collective-permute-done((bf16[256,2048]{1,0:T(8,128)(2,1)S(1)}, bf16[256,2048]{1,0:T(8,128)(2,1)}, u32[]{:S(2)}, u32[]{:S(2)}) %collective-permute-start.29) | collective-permute-done | bytes 1048608 | tf_op jit(solution)/shard_map/ppermute | solution.py:140
  272.5 5.1 collective-permute-start.30
  281.8 12.2 %collective-permute-done.40 = bf16[256,2048]{1,0:T(8,128)(2,1)S(1)} collective-permute-done((bf16[256,2048]{1,0:T(8,128)(2,1)S(1)}, bf16[256,2048]{1,0:T(8,128)(2,1)S(1)}, u32[]{:S(2)}, u32[]{:S(2)}) %collective-permute-start.40) | collective-permute-done | bytes 1048608 | tf_op jit(solution)/shard_map/ppermute | solution.py:45
  295.1 17.4 %collective-permute-done.41 = bf16[256,2048]{1,0:T(8,128)(2,1)S(1)} collective-permute-done((bf16[256,2048]{1,0:T(8,128)(2,1)S(1)}, bf16[256,2048]{1,0:T(8,128)(2,1)S(1)}, u32[]{:S(2)}, u32[]{:S(2)}) %collective-permute-start.41) | collective-permute-done | bytes 1048608 | tf_op jit(solution)/shard_map/ppermute | solution.py:45
  318.2 5.2 permute_blocks.4
  335.2 5.2 permute_blocks.5
  340.5 8.6 collective-permute-done.45
  355.2 21.1 %collective-permute-done.35 = bf16[256,2048]{1,0:T(8,128)(2,1)} collective-permute-done((bf16[256,2048]{1,0:T(8,128)(2,1)}, bf16[256,2048]{1,0:T(8,128)(2,1)}, u32[]{:S(2)}, u32[]{:S(2)}) %collective-permute-start.35) | collective-permute-done | bytes 1048608 | tf_op jit(solution)/shard_map/ppermute | solution.py:113
  377.6 23.6 %collective-permute-done.34 = bf16[256,2048]{1,0:T(8,128)(2,1)S(1)} collective-permute-done((bf16[256,2048]{1,0:T(8,128)(2,1)}, bf16[256,2048]{1,0:T(8,128)(2,1)S(1)}, u32[]{:S(2)}, u32[]{:S(2)}) %collective-permute-start.34) | collective-permute-done | bytes 1048608 | tf_op jit(solution)/shard_map/ppermute | solution.py:112
  402.0 44.7 %collective-permute-done.36 = bf16[256,2048]{1,0:T(8,128)(2,1)S(1)} collective-permute-done((bf16[256,2048]{1,0:T(8,128)(2,1)}, bf16[256,2048]{1,0:T(8,128)(2,1)S(1)}, u32[]{:S(2)}, u32[]{:S(2)}) %collective-permute-start.36) | collective-permute-done | bytes 1048608 | tf_op jit(solution)/shard_map/ppermute | solution.py:113
  453.7 4.8 constant_dynamic-update-slice_fusion.34
  459.2 15.7 %collective-permute-done.37 = bf16[256,2048]{1,0:T(8,128)(2,1)S(1)} collective-permute-done((bf16[256,2048]{1,0:T(8,128)(2,1)S(1)}, bf16[256,2048]{1,0:T(8,128)(2,1)S(1)}, u32[]{:S(2)}, u32[]{:S(2)}) %collective-permute-start.37) | collective-permute-done | bytes 1048608 | tf_op jit(solution)/shard_map/ppermute | solution.py:113
  480.7 13.0 %fusion.46 = f32[1024,2048]{1,0:T(8,128)} fusion(bf16[1024,2048]{1,0:T(8,128)(2,1)} %add_dynamic-update-slice_fusion.3, bf16[2048,2048]{1,0:T(8,128)(2,1)S(1)} %copy-done.53), kind=kOutput, calls=%fused_computation.228 | convolution fusion | flops 8589934592 | bytes 20971520 | tf_op jit(solution)/shard_map/dot_general | solution.py:30
  493.8 13.1 %multiply_convert_fusion.1 = (bf16[1024,1024]{1,0:T(8,128)(2,1)S(1)}, bf16[1024,1024]{1,0:T(8,128)(2,1)S(1)}, bf16[1024,1024]{1,0:T(8,128)(2,1)}) fusion(f32[1024,2048]{1,0:T(8,128)} %fusion.46, bf16[1024,2048]{1,0:T(8,128)(2,1)} %all-gather.2.cloned.1.call-done, bf16[2048,1024]{0,1:T(8,128)(2,1)} %copy-done.57), kind=kOutput, calls=%fused_computation.13 | convolution fusion | flops 4310695936 | bytes 23068672 | tf_op jit(solution)/shard_map/dot_general | solution.py:30
  508.2 11.3 %convolution_convert_fusion.2 = bf16[1024,2048]{1,0:T(8,128)(2,1)S(1)} fusion(bf16[2048,2048]{1,0:T(8,128)(2,1)} %constant_dynamic-update-slice_fusion.34, bf16[1024,1024]{1,0:T(8,128)(2,1)S(1)} %get-tuple-element.156, bf16[1024,1024]{1,0:T(8,128)(2,1)S(1)} %get-tuple-element.155), kind=kOutput, calls=%fused_computation.19 | convolution fusion | flops 8600420352 | bytes 16777216 | tf_op jit(solution)/shard_map/dot_general | solution.py:30
  522.4 19.2 %collective-permute-done.48 = bf16[256,2048]{1,0:T(8,128)(2,1)S(1)} collective-permute-done((bf16[256,2048]{1,0:T(8,128)(2,1)S(1)}, bf16[256,2048]{1,0:T(8,128)(2,1)S(1)}, u32[]{:S(2)}, u32[]{:S(2)}) %collective-permute-start.48) | collective-permute-done | bytes 1048608 | tf_op jit(solution)/shard_map/ppermute | solution.py:140
  546.4 19.3 %collective-permute-done.49 = bf16[256,2048]{1,0:T(8,128)(2,1)S(1)} collective-permute-done((bf16[256,2048]{1,0:T(8,128)(2,1)S(1)}, bf16[256,2048]{1,0:T(8,128)(2,1)S(1)}, u32[]{:S(2)}, u32[]{:S(2)}) %collective-permute-start.49) | collective-permute-done | bytes 1048608 | tf_op jit(solution)/shard_map/ppermute | solution.py:140
  567.3 13.8 %convolution_convert_fusion.1 = bf16[2048,2048]{0,1:T(8,128)(2,1)} fusion(bf16[1024,2048]{1,0:T(8,128)(2,1)} %add_dynamic-update-slice_fusion.3, bf16[1024,1024]{1,0:T(8,128)(2,1)S(1)} %copy-done.73, bf16[1024,1024]{1,0:T(8,128)(2,1)S(1)} %copy-done.71), kind=kOutput, calls=%fused_computation.6 | convolution fusion | flops 8602517504 | bytes 16777216 | tf_op jit(solution)/shard_map/dot_general | solution.py:30
  581.2 4.9 slice.342
  586.1 5.0 collective-permute-start.50
  593.2 4.9 convolution_convert_fusion.4
  601.8 12.3 %collective-permute-done.50 = bf16[256,2048]{1,0:T(8,128)(2,1)S(1)} collective-permute-done((bf16[256,2048]{1,0:T(8,128)(2,1)S(1)}, bf16[256,2048]{1,0:T(8,128)(2,1)S(1)}, u32[]{:S(2)}, u32[]{:S(2)}) %collective-permute-start.50) | collective-permute-done | bytes 1048608 | tf_op jit(solution)/shard_map/ppermute | solution.py:140
  614.1 5.4 collective-permute-done.53
  630.3 5.4 collective-permute-start.67
  636.4 5.5 collective-permute-start.54
  641.9 10.8 collective-permute-done.55
  654.0 5.6 add_convert_fusion.1
  663.3 4.6 collective-permute-start.63
  670.2 8.5 collective-permute-done.56
  680.2 6.1 convolution_convert_fusion.5
  692.3 19.9 %collective-permute-done.62 = bf16[256,2048]{0,1:T(8,128)(2,1)} collective-permute-done((bf16[256,2048]{0,1:T(8,128)(2,1)}, bf16[256,2048]{0,1:T(8,128)(2,1)}, u32[]{:S(2)}, u32[]{:S(2)}) %collective-permute-start.62) | collective-permute-done | bytes 1048608 | tf_op jit(solution)/shard_map/ppermute | solution.py:45
  727.6 6.5 fusion.47.refs_8_.db_ref
  736.0 22.3 %collective-permute-start.70 = (f32[8,128]{1,0:T(8,128)S(1)}, f32[8,128]{1,0:T(8,128)S(1)}, u32[]{:S(2)}, u32[]{:S(2)}) collective-permute-start(f32[8,128]{1,0:T(8,128)S(1)} %bitcast.174), channel_id=1, source_target_pairs={{0,3},{1,0},{2,1},{3,2},{4,7},{5,4},{6,5},{7,6},{8,11},{9,8},{10,9... | collective-permute-start | bytes 12296 | tf_op jit(solution)/shard_map/ppermute | solution.py:80
  759.1 9.2 attention_backward.1.dqkv_ref
  769.4 7.2 convolution_convert_fusion.3
  782.4 32.6 %mamba_backward.1 = (bf16[1024,2688]{1,0:T(8,128)(2,1)}, f32[8,768]{1,0:T(8,128)S(1)}, f32[8,768]{1,0:T(8,128)S(1)}, f32[8,512]{1,0:T(8,128)S(1)}, f32[8,128]{1,0:T(8,128)S(1)}) custom-call(f32[1024,2688]{1,0:T(8,128)} %fusion.1.refs_0_.refs_1_.refs_2_.refs_3_.p_ref.halo_ref, f32[1024,2688]{1,0:T(8,128)} %fusion.1.refs_0_.refs_1_.refs_2_.refs_3_.p_ref.halo_ref, ...), custom_call_target="tpu_custom_call" | custom-call | flops 12884901888 | bytes 20447232 | tf_op jit(solution)/shard_map/mamba_backward/pallas_call | solution.py:681
  819.4 17.2 %convolution_convert_fusion = bf16[2048,2688]{1,0:T(8,128)(2,1)} fusion(bf16[1024,2048]{1,0:T(8,128)(2,1)S(1)} %copy-done.1, bf16[1024,2688]{1,0:T(8,128)(2,1)} %get-tuple-element.47), kind=kOutput, calls=%fused_computation | convolution fusion | flops 11279794176 | bytes 20709376 | tf_op jit(solution)/shard_map/dot_general | solution.py:30
  836.7 17.9 %multiply_reduce_fusion = (f32[2048]{0:T(1024)S(1)}, bf16[1024,2048]{1,0:T(8,128)(2,1)}) fusion(bf16[1024,2048]{1,0:T(8,128)(2,1)S(1)} %copy-done.1, f32[2048]{0:T(1024)S(1)} %bitcast.120, bf16[1024,2688]{1,0:T(8,128)(2,1)} %get-tuple-element.47, bf16[2048,1152]{1,0:T(8,128)(2,1)} %constant_dynamic-update-slice_fusion.16, ...), kind=kOutput, calls=%fused_computation.3 | convolution fusion | flops 11306792960 | bytes 24920064 | tf_op jit(solution)/shard_map/dot_general | solution.py:30
  854.6 5.3 slice.355
  863.2 5.3 collective-permute-start.71
  883.7 7.3 collective-permute-done.71
  897.6 5.4 collective-permute-start.72
  910.7 13.0 %collective-permute-done.72 = bf16[256,2048]{1,0:T(8,128)(2,1)} collective-permute-done((bf16[256,2048]{1,0:T(8,128)(2,1)S(1)}, bf16[256,2048]{1,0:T(8,128)(2,1)}, u32[]{:S(2)}, u32[]{:S(2)}) %collective-permute-start.72) | collective-permute-done | bytes 1048608 | tf_op jit(solution)/shard_map/ppermute | solution.py:140
  929.4 6.1 collective-permute-start.73
  941.6 5.5 add_convert_fusion
  958.4 21.8 %collective-permute-done.76 = bf16[256,2048]{1,0:T(8,128)(2,1)} collective-permute-done((bf16[256,2048]{1,0:T(8,128)(2,1)}, bf16[256,2048]{1,0:T(8,128)(2,1)}, u32[]{:S(2)}, u32[]{:S(2)}) %collective-permute-start.76) | collective-permute-done | bytes 1048608 | tf_op jit(solution)/shard_map/ppermute | solution.py:141
  987.1 5.6 permute_blocks.7
  992.7 19.7 %collective-permute-done.79 = bf16[256,2688]{1,0:T(8,128)(2,1)} collective-permute-done((bf16[256,2688]{1,0:T(8,128)(2,1)}, bf16[256,2688]{1,0:T(8,128)(2,1)}, u32[]{:S(2)}, u32[]{:S(2)}) %collective-permute-start.79) | collective-permute-done | bytes 1376288 | tf_op jit(solution)/shard_map/ppermute | solution.py:45
  1017.2 19.5 %collective-permute-start.87 = (f32[64,1152]{1,0:T(8,128)}, f32[64,1152]{1,0:T(8,128)}, u32[]{:S(2)}, u32[]{:S(2)}) collective-permute-start(f32[64,1152]{1,0:T(8,128)} %get-tuple-element.187), channel_id=1, source_target_pairs={{0,3},{1,0},{2,1},{3,2},{4,7},{5,4},{6,5},{7,6},{8,11},{9,8},{10,9... | collective-permute-start | bytes 884744 | tf_op jit(solution)/shard_map/ppermute | solution.py:80
  1044.4 17.4 %collective-permute-done.86 = f32[64,1152]{1,0:T(8,128)} collective-permute-done((f32[64,1152]{1,0:T(8,128)}, f32[64,1152]{1,0:T(8,128)}, u32[]{:S(2)}, u32[]{:S(2)}) %collective-permute-start.86) | collective-permute-done | bytes 294944 | tf_op jit(solution)/shard_map/ppermute | solution.py:80
  1068.5 5.2 permute_blocks.6
  (505 shorter events, 310.8 us)
Async XLA Ops:
  7.2 486.5 %all-gather.2.cloned.1.call-start = ((), (), s32[]{:S(2)}) async-start(), calls=%async_computation.1 | async-start | bytes 5242880 | tf_op jit(solution)/shard_map/all_gather | solution.py:865
  18.4 35.1 %collective-permute-start.14 = (bf16[256,1536]{1,0:T(8,128)(2,1)S(1)}, bf16[256,1536]{1,0:T(8,128)(2,1)}, u32[]{:S(2)}, u32[]{:S(2)}) collective-permute-start(bf16[256,1536]{1,0:T(8,128)(2,1)S(1)} %bitcast.134), channel_id=1, source_target_pairs={{0,16},{4,20},{8,24},{12,28},{16,0},{20,4},{24,8},{28,12},{1,17},{... | collective-permute-start | bytes 2359304 | tf_op jit(solution)/shard_map/ppermute | solution.py:45
  23.1 32.8 %collective-permute-start.15 = (bf16[256,1536]{1,0:T(8,128)(2,1)S(1)}, bf16[256,1536]{1,0:T(8,128)(2,1)}, u32[]{:S(2)}, u32[]{:S(2)}) collective-permute-start(bf16[256,1536]{1,0:T(8,128)(2,1)S(1)} %bitcast.136), channel_id=1, source_target_pairs={{0,24},{4,28},{8,16},{12,20},{16,8},{20,12},{24,0},{28,4},{1,25},{... | collective-permute-start | bytes 2359304 | tf_op jit(solution)/shard_map/ppermute | solution.py:45
  25.2 48.4 %collective-permute-start.4 = (bf16[256,2048]{1,0:T(8,128)(2,1)S(1)}, bf16[256,2048]{1,0:T(8,128)(2,1)}, u32[]{:S(2)}, u32[]{:S(2)}) collective-permute-start(bf16[256,2048]{1,0:T(8,128)(2,1)S(1)} %bitcast.125), channel_id=1, source_target_pairs={{1,0},{2,1},{3,2},{5,4},{6,5},{7,6},{9,8},{10,9},{11,10},{13,12},{... | collective-permute-start | bytes 3145736 | tf_op jit(solution)/shard_map/ppermute | solution.py:113
  26.8 35.0 %collective-permute-start.9 = (bf16[16,256]{1,0:T(8,128)(2,1)S(1)}, bf16[16,256]{1,0:T(8,128)(2,1)S(1)}, u32[]{:S(2)}, u32[]{:S(2)}) collective-permute-start(bf16[16,256]{1,0:T(8,128)(2,1)S(1)} %pad_maximum_fusion.8), channel_id=1, source_target_pairs={{0,8},{4,12},{8,0},{12,4},{16,24},{20,28},{24,16},{28,20},{1,9},{5... | collective-permute-start | bytes 24584 | tf_op jit(solution)/shard_map/ppermute | solution.py:45
  64.4 29.5 %collective-permute-start.3 = (bf16[256,2048]{1,0:T(8,128)(2,1)S(1)}, bf16[256,2048]{1,0:T(8,128)(2,1)}, u32[]{:S(2)}, u32[]{:S(2)}) collective-permute-start(bf16[256,2048]{1,0:T(8,128)(2,1)S(1)} %bitcast.126), channel_id=1, source_target_pairs={{0,1},{1,2},{2,3},{4,5},{5,6},{6,7},{8,9},{9,10},{10,11},{12,13},{... | collective-permute-start | bytes 3145736 | tf_op jit(solution)/shard_map/ppermute | solution.py:112
  73.7 27.8 %collective-permute-start.5 = (bf16[256,2048]{1,0:T(8,128)(2,1)}, bf16[256,2048]{1,0:T(8,128)(2,1)}, u32[]{:S(2)}, u32[]{:S(2)}) collective-permute-start(bf16[256,2048]{1,0:T(8,128)(2,1)} %collective-permute-done.4), channel_id=1, source_target_pairs={{1,0},{2,1},{5,4},{6,5},{9,8},{10,9},{13,12},{14,13},{17,16},{18,1... | collective-permute-start | bytes 3145736 | tf_op jit(solution)/shard_map/ppermute | solution.py:113
  88.7 54.3 %collective-permute-start.16 = (bf16[1024,1536]{1,0:T(8,128)(2,1)}, bf16[1024,1536]{1,0:T(8,128)(2,1)}, u32[]{:S(2)}, u32[]{:S(2)}) collective-permute-start(bf16[1024,1536]{1,0:T(8,128)(2,1)} %get-tuple-element.198), channel_id=1, source_target_pairs={{0,4},{4,0},{8,12},{12,8},{16,20},{20,16},{24,28},{28,24},{1,5},{5... | collective-permute-start | bytes 9437192 | tf_op jit(solution)/shard_map/ppermute | solution.py:45
  93.9 26.3 %collective-permute-start.7 = (bf16[256,2048]{1,0:T(8,128)(2,1)}, bf16[256,2048]{1,0:T(8,128)(2,1)}, u32[]{:S(2)}, u32[]{:S(2)}) collective-permute-start(bf16[256,2048]{1,0:T(8,128)(2,1)} %collective-permute-done.3), channel_id=1, source_target_pairs={{1,2},{2,3},{5,6},{6,7},{9,10},{10,11},{13,14},{14,15},{17,18},{18... | collective-permute-start | bytes 3145736 | tf_op jit(solution)/shard_map/ppermute | solution.py:112
  101.5 27.0 %collective-permute-start.6 = (bf16[256,2048]{1,0:T(8,128)(2,1)}, bf16[256,2048]{1,0:T(8,128)(2,1)}, u32[]{:S(2)}, u32[]{:S(2)}) collective-permute-start(bf16[256,2048]{1,0:T(8,128)(2,1)} %collective-permute-done.5), channel_id=1, source_target_pairs={{1,0},{5,4},{9,8},{13,12},{17,16},{21,20},{25,24},{29,28}} | collective-permute-start | bytes 3145736 | tf_op jit(solution)/shard_map/ppermute | solution.py:113
  102.8 38.5 %collective-permute-start.20 = (bf16[1024,1152]{1,0:T(8,128)(2,1)}, bf16[1024,1152]{1,0:T(8,128)(2,1)S(1)}, u32[]{:S(2)}, u32[]{:S(2)}) collective-permute-start(bf16[1024,1152]{1,0:T(8,128)(2,1)} %copy-done.51), channel_id=1, source_target_pairs={{0,4},{4,0},{8,12},{12,8},{16,20},{20,16},{24,28},{28,24},{1,5},{5... | collective-permute-start | bytes 7077896 | tf_op jit(solution)/shard_map/ppermute | solution.py:45
  120.3 81.0 %collective-permute-start.24 = (bf16[1024,1024]{0,1:T(8,128)(2,1)}, bf16[1024,1024]{0,1:T(8,128)(2,1)S(1)}, u32[]{:S(2)}, u32[]{:S(2)}) collective-permute-start(bf16[1024,1024]{0,1:T(8,128)(2,1)} %get-tuple-element.216), channel_id=1, source_target_pairs={{0,4},{4,0},{8,12},{12,8},{16,20},{20,16},{24,28},{28,24},{1,5},{5... | collective-permute-start | bytes 6291464 | tf_op jit(solution)/shard_map/ppermute | solution.py:45
  209.8 24.9 %collective-permute-start.28 = (bf16[256,2048]{1,0:T(8,128)(2,1)S(1)}, bf16[256,2048]{1,0:T(8,128)(2,1)}, u32[]{:S(2)}, u32[]{:S(2)}) collective-permute-start(bf16[256,2048]{1,0:T(8,128)(2,1)S(1)} %get-tuple-element.176), channel_id=1, source_target_pairs={{0,1},{4,5},{8,9},{12,13},{16,17},{20,21},{24,25},{28,29}} | collective-permute-start | bytes 3145736 | tf_op jit(solution)/shard_map/ppermute | solution.py:140
  215.5 26.6 %collective-permute-start.31 = (bf16[256,2048]{1,0:T(8,128)(2,1)S(1)}, bf16[256,2048]{1,0:T(8,128)(2,1)}, u32[]{:S(2)}, u32[]{:S(2)}) collective-permute-start(bf16[256,2048]{1,0:T(8,128)(2,1)S(1)} %get-tuple-element.177), channel_id=1, source_target_pairs={{3,2},{7,6},{11,10},{15,14},{19,18},{23,22},{27,26},{31,30}} | collective-permute-start | bytes 3145736 | tf_op jit(solution)/shard_map/ppermute | solution.py:141
  267.8 26.2 %collective-permute-start.40 = (bf16[256,2048]{1,0:T(8,128)(2,1)S(1)}, bf16[256,2048]{1,0:T(8,128)(2,1)S(1)}, u32[]{:S(2)}, u32[]{:S(2)}) collective-permute-start(bf16[256,2048]{1,0:T(8,128)(2,1)S(1)} %bitcast.128), channel_id=1, source_target_pairs={{0,8},{4,12},{8,0},{12,4},{16,24},{20,28},{24,16},{28,20},{1,9},{5... | collective-permute-start | bytes 3145736 | tf_op jit(solution)/shard_map/ppermute | solution.py:45
  269.3 43.2 %collective-permute-start.41 = (bf16[256,2048]{1,0:T(8,128)(2,1)S(1)}, bf16[256,2048]{1,0:T(8,128)(2,1)S(1)}, u32[]{:S(2)}, u32[]{:S(2)}) collective-permute-start(bf16[256,2048]{1,0:T(8,128)(2,1)S(1)} %bitcast.129), channel_id=1, source_target_pairs={{0,16},{4,20},{8,24},{12,28},{16,0},{20,4},{24,8},{28,12},{1,17},{... | collective-permute-start | bytes 3145736 | tf_op jit(solution)/shard_map/ppermute | solution.py:45
  270.0 43.7 %collective-permute-start.42 = (bf16[256,2048]{1,0:T(8,128)(2,1)S(1)}, bf16[256,2048]{1,0:T(8,128)(2,1)S(1)}, u32[]{:S(2)}, u32[]{:S(2)}) collective-permute-start(bf16[256,2048]{1,0:T(8,128)(2,1)S(1)} %bitcast.130), channel_id=1, source_target_pairs={{0,24},{4,28},{8,16},{12,20},{16,8},{20,12},{24,0},{28,4},{1,25},{... | collective-permute-start | bytes 3145736 | tf_op jit(solution)/shard_map/ppermute | solution.py:45
  272.5 51.5 %collective-permute-start.30 = (bf16[256,2048]{1,0:T(8,128)(2,1)}, bf16[256,2048]{1,0:T(8,128)(2,1)}, u32[]{:S(2)}, u32[]{:S(2)}) collective-permute-start(bf16[256,2048]{1,0:T(8,128)(2,1)} %get-tuple-element.174), channel_id=1, source_target_pairs={{0,1},{1,2},{2,3},{4,5},{5,6},{6,7},{8,9},{9,10},{10,11},{12,13},{... | collective-permute-start | bytes 3145736 | tf_op jit(solution)/shard_map/ppermute | solution.py:140
  280.5 46.3 %collective-permute-start.33 = (bf16[256,2048]{1,0:T(8,128)(2,1)}, bf16[256,2048]{1,0:T(8,128)(2,1)}, u32[]{:S(2)}, u32[]{:S(2)}) collective-permute-start(bf16[256,2048]{1,0:T(8,128)(2,1)} %add_convert_fusion.14), channel_id=1, source_target_pairs={{1,0},{2,1},{3,2},{5,4},{6,5},{7,6},{9,8},{10,9},{11,10},{13,12},{... | collective-permute-start | bytes 3145736 | tf_op jit(solution)/shard_map/ppermute | solution.py:141
  318.2 135.5 %collective-permute-start.43 = (bf16[1024,2048]{1,0:T(8,128)(2,1)}, bf16[1024,2048]{1,0:T(8,128)(2,1)}, u32[]{:S(2)}, u32[]{:S(2)}) collective-permute-start(bf16[1024,2048]{1,0:T(8,128)(2,1)} %get-tuple-element.189), channel_id=1, source_target_pairs={{0,4},{4,0},{8,12},{12,8},{16,20},{20,16},{24,28},{28,24},{1,5},{5... | collective-permute-start | bytes 12582920 | tf_op jit(solution)/shard_map/ppermute | solution.py:45
  323.7 25.4 %collective-permute-start.45 = (bf16[256,1024]{0,1:T(8,128)(2,1)S(1)}, bf16[256,1024]{0,1:T(8,128)(2,1)}, u32[]{:S(2)}, u32[]{:S(2)}) collective-permute-start(bf16[256,1024]{0,1:T(8,128)(2,1)S(1)} %bitcast.143), channel_id=1, source_target_pairs={{0,16},{4,20},{8,24},{12,28},{16,0},{20,4},{24,8},{28,12},{1,17},{... | collective-permute-start | bytes 1572872 | tf_op jit(solution)/shard_map/ppermute | solution.py:45
  324.0 25.1 %collective-permute-start.46 = (bf16[256,1024]{0,1:T(8,128)(2,1)S(1)}, bf16[256,1024]{0,1:T(8,128)(2,1)}, u32[]{:S(2)}, u32[]{:S(2)}) collective-permute-start(bf16[256,1024]{0,1:T(8,128)(2,1)S(1)} %bitcast.144), channel_id=1, source_target_pairs={{0,24},{4,28},{8,16},{12,20},{16,8},{20,12},{24,0},{28,4},{1,25},{... | collective-permute-start | bytes 1572872 | tf_op jit(solution)/shard_map/ppermute | solution.py:45
  333.9 42.5 %collective-permute-start.35 = (bf16[256,2048]{1,0:T(8,128)(2,1)}, bf16[256,2048]{1,0:T(8,128)(2,1)}, u32[]{:S(2)}, u32[]{:S(2)}) collective-permute-start(bf16[256,2048]{1,0:T(8,128)(2,1)} %get-tuple-element.152), channel_id=1, source_target_pairs={{1,0},{2,1},{3,2},{5,4},{6,5},{7,6},{9,8},{10,9},{11,10},{13,12},{... | collective-permute-start | bytes 3145736 | tf_op jit(solution)/shard_map/ppermute | solution.py:113
  340.4 725.6 %reduce-scatter.2.cloned.1.call-start = ((), (), s32[]{:S(2)}) async-start(), calls=%async_computation.2 | async-start | bytes 5242880 | tf_op jit(solution)/shard_map/reduce_scatter | solution.py:901
  350.9 100.5 %collective-permute-start.47 = (bf16[1024,1024]{0,1:T(8,128)(2,1)S(1)}, bf16[1024,1024]{0,1:T(8,128)(2,1)S(1)}, u32[]{:S(2)}, u32[]{:S(2)}) collective-permute-start(bf16[1024,1024]{0,1:T(8,128)(2,1)S(1)} %pad_maximum_fusion.6), channel_id=1, source_target_pairs={{0,4},{4,0},{8,12},{12,8},{16,20},{20,16},{24,28},{28,24},{1,5},{5... | collective-permute-start | bytes 6291464 | tf_op jit(solution)/shard_map/ppermute | solution.py:45
  351.0 50.3 %collective-permute-start.34 = (bf16[256,2048]{1,0:T(8,128)(2,1)}, bf16[256,2048]{1,0:T(8,128)(2,1)S(1)}, u32[]{:S(2)}, u32[]{:S(2)}) collective-permute-start(bf16[256,2048]{1,0:T(8,128)(2,1)} %get-tuple-element.152), channel_id=1, source_target_pairs={{0,1},{1,2},{2,3},{4,5},{5,6},{6,7},{8,9},{9,10},{10,11},{12,13},{... | collective-permute-start | bytes 3145736 | tf_op jit(solution)/shard_map/ppermute | solution.py:112
  376.4 70.4 %collective-permute-start.36 = (bf16[256,2048]{1,0:T(8,128)(2,1)}, bf16[256,2048]{1,0:T(8,128)(2,1)S(1)}, u32[]{:S(2)}, u32[]{:S(2)}) collective-permute-start(bf16[256,2048]{1,0:T(8,128)(2,1)} %collective-permute-done.35), channel_id=1, source_target_pairs={{1,0},{2,1},{5,4},{6,5},{9,8},{10,9},{13,12},{14,13},{17,16},{18,1... | collective-permute-start | bytes 3145736 | tf_op jit(solution)/shard_map/ppermute | solution.py:113
  401.3 57.2 %collective-permute-start.38 = (bf16[256,2048]{1,0:T(8,128)(2,1)S(1)}, bf16[256,2048]{1,0:T(8,128)(2,1)S(1)}, u32[]{:S(2)}, u32[]{:S(2)}) collective-permute-start(bf16[256,2048]{1,0:T(8,128)(2,1)S(1)} %collective-permute-done.34), channel_id=1, source_target_pairs={{1,2},{2,3},{5,6},{6,7},{9,10},{10,11},{13,14},{14,15},{17,18},{18... | collective-permute-start | bytes 3145736 | tf_op jit(solution)/shard_map/ppermute | solution.py:112
  446.7 28.3 %collective-permute-start.37 = (bf16[256,2048]{1,0:T(8,128)(2,1)S(1)}, bf16[256,2048]{1,0:T(8,128)(2,1)S(1)}, u32[]{:S(2)}, u32[]{:S(2)}) collective-permute-start(bf16[256,2048]{1,0:T(8,128)(2,1)S(1)} %collective-permute-done.36), channel_id=1, source_target_pairs={{1,0},{5,4},{9,8},{13,12},{17,16},{21,20},{25,24},{29,28}} | collective-permute-start | bytes 3145736 | tf_op jit(solution)/shard_map/ppermute | solution.py:113
  521.3 25.1 %collective-permute-start.51 = (bf16[256,2048]{1,0:T(8,128)(2,1)S(1)}, bf16[256,2048]{1,0:T(8,128)(2,1)S(1)}, u32[]{:S(2)}, u32[]{:S(2)}) collective-permute-start(bf16[256,2048]{1,0:T(8,128)(2,1)S(1)} %get-tuple-element.173), channel_id=1, source_target_pairs={{3,2},{7,6},{11,10},{15,14},{19,18},{23,22},{27,26},{31,30}} | collective-permute-start | bytes 3145736 | tf_op jit(solution)/shard_map/ppermute | solution.py:141
  566.6 24.5 %collective-permute-start.52 = (bf16[256,2048]{1,0:T(8,128)(2,1)S(1)}, bf16[256,2048]{1,0:T(8,128)(2,1)S(1)}, u32[]{:S(2)}, u32[]{:S(2)}) collective-permute-start(bf16[256,2048]{1,0:T(8,128)(2,1)S(1)} %get-tuple-element.171), channel_id=1, source_target_pairs={{2,1},{3,2},{6,5},{7,6},{10,9},{11,10},{14,13},{15,14},{18,17},{19... | collective-permute-start | bytes 3145736 | tf_op jit(solution)/shard_map/ppermute | solution.py:141
  586.1 50.3 %collective-permute-start.60 = (bf16[1024,2048]{0,1:T(8,128)(2,1)}, bf16[1024,2048]{0,1:T(8,128)(2,1)}, u32[]{:S(2)}, u32[]{:S(2)}) collective-permute-start(bf16[1024,2048]{0,1:T(8,128)(2,1)} %slice.342), channel_id=1, source_target_pairs={{0,4},{4,0},{8,12},{12,8},{16,20},{20,16},{24,28},{28,24},{1,5},{5... | collective-permute-start | bytes 12582920 | tf_op jit(solution)/shard_map/ppermute | solution.py:45
  586.1 28.0 %collective-permute-start.50 = (bf16[256,2048]{1,0:T(8,128)(2,1)S(1)}, bf16[256,2048]{1,0:T(8,128)(2,1)S(1)}, u32[]{:S(2)}, u32[]{:S(2)}) collective-permute-start(bf16[256,2048]{1,0:T(8,128)(2,1)S(1)} %get-tuple-element.170), channel_id=1, source_target_pairs={{0,1},{1,2},{2,3},{4,5},{5,6},{6,7},{8,9},{9,10},{10,11},{12,13},{... | collective-permute-start | bytes 3145736 | tf_op jit(solution)/shard_map/ppermute | solution.py:140
  591.5 28.0 %collective-permute-start.53 = (bf16[256,2048]{1,0:T(8,128)(2,1)S(1)}, bf16[256,2048]{1,0:T(8,128)(2,1)S(1)}, u32[]{:S(2)}, u32[]{:S(2)}) collective-permute-start(bf16[256,2048]{1,0:T(8,128)(2,1)S(1)} %add_convert_fusion.10), channel_id=1, source_target_pairs={{1,0},{2,1},{3,2},{5,4},{6,5},{7,6},{9,8},{10,9},{11,10},{13,12},{... | collective-permute-start | bytes 3145736 | tf_op jit(solution)/shard_map/ppermute | solution.py:141
  601.6 25.5 %collective-permute-start.64 = (bf16[1024,1024]{1,0:T(8,128)(2,1)}, bf16[1024,1024]{1,0:T(8,128)(2,1)}, u32[]{:S(2)}, u32[]{:S(2)}) collective-permute-start(bf16[1024,1024]{1,0:T(8,128)(2,1)} %slice.348), channel_id=1, source_target_pairs={{0,4},{4,0},{8,12},{12,8},{16,20},{20,16},{24,28},{28,24},{1,5},{5... | collective-permute-start | bytes 6291464 | tf_op jit(solution)/shard_map/ppermute | solution.py:45
  625.7 27.0 %collective-permute-start.55 = (bf16[256,2048]{1,0:T(8,128)(2,1)}, bf16[256,2048]{1,0:T(8,128)(2,1)}, u32[]{:S(2)}, u32[]{:S(2)}) collective-permute-start(bf16[256,2048]{1,0:T(8,128)(2,1)} %get-tuple-element.149), channel_id=1, source_target_pairs={{1,0},{2,1},{3,2},{5,4},{6,5},{7,6},{9,8},{10,9},{11,10},{13,12},{... | collective-permute-start | bytes 3145736 | tf_op jit(solution)/shard_map/ppermute | solution.py:113
  630.3 32.9 %collective-permute-start.67 = (bf16[256,1024]{1,0:T(8,128)(2,1)S(1)}, bf16[256,1024]{1,0:T(8,128)(2,1)S(1)}, u32[]{:S(2)}, u32[]{:S(2)}) collective-permute-start(bf16[256,1024]{1,0:T(8,128)(2,1)S(1)} %get-tuple-element.182), channel_id=1, source_target_pairs={{0,24},{4,28},{8,16},{12,20},{16,8},{20,12},{24,0},{28,4},{1,25},{... | collective-permute-start | bytes 1572872 | tf_op jit(solution)/shard_map/ppermute | solution.py:45
  635.7 32.1 %collective-permute-start.66 = (bf16[256,1024]{1,0:T(8,128)(2,1)S(1)}, bf16[256,1024]{1,0:T(8,128)(2,1)}, u32[]{:S(2)}, u32[]{:S(2)}) collective-permute-start(bf16[256,1024]{1,0:T(8,128)(2,1)S(1)} %get-tuple-element.183), channel_id=1, source_target_pairs={{0,16},{4,20},{8,24},{12,28},{16,0},{20,4},{24,8},{28,12},{1,17},{... | collective-permute-start | bytes 1572872 | tf_op jit(solution)/shard_map/ppermute | solution.py:45
  635.7 32.8 %collective-permute-start.65 = (bf16[256,1024]{1,0:T(8,128)(2,1)S(1)}, bf16[256,1024]{1,0:T(8,128)(2,1)}, u32[]{:S(2)}, u32[]{:S(2)}) collective-permute-start(bf16[256,1024]{1,0:T(8,128)(2,1)S(1)} %get-tuple-element.181), channel_id=1, source_target_pairs={{0,8},{4,12},{8,0},{12,4},{16,24},{20,28},{24,16},{28,20},{1,9},{5... | collective-permute-start | bytes 1572872 | tf_op jit(solution)/shard_map/ppermute | solution.py:45
  636.4 32.3 %collective-permute-start.54 = (bf16[256,2048]{1,0:T(8,128)(2,1)}, bf16[256,2048]{1,0:T(8,128)(2,1)}, u32[]{:S(2)}, u32[]{:S(2)}) collective-permute-start(bf16[256,2048]{1,0:T(8,128)(2,1)} %get-tuple-element.149), channel_id=1, source_target_pairs={{0,1},{1,2},{2,3},{4,5},{5,6},{6,7},{8,9},{9,10},{10,11},{12,13},{... | collective-permute-start | bytes 3145736 | tf_op jit(solution)/shard_map/ppermute | solution.py:112
  652.7 26.1 %collective-permute-start.56 = (bf16[256,2048]{1,0:T(8,128)(2,1)}, bf16[256,2048]{1,0:T(8,128)(2,1)}, u32[]{:S(2)}, u32[]{:S(2)}) collective-permute-start(bf16[256,2048]{1,0:T(8,128)(2,1)} %collective-permute-done.55), channel_id=1, source_target_pairs={{1,0},{2,1},{5,4},{6,5},{9,8},{10,9},{13,12},{14,13},{17,16},{18,1... | collective-permute-start | bytes 3145736 | tf_op jit(solution)/shard_map/ppermute | solution.py:113
  663.3 29.0 %collective-permute-start.63 = (bf16[256,2048]{0,1:T(8,128)(2,1)}, bf16[256,2048]{0,1:T(8,128)(2,1)}, u32[]{:S(2)}, u32[]{:S(2)}) collective-permute-start(bf16[256,2048]{0,1:T(8,128)(2,1)} %get-tuple-element.168), channel_id=1, source_target_pairs={{0,24},{4,28},{8,16},{12,20},{16,8},{20,12},{24,0},{28,4},{1,25},{... | collective-permute-start | bytes 3145736 | tf_op jit(solution)/shard_map/ppermute | solution.py:45
  667.9 44.3 %collective-permute-start.62 = (bf16[256,2048]{0,1:T(8,128)(2,1)}, bf16[256,2048]{0,1:T(8,128)(2,1)}, u32[]{:S(2)}, u32[]{:S(2)}) collective-permute-start(bf16[256,2048]{0,1:T(8,128)(2,1)} %get-tuple-element.169), channel_id=1, source_target_pairs={{0,16},{4,20},{8,24},{12,28},{16,0},{20,4},{24,8},{28,12},{1,17},{... | collective-permute-start | bytes 3145736 | tf_op jit(solution)/shard_map/ppermute | solution.py:45
  668.6 44.7 %collective-permute-start.61 = (bf16[256,2048]{0,1:T(8,128)(2,1)}, bf16[256,2048]{0,1:T(8,128)(2,1)}, u32[]{:S(2)}, u32[]{:S(2)}) collective-permute-start(bf16[256,2048]{0,1:T(8,128)(2,1)} %get-tuple-element.167), channel_id=1, source_target_pairs={{0,8},{4,12},{8,0},{12,4},{16,24},{20,28},{24,16},{28,20},{1,9},{5... | collective-permute-start | bytes 3145736 | tf_op jit(solution)/shard_map/ppermute | solution.py:45
  668.6 49.6 %collective-permute-start.58 = (bf16[256,2048]{1,0:T(8,128)(2,1)}, bf16[256,2048]{1,0:T(8,128)(2,1)}, u32[]{:S(2)}, u32[]{:S(2)}) collective-permute-start(bf16[256,2048]{1,0:T(8,128)(2,1)} %collective-permute-done.54), channel_id=1, source_target_pairs={{1,2},{2,3},{5,6},{6,7},{9,10},{10,11},{13,14},{14,15},{17,18},{18... | collective-permute-start | bytes 3145736 | tf_op jit(solution)/shard_map/ppermute | solution.py:112
  678.8 40.2 %collective-permute-start.57 = (bf16[256,2048]{1,0:T(8,128)(2,1)}, bf16[256,2048]{1,0:T(8,128)(2,1)}, u32[]{:S(2)}, u32[]{:S(2)}) collective-permute-start(bf16[256,2048]{1,0:T(8,128)(2,1)} %collective-permute-done.56), channel_id=1, source_target_pairs={{1,0},{5,4},{9,8},{13,12},{17,16},{21,20},{25,24},{29,28}} | collective-permute-start | bytes 3145736 | tf_op jit(solution)/shard_map/ppermute | solution.py:113
  736.0 44.1 %collective-permute-start.70 = (f32[8,128]{1,0:T(8,128)S(1)}, f32[8,128]{1,0:T(8,128)S(1)}, u32[]{:S(2)}, u32[]{:S(2)}) collective-permute-start(f32[8,128]{1,0:T(8,128)S(1)} %bitcast.174), channel_id=1, source_target_pairs={{0,3},{1,0},{2,1},{3,2},{4,7},{5,4},{6,5},{7,6},{8,11},{9,8},{10,9... | collective-permute-start | bytes 12296 | tf_op jit(solution)/shard_map/ppermute | solution.py:80
  780.1 123.6 %collective-permute-start.95 = (bf16[1024,1024]{1,0:T(8,128)(2,1)}, bf16[1024,1024]{1,0:T(8,128)(2,1)}, u32[]{:S(2)}, u32[]{:S(2)}) collective-permute-start(bf16[1024,1024]{1,0:T(8,128)(2,1)} %slice.384), channel_id=1, source_target_pairs={{0,4},{4,0},{8,12},{12,8},{16,20},{20,16},{24,28},{28,24},{1,5},{5... | collective-permute-start | bytes 6291464 | tf_op jit(solution)/shard_map/ppermute | solution.py:45
  815.0 48.3 %collective-permute-start.90 = (f32[8,512]{1,0:T(8,128)S(1)}, f32[8,512]{1,0:T(8,128)S(1)}, u32[]{:S(2)}, u32[]{:S(2)}) collective-permute-start(f32[8,512]{1,0:T(8,128)S(1)} %get-tuple-element.51), channel_id=1, source_target_pairs={{0,3},{1,0},{2,1},{3,2},{4,7},{5,4},{6,5},{7,6},{8,11},{9,8},{10,9... | collective-permute-start | bytes 49160 | tf_op jit(solution)/shard_map/ppermute | solution.py:80
  818.3 50.3 %collective-permute-start.89 = (f32[8,512]{1,0:T(8,128)S(1)}, f32[8,512]{1,0:T(8,128)S(1)}, u32[]{:S(2)}, u32[]{:S(2)}) collective-permute-start(f32[8,512]{1,0:T(8,128)S(1)} %get-tuple-element.51), channel_id=1, source_target_pairs={{0,2},{1,3},{2,0},{3,1},{4,6},{5,7},{6,4},{7,5},{8,10},{9,11},{10,... | collective-permute-start | bytes 49160 | tf_op jit(solution)/shard_map/ppermute | solution.py:80
  819.4 49.5 %collective-permute-start.88 = (f32[8,512]{1,0:T(8,128)S(1)}, f32[8,512]{1,0:T(8,128)S(1)}, u32[]{:S(2)}, u32[]{:S(2)}) collective-permute-start(f32[8,512]{1,0:T(8,128)S(1)} %get-tuple-element.51), channel_id=1, source_target_pairs={{0,1},{1,2},{2,3},{3,0},{4,5},{5,6},{6,7},{7,4},{8,9},{9,10},{10,1... | collective-permute-start | bytes 49160 | tf_op jit(solution)/shard_map/ppermute | solution.py:80
  859.9 81.7 %collective-permute-start.77 = (bf16[1024,2688]{1,0:T(8,128)(2,1)}, bf16[1024,2688]{1,0:T(8,128)(2,1)}, u32[]{:S(2)}, u32[]{:S(2)}) collective-permute-start(bf16[1024,2688]{1,0:T(8,128)(2,1)} %slice.355), channel_id=1, source_target_pairs={{0,4},{4,0},{8,12},{12,8},{16,20},{20,16},{24,28},{28,24},{1,5},{5... | collective-permute-start | bytes 16515080 | tf_op jit(solution)/shard_map/ppermute | solution.py:45
  863.2 27.7 %collective-permute-start.71 = (bf16[256,2048]{1,0:T(8,128)(2,1)}, bf16[256,2048]{1,0:T(8,128)(2,1)}, u32[]{:S(2)}, u32[]{:S(2)}) collective-permute-start(bf16[256,2048]{1,0:T(8,128)(2,1)} %get-tuple-element.165), channel_id=1, source_target_pairs={{0,1},{4,5},{8,9},{12,13},{16,17},{20,21},{24,25},{28,29}} | collective-permute-start | bytes 3145736 | tf_op jit(solution)/shard_map/ppermute | solution.py:140
  897.6 26.1 %collective-permute-start.72 = (bf16[256,2048]{1,0:T(8,128)(2,1)S(1)}, bf16[256,2048]{1,0:T(8,128)(2,1)}, u32[]{:S(2)}, u32[]{:S(2)}) collective-permute-start(bf16[256,2048]{1,0:T(8,128)(2,1)S(1)} %add_convert_fusion.8), channel_id=1, source_target_pairs={{0,1},{1,2},{4,5},{5,6},{8,9},{9,10},{12,13},{13,14},{16,17},{17,1... | collective-permute-start | bytes 3145736 | tf_op jit(solution)/shard_map/ppermute | solution.py:140
  908.2 27.3 %collective-permute-start.97 = (bf16[256,1024]{1,0:T(8,128)(2,1)S(1)}, bf16[256,1024]{1,0:T(8,128)(2,1)S(1)}, u32[]{:S(2)}, u32[]{:S(2)}) collective-permute-start(bf16[256,1024]{1,0:T(8,128)(2,1)S(1)} %get-tuple-element.180), channel_id=1, source_target_pairs={{0,16},{4,20},{8,24},{12,28},{16,0},{20,4},{24,8},{28,12},{1,17},{... | collective-permute-start | bytes 1572872 | tf_op jit(solution)/shard_map/ppermute | solution.py:45
  910.2 25.3 %collective-permute-start.96 = (bf16[256,1024]{1,0:T(8,128)(2,1)S(1)}, bf16[256,1024]{1,0:T(8,128)(2,1)S(1)}, u32[]{:S(2)}, u32[]{:S(2)}) collective-permute-start(bf16[256,1024]{1,0:T(8,128)(2,1)S(1)} %get-tuple-element.178), channel_id=1, source_target_pairs={{0,8},{4,12},{8,0},{12,4},{16,24},{20,28},{24,16},{28,20},{1,9},{5... | collective-permute-start | bytes 1572872 | tf_op jit(solution)/shard_map/ppermute | solution.py:45
  929.4 29.0 %collective-permute-start.73 = (bf16[256,2048]{1,0:T(8,128)(2,1)}, bf16[256,2048]{1,0:T(8,128)(2,1)}, u32[]{:S(2)}, u32[]{:S(2)}) collective-permute-start(bf16[256,2048]{1,0:T(8,128)(2,1)} %get-tuple-element.163), channel_id=1, source_target_pairs={{0,1},{1,2},{2,3},{4,5},{5,6},{6,7},{8,9},{9,10},{10,11},{12,13},{... | collective-permute-start | bytes 3145736 | tf_op jit(solution)/shard_map/ppermute | solution.py:140
  940.3 39.9 %collective-permute-start.76 = (bf16[256,2048]{1,0:T(8,128)(2,1)}, bf16[256,2048]{1,0:T(8,128)(2,1)}, u32[]{:S(2)}, u32[]{:S(2)}) collective-permute-start(bf16[256,2048]{1,0:T(8,128)(2,1)} %add_convert_fusion.5), channel_id=1, source_target_pairs={{1,0},{2,1},{3,2},{5,4},{6,5},{7,6},{9,8},{10,9},{11,10},{13,12},{... | collective-permute-start | bytes 3145736 | tf_op jit(solution)/shard_map/ppermute | solution.py:141
  951.7 41.1 %collective-permute-start.80 = (bf16[256,2688]{1,0:T(8,128)(2,1)}, bf16[256,2688]{1,0:T(8,128)(2,1)}, u32[]{:S(2)}, u32[]{:S(2)}) collective-permute-start(bf16[256,2688]{1,0:T(8,128)(2,1)} %get-tuple-element.161), channel_id=1, source_target_pairs={{0,24},{4,28},{8,16},{12,20},{16,8},{20,12},{24,0},{28,4},{1,25},{... | collective-permute-start | bytes 4128776 | tf_op jit(solution)/shard_map/ppermute | solution.py:45
  952.9 59.5 %collective-permute-start.79 = (bf16[256,2688]{1,0:T(8,128)(2,1)}, bf16[256,2688]{1,0:T(8,128)(2,1)}, u32[]{:S(2)}, u32[]{:S(2)}) collective-permute-start(bf16[256,2688]{1,0:T(8,128)(2,1)} %get-tuple-element.162), channel_id=1, source_target_pairs={{0,16},{4,20},{8,24},{12,28},{16,0},{20,4},{24,8},{28,12},{1,17},{... | collective-permute-start | bytes 4128776 | tf_op jit(solution)/shard_map/ppermute | solution.py:45
  954.6 57.9 %collective-permute-start.78 = (bf16[256,2688]{1,0:T(8,128)(2,1)}, bf16[256,2688]{1,0:T(8,128)(2,1)}, u32[]{:S(2)}, u32[]{:S(2)}) collective-permute-start(bf16[256,2688]{1,0:T(8,128)(2,1)} %get-tuple-element.160), channel_id=1, source_target_pairs={{0,8},{4,12},{8,0},{12,4},{16,24},{20,28},{24,16},{28,20},{1,9},{5... | collective-permute-start | bytes 4128776 | tf_op jit(solution)/shard_map/ppermute | solution.py:45
  1017.2 27.3 %collective-permute-start.87 = (f32[64,1152]{1,0:T(8,128)}, f32[64,1152]{1,0:T(8,128)}, u32[]{:S(2)}, u32[]{:S(2)}) collective-permute-start(f32[64,1152]{1,0:T(8,128)} %get-tuple-element.187), channel_id=1, source_target_pairs={{0,3},{1,0},{2,1},{3,2},{4,7},{5,4},{6,5},{7,6},{8,11},{9,8},{10,9... | collective-permute-start | bytes 884744 | tf_op jit(solution)/shard_map/ppermute | solution.py:80
  1036.7 25.1 %collective-permute-start.86 = (f32[64,1152]{1,0:T(8,128)}, f32[64,1152]{1,0:T(8,128)}, u32[]{:S(2)}, u32[]{:S(2)}) collective-permute-start(f32[64,1152]{1,0:T(8,128)} %get-tuple-element.188), channel_id=1, source_target_pairs={{0,2},{1,3},{2,0},{3,1},{4,6},{5,7},{6,4},{7,5},{8,10},{9,11},{10,... | collective-permute-start | bytes 884744 | tf_op jit(solution)/shard_map/ppermute | solution.py:80
  1036.7 25.1 %collective-permute-start.85 = (f32[64,1152]{1,0:T(8,128)}, f32[64,1152]{1,0:T(8,128)}, u32[]{:S(2)}, u32[]{:S(2)}) collective-permute-start(f32[64,1152]{1,0:T(8,128)} %get-tuple-element.186), channel_id=1, source_target_pairs={{0,1},{1,2},{2,3},{3,0},{4,5},{5,6},{6,7},{7,4},{8,9},{9,10},{10,1... | collective-permute-start | bytes 884744 | tf_op jit(solution)/shard_map/ppermute | solution.py:80
  (111 other events, 2049.9 us)
Sparse Core Ops, SparseCore 0:
  340.5 112.7 all-gather.1
  768.5 78.7 reduce-scatter.1

commit v2 on v1

v2 whole, which is shorter than its diff:
```python
from functools import partial

import jax
import jax.numpy as jnp
import numpy as np
from jax import lax
from jax.experimental import pallas as pl
from jax.experimental.pallas import tpu as pltpu
from jax.sharding import PartitionSpec as P

QUERY_HEADS = 8
KEY_VALUE_HEADS = 2
HEAD_SIZE = 128
HM = 48
P_SIZE = 64
LANES = 128
NORM_EPS = 1e-05
ROPE_BASE = 100000000000.0
MASK_FILL = -1e30
F32 = jnp.float32
BF16 = jnp.bfloat16
NN = (((1,), (0,)), ((), ()))
NT = (((1,), (1,)), ((), ()))
TN = (((0,), (0,)), ((), ()))
VMEM_LIMIT = 48 * 1024 * 1024


def dot(left, right, dims=NN):
    return lax.dot_general(left, right, dims, preferred_element_type=F32)


def sums_of(zero_one, value):
    high = value.astype(BF16)
    value = value - high.astype(F32)
    middle = value.astype(BF16)
    low = (value - middle.astype(F32)).astype(BF16)
    width = value.shape[1]
    out = dot(zero_one, jnp.concatenate([high, middle, low], axis=1))
    return out[:, :width] + out[:, width : 2 * width] + out[:, 2 * width :]


def sigmoid(v):
    return 0.5 * jnp.tanh(0.5 * v) + 0.5


def send_dp(value, mask):
    size = lax.axis_size("dp")
    return lax.ppermute(value, "dp", [(i, i ^ mask) for i in range(size)])


def chip_gather(rows, *earlier):
    chips = lax.axis_size("dp") // 2
    if earlier:
        rows = after(rows, *earlier)
    return [rows] + [send_dp(rows, 2 * k) for k in range(1, chips)]


def core_gather(pieces, *earlier):
    if earlier:
        pieces = ordered(pieces, *earlier)
    chips = len(pieces)
    me = lax.axis_index("dp")
    chip, core = lax.div(me, 2), lax.rem(me, 2)
    rows, width = pieces[0].shape
    mine = jnp.zeros((chips, rows, width), pieces[0].dtype)
    for k, piece in enumerate(pieces):
        mine = lax.dynamic_update_slice(mine, piece[None], (chip ^ k, 0, 0))
    other = send_dp(mine, 1)
    out = jnp.zeros((chips, 2, rows, width), mine.dtype)
    out = lax.dynamic_update_slice(out, mine[:, None], (0, core, 0, 0))
    out = lax.dynamic_update_slice(out, other[:, None], (0, 1 - core, 0, 0))
    return out.reshape(2 * chips * rows, width)


def core_scatter(grad, *earlier):
    chips = lax.axis_size("dp") // 2
    core = lax.rem(lax.axis_index("dp"), 2)
    blocks = grad.reshape(chips, 2, -1, grad.shape[1])
    other = send_dp(lax.dynamic_index_in_dim(blocks, 1 - core, 1, keepdims=False), 1)
    if earlier:
        other = after(other, *earlier)
    mine = lax.dynamic_index_in_dim(blocks, core, 1, keepdims=False)
    return (mine.astype(F32) + other.astype(F32)).astype(grad.dtype)


def chip_scatter(pair):
    chips = pair.shape[0]
    chip = lax.div(lax.axis_index("dp"), 2)
    pieces = [lax.dynamic_index_in_dim(pair, chip, 0, keepdims=False)]
    for k in range(1, chips):
        piece = lax.dynamic_index_in_dim(pair, chip ^ k, 0, keepdims=False)
        pieces.append(send_dp(piece, 2 * k))
    return pieces


def add_up(pieces, *earlier):
    if earlier:
        pieces = ordered(pieces, *earlier)
    total = pieces[0].astype(F32)
    for piece in pieces[1:]:
        total = total + piece.astype(F32)
    return total


def dp_sum(value):
    chips = lax.axis_size("dp") // 2
    value = value + send_dp(value, 1)
    total = value
    for k in range(1, chips):
        total = total + send_dp(value, 2 * k)
    return total


def send_z(value, shift):
    size = lax.axis_size("tensor")
    return lax.ppermute(value, "tensor", [(i, (i + shift) % size) for i in range(size)])


def z_gather_direct(rows):
    size = lax.axis_size("tensor")
    me = lax.axis_index("tensor")
    count = rows.shape[0]
    out = jnp.zeros((size * count,) + rows.shape[1:], rows.dtype)
    pieces = [rows] + [send_z(rows, k) for k in range(1, size)]
    for k, piece in enumerate(pieces):
        out = lax.dynamic_update_slice_in_dim(out, piece, lax.rem(me - k + size, size) * count, 0)
    return out


def z_scatter_direct(total):
    size = lax.axis_size("tensor")
    me = lax.axis_index("tensor")
    count = total.shape[0] // size
    mine = lax.dynamic_slice_in_dim(total, me * count, count, 0).astype(F32)
    for k in range(1, size):
        piece = lax.dynamic_slice_in_dim(total, lax.rem(me + k, size) * count, count, 0)
        mine = mine + send_z(piece, k).astype(F32)
    return mine


def ordered(values, *earlier):
    return lax.optimization_barrier((tuple(values), earlier))[0]


def z_gather_first(rows):
    size = lax.axis_size("tensor")
    right = lax.ppermute(rows, "tensor", [(i, i + 1) for i in range(size - 1)])
    left = lax.ppermute(rows, "tensor", [(i, i - 1) for i in range(1, size)])
    return [right, left]


def z_gather_parts(parts, hooks=None, first=None):
    size = lax.axis_size("tensor")
    hooks = hooks or {}
    moved = [[] for _ in parts]
    for h, rows in enumerate(parts):
        right = left = rows
        for s in range(size - 1):
            if s == 0 and h == 0 and first is not None:
                right, left = first
                moved[h].append(first)
                continue
            earlier = list(hooks.get((h, s), []))
            if s or earlier:
                right, left = ordered((right, left), *earlier)
            right = lax.ppermute(right, "tensor", [(i, i + 1) for i in range(s, size - 1)])
            left = lax.ppermute(left, "tensor", [(i, i - 1) for i in range(1, size - s)])
            moved[h].append([right, left])
    return moved


def line_gather(parts, *earlier):
    out = []
    for part in parts:
        if earlier:
            part = after(part, *earlier)
        out.append(lax.all_gather(part, "tensor", axis=0, tiled=True))
    return out


def line_scatter(parts, *earlier):
    out = []
    for part in parts:
        if earlier:
            part = after(part, *earlier)
        out.append(
            lax.psum_scatter(part, "tensor", scatter_dimension=0, tiled=True).astype(F32)
        )
    return out


def line_sends(parts, *earlier):
    size = lax.axis_size("tensor")
    me = lax.axis_index("tensor")
    count = parts[0].shape[0] // size
    pieces = []
    for k in range(size):
        index = lax.rem(me + k, size) * count
        piece = [lax.dynamic_slice_in_dim(part, index, count, 0) for part in parts]
        piece = jnp.concatenate(piece, axis=0)
        if k:
            if earlier:
                piece = after(piece, *earlier)
            piece = send_z(piece, k)
        pieces.append(piece)
    return pieces


def place_kernel(place_ref, in_ref, out_ref):
    out_ref[...] = in_ref[...]


def z_place(rows, moved):
    size = lax.axis_size("tensor")
    me = lax.axis_index("tensor")
    count, width = rows.shape
    out = pl.pallas_call(
        place_kernel,
        grid_spec=pltpu.PrefetchScalarGridSpec(
            num_scalar_prefetch=1,
            grid=(1,),
            in_specs=[pl.BlockSpec((count, width), lambda i, place_ref: (0, 0))],
            out_specs=pl.BlockSpec((count, width), lambda i, place_ref: (place_ref[0], 0)),
        ),
        out_shape=jax.ShapeDtypeStruct((size * count, width), rows.dtype),
        cost_estimate=pl.CostEstimate(
            flops=0, bytes_accessed=4 * rows.size, transcendentals=0
        ),
        name="place",
    )(me.astype(jnp.int32).reshape(1), rows)
    for d in range(1, size):
        piece = moved[d - 1][0] + moved[size - d - 1][1]
        at = lax.rem(me - d + size, size) * count
        out = lax.dynamic_update_slice_in_dim(out, piece, at, 0)
    return out


def block_of(total, index, size):
    if isinstance(total, list):
        return jnp.concatenate([block_of(t, index, size) for t in total], axis=0)
    count = total.shape[0] // size
    return lax.dynamic_slice_in_dim(total, index * count, count, 0)


def z_scatter_first(parts):
    size = lax.axis_size("tensor")
    right = lax.ppermute(block_of(parts[0], size - 1, size), "tensor", [(0, 1)])
    left = lax.ppermute(block_of(parts[0], 0, size), "tensor", [(size - 1, size - 2)])
    return [right, left]


def z_scatter_parts(parts, hooks=None, first=None):
    size = lax.axis_size("tensor")
    me = lax.axis_index("tensor")
    hooks = hooks or {}
    sums, moved = [], [[] for _ in parts]
    for h, total in enumerate(parts):

        def part(offset, total=total):
            return block_of(total, jnp.clip(me + offset, 0, size - 1), size)

        right = left = None
        for s in range(size - 1):
            if s == 0 and h == 0 and first is not None:
                right, left = first
                moved[h].append(first)
                continue
            d = size - 1 - s
            to_right, to_left = part(d), part(-d)
            if s:
                to_right = (to_right.astype(F32) + right.astype(F32)).astype(BF16)
                to_left = (to_left.astype(F32) + left.astype(F32)).astype(BF16)
            earlier = list(hooks.get((h, s), []))
            if h:
                earlier += moved[h - 1][s]
            to_right, to_left = ordered((to_right, to_left), *earlier)
            right = lax.ppermute(to_right, "tensor", [(i, i + 1) for i in range(s + 1)])
            left = lax.ppermute(to_left, "tensor", [(i, i - 1) for i in range(size - 1 - s, size)])
            moved[h].append([right, left])
        sums.append(part(0).astype(F32) + right.astype(F32) + left.astype(F32))
    return sums, moved


def z_sum(value):
    size = lax.axis_size("tensor")
    total = value
    for k in range(1, size):
        total = total + send_z(value, k)
    return total


def tile_of(width):
    return max(t for t in range(LANES, 513, LANES) if width % t == 0)


def norm_project_kernel(members, x_ref, gain_ref, w_ref, *refs):
    normed_ref, out_ref = refs[-2:]
    block, rows = x_ref.shape[1] // members, w_ref.shape[0] // members

    @pl.when(pl.program_id(0) == 0)
    def _():
        x = x_ref[...].astype(F32)
        mean = jnp.sum(x * x, axis=1, keepdims=True) * (1.0 / x.shape[1])
        normed_ref[...] = (x * lax.rsqrt(mean + NORM_EPS) * gain_ref[...]).astype(BF16)

    out = None
    for j in range(members):
        part = dot(
            normed_ref[:, j * block : (j + 1) * block], w_ref[j * rows : j * rows + block, :]
        )
        out = part if out is None else out + part
    out_ref[...] = out


def norm_project(x, gain, weights, held, index, parts, members):
    rows, model = x.shape
    total, width = rows * parts, weights.shape[1]
    tile = tile_of(width)
    return pl.pallas_call(
        partial(norm_project_kernel, members),
        grid=(width // tile,),
        in_specs=[
            pl.BlockSpec((rows, model), lambda j: (0, 0)),
            pl.BlockSpec((1, model), lambda j: (0, 0)),
            pl.BlockSpec((weights.shape[0], tile), lambda j: (0, j)),
        ]
        + [pl.BlockSpec(memory_space=pl.ANY)] * len(held),
        out_specs=[
            pl.BlockSpec((rows, model), lambda j: (index, 0)),
            pl.BlockSpec((rows, tile), lambda j: (index, j)),
        ],
        out_shape=[
            jax.ShapeDtypeStruct((total, model), BF16),
            jax.ShapeDtypeStruct((total, width), F32),
        ],
        input_output_aliases={3: 0, 4: 1} if held else {},
        compiler_params=pltpu.CompilerParams(vmem_limit_bytes=VMEM_LIMIT),
        cost_estimate=pl.CostEstimate(
            flops=2 * rows * model * width,
            bytes_accessed=2 * (rows + width) * model + 4 * rows * width,
            transcendentals=0,
        ),
        name="norm_project",
    )(x, gain, weights, *held)


def gradient_kernel(parts, *refs):
    out_ref = refs[-1]
    count = len(parts)
    lefts, rights = list(refs[: sum(parts)]), refs[sum(parts) : sum(parts) + count]
    at = 0
    for number, right in zip(parts, rights):
        width = right.shape[1]
        rows = right.shape[0] // number
        total = None
        for h in range(number):
            part = dot(lefts.pop(0)[...], right[h * rows : (h + 1) * rows, :], TN)
            total = part if total is None else total + part
        out_ref[:, at : at + width] = total.astype(BF16)
        at += width


def gradient(lefts, rights, held, piece, pieces):
    model = lefts[0][0].shape[1]
    width = sum(right.shape[1] for right in rights)
    tile = min(256, model // pieces)
    steps = model // pieces // tile
    parts = [len(left) for left in lefts]
    flat = [part for left in lefts for part in left]
    held = [] if held is None else [held]
    return pl.pallas_call(
        partial(gradient_kernel, parts),
        grid=(steps,),
        in_specs=[
            pl.BlockSpec((part.shape[0], tile), lambda j: (0, piece * steps + j)) for part in flat
        ]
        + [pl.BlockSpec(right.shape, lambda j: (0, 0)) for right in rights]
        + [pl.BlockSpec(memory_space=pl.ANY)] * len(held),
        out_specs=pl.BlockSpec((tile, width), lambda j: (piece * steps + j, 0)),
        out_shape=jax.ShapeDtypeStruct((model, width), BF16),
        input_output_aliases={len(flat) + len(rights): 0} if held else {},
        compiler_params=pltpu.CompilerParams(vmem_limit_bytes=VMEM_LIMIT),
        cost_estimate=pl.CostEstimate(
            flops=2 * rights[0].shape[0] * (model // pieces) * width,
            bytes_accessed=2 * (rights[0].shape[0] * (model + width) + model * width) // pieces,
            transcendentals=0,
        ),
        name="gradient",
    )(*flat, *rights, *held)


def feed_forward_kernel(parts, *refs):
    xs, ds = refs[:parts], refs[parts : 2 * parts]
    gate_ref, up_ref, down_ref, act_ref, d_gate_ref, d_up_ref = refs[2 * parts :]
    for h in range(parts):
        rows = xs[h].shape[0]
        here = slice(h * rows, (h + 1) * rows)
        gate = dot(xs[h][...], gate_ref[...])
        up = dot(xs[h][...], up_ref[...])
        sig_gate = sigmoid(gate)
        silu_gate = gate * sig_gate
        act_ref[here, :] = (silu_gate * up).astype(BF16)
        d_act = dot(ds[h][...], down_ref[...])
        d_gate = d_act * up * (sig_gate * (1.0 + gate * (1.0 - sig_gate)))
        d_gate_ref[here, :] = d_gate.astype(BF16)
        d_up_ref[here, :] = (d_act * silu_gate).astype(BF16)


def feed_forward(normed, d_out, weights, hidden_units):
    parts, (rows, model) = len(normed), normed[0].shape
    tile = min(256, hidden_units)
    steps = hidden_units // tile

    def columns(first):
        return pl.BlockSpec((model, tile), lambda j: (0, first * steps + j))

    whole = pl.BlockSpec((rows, model), lambda j: (0, 0))
    out = jax.ShapeDtypeStruct((rows * parts, hidden_units), BF16)
    return pl.pallas_call(
        partial(feed_forward_kernel, parts),
        grid=(steps,),
        in_specs=[whole] * (2 * parts) + [columns(0), columns(1), columns(2)],
        out_specs=[pl.BlockSpec((rows * parts, tile), lambda j: (0, j))] * 3,
        out_shape=[out] * 3,
        compiler_params=pltpu.CompilerParams(vmem_limit_bytes=VMEM_LIMIT),
        cost_estimate=pl.CostEstimate(
            flops=6 * rows * parts * model * hidden_units,
            bytes_accessed=2 * (2 * rows * parts + 3 * hidden_units) * model,
            transcendentals=rows * parts * hidden_units,
        ),
        name="feed_forward",
    )(*normed, *d_out, weights, weights, weights)


def branch_back_kernel(parts, *refs):
    w_ref, gm_ref, out_ref, inner_ref = refs[parts:]
    first = pl.program_id(0) == 0

    @pl.when(first)
    def _():
        inner_ref[...] = jnp.zeros_like(inner_ref)

    for h in range(parts):
        rows = refs[h].shape[0]
        here = slice(h * rows, (h + 1) * rows)
        out = dot(refs[h][...], w_ref[...])
        out_ref[here, :] = out
        inner = jnp.sum(out * gm_ref[here, :].astype(F32), axis=1, keepdims=True)
        inner_ref[here, :] += jnp.where(first, 0.0, inner)


def branch_back(d_branch, weights, gm):
    parts, (rows, model) = len(d_branch), d_branch[0].shape
    tile = weights.shape[1] - gm.shape[1]
    steps = weights.shape[1] // tile
    total = rows * parts
    return pl.pallas_call(
        partial(branch_back_kernel, parts),
        grid=(steps,),
        in_specs=[pl.BlockSpec((rows, model), lambda j: (0, 0))] * parts
        + [
            pl.BlockSpec((model, tile), lambda j: (0, j)),
            pl.BlockSpec((total, tile), lambda j: (0, jnp.maximum(j - 1, 0))),
        ],
        out_specs=[
            pl.BlockSpec((total, tile), lambda j: (0, j)),
            pl.BlockSpec((total, LANES), lambda j: (0, 0)),
        ],
        out_shape=[
            jax.ShapeDtypeStruct((total, weights.shape[1]), F32),
            jax.ShapeDtypeStruct((total, LANES), F32),
        ],
        compiler_params=pltpu.CompilerParams(vmem_limit_bytes=VMEM_LIMIT),
        cost_estimate=pl.CostEstimate(
            flops=2 * total * model * weights.shape[1],
            bytes_accessed=2 * (total + weights.shape[1]) * model,
            transcendentals=0,
        ),
        name="branch_back",
    )(*d_branch, weights, gm)


def transposed_kernel(count, *refs):
    out = None
    for left, right in zip(refs[:count], refs[count : 2 * count]):
        part = dot(left[...], right[...], NT)
        out = part if out is None else out + part
    refs[-1][...] = out.astype(BF16)


def transposed_product(lefts, weights, first):
    rows, width = lefts[0].shape
    model = weights.shape[0]
    tile = min(512, model)
    count = len(lefts)

    def columns(k):
        return pl.BlockSpec((tile, width), lambda j: (j, first + k))

    return pl.pallas_call(
        partial(transposed_kernel, count),
        grid=(model // tile,),
        in_specs=[pl.BlockSpec((rows, width), lambda j: (0, 0))] * count
        + [columns(k) for k in range(count)],
        out_specs=pl.BlockSpec((rows, tile), lambda j: (0, j)),
        out_shape=jax.ShapeDtypeStruct((rows, model), BF16),
        compiler_params=pltpu.CompilerParams(vmem_limit_bytes=VMEM_LIMIT),
        cost_estimate=pl.CostEstimate(
            flops=2 * rows * model * width * count,
            bytes_accessed=2 * ((rows + model) * width * count + rows * model),
            transcendentals=0,
        ),
        name="transposed_product",
    )(*lefts, *([weights] * count))


def branch_kernel(att_ref, gm_ref, rstd_ref, w_ref, out_ref):
    split = att_ref.shape[1]
    out = dot(att_ref[...], w_ref[:, :split], NT)
    out = out + rstd_ref[...] * dot(gm_ref[...], w_ref[:, split:], NT)
    out_ref[...] = out.astype(BF16)


def branch_product(attended, gm, rstd, weights):
    rows = attended.shape[0]
    model, width = weights.shape
    tile = min(512, model)

    def whole(array):
        return pl.BlockSpec(array.shape, lambda j: (0, 0))

    return pl.pallas_call(
        branch_kernel,
        grid=(model // tile,),
        in_specs=[
            whole(attended),
            whole(gm),
            whole(rstd),
            pl.BlockSpec((tile, width), lambda j: (j, 0)),
        ],
        out_specs=pl.BlockSpec((rows, tile), lambda j: (0, j)),
        out_shape=jax.ShapeDtypeStruct((rows, model), BF16),
        compiler_params=pltpu.CompilerParams(vmem_limit_bytes=VMEM_LIMIT),
        cost_estimate=pl.CostEstimate(
            flops=2 * rows * model * width,
            bytes_accessed=2 * ((rows + model) * width + rows * model),
            transcendentals=0,
        ),
        name="branch",
    )(attended, gm, rstd, weights)


def back_kernel(block, d_ref, w_ref, out_ref):
    count = out_ref.shape[1] // block
    rows = w_ref.shape[0] // count
    for k in range(count):
        out = dot(d_ref[...], w_ref[k * rows : k * rows + block, :], NT)
        out_ref[:, k * block : (k + 1) * block] = out.astype(BF16)


def back_product(d_all, weights, index, parts, members, model):
    rows, block = d_all.shape[0] // parts, model // members
    each = 2
    return pl.pallas_call(
        partial(back_kernel, block),
        grid=(members // each,),
        in_specs=[
            pl.BlockSpec((rows, d_all.shape[1]), lambda j: (index, 0)),
            pl.BlockSpec((each * weights.shape[0] // members, weights.shape[1]), lambda j: (j, 0)),
        ],
        out_specs=pl.BlockSpec((rows, each * block), lambda j: (0, j)),
        out_shape=jax.ShapeDtypeStruct((rows, model), BF16),
        compiler_params=pltpu.CompilerParams(vmem_limit_bytes=VMEM_LIMIT),
        cost_estimate=pl.CostEstimate(
            flops=2 * rows * model * d_all.shape[1],
            bytes_accessed=2 * (rows * d_all.shape[1] + weights.size + rows * model),
            transcendentals=0,
        ),
        name="back_product",
    )(d_all, weights)


def rotary_rows(length):
    half = HEAD_SIZE // 2
    freqs = np.float32(ROPE_BASE) ** (
        -np.arange(half).astype(np.float32) * np.float32(2.0) / np.float32(HEAD_SIZE)
    )
    angles = np.arange(length).astype(np.float32)[:, None] * freqs.astype(np.float32)[None, :]
    cosine, sine = np.cos(angles), np.sin(angles)
    return (
        np.concatenate([cosine, cosine], axis=1).astype(np.float32),
        np.concatenate([-sine, sine], axis=1).astype(np.float32),
    )


def rotate(value, cosine, sine):
    return value * cosine + pltpu.roll(value, HEAD_SIZE // 2, 1) * sine


def chunk_place(index, parts, members):
    return lax.rem(index, parts) * members + lax.div(index, parts)


def in_sequence(ref, places, rows, columns=slice(None)):
    return jnp.concatenate([ref[p * rows : (p + 1) * rows, columns] for p in places], axis=0)


def attention_probs(q_ref, keys, cos_ref, sin_ref, allowed, start, stop, places, rows):
    here = places[start // rows : stop // rows]
    query = in_sequence(q_ref, here, rows)
    query = rotate(query, cos_ref[start:stop, :], sin_ref[start:stop, :]).astype(BF16)
    scores = dot(query, keys, NT) * (HEAD_SIZE**-0.5)
    scores = jnp.where(allowed, scores, MASK_FILL)
    raised = jnp.exp(scores - jnp.max(scores, axis=1, keepdims=True))
    return query, raised * (1.0 / jnp.sum(raised, axis=1, keepdims=True))


def attention_mask(aux_ref, segr_ref, start, stop):
    rows = start + lax.broadcasted_iota(jnp.int32, (stop - start, stop), 0)
    cols = lax.broadcasted_iota(jnp.int32, (stop - start, stop), 1)
    return (aux_ref[start:stop, 0:1] == segr_ref[0:1, :stop]) & (rows >= cols)


def attention_forward_kernel(heads, block, places, *refs):
    q_refs = refs[:heads]
    k_ref, v_ref, cos_ref, sin_ref, aux_ref, segr_ref, out_ref = refs[heads:]
    length = k_ref.shape[0]
    rows = length // len(places)
    keys = rotate(in_sequence(k_ref, places, rows), cos_ref[...], sin_ref[...]).astype(BF16)
    vals = in_sequence(v_ref, places, rows).astype(BF16)
    for start in range(0, length, block):
        stop = start + block
        allowed = attention_mask(aux_ref, segr_ref, start, stop)
        for h in range(heads):
            _, probs = attention_probs(
                q_refs[h], keys[:stop], cos_ref, sin_ref, allowed, start, stop, places, rows
            )
            out = dot(probs.astype(BF16), vals[:stop]).astype(BF16)
            columns = slice(h * HEAD_SIZE, (h + 1) * HEAD_SIZE)
            for c in range(block // rows):
                p = places[start // rows + c]
                out_ref[p * rows : (p + 1) * rows, columns] = out[c * rows : (c + 1) * rows]


def attention_backward_kernel(heads, block, places, *refs):
    q_refs = refs[:heads]
    k_ref, v_ref, cos_ref, sin_ref, aux_ref, segr_ref, do_ref, out_ref, dk, dv = refs[heads:]
    length = k_ref.shape[0]
    rows = length // len(places)
    scale = HEAD_SIZE**-0.5
    keys = rotate(in_sequence(k_ref, places, rows), cos_ref[...], sin_ref[...]).astype(BF16)
    vals = in_sequence(v_ref, places, rows).astype(BF16)
    dk[...] = jnp.zeros_like(dk)
    dv[...] = jnp.zeros_like(dv)
    for start in range(0, length, block):
        stop = start + block
        allowed = attention_mask(aux_ref, segr_ref, start, stop)
        here = places[start // rows : stop // rows]
        for h in range(heads):
            columns = slice(h * HEAD_SIZE, (h + 1) * HEAD_SIZE)
            query, probs = attention_probs(
                q_refs[h], keys[:stop], cos_ref, sin_ref, allowed, start, stop, places, rows
            )
            given = in_sequence(do_ref, here, rows, columns).astype(BF16)
            d_probs = dot(given, vals[:stop], NT)
            delta = jnp.sum(probs * d_probs, axis=1, keepdims=True)
            d_scores = (probs * (d_probs - delta)).astype(BF16)
            d_query = dot(d_scores, keys[:stop]) * scale
            d_query = rotate(d_query, cos_ref[start:stop, :], -sin_ref[start:stop, :]).astype(BF16)
            for c, p in enumerate(here):
                out_ref[p * rows : (p + 1) * rows, columns] = d_query[c * rows : (c + 1) * rows]
            dk[:stop, :] += dot(d_scores, query, TN)
            dv[:stop, :] += dot(probs.astype(BF16), given, TN)
    d_keys = rotate(dk[...] * scale, cos_ref[...], -sin_ref[...]).astype(BF16)
    d_vals = dv[...].astype(BF16)
    for c, p in enumerate(places):
        there = slice(p * rows, (p + 1) * rows)
        out_ref[there, heads * HEAD_SIZE : (heads + 1) * HEAD_SIZE] = d_keys[
            c * rows : (c + 1) * rows
        ]
        out_ref[there, (heads + 1) * HEAD_SIZE :] = d_vals[c * rows : (c + 1) * rows]


def attention_call(
    kernel, name, panel, first, heads, tables, aux, segr, extra, width, scratch, places
):
    length = panel.shape[0]

    def column(index):
        return pl.BlockSpec((length, HEAD_SIZE), lambda i: (0, index))

    def whole(array):
        return pl.BlockSpec(array.shape, lambda i: (0, 0))

    specs = [column(first // HEAD_SIZE + h) for h in range(heads + 2)]
    operands = [*tables, aux, segr]
    specs += [whole(a) for a in operands]
    if extra is not None:
        specs.append(pl.BlockSpec((length, heads * HEAD_SIZE), lambda i: (0, 0)))
        operands.append(extra)
    return pl.pallas_call(
        partial(kernel, heads, min(256, length), places),
        grid=(1,),
        in_specs=specs,
        out_specs=pl.BlockSpec((length, width), lambda i: (0, 0)),
        out_shape=jax.ShapeDtypeStruct((length, width), BF16),
        scratch_shapes=scratch,
        compiler_params=pltpu.CompilerParams(vmem_limit_bytes=VMEM_LIMIT),
        cost_estimate=pl.CostEstimate(
            flops=(5000 if extra is not None else 3300) * heads * length * length,
            bytes_accessed=4 * length * 12 * HEAD_SIZE,
            transcendentals=heads * length * length,
        ),
        name=name,
    )(*([panel] * (heads + 2)), *operands)


def split_pair(value):
    high = value.astype(BF16)
    return high, (value - high.astype(F32)).astype(BF16)


def widen(value, expand_ref):
    high, rest = split_pair(value)
    return dot(jnp.concatenate([high, rest], axis=1), expand_ref[...])


def by_head(value, reduce_ref):
    high, rest = split_pair(value)
    return dot(high, reduce_ref[...]) + dot(rest, reduce_ref[...])


def conv_rows(current, halo, pad, taps_ref, aux):
    rows = current.shape[0]
    pad[0:8, :] = halo
    pad[8 : 8 + rows, :] = current
    out = taps_ref[3:4, :] * current
    for k in range(1, 4):
        out = out + taps_ref[3 - k : 4 - k, :] * (pad[8 - k : 8 - k + rows, :] * aux[:, k : k + 1])
    return out


def head_scalars(dt_raw, par_ref, lower):
    biased = dt_raw + par_ref[1:2, :]
    step = jnp.maximum(biased, 0.0) + jnp.log1p(jnp.exp(-jnp.abs(biased)))
    log_decay = -step * jnp.exp(par_ref[0:1, :])
    cumulative = sums_of(lower, log_decay)
    return biased, step, log_decay, cumulative


def triangle(rows, flip):
    i = lax.broadcasted_iota(jnp.int32, (rows, rows), 0)
    j = lax.broadcasted_iota(jnp.int32, (rows, rows), 1)
    return (i <= j) if flip else (i >= j)


def mamba_forward_kernel(
    cols,
    p_ref,
    halo_ref,
    aux_ref,
    segr_ref,
    cx_ref,
    cbc_ref,
    par_ref,
    dskip_ref,
    mgain_ref,
    expand_ref,
    gm_ref,
    sq_ref,
    y_ref,
    st_ref,
    state,
    pad_x,
    pad_bc,
):
    width, states = cols["width"], cols["states"]
    rows = p_ref.shape[0]
    r_ref, halo_r_ref = p_ref.at[:, 2 * width :], halo_ref.at[:, 2 * width :]
    x0, bc0, dt0 = cols["x"], cols["bc"], cols["dt"]

    @pl.when(pl.program_id(0) == 0)
    def _():
        state[...] = jnp.zeros_like(state)

    aux = aux_ref[...]
    u_x = conv_rows(
        p_ref[:, x0 : x0 + width], halo_ref[:, x0 : x0 + width], pad_x, cx_ref, aux
    )
    x_conv = u_x * sigmoid(u_x)
    u_bc = conv_rows(
        r_ref[:, bc0 : bc0 + 2 * states], halo_r_ref[:, bc0 : bc0 + 2 * states], pad_bc, cbc_ref, aux
    )
    bc = (u_bc * sigmoid(u_bc)).astype(BF16)
    keys, query = bc[:, :states], bc[:, states:]
    lower = triangle(rows, False)
    _, step, _, cum = head_scalars(
        r_ref[:, dt0 : dt0 + LANES], par_ref, lower.astype(F32).astype(BF16)
    )
    cum_t = cum.T
    last = cum[rows - 1 : rows, :]
    entering = jnp.exp(cum) * aux[:, 7:8]
    leaving = jnp.exp(last - cum) * aux[:, 8:9]
    wide = widen(jnp.concatenate([step, entering, leaving], axis=0), expand_ref)
    step_w, enter_w, leave_w = wide[:rows], wide[rows : 2 * rows], wide[2 * rows :]
    xs = x_conv * step_w
    xs_low = xs.astype(BF16)
    mask = lower & (aux[:, 0:1] == segr_ref[0:1, :])
    c_dot_b = dot(query, keys, NT)
    held = state[...]
    held_low = held.astype(BF16)
    st_ref[0] = held_low
    carried = dot(query, held_low) * enter_w
    lane = lax.broadcasted_iota(jnp.int32, (rows, LANES), 1)
    parts = []
    for pair in range(width // LANES):
        pair_x = xs_low[:, pair * LANES : (pair + 1) * LANES]
        sides = []
        for e in range(2):
            h = 2 * pair + e
            gap = cum[:, h : h + 1] - cum_t[h : h + 1, :]
            decay = jnp.exp(jnp.where(mask, gap, MASK_FILL))
            sides.append(dot((decay * c_dot_b).astype(BF16), pair_x))
        parts.append(jnp.where(lane < P_SIZE, sides[0], sides[1]))
    y = jnp.concatenate(parts, axis=1) + carried + dskip_ref[0:1, :] * x_conv
    state[...] = held * enter_w[rows - 1 : rows, :] + dot(
        keys, (leave_w * xs).astype(BF16), TN
    )
    z = p_ref[:, :width]
    gated = y * (z * sigmoid(z))
    y_ref[...] = y
    gm_ref[...] = (gated * mgain_ref[0:1, :]).astype(BF16)
    sq_ref[...] = jnp.broadcast_to(jnp.sum(gated * gated, axis=1, keepdims=True), sq_ref.shape)


def mamba_backward_kernel(
    cols,
    p_ref,
    halo_ref,
    aux_ref,
    segr_ref,
    cx_ref,
    cbc_ref,
    par_ref,
    dskip_ref,
    mgain_ref,
    expand_ref,
    reduce_ref,
    y_ref,
    st_ref,
    db_ref,
    aux2_ref,
    dqkv_ref,
    da_ref,
    gw_ref,
    gcx_ref,
    gcbc_ref,
    gh_ref,
    d_state,
    pad_x,
    pad_bc,
    fut_x,
    fut_bc,
):
    width, states = cols["width"], cols["states"]
    rows = p_ref.shape[0]
    r_ref, halo_r_ref = p_ref.at[:, 2 * width :], halo_ref.at[:, 2 * width :]
    x0, q0, bc0, dt0 = cols["x"], cols["q"], cols["bc"], cols["dt"]
    dp_ref = da_ref.at[:, : 2 * width]
    dr_ref = da_ref.at[:, 2 * width :]
    first_step = pl.program_id(0) == 0

    @pl.when(first_step)
    def _():
        d_state[...] = jnp.zeros_like(d_state)
        gw_ref[...] = jnp.zeros_like(gw_ref)
        gcx_ref[...] = jnp.zeros_like(gcx_ref)
        gcbc_ref[...] = jnp.zeros_like(gcbc_ref)
        gh_ref[...] = jnp.zeros_like(gh_ref)
        fut_x[...] = jnp.zeros_like(fut_x)
        fut_bc[...] = jnp.zeros_like(fut_bc)

    aux = aux_ref[...]
    u_x = conv_rows(
        p_ref[:, x0 : x0 + width], halo_ref[:, x0 : x0 + width], pad_x, cx_ref, aux
    )
    sig_x = sigmoid(u_x)
    x_conv = u_x * sig_x
    u_bc = conv_rows(
        r_ref[:, bc0 : bc0 + 2 * states], halo_r_ref[:, bc0 : bc0 + 2 * states], pad_bc, cbc_ref, aux
    )
    sig_bc = sigmoid(u_bc)
    bc = (u_bc * sig_bc).astype(BF16)
    keys, query = bc[:, :states], bc[:, states:]
    lower = triangle(rows, False).astype(F32).astype(BF16)
    biased, step, log_decay, cum = head_scalars(r_ref[:, dt0 : dt0 + LANES], par_ref, lower)
    cum_t = cum.T
    last = cum[rows - 1 : rows, :]
    entering = jnp.exp(cum) * aux[:, 7:8]
    leaving = jnp.exp(last - cum) * aux[:, 8:9]
    wide = widen(jnp.concatenate([step, entering, leaving], axis=0), expand_ref)
    step_w, enter_w, leave_w = wide[:rows], wide[rows : 2 * rows], wide[2 * rows :]
    xs = x_conv * step_w
    xs_low = xs.astype(BF16)

    y = y_ref[...]
    z = p_ref[:, :width]
    sig_z = sigmoid(z)
    silu_z = z * sig_z
    gated = y * silu_z
    rstd = aux2_ref[:, 0:1]
    inner = aux2_ref[:, 1:2]
    d_mixed = db_ref[:, db_ref.shape[1] - width :]
    g_mgain = jnp.sum(d_mixed * (gated * rstd), axis=0, keepdims=True)
    d_gated = rstd * (d_mixed * mgain_ref[0:1, :]) - gated * inner
    d_y = d_gated * silu_z
    dp_ref[:, :width] = (d_gated * y * (sig_z * (1.0 + z * (1.0 - sig_z)))).astype(BF16)
    gw_ref[0:1, :] += g_mgain
    gw_ref[1:2, :] += jnp.sum(d_y * x_conv, axis=0, keepdims=True)

    dy_low = d_y.astype(BF16)
    held_low = st_ref[0]
    d_next = d_state[...]
    d_next_low = d_next.astype(BF16)
    entered_dy = (enter_w * d_y).astype(BF16)
    left_xs = (leave_w * xs).astype(BF16)
    from_next = leave_w * dot(keys, d_next_low)
    mask_t = triangle(rows, True) & (aux[:, 0:1] == segr_ref[0:1, :])
    b_dot_c = dot(keys, query, NT)
    lane = lax.broadcasted_iota(jnp.int32, (rows, LANES), 1)
    d_gram = jnp.zeros((rows, rows), F32)
    parts = []
    for pair in range(width // LANES):
        pair_dy = dy_low[:, pair * LANES : (pair + 1) * LANES]
        pair_x = xs_low[:, pair * LANES : (pair + 1) * LANES]
        sides = []
        for e in range(2):
            h = 2 * pair + e
            gap = cum_t[h : h + 1, :] - cum[:, h : h + 1]
            decay = jnp.exp(jnp.where(mask_t, gap, MASK_FILL))
            sides.append(dot((decay * b_dot_c).astype(BF16), pair_dy))
            inside = (lane < P_SIZE) if e == 0 else (lane >= P_SIZE)
            only = jnp.where(inside, pair_x, jnp.zeros_like(pair_x))
            d_gram = d_gram + decay * dot(only, pair_dy, NT)
        parts.append(jnp.where(lane < P_SIZE, sides[0], sides[1]))
    d_xs_inner = jnp.concatenate(parts, axis=1)
    d_xs = d_xs_inner + from_next
    d_gram = d_gram.astype(BF16)
    d_keys = dot(d_gram, query) + dot(left_xs, d_next_low, NT)
    d_query = dot(d_gram, keys, TN) + dot(entered_dy, held_low, NT)
    keep_w = enter_w[rows - 1 : rows, :]
    d_state[...] = dot(query, entered_dy, TN) + keep_w * d_next

    y_scan = y - dskip_ref[0:1, :] * x_conv
    pairs = dy_low.astype(F32) * y_scan - xs_low.astype(F32) * d_xs_inner
    d_cum = by_head(pairs - xs * from_next, reduce_ref)
    at_last = jnp.sum(xs * from_next, axis=0, keepdims=True) + keep_w * jnp.sum(
        held_low.astype(F32) * d_next, axis=0, keepdims=True
    )
    at_last = by_head(jnp.broadcast_to(at_last, (8, width)), reduce_ref)[0:1, :]
    d_log = sums_of(triangle(rows, True).astype(F32).astype(BF16), d_cum) + at_last
    d_step = by_head(x_conv * d_xs, reduce_ref) - d_log * jnp.exp(par_ref[0:1, :])
    d_dt = d_step * sigmoid(biased)
    dr_ref[:, dt0 : dt0 + LANES] = d_dt.astype(BF16)
    gh_ref[0:1, :] += jnp.sum(d_log * log_decay, axis=0, keepdims=True)
    gh_ref[1:2, :] += jnp.sum(d_dt, axis=0, keepdims=True)

    d_ux = (dskip_ref[0:1, :] * d_y + step_w * d_xs) * (sig_x * (1.0 + u_x * (1.0 - sig_x)))
    d_conv = jnp.concatenate([d_keys, d_query], axis=1)
    d_ubc = d_conv * (sig_bc * (1.0 + u_bc * (1.0 - sig_bc)))
    for grad, pad, fut, taps_ref, g_ref, d_ref, c0 in (
        (d_ux, pad_x, fut_x, cx_ref, gcx_ref, dp_ref, x0),
        (d_ubc, pad_bc, fut_bc, cbc_ref, gcbc_ref, dr_ref, bc0),
    ):
        size = grad.shape[1]
        g_ref[3:4, :] += jnp.sum(grad * pad[8 : 8 + rows, :], axis=0, keepdims=True)
        for k in range(1, 4):
            shifted = pad[8 - k : 8 - k + rows, :] * aux[:, k : k + 1]
            g_ref[3 - k : 4 - k, :] += jnp.sum(grad * shifted, axis=0, keepdims=True)
        fut[0:rows, :] = grad
        d_in = taps_ref[3:4, :] * grad
        for k in range(1, 4):
            d_in = d_in + taps_ref[3 - k : 4 - k, :] * (
                fut[k : k + rows, :] * aux[:, 3 + k : 4 + k]
            )
        fut[rows : rows + 8, :] = grad[0:8, :]
        d_ref[:, c0 : c0 + size] = d_in.astype(BF16)
    dr_ref[:, q0 : q0 + dqkv_ref.shape[1]] = dqkv_ref[...]


def head_maps(width):
    expand = (np.arange(width)[None, :] // P_SIZE == np.arange(LANES)[:, None]).astype(np.float32)
    return (
        jnp.asarray(np.concatenate([expand, expand], axis=0), BF16),
        jnp.asarray(expand.T, BF16),
    )


def mamba_specs(chunk, chunk_of, parts, members):
    def place(i):
        return chunk_place(chunk_of(i), parts, members)

    def rows(array):
        return pl.BlockSpec((chunk, array.shape[1]), lambda i: (place(i), 0))

    def fixed(array):
        return pl.BlockSpec(array.shape, lambda i: (0, 0))

    def before(i):
        earlier = chunk_place(jnp.maximum(chunk_of(i) - 1, 0), parts, members)
        return ((earlier + 1) * (chunk // 8) - 1, 0)

    def halo(array):
        return pl.BlockSpec((8, array.shape[1]), before)

    aux = pl.BlockSpec((chunk, LANES), lambda i: (chunk_of(i), 0))
    seg = pl.BlockSpec((8, chunk), lambda i: (0, chunk_of(i)))
    return rows, fixed, halo, aux, seg


def mamba_forward(cols, panel, aux, segr, cx, cbc, par, dskip, mgain, chunk, parts, members):
    length = panel.shape[0]
    width, states = cols["width"], cols["states"]
    chunks = length // chunk
    expand, _ = head_maps(width)
    rows, fixed, halo, by_aux, seg = mamba_specs(chunk, lambda i: i, parts, members)
    small = [cx, cbc, par, dskip, mgain, expand]
    shapes = [
        jax.ShapeDtypeStruct((length, width), BF16),
        jax.ShapeDtypeStruct((length, LANES), F32),
        jax.ShapeDtypeStruct((length, width), F32),
        jax.ShapeDtypeStruct((chunks, states, width), BF16),
    ]
    return pl.pallas_call(
        partial(mamba_forward_kernel, cols),
        grid=(chunks,),
        in_specs=[rows(panel), halo(panel), by_aux, seg] + [fixed(a) for a in small],
        out_specs=[
            rows(shapes[0]),
            rows(shapes[1]),
            rows(shapes[2]),
            pl.BlockSpec((1, states, width), lambda i: (i, 0, 0)),
        ],
        out_shape=shapes,
        scratch_shapes=[
            pltpu.VMEM((states, width), F32),
            pltpu.VMEM((chunk + 8, width), F32),
            pltpu.VMEM((chunk + 8, 2 * states), F32),
        ],
        compiler_params=pltpu.CompilerParams(vmem_limit_bytes=VMEM_LIMIT),
        cost_estimate=pl.CostEstimate(
            flops=20000 * length * width,
            bytes_accessed=4 * (panel.size + 3 * length * width),
            transcendentals=length * width * 4,
        ),
        name="mamba_forward",
    )(panel, panel, aux, segr, *small)


def mamba_backward(
    cols,
    panel,
    aux,
    segr,
    cx,
    cbc,
    par,
    dskip,
    mgain,
    y,
    held,
    d_branch_in,
    aux2,
    d_qkv,
    chunk,
    parts,
    members,
):
    length = panel.shape[0]
    width, states = cols["width"], cols["states"]
    chunks = length // chunk
    expand, reduce = head_maps(width)
    rows, fixed, halo, by_aux, seg = mamba_specs(
        chunk, lambda i: chunks - 1 - i, parts, members
    )
    small = [cx, cbc, par, dskip, mgain, expand, reduce]
    sums = [(8, width), (8, width), (8, 2 * states), (8, LANES)]
    whole = jax.ShapeDtypeStruct(panel.shape, BF16)
    return pl.pallas_call(
        partial(mamba_backward_kernel, cols),
        grid=(chunks,),
        in_specs=[rows(panel), halo(panel), by_aux, seg]
        + [fixed(a) for a in small]
        + [
            rows(y),
            pl.BlockSpec((1, states, width), lambda i: (chunks - 1 - i, 0, 0)),
            rows(d_branch_in),
            rows(aux2),
            rows(d_qkv),
        ],
        out_specs=[rows(whole)] + [pl.BlockSpec(s, lambda i: (0, 0)) for s in sums],
        out_shape=[whole]
        + [jax.ShapeDtypeStruct(s, F32) for s in sums],
        scratch_shapes=[
            pltpu.VMEM((states, width), F32),
            pltpu.VMEM((chunk + 8, width), F32),
            pltpu.VMEM((chunk + 8, 2 * states), F32),
            pltpu.VMEM((chunk + 8, width), F32),
            pltpu.VMEM((chunk + 8, 2 * states), F32),
        ],
        compiler_params=pltpu.CompilerParams(vmem_limit_bytes=VMEM_LIMIT),
        cost_estimate=pl.CostEstimate(
            flops=47000 * length * width,
            bytes_accessed=4 * (panel.size + 3 * length * width),
            transcendentals=length * width * 4,
        ),
        name="mamba_backward",
    )(panel, panel, aux, segr, *small, y, held, d_branch_in, aux2, d_qkv)


def pad_rows(value, rows):
    return jnp.pad(value, ((0, rows - value.shape[0]), (0, 0)))


def segment_tables(segment, chunk):
    length = segment.shape[0]
    seg = segment.astype(F32)
    columns = [seg]
    for k in range(1, 4):
        before = jnp.concatenate([jnp.full((k,), -1.0, F32), seg[:-k]])
        columns.append((before == seg).astype(F32))
    for k in range(1, 4):
        after = jnp.concatenate([seg[k:], jnp.full((k,), -1.0, F32)])
        columns.append((after == seg).astype(F32))
    blocks = seg.reshape(-1, chunk)
    ends = blocks[:, -1:]
    prior = jnp.concatenate([jnp.full((1, 1), -1.0, F32), ends[:-1]], axis=0)
    columns.append((blocks == prior).astype(F32).reshape(-1))
    columns.append((blocks == ends).astype(F32).reshape(-1))
    stacked = jnp.stack(columns + [jnp.zeros_like(seg)] * (16 - len(columns)), axis=0)
    return jnp.pad(stacked.T, ((0, 0), (0, LANES - 16))), jnp.broadcast_to(seg, (8, length))


def rms_factor(hidden):
    return lax.rsqrt(jnp.mean(hidden * hidden, axis=-1, keepdims=True) + NORM_EPS)


def norm_backward(hidden, gain, d_normed, grad_h):
    factor = rms_factor(hidden)
    weighted = gain * d_normed
    inner_mean = jnp.mean(weighted * hidden, axis=-1, keepdims=True)
    return grad_h + factor * weighted - hidden * factor**3 * inner_mean, factor


def after(value, *earlier):
    return lax.optimization_barrier((value, *earlier))[0]


def local(
    inputs,
    cotangent,
    seg_ids,
    norm_gains,
    w_q,
    key_value_weight,
    w_zx,
    w_bc,
    w_dt,
    a_log,
    dt_bias,
    d_skip,
    conv_x,
    conv_bc,
    m_gain,
    w_ao,
    w_mo,
    w_gu,
    w_down,
):
    members = lax.axis_size("dp")
    size_z = lax.axis_size("tensor")
    me_z = lax.axis_index("tensor")
    length = seg_ids.shape[1]
    count, model = inputs.shape[1:]
    block = model // members
    owned = key_value_weight.shape[1]
    heads = w_q.shape[2] // HEAD_SIZE
    kv_head = me_z * heads // (QUERY_HEADS // KEY_VALUE_HEADS)
    width = w_zx.shape[3]
    m_heads = w_dt.shape[2]
    states2 = w_bc.shape[2]
    hidden_units = w_gu.shape[3]
    taps = conv_bc.shape[2]
    gains_own = norm_gains.shape[2]
    cols = {"width": width, "states": states2 // 2, "x": width, "q": 0}
    cols["k"] = cols["q"] + heads * HEAD_SIZE
    cols["v"] = cols["k"] + HEAD_SIZE
    cols["bc"] = cols["v"] + HEAD_SIZE
    cols["dt"] = cols["bc"] + states2
    att_width = heads * HEAD_SIZE
    parts = 2 if count % 256 == 0 else 1
    sub = count // parts
    chunk = sub
    chunks = length // chunk
    late = parts - 1
    places = [(c % parts) * size_z + c // parts for c in range(chunks)]

    def split(value):
        return [value[h * sub : (h + 1) * sub] for h in range(parts)]

    def by_part(value):
        rows = size_z * sub
        return [value[h * rows : (h + 1) * rows] for h in range(parts)]

    lane_rows = 2 * KEY_VALUE_HEADS * HEAD_SIZE + states2
    shared = jnp.concatenate(
        [
            jnp.pad(norm_gains[0], ((0, 0), (0, lane_rows - gains_own))),
            jnp.pad(conv_bc[0], ((0, 10), (0, lane_rows - taps))),
            jnp.concatenate([key_value_weight[0], w_bc[0]], axis=1),
        ],
        axis=0,
    )
    def scatter_dp(value):
        return lax.psum_scatter(value, "dp", scatter_dimension=0, tiled=True)

    def gather_dp(value, *earlier):
        if earlier:
            value = after(value, *earlier)
        return lax.all_gather(value, "dp", axis=0, tiled=True)

    x_parts = split(inputs[0])
    x_first = z_gather_first(x_parts[0])
    shared = z_gather_direct(shared).reshape(size_z, 16 + owned, lane_rows)
    tiny = shared[:, :16]
    shared = shared[:, 16:].reshape(block, lane_rows)
    kv_cols = [
        lax.dynamic_slice_in_dim(shared, (base + kv_head) * HEAD_SIZE, HEAD_SIZE, 1)
        for base in (0, KEY_VALUE_HEADS)
    ]
    panel_rest = jnp.concatenate(
        [w_q[0]]
        + kv_cols
        + [
            shared[:, 2 * KEY_VALUE_HEADS * HEAD_SIZE :],
            jnp.pad(w_dt[0], ((0, 0), (0, LANES - m_heads))),
        ],
        axis=1,
    )
    rest_width = panel_rest.shape[1]
    tiny = jnp.concatenate(
        [
            jnp.swapaxes(tiny[:, :2, :gains_own], 0, 1).reshape(2, block),
            jnp.pad(
                jnp.swapaxes(tiny[:, 2:6, :taps], 0, 1).reshape(4, size_z * taps),
                ((0, 10), (0, block - size_z * taps)),
            ),
        ],
        axis=0,
    )
    panel_rows = jnp.concatenate([w_zx[0].reshape(block, 2 * width), panel_rest], axis=1)
    all_width = panel_rows.shape[1]
    tiny = jnp.pad(tiny, ((0, 0), (0, all_width - block)))
    panel_rows, tiny = ordered((panel_rows, tiny), *x_first)
    panel_rows = jnp.concatenate([panel_rows, tiny], axis=0)
    w_all = gather_dp(panel_rows)
    x_moved = z_gather_parts(x_parts, None, x_first)
    tiny = w_all.reshape(members, block + 16, all_width)[:, block:, :block].astype(F32)
    gains = jnp.swapaxes(tiny[:, :2], 0, 1).reshape(2, model)
    convbc_all = jnp.swapaxes(tiny[:, 2:6, : size_z * taps], 0, 1).reshape(4, states2)
    gain1, gain2 = gains[0:1], gains[1:2]
    w_b = gather_dp(jnp.concatenate([w_ao[0], w_mo[0]], axis=0).T, panel_rows)
    w_cd = jnp.concatenate([w_gu[0].reshape(block, 2 * hidden_units), w_down[0].T], axis=1)
    w_cd = gather_dp(w_cd, panel_rows)

    seg_own, a_own, dtb_own, dskip_own, cx_own, mgain_own = ordered(
        [seg_ids[0], a_log[0], dt_bias[0], d_skip[0], conv_x[0], m_gain[0]], panel_rows
    )
    aux, segr = segment_tables(seg_own, chunk)
    tables = [jnp.asarray(t) for t in rotary_rows(length)]
    cx = pad_rows(cx_own, 8)
    cbc = pad_rows(convbc_all, 8)
    par = jnp.pad(jnp.stack([a_own, dtb_own]), ((0, 6), (0, LANES - m_heads)))
    dskip = jnp.broadcast_to(jnp.repeat(dskip_own, P_SIZE)[None, :], (8, width))
    mgain = jnp.broadcast_to(mgain_own[None, :], (8, width))
    setup = (aux, segr, cx, cbc, par, dskip, mgain)

    held = ()
    d_moved = None
    for h in range(parts):
        x_all = z_place(x_parts[h], x_moved[h])
        held = norm_project(x_all, gain1, w_all, held, h, parts, members)
        if d_moved is None:
            d_moved = z_gather_parts([after(cotangent[0], held[0])])[0]
    normed1, panel = held
    panel = after(panel, *d_moved[0])
    gm, squares, y_out, held = mamba_forward(cols, panel, *setup, chunk, parts, size_z)
    squares = z_sum(squares[:, 0].reshape(-1, LANES)).reshape(length, 1)
    attended = attention_call(
        attention_forward_kernel,
        "attention_forward",
        after(panel, y_out, *d_moved[min(1, size_z - 2)]),
        2 * width + cols["q"],
        heads,
        tables,
        aux,
        segr,
        None,
        att_width,
        [],
        places,
    )
    rstd = lax.rsqrt(squares / (HM * P_SIZE) + NORM_EPS)
    branch = branch_product(attended, gm, rstd, w_b)
    sums, moved = z_scatter_parts(by_part(branch), {(0, size_z - 2): d_moved[-1]})
    x_own = after(inputs[0], branch).astype(F32)
    h_mid, normed2_own = [], []
    for h, x in enumerate(split(x_own)):
        total = sums[h]
        if h:
            total = after(total, normed2_own[h - 1])
        h_mid.append(x + total)
        normed2_own.append((h_mid[h] * rms_factor(h_mid[h]) * gain2).astype(BF16))
    moved = z_gather_parts(normed2_own)
    d_out = [
        z_place(own, [[split(right)[h], split(left)[h]] for right, left in d_moved])
        for h, own in enumerate(split(cotangent[0]))
    ]
    normed2 = [z_place(own, m) for own, m in zip(normed2_own, moved)]
    act, d_gate, d_up = feed_forward(normed2, d_out, w_cd, hidden_units)
    d_norm2 = transposed_product([d_gate, d_up], w_cd, 0)
    first = z_scatter_first(by_part(d_norm2))
    sums, moved = z_scatter_parts(by_part(d_norm2), None, first)
    g_cd, pieces = None, 4
    steps = [first, moved[late][0], moved[0][-1], moved[late][-1]]
    for piece in range(pieces):
        left, right = ordered((normed2, d_out), *steps[piece])
        g_cd = gradient([left, left, right], [d_gate, d_up, act], g_cd, piece, pieces)
    g_cd = scatter_dp(g_cd)
    grad_mid, grad_low = [], []
    for h, part in enumerate(split(cotangent[0])):
        total = sums[h]
        if h:
            total = after(total, grad_low[h - 1])
        grad, _ = norm_backward(h_mid[h], gain2, total, part.astype(F32))
        grad_mid.append(grad)
        grad_low.append(grad.astype(BF16))
    h_mid_all = jnp.concatenate(h_mid, axis=0)
    ffn = transposed_product([after(act, *moved[0][-1])], w_cd, 2)
    if parts > 1:
        ffn = jnp.swapaxes(ffn.reshape(parts, size_z, sub, model), 0, 1).reshape(length, model)
    moved = z_gather_parts(grad_low, {(late, 1): [ffn]})
    d_branch = [z_place(own, m) for own, m in zip(grad_low, moved)]
    ffn = line_scatter([ffn], *moved[late][-1])[0]
    g_c, g_d = g_cd[:, : 2 * hidden_units], g_cd[:, 2 * hidden_units :]

    d_b, inner = branch_back(d_branch, w_b, gm)
    inner = z_sum(inner[:, 0].reshape(-1, LANES)).reshape(length, 1)
    d_qkv = attention_call(
        attention_backward_kernel,
        "attention_backward",
        after(panel, g_cd),
        2 * width + cols["q"],
        heads,
        tables,
        aux,
        segr,
        d_b,
        att_width + 2 * HEAD_SIZE,
        [pltpu.VMEM((length, HEAD_SIZE), F32), pltpu.VMEM((length, HEAD_SIZE), F32)],
        places,
    )
    aux2 = jnp.pad(
        jnp.concatenate([rstd, rstd**3 * inner / (HM * P_SIZE)], axis=1),
        ((0, 0), (0, LANES - 2)),
    )
    d_all, g_wide, g_cx, g_cbc, g_heads = mamba_backward(
        cols, panel, *setup, y_out, held, d_b, aux2, d_qkv, chunk, parts, size_z
    )
    mixed = (after(gm, aux2).astype(F32) * rstd).astype(BF16)
    mixed = jnp.concatenate([attended, mixed], axis=1)
    g_all = gradient([[normed1], d_branch], [d_all, mixed], None, 0, 1)
    d_norm1, low = [], g_all
    for h in range(parts):
        low = back_product(after(d_all, low), w_all, h, parts, members, model)
        d_norm1.append(low)
    low = d_norm1[-1:]
    g_all = scatter_dp(g_all)
    g_zx = g_all[:, : 2 * width].astype(F32)
    g_rest = g_all[:, 2 * width : all_width]
    g_b = g_all[:, all_width:].astype(F32)
    by_dp = [
        g_cbc[:4].reshape(-1, LANES),
        g_heads[0:2],
        jnp.pad(g_wide[1].reshape(m_heads, P_SIZE).sum(axis=1), (0, LANES - m_heads))[None],
        g_cx[:4].reshape(-1, LANES),
        g_wide[0].reshape(-1, LANES),
    ]
    ends = np.cumsum([v.shape[0] for v in by_dp])
    by_dp = jnp.concatenate(by_dp, axis=0)
    by_dp = pad_rows(by_dp, -(-by_dp.shape[0] // 8) * 8)
    by_dp = dp_sum(after(by_dp, *low))
    dp_taps = size_z * taps
    g_convbc = lax.dynamic_slice_in_dim(
        by_dp[: ends[0]].reshape(4, states2), lax.axis_index("dp") * dp_taps, dp_taps, 1
    )
    g_convbc = jnp.pad(
        g_convbc.T.reshape(size_z, taps, 4), ((0, 0), (0, owned - taps), (0, 0))
    ).reshape(block, 4)
    g_alog = by_dp[ends[0] : ends[0] + 1, :m_heads]
    g_dtbias = by_dp[ends[0] + 1 : ends[1], :m_heads]
    g_dskip = by_dp[ends[1] : ends[2], :m_heads]
    g_convx = by_dp[ends[2] : ends[3]].reshape(1, 4, width)
    g_mgain = by_dp[ends[3] : ends[4]].reshape(1, width)

    g_rest = g_rest.astype(F32)
    first = cols["q"]
    gain1_own = jnp.sum(panel_rest.astype(F32) * g_rest, axis=1) + jnp.sum(
        w_zx[0].reshape(block, 2 * width).astype(F32) * g_zx, axis=1
    )
    gain2_own = jnp.sum(
        w_gu[0].reshape(block, 2 * hidden_units).astype(F32) * g_c.astype(F32),
        axis=1,
    )
    mine = lax.axis_index("dp") * block
    gain1_own = gain1_own / lax.dynamic_slice_in_dim(gain1[0], mine, block, 0)
    gain2_own = gain2_own / lax.dynamic_slice_in_dim(gain2[0], mine, block, 0)
    small = jnp.concatenate([gain1_own[:, None], gain2_own[:, None], g_convbc], axis=1)
    g_q = g_rest[:, : cols["k"] - first]
    g_dt = g_rest[:, cols["dt"] - first : cols["dt"] - first + m_heads]
    kv_part = jnp.zeros((block, 2 * KEY_VALUE_HEADS * HEAD_SIZE), F32)
    for base, name in ((0, "k"), (KEY_VALUE_HEADS, "v")):
        at = cols[name] - first
        kv_part = lax.dynamic_update_slice_in_dim(
            kv_part, g_rest[:, at : at + HEAD_SIZE], (base + kv_head) * HEAD_SIZE, 1
        )
    kv_total = 2 * KEY_VALUE_HEADS * HEAD_SIZE
    shared_grad = jnp.concatenate(
        [
            kv_part,
            g_rest[:, cols["bc"] - first : cols["dt"] - first],
            jnp.pad(small, ((0, 0), (0, LANES - small.shape[1]))),
        ],
        axis=1,
    )
    sums, moved = z_scatter_parts(d_norm1, {(late, 1): [ffn]})
    hidden_out = (h_mid_all + ffn).astype(BF16)
    shared_grad = z_scatter_direct(shared_grad.astype(BF16))
    small = shared_grad[:, kv_total + states2 :]
    shared_grad = shared_grad[:, : kv_total + states2]
    g_gains = small[:, :2].T[None]
    g_convbc = small[:taps, 2:6].T[None]
    norm_sum = jnp.concatenate(sums, axis=0)
    grad_in, _ = norm_backward(x_own, gain1, norm_sum, jnp.concatenate(grad_mid, axis=0))
    input_grad = grad_in

    return (
        hidden_out[None],
        input_grad[None],
        g_gains,
        g_q[None],
        shared_grad[None, :, :kv_total],
        g_zx.reshape(1, block, 2, width),
        shared_grad[None, :, kv_total:],
        g_dt[None],
        g_alog,
        g_dtbias,
        g_dskip,
        g_convx,
        g_convbc,
        g_mgain,
        g_b[:, :att_width].T[None],
        g_b[:, att_width:].T[None],
        g_c.astype(F32).reshape(1, block, 2, hidden_units),
        g_d.astype(F32).T[None],
    )


def solution(mesh):
    return jax.shard_map(
        local,
        mesh=mesh,
        in_specs=(
            P("dp", "tensor", None),
            P("dp", "tensor", None),
            P("dp", None),
            P(None, None, ("dp", "tensor")),
            P(None, "dp", "tensor"),
            P(None, ("dp", "tensor"), None),
            P(None, "dp", None, "tensor"),
            P(None, ("dp", "tensor"), None),
            P(None, "dp", "tensor"),
            P(None, "tensor"),
            P(None, "tensor"),
            P(None, "tensor"),
            P(None, None, "tensor"),
            P(None, None, ("dp", "tensor")),
            P(None, "tensor"),
            P(None, "tensor", "dp"),
            P(None, "tensor", "dp"),
            P(None, "dp", None, "tensor"),
            P(None, "tensor", "dp"),
        ),
        out_specs=(
            P("dp", "tensor", None),
            P("dp", "tensor", None),
            P(None, None, ("dp", "tensor")),
            P(None, "dp", "tensor"),
            P(None, ("dp", "tensor"), None),
            P(None, "dp", None, "tensor"),
            P(None, ("dp", "tensor"), None),
            P(None, "dp", "tensor"),
            P(None, "tensor"),
            P(None, "tensor"),
            P(None, "tensor"),
            P(None, None, "tensor"),
            P(None, None, ("dp", "tensor")),
            P(None, "tensor"),
            P(None, "tensor", "dp"),
            P(None, "tensor", "dp"),
            P(None, "dp", None, "tensor"),
            P(None, "tensor", "dp"),
        ),
        check_vma=False,
    )
```

time: 1090 us -> 832 us (0.76)
  waiting for transfers between devices: 415 us -> 214 us
  Pallas kernels: 87.4 us -> 239 us
  matrix products: 136 us -> 0 us
  local copies, waits for them, and re-layouts: 119 us -> 74.3 us
  starting transfers between devices: 212 us -> 193 us
  other arithmetic: 94.1 us -> 82.4 us
    pallas_call x7 -> x24, Pallas kernels: 40.8 us -> 193 us  [the longest x5 55.6 us: gradient(): pl.pallas_call(partial(gradient_kernel, parts), grid=(steps,), in_specs=[...]
    dot_general x13 -> x0, matrix products: 136 us -> none  [dot(): return lax.dot_general(left, right, dims, preferred_element_type=F32)]
    ppermute x48 -> x4, waiting for transfers between devices: 125 us -> 0.01 us  [send_dp(): return lax.ppermute(value, 'dp', [(i, i ^ mask) for i in range(size)])]
    ppermute x36 -> x78, waiting for transfers between devices: 272 us -> 178 us  [the longest x20 82.9 us: z_gather_parts(): lax.ppermute(left, 'tensor', [(i, i - 1) for i in range(1, size - s)])]
    ppermute x36 -> x78, starting transfers between devices: 87.2 us -> 166 us  [the longest x17 70 us: z_scatter_parts(): right = lax.ppermute(to_right, 'tensor', [(i, i + 1) for i in range(s + 1)])]
    ppermute x48 -> x4, starting transfers between devices: 55 us -> 3.62 us  [send_dp(): return lax.ppermute(value, 'dp', [(i, i ^ mask) for i in range(size)])]
    ppermute x15 -> x12, starting transfers between devices: 69.9 us -> 23 us  [send_z(): lax.ppermute(value, 'tensor', [(i, (i + shift) % size) for i in range(siz...]
    unnamed x179 -> x226, local copies, waits for them, and re-layouts: 61.3 us -> 34.2 us
  transfers between devices with their start and end apart: 101 -> 100, of which waited for: 37 -> 42; matrix products, arithmetic and copies ran while one was open for 25% -> 15% of each run, Pallas kernels for 8% -> 24%
where the time goes in v2:
time: 832 us; the launch traced here: 820 us
  Pallas kernels  239 us (29%)
  waiting for transfers between devices  214 us (26%)
  starting transfers between devices  193 us (23%)
  other arithmetic  82.4 us (10%)
  local copies, waits for them, and re-layouts  74.3 us (9%)
  between operations  16.9 us (2%)
    ppermute x20, waiting for transfers between devices, z_gather_parts(): lax.ppermute(left, 'tensor', [(i, i - 1) for i in range(1, size - s)])  82.9 us
    ppermute x17, waiting for transfers between devices, z_scatter_parts(): right = lax.ppermute(to_right, 'tensor', [(i, i + 1) for i in range(s + 1)])  72.5 us
    ppermute x17, starting transfers between devices, z_scatter_parts(): right = lax.ppermute(to_right, 'tensor', [(i, i + 1) for i in range(s + 1)])  70 us
    pallas_call x5, Pallas kernels, gradient(): pl.pallas_call(partial(gradient_kernel, parts), grid=(steps,), in_specs=[...  55.6 us
    ppermute x20, starting transfers between devices, z_gather_parts(): lax.ppermute(right, 'tensor', [(i, i + 1) for i in range(s, size - 1)])  41.9 us
    unnamed x226, local copies, waits for them, and re-layouts  34.2 us
    dynamic_update_slice x20, other arithmetic, z_place(): out = lax.dynamic_update_slice_in_dim(out, piece, at, 0)  32.9 us
    pallas_call x1, Pallas kernels, mamba_backward(): pl.pallas_call(partial(mamba_backward_kernel, cols), grid=(chunks,), in_s...  31.7 us
  transfers between devices with their start and end apart: 100, of which 42 were waited for; matrix products, arithmetic and copies ran while one was open for 15% of the time, Pallas kernels for 24%

profile of v2, /device:TPU:0, one launch (start us, length us, event | category | flops | bytes accessed | tf_op | source)
XLA Modules:
  0.0 819.9 jit_solution(5675499777523578076)
XLA Ops:
  8.7 5.8 collective-permute-start.9
  23.7 12.4 %collective-permute-done.6 = bf16[80,1024]{1,0:T(8,128)(2,1)} collective-permute-done((bf16[80,1024]{1,0:T(8,128)(2,1)S(1)}, bf16[80,1024]{1,0:T(8,128)(2,1)}, u32[]{:S(2)}, u32[]{:S(2)}) %collective-permute-start.6) | collective-permute-done | bytes 163872 | tf_op jit(solution)/shard_map/ppermute | solution.py:116
  37.0 5.0 collective-permute-done.7
  70.4 6.5 collective-permute-done.1
  79.3 8.8 %collective-permute-done.12 = bf16[128,2048]{1,0:T(8,128)(2,1)} collective-permute-done((bf16[128,2048]{1,0:T(8,128)(2,1)}, bf16[128,2048]{1,0:T(8,128)(2,1)}, u32[]{:S(2)}, u32[]{:S(2)}) %collective-permute-start.12) | collective-permute-done | bytes 524320 | tf_op jit(solution)/shard_map/ppermute | solution.py:167
  90.3 9.0 %collective-permute-done.3 = bf16[128,2048]{1,0:T(8,128)(2,1)} collective-permute-done((bf16[128,2048]{1,0:T(8,128)(2,1)}, bf16[128,2048]{1,0:T(8,128)(2,1)}, u32[]{:S(2)}, u32[]{:S(2)}) %collective-permute-start.3) | collective-permute-done | bytes 524320 | tf_op jit(solution)/shard_map/ppermute | solution.py:167
  101.4 9.1 %collective-permute-done.13 = bf16[128,2048]{1,0:T(8,128)(2,1)S(1)} collective-permute-done((bf16[128,2048]{1,0:T(8,128)(2,1)}, bf16[128,2048]{1,0:T(8,128)(2,1)S(1)}, u32[]{:S(2)}, u32[]{:S(2)}) %collective-permute-start.13) | collective-permute-done | bytes 524320 | tf_op jit(solution)/shard_map/ppermute | solution.py:167
  114.6 4.9 collective-permute-done.4
  125.7 13.8 %norm_project.2 = (bf16[1024,2048]{1,0:T(8,128)(2,1)}, f32[1024,2688]{1,0:T(8,128)}) custom-call(bf16[512,2048]{1,0:T(8,128)(2,1)S(1)} %copy-done.16, f32[1,2048]{1,0:T(1,128)S(1)} %bitcast.137, bf16[2176,2688]{1,0:T(8,128)(2,1)} %all-gather.4.cloned.1.call-done.w_ref), custom_call_target="tpu_custom_call" | custom-call | flops 5637144576 | bytes 18612224 | tf_op jit(solution)/shard_map/norm_project/pallas_call | solution.py:319
  144.5 13.9 %norm_project.3 = (bf16[1024,2048]{1,0:T(8,128)(2,1)}, f32[1024,2688]{1,0:T(8,128)}) custom-call(bf16[512,2048]{1,0:T(8,128)(2,1)S(1)} %get-tuple-element.435.x_ref, f32[1,2048]{1,0:T(1,128)S(1)} %bitcast.138, bf16[2176,2688]{1,0:T(8,128)(2,1)} %all-gather.4.cloned.1.call-done.w_ref, ...), custom_call_target="tpu_custom_call", output_to_operand_aliasing={{0}: (3, {}), {1}: (4, {})} | custom-call | flops 5637144576 | bytes 18612224 | tf_op jit(solution)/shard_map/norm_project/pallas_call | solution.py:319
  158.4 4.0 collective-permute-done.15
  162.4 5.1 collective-permute-done.16
  170.6 13.7 %mamba_forward.1 = (bf16[1024,768]{1,0:T(8,128)(2,1)S(1)}, f32[1024,128]{1,0:T(8,128)S(1)}, f32[1024,768]{1,0:T(8,128)}, bf16[8,256,768]{2,1,0:T(8,128)(2,1)}) custom-call(f32[1024,2688]{1,0:T(8,128)} %get-tuple-element.233.p_ref.halo_ref.refs_0_.refs_1_.refs_2_.refs_3_, f32[1024,2688]{1,0:T(8,128)} %get-tuple-element.233.p_ref.halo_ref.refs_0_.refs_1_.refs_2_.refs_3_, ...), custom_call_target="tpu_custom_call" | custom-call | flops 15728640000 | bytes 20447232 | tf_op jit(solution)/shard_map/mamba_forward/pallas_call | solution.py:1034
  186.3 5.7 collective-permute-start.20
  198.5 6.0 attention_forward.1.att_ref
  206.1 7.8 branch.1
  221.5 7.5 collective-permute-done.22
  235.1 6.4 collective-permute-start.30
  247.9 5.4 collective-permute-done.30
  255.9 4.5 collective-permute-done.24
  261.1 5.8 collective-permute-start.32
  279.5 5.3 collective-permute-done.28
  286.1 4.9 collective-permute-start.34
  292.9 5.1 collective-permute-start.36
  299.2 4.2 collective-permute-done.34
  305.8 5.2 collective-permute-start.42
  326.3 6.7 collective-permute-done.39
  347.6 8.7 %collective-permute-done.45 = bf16[128,2048]{1,0:T(8,128)(2,1)} collective-permute-done((bf16[128,2048]{1,0:T(8,128)(2,1)}, bf16[128,2048]{1,0:T(8,128)(2,1)}, u32[]{:S(2)}, u32[]{:S(2)}) %collective-permute-start.45) | collective-permute-done | bytes 524320 | tf_op jit(solution)/shard_map/ppermute | solution.py:167
  372.7 20.4 %feed_forward.1 = (bf16[1024,1024]{1,0:T(8,128)(2,1)S(1)}, bf16[1024,1024]{1,0:T(8,128)(2,1)S(1)}, bf16[1024,1024]{1,0:T(8,128)(2,1)}) custom-call(bf16[512,2048]{1,0:T(8,128)(2,1)} %add_dynamic-update-slice_fusion.9.refs_0_.refs_2_, bf16[512,2048]{1,0:T(8,128)(2,1)} %copy-done.1, bf16[512,2048]{1,0:T(8,128)(2,1)} %get-tuple-element.231.refs_2_.refs_4_, ...), custom_call_target="tpu_custom_call" | custom-call | flops 12884901888 | bytes 20971520 | tf_op jit(solution)/shard_map/feed_forward/pallas_call | solution.py:419
  396.7 12.1 %transposed_product.2 = bf16[1024,2048]{1,0:T(8,128)(2,1)} custom-call(bf16[1024,1024]{1,0:T(8,128)(2,1)S(1)} %get-tuple-element.191.refs_0_.refs_6_, bf16[1024,1024]{1,0:T(8,128)(2,1)S(1)} %copy-done.7, bf16[2048,3072]{1,0:T(8,128)(2,1)} %all-gather.8.cloned.1.call-done.refs_4_.refs_5_.refs_6_.refs_2_.refs_3_.refs_1_, ...), custom_call_target="tpu_custom_call" | custom-call | flops 8589934592 | bytes 16777216 | tf_op jit(solution)/shard_map/transposed_product/pallas_call | solution.py:500
  415.4 7.4 collective-permute-done.48
  423.5 4.4 collective-permute-start.54
  431.0 5.0 collective-permute-done.54
  436.4 9.2 %collective-permute-done.50 = bf16[128,2048]{1,0:T(8,128)(2,1)S(1)} collective-permute-done((bf16[128,2048]{1,0:T(8,128)(2,1)S(1)}, bf16[128,2048]{1,0:T(8,128)(2,1)S(1)}, u32[]{:S(2)}, u32[]{:S(2)}) %collective-permute-start.50) | collective-permute-done | bytes 524320 | tf_op jit(solution)/shard_map/ppermute | solution.py:277
  446.2 5.0 collective-permute-start.56
  451.7 5.5 collective-permute-start.52
  458.5 8.1 gradient.5.refs_9_
  471.1 6.3 collective-permute-start.58
  477.4 8.1 gradient.6.refs_9_
  485.5 8.1 gradient.7.refs_9_
  493.6 8.2 gradient.8
  507.2 4.0 collective-permute-start.66
  516.8 5.4 collective-permute-start.60
  528.2 7.9 transposed_product.3
  536.2 4.8 copy.135
  549.8 12.4 %collective-permute-done.63 = bf16[128,2048]{1,0:T(8,128)(2,1)} collective-permute-done((bf16[128,2048]{1,0:T(8,128)(2,1)}, bf16[128,2048]{1,0:T(8,128)(2,1)}, u32[]{:S(2)}, u32[]{:S(2)}) %collective-permute-start.63) | collective-permute-done | bytes 524320 | tf_op jit(solution)/shard_map/ppermute | solution.py:167
  580.8 8.7 %branch_back.1 = (f32[1024,1024]{1,0:T(8,128)}, f32[1024,128]{1,0:T(8,128)S(1)}) custom-call(bf16[512,2048]{1,0:T(8,128)(2,1)S(1)} %copy-done.22, bf16[512,2048]{1,0:T(8,128)(2,1)} %copy-done.18, bf16[2048,1024]{1,0:T(8,128)(2,1)} %all-gather.6.cloned.1.call-done.w_ref.refs_2_, bf16[1024,768]{1,0:T(8,128)(2,1)S(1)} %copy-done.26), custom_call_target="tpu_custom_call" | custom-call | flops 4294967296 | bytes 8388608 | tf_op jit(solution)/shard_map/branch_back/pallas_call | solution.py:457
  601.3 10.0 %attention_backward.1.dqkv_ref = bf16[1024,512]{1,0:T(8,128)(2,1)S(1)} custom-call(f32[1024,2688]{1,0:T(8,128)} %get-tuple-element.233.p_ref.halo_ref.refs_0_.refs_1_.refs_2_.refs_3_, f32[1024,2688]{1,0:T(8,128)} %get-tuple-element.233.p_ref.halo_ref.refs_0_.refs_1_.refs_2_.refs_3_, ...), custom_call_target="tpu_custom_call" | custom-call | flops 10485760000 | bytes 6291456 | tf_op jit(solution)/shard_map/attention_backward/pallas_call | solution.py:701
  611.4 31.7 %mamba_backward.1 = (bf16[1024,2688]{1,0:T(8,128)(2,1)}, f32[8,768]{1,0:T(8,128)S(1)}, f32[8,768]{1,0:T(8,128)S(1)}, f32[8,512]{1,0:T(8,128)S(1)}, f32[8,128]{1,0:T(8,128)S(1)}) custom-call(f32[1024,2688]{1,0:T(8,128)} %get-tuple-element.233.p_ref.halo_ref.refs_0_.refs_1_.refs_2_.refs_3_, ...), custom_call_target="tpu_custom_call" | custom-call | flops 36962304000 | bytes 20447232 | tf_op jit(solution)/shard_map/mamba_backward/pallas_call | solution.py:1089
  643.1 23.1 %gradient.9 = bf16[2048,3712]{1,0:T(8,128)(2,1)} custom-call(bf16[1024,2048]{1,0:T(8,128)(2,1)} %get-tuple-element.235.refs_0_, bf16[512,2048]{1,0:T(8,128)(2,1)S(1)} %copy-done.23, bf16[512,2048]{1,0:T(8,128)(2,1)S(1)} %copy-done.19, bf16[1024,2688]{1,0:T(8,128)(2,1)} %get-tuple-element.244.refs_3_.d_ref, bf16[1024,1024]{1,0:T(8,128)(2,1)} %pad_maximum_fusion.refs_4_), custom_call_target="tpu_custom_call" | custom-call | flops 15569256448 | bytes 27000832 | tf_op jit(solution)/shard_map/gradient/pallas_call | solution.py:371
  666.3 7.3 reduce-scatter.4.cloned.1.call-done
  676.1 10.3 %back_product.2 = bf16[512,2048]{1,0:T(8,128)(2,1)S(1)} custom-call(bf16[1024,2688]{1,0:T(8,128)(2,1)} %get-tuple-element.244.refs_3_.d_ref, bf16[2176,2688]{1,0:T(8,128)(2,1)} %all-gather.4.cloned.1.call-done.w_ref), custom_call_target="tpu_custom_call" | custom-call | flops 5637144576 | bytes 16547840 | tf_op jit(solution)/shard_map/back_product/pallas_call | solution.py:564
  687.5 3.8 collective-permute-start.75
  693.3 11.2 %back_product.3 = bf16[512,2048]{1,0:T(8,128)(2,1)S(1)} custom-call(bf16[1024,2688]{1,0:T(8,128)(2,1)} %get-tuple-element.244.refs_3_.d_ref, bf16[2176,2688]{1,0:T(8,128)(2,1)} %all-gather.4.cloned.1.call-done.w_ref), custom_call_target="tpu_custom_call" | custom-call | flops 5637144576 | bytes 16547840 | tf_op jit(solution)/shard_map/back_product/pallas_call | solution.py:564
  712.8 4.0 reshape.267
  724.0 9.0 %collective-permute-done.81 = bf16[128,2048]{1,0:T(8,128)(2,1)S(1)} collective-permute-done((bf16[128,2048]{1,0:T(8,128)(2,1)}, bf16[128,2048]{1,0:T(8,128)(2,1)S(1)}, u32[]{:S(2)}, u32[]{:S(2)}) %collective-permute-start.81) | collective-permute-done | bytes 524320 | tf_op jit(solution)/shard_map/ppermute | solution.py:277
  734.4 7.6 collective-permute-done.77
  743.4 5.0 collective-permute-start.83
  749.9 3.8 collective-permute-start.79
  755.8 4.5 collective-permute-done.83
  763.9 4.8 collective-permute-done.79
  769.9 5.7 collective-permute-start.85
  777.3 5.3 collective-permute-done.86
  794.0 5.9 collective-permute-start.93
  (573 shorter events, 297.7 us)
Async XLA Ops:
  7.2 116.0 %all-gather.4.cloned.1.call-start = ((), (), s32[]{:S(2)}) async-start(), calls=%async_computation.3 | async-start | bytes 13160448 | tf_op jit(solution)/shard_map/all_gather | solution.py:1230
  8.7 41.7 %collective-permute-start.9 = (bf16[128,2048]{1,0:T(8,128)(2,1)S(1)}, bf16[128,2048]{1,0:T(8,128)(2,1)}, u32[]{:S(2)}, u32[]{:S(2)}) collective-permute-start(bf16[128,2048]{1,0:T(8,128)(2,1)S(1)} %get-tuple-element.388.in_ref), channel_id=1, source_target_pairs={{0,1},{1,2},{2,3},{4,5},{5,6},{6,7},{8,9},{9,10},{10,11},{12,13},{... | collective-permute-start | bytes 1572872 | tf_op jit(solution)/shard_map/ppermute | solution.py:147
  14.4 35.9 %collective-permute-start.10 = (bf16[128,2048]{1,0:T(8,128)(2,1)S(1)}, bf16[128,2048]{1,0:T(8,128)(2,1)}, u32[]{:S(2)}, u32[]{:S(2)}) collective-permute-start(bf16[128,2048]{1,0:T(8,128)(2,1)S(1)} %get-tuple-element.388.in_ref), channel_id=1, source_target_pairs={{1,0},{2,1},{3,2},{5,4},{6,5},{7,6},{9,8},{10,9},{11,10},{13,12},{... | collective-permute-start | bytes 1572872 | tf_op jit(solution)/shard_map/ppermute | solution.py:148
  15.9 20.2 %collective-permute-start.6 = (bf16[80,1024]{1,0:T(8,128)(2,1)S(1)}, bf16[80,1024]{1,0:T(8,128)(2,1)}, u32[]{:S(2)}, u32[]{:S(2)}) collective-permute-start(bf16[80,1024]{1,0:T(8,128)(2,1)S(1)} %get-tuple-element.401), channel_id=1, source_target_pairs={{0,1},{1,2},{2,3},{3,0},{4,5},{5,6},{6,7},{7,4},{8,9},{9,10},{10,1... | collective-permute-start | bytes 491528 | tf_op jit(solution)/shard_map/ppermute | solution.py:116
  18.6 23.4 %collective-permute-start.7 = (bf16[80,1024]{1,0:T(8,128)(2,1)S(1)}, bf16[80,1024]{1,0:T(8,128)(2,1)}, u32[]{:S(2)}, u32[]{:S(2)}) collective-permute-start(bf16[80,1024]{1,0:T(8,128)(2,1)S(1)} %get-tuple-element.401), channel_id=1, source_target_pairs={{0,2},{1,3},{2,0},{3,1},{4,6},{5,7},{6,4},{7,5},{8,10},{9,11},{10,... | collective-permute-start | bytes 491528 | tf_op jit(solution)/shard_map/ppermute | solution.py:116
  21.1 21.8 %collective-permute-start.8 = (bf16[80,1024]{1,0:T(8,128)(2,1)S(1)}, bf16[80,1024]{1,0:T(8,128)(2,1)}, u32[]{:S(2)}, u32[]{:S(2)}) collective-permute-start(bf16[80,1024]{1,0:T(8,128)(2,1)S(1)} %get-tuple-element.401), channel_id=1, source_target_pairs={{0,3},{1,0},{2,1},{3,2},{4,7},{5,4},{6,5},{7,6},{8,11},{9,8},{10,9... | collective-permute-start | bytes 491528 | tf_op jit(solution)/shard_map/ppermute | solution.py:116
  51.6 152.9 %all-gather.6.cloned.1.call-start = ((), (), s32[]{:S(2)}) async-start(), calls=%async_computation.4 | async-start | bytes 4718592 | tf_op jit(solution)/shard_map/all_gather | solution.py:1230
  54.0 317.4 %all-gather.8.cloned.1.call-start = ((), (), s32[]{:S(2)}) async-start(), calls=%async_computation.5 | async-start | bytes 14155776 | tf_op jit(solution)/shard_map/all_gather | solution.py:1230
  56.8 544.5 %reduce-scatter.6.cloned.1.call-start = ((), (), s32[]{:S(2)}) async-start(), calls=%async_computation.7 | async-start | bytes 14155776 | tf_op jit(solution)/shard_map/reduce_scatter | solution.py:1225
  60.4 16.5 %collective-permute-start.1 = (bf16[128,2048]{1,0:T(8,128)(2,1)S(1)}, bf16[128,2048]{1,0:T(8,128)(2,1)}, u32[]{:S(2)}, u32[]{:S(2)}) collective-permute-start(bf16[128,2048]{1,0:T(8,128)(2,1)S(1)} %get-tuple-element.389.in_ref), channel_id=1, source_target_pairs={{1,0},{2,1},{3,2},{5,4},{6,5},{7,6},{9,8},{10,9},{11,10},{13,12},{... | collective-permute-start | bytes 1572872 | tf_op jit(solution)/shard_map/ppermute | solution.py:167
  67.2 21.0 %collective-permute-start.12 = (bf16[128,2048]{1,0:T(8,128)(2,1)}, bf16[128,2048]{1,0:T(8,128)(2,1)}, u32[]{:S(2)}, u32[]{:S(2)}) collective-permute-start(bf16[128,2048]{1,0:T(8,128)(2,1)} %collective-permute-done.10), channel_id=1, source_target_pairs={{1,0},{2,1},{5,4},{6,5},{9,8},{10,9},{13,12},{14,13},{17,16},{18,1... | collective-permute-start | bytes 1572872 | tf_op jit(solution)/shard_map/ppermute | solution.py:167
  77.6 21.8 %collective-permute-start.3 = (bf16[128,2048]{1,0:T(8,128)(2,1)}, bf16[128,2048]{1,0:T(8,128)(2,1)}, u32[]{:S(2)}, u32[]{:S(2)}) collective-permute-start(bf16[128,2048]{1,0:T(8,128)(2,1)} %collective-permute-done.1), channel_id=1, source_target_pairs={{1,0},{2,1},{5,4},{6,5},{9,8},{10,9},{13,12},{14,13},{17,16},{18,1... | collective-permute-start | bytes 1572872 | tf_op jit(solution)/shard_map/ppermute | solution.py:167
  88.1 22.4 %collective-permute-start.13 = (bf16[128,2048]{1,0:T(8,128)(2,1)}, bf16[128,2048]{1,0:T(8,128)(2,1)S(1)}, u32[]{:S(2)}, u32[]{:S(2)}) collective-permute-start(bf16[128,2048]{1,0:T(8,128)(2,1)} %collective-permute-done.12), channel_id=1, source_target_pairs={{1,0},{5,4},{9,8},{13,12},{17,16},{21,20},{25,24},{29,28}} | collective-permute-start | bytes 1572872 | tf_op jit(solution)/shard_map/ppermute | solution.py:167
  89.6 31.2 %collective-permute-start.14 = (bf16[128,2048]{1,0:T(8,128)(2,1)}, bf16[128,2048]{1,0:T(8,128)(2,1)S(1)}, u32[]{:S(2)}, u32[]{:S(2)}) collective-permute-start(bf16[128,2048]{1,0:T(8,128)(2,1)} %collective-permute-done.11), channel_id=1, source_target_pairs={{2,3},{6,7},{10,11},{14,15},{18,19},{22,23},{26,27},{30,31}} | collective-permute-start | bytes 1572872 | tf_op jit(solution)/shard_map/ppermute | solution.py:166
  99.4 20.1 %collective-permute-start.4 = (bf16[128,2048]{1,0:T(8,128)(2,1)}, bf16[128,2048]{1,0:T(8,128)(2,1)S(1)}, u32[]{:S(2)}, u32[]{:S(2)}) collective-permute-start(bf16[128,2048]{1,0:T(8,128)(2,1)} %collective-permute-done.3), channel_id=1, source_target_pairs={{1,0},{5,4},{9,8},{13,12},{17,16},{21,20},{25,24},{29,28}} | collective-permute-start | bytes 1572872 | tf_op jit(solution)/shard_map/ppermute | solution.py:167
  100.7 20.2 %collective-permute-start.5 = (bf16[128,2048]{1,0:T(8,128)(2,1)S(1)}, bf16[128,2048]{1,0:T(8,128)(2,1)S(1)}, u32[]{:S(2)}, u32[]{:S(2)}) collective-permute-start(bf16[128,2048]{1,0:T(8,128)(2,1)S(1)} %collective-permute-done.2), channel_id=1, source_target_pairs={{2,3},{6,7},{10,11},{14,15},{18,19},{22,23},{26,27},{30,31}} | collective-permute-start | bytes 1572872 | tf_op jit(solution)/shard_map/ppermute | solution.py:166
  139.6 22.9 %collective-permute-start.15 = (bf16[256,2048]{1,0:T(8,128)(2,1)}, bf16[256,2048]{1,0:T(8,128)(2,1)}, u32[]{:S(2)}, u32[]{:S(2)}) collective-permute-start(bf16[256,2048]{1,0:T(8,128)(2,1)} %bitcast.17), channel_id=1, source_target_pairs={{0,1},{1,2},{2,3},{4,5},{5,6},{6,7},{8,9},{9,10},{10,11},{12,13},{... | collective-permute-start | bytes 3145736 | tf_op jit(solution)/shard_map/ppermute | solution.py:166
  142.3 25.2 %collective-permute-start.16 = (bf16[256,2048]{1,0:T(8,128)(2,1)}, bf16[256,2048]{1,0:T(8,128)(2,1)}, u32[]{:S(2)}, u32[]{:S(2)}) collective-permute-start(bf16[256,2048]{1,0:T(8,128)(2,1)} %bitcast.17), channel_id=1, source_target_pairs={{1,0},{2,1},{3,2},{5,4},{6,5},{7,6},{9,8},{10,9},{11,10},{13,12},{... | collective-permute-start | bytes 3145736 | tf_op jit(solution)/shard_map/ppermute | solution.py:167
  167.6 30.9 %collective-permute-start.17 = (bf16[256,2048]{1,0:T(8,128)(2,1)}, bf16[256,2048]{1,0:T(8,128)(2,1)}, u32[]{:S(2)}, u32[]{:S(2)}) collective-permute-start(bf16[256,2048]{1,0:T(8,128)(2,1)} %collective-permute-done.15), channel_id=1, source_target_pairs={{1,2},{2,3},{5,6},{6,7},{9,10},{10,11},{13,14},{14,15},{17,18},{18... | collective-permute-start | bytes 3145736 | tf_op jit(solution)/shard_map/ppermute | solution.py:166
  169.2 29.2 %collective-permute-start.18 = (bf16[256,2048]{1,0:T(8,128)(2,1)}, bf16[256,2048]{1,0:T(8,128)(2,1)}, u32[]{:S(2)}, u32[]{:S(2)}) collective-permute-start(bf16[256,2048]{1,0:T(8,128)(2,1)} %collective-permute-done.16), channel_id=1, source_target_pairs={{1,0},{2,1},{5,4},{6,5},{9,8},{10,9},{13,12},{14,13},{17,16},{18,1... | collective-permute-start | bytes 3145736 | tf_op jit(solution)/shard_map/ppermute | solution.py:167
  230.6 15.9 %collective-permute-start.31 = (bf16[128,2048]{1,0:T(8,128)(2,1)}, bf16[128,2048]{1,0:T(8,128)(2,1)}, u32[]{:S(2)}, u32[]{:S(2)}) collective-permute-start(bf16[128,2048]{1,0:T(8,128)(2,1)} %get-tuple-element.175), channel_id=1, source_target_pairs={{3,2},{7,6},{11,10},{15,14},{19,18},{23,22},{27,26},{31,30}} | collective-permute-start | bytes 1572872 | tf_op jit(solution)/shard_map/ppermute | solution.py:278
  232.2 37.3 %collective-permute-start.26 = (bf16[256,2048]{1,0:T(8,128)(2,1)}, bf16[256,2048]{1,0:T(8,128)(2,1)}, u32[]{:S(2)}, u32[]{:S(2)}) collective-permute-start(bf16[256,2048]{1,0:T(8,128)(2,1)} %collective-permute-done.17), channel_id=1, source_target_pairs={{2,3},{6,7},{10,11},{14,15},{18,19},{22,23},{26,27},{30,31}} | collective-permute-start | bytes 3145736 | tf_op jit(solution)/shard_map/ppermute | solution.py:166
  233.8 35.7 %collective-permute-start.27 = (bf16[256,2048]{1,0:T(8,128)(2,1)}, bf16[256,2048]{1,0:T(8,128)(2,1)}, u32[]{:S(2)}, u32[]{:S(2)}) collective-permute-start(bf16[256,2048]{1,0:T(8,128)(2,1)} %collective-permute-done.18), channel_id=1, source_target_pairs={{1,0},{5,4},{9,8},{13,12},{17,16},{21,20},{25,24},{29,28}} | collective-permute-start | bytes 3145736 | tf_op jit(solution)/shard_map/ppermute | solution.py:167
  235.1 18.2 %collective-permute-start.30 = (bf16[128,2048]{1,0:T(8,128)(2,1)}, bf16[128,2048]{1,0:T(8,128)(2,1)}, u32[]{:S(2)}, u32[]{:S(2)}) collective-permute-start(bf16[128,2048]{1,0:T(8,128)(2,1)} %get-tuple-element.174), channel_id=1, source_target_pairs={{0,1},{4,5},{8,9},{12,13},{16,17},{20,21},{24,25},{28,29}} | collective-permute-start | bytes 1572872 | tf_op jit(solution)/shard_map/ppermute | solution.py:277
  244.4 16.0 %collective-permute-start.24 = (bf16[128,2048]{1,0:T(8,128)(2,1)}, bf16[128,2048]{1,0:T(8,128)(2,1)}, u32[]{:S(2)}, u32[]{:S(2)}) collective-permute-start(bf16[128,2048]{1,0:T(8,128)(2,1)} %get-tuple-element.168), channel_id=1, source_target_pairs={{0,1},{1,2},{4,5},{5,6},{8,9},{9,10},{12,13},{13,14},{16,17},{17,1... | collective-permute-start | bytes 1572872 | tf_op jit(solution)/shard_map/ppermute | solution.py:277
  260.4 14.5 %collective-permute-start.33 = (bf16[128,2048]{1,0:T(8,128)(2,1)}, bf16[128,2048]{1,0:T(8,128)(2,1)S(1)}, u32[]{:S(2)}, u32[]{:S(2)}) collective-permute-start(bf16[128,2048]{1,0:T(8,128)(2,1)} %get-tuple-element.177), channel_id=1, source_target_pairs={{2,1},{3,2},{6,5},{7,6},{10,9},{11,10},{14,13},{15,14},{18,17},{19... | collective-permute-start | bytes 1572872 | tf_op jit(solution)/shard_map/ppermute | solution.py:278
  261.1 17.0 %collective-permute-start.32 = (bf16[128,2048]{1,0:T(8,128)(2,1)}, bf16[128,2048]{1,0:T(8,128)(2,1)}, u32[]{:S(2)}, u32[]{:S(2)}) collective-permute-start(bf16[128,2048]{1,0:T(8,128)(2,1)} %get-tuple-element.176), channel_id=1, source_target_pairs={{0,1},{1,2},{4,5},{5,6},{8,9},{9,10},{12,13},{13,14},{16,17},{17,1... | collective-permute-start | bytes 1572872 | tf_op jit(solution)/shard_map/ppermute | solution.py:277
  269.5 15.3 %collective-permute-start.28 = (bf16[128,2048]{1,0:T(8,128)(2,1)}, bf16[128,2048]{1,0:T(8,128)(2,1)S(1)}, u32[]{:S(2)}, u32[]{:S(2)}) collective-permute-start(bf16[128,2048]{1,0:T(8,128)(2,1)} %get-tuple-element.172), channel_id=1, source_target_pairs={{0,1},{1,2},{2,3},{4,5},{5,6},{6,7},{8,9},{9,10},{10,11},{12,13},{... | collective-permute-start | bytes 1572872 | tf_op jit(solution)/shard_map/ppermute | solution.py:277
  284.9 14.4 %collective-permute-start.35 = (bf16[128,2048]{1,0:T(8,128)(2,1)S(1)}, bf16[128,2048]{1,0:T(8,128)(2,1)S(1)}, u32[]{:S(2)}, u32[]{:S(2)}) collective-permute-start(bf16[128,2048]{1,0:T(8,128)(2,1)S(1)} %get-tuple-element.179), channel_id=1, source_target_pairs={{1,0},{2,1},{3,2},{5,4},{6,5},{7,6},{9,8},{10,9},{11,10},{13,12},{... | collective-permute-start | bytes 1572872 | tf_op jit(solution)/shard_map/ppermute | solution.py:278
  286.1 17.3 %collective-permute-start.34 = (bf16[128,2048]{1,0:T(8,128)(2,1)S(1)}, bf16[128,2048]{1,0:T(8,128)(2,1)S(1)}, u32[]{:S(2)}, u32[]{:S(2)}) collective-permute-start(bf16[128,2048]{1,0:T(8,128)(2,1)S(1)} %get-tuple-element.178), channel_id=1, source_target_pairs={{0,1},{1,2},{2,3},{4,5},{5,6},{6,7},{8,9},{9,10},{10,11},{12,13},{... | collective-permute-start | bytes 1572872 | tf_op jit(solution)/shard_map/ppermute | solution.py:277
  292.9 21.8 %collective-permute-start.36 = (bf16[128,2048]{1,0:T(8,128)(2,1)S(1)}, bf16[128,2048]{1,0:T(8,128)(2,1)}, u32[]{:S(2)}, u32[]{:S(2)}) collective-permute-start(bf16[128,2048]{1,0:T(8,128)(2,1)S(1)} %multiply_convert_fusion.2.in_ref), channel_id=1, source_target_pairs={{0,1},{1,2},{2,3},{4,5},{5,6},{6,7},{8,9},{9,10},{10,11},{12,13},{... | collective-permute-start | bytes 1572872 | tf_op jit(solution)/shard_map/ppermute | solution.py:166
  297.9 16.7 %collective-permute-start.37 = (bf16[128,2048]{1,0:T(8,128)(2,1)S(1)}, bf16[128,2048]{1,0:T(8,128)(2,1)}, u32[]{:S(2)}, u32[]{:S(2)}) collective-permute-start(bf16[128,2048]{1,0:T(8,128)(2,1)S(1)} %multiply_convert_fusion.2.in_ref), channel_id=1, source_target_pairs={{1,0},{2,1},{3,2},{5,4},{6,5},{7,6},{9,8},{10,9},{11,10},{13,12},{... | collective-permute-start | bytes 1572872 | tf_op jit(solution)/shard_map/ppermute | solution.py:167
  305.8 28.5 %collective-permute-start.42 = (bf16[128,2048]{1,0:T(8,128)(2,1)}, bf16[128,2048]{1,0:T(8,128)(2,1)}, u32[]{:S(2)}, u32[]{:S(2)}) collective-permute-start(bf16[128,2048]{1,0:T(8,128)(2,1)} %multiply_convert_fusion.1.in_ref), channel_id=1, source_target_pairs={{0,1},{1,2},{2,3},{4,5},{5,6},{6,7},{8,9},{9,10},{10,11},{12,13},{... | collective-permute-start | bytes 1572872 | tf_op jit(solution)/shard_map/ppermute | solution.py:166
  311.0 23.3 %collective-permute-start.43 = (bf16[128,2048]{1,0:T(8,128)(2,1)}, bf16[128,2048]{1,0:T(8,128)(2,1)}, u32[]{:S(2)}, u32[]{:S(2)}) collective-permute-start(bf16[128,2048]{1,0:T(8,128)(2,1)} %multiply_convert_fusion.1.in_ref), channel_id=1, source_target_pairs={{1,0},{2,1},{3,2},{5,4},{6,5},{7,6},{9,8},{10,9},{11,10},{13,12},{... | collective-permute-start | bytes 1572872 | tf_op jit(solution)/shard_map/ppermute | solution.py:167
  316.1 16.9 %collective-permute-start.39 = (bf16[128,2048]{1,0:T(8,128)(2,1)}, bf16[128,2048]{1,0:T(8,128)(2,1)}, u32[]{:S(2)}, u32[]{:S(2)}) collective-permute-start(bf16[128,2048]{1,0:T(8,128)(2,1)} %collective-permute-done.37), channel_id=1, source_target_pairs={{1,0},{2,1},{5,4},{6,5},{9,8},{10,9},{13,12},{14,13},{17,16},{18,1... | collective-permute-start | bytes 1572872 | tf_op jit(solution)/shard_map/ppermute | solution.py:167
  333.0 25.3 %collective-permute-start.40 = (bf16[128,2048]{1,0:T(8,128)(2,1)}, bf16[128,2048]{1,0:T(8,128)(2,1)}, u32[]{:S(2)}, u32[]{:S(2)}) collective-permute-start(bf16[128,2048]{1,0:T(8,128)(2,1)} %collective-permute-done.39), channel_id=1, source_target_pairs={{1,0},{5,4},{9,8},{13,12},{17,16},{21,20},{25,24},{29,28}} | collective-permute-start | bytes 1572872 | tf_op jit(solution)/shard_map/ppermute | solution.py:167
  335.8 20.6 %collective-permute-start.45 = (bf16[128,2048]{1,0:T(8,128)(2,1)}, bf16[128,2048]{1,0:T(8,128)(2,1)}, u32[]{:S(2)}, u32[]{:S(2)}) collective-permute-start(bf16[128,2048]{1,0:T(8,128)(2,1)} %collective-permute-done.43), channel_id=1, source_target_pairs={{1,0},{2,1},{5,4},{6,5},{9,8},{10,9},{13,12},{14,13},{17,16},{18,1... | collective-permute-start | bytes 1572872 | tf_op jit(solution)/shard_map/ppermute | solution.py:167
  346.8 15.8 %collective-permute-start.41 = (bf16[128,2048]{1,0:T(8,128)(2,1)}, bf16[128,2048]{1,0:T(8,128)(2,1)S(1)}, u32[]{:S(2)}, u32[]{:S(2)}) collective-permute-start(bf16[128,2048]{1,0:T(8,128)(2,1)} %collective-permute-done.38), channel_id=1, source_target_pairs={{2,3},{6,7},{10,11},{14,15},{18,19},{22,23},{26,27},{30,31}} | collective-permute-start | bytes 1572872 | tf_op jit(solution)/shard_map/ppermute | solution.py:166
  429.0 16.5 %collective-permute-start.50 = (bf16[128,2048]{1,0:T(8,128)(2,1)S(1)}, bf16[128,2048]{1,0:T(8,128)(2,1)S(1)}, u32[]{:S(2)}, u32[]{:S(2)}) collective-permute-start(bf16[128,2048]{1,0:T(8,128)(2,1)S(1)} %get-tuple-element.193), channel_id=1, source_target_pairs={{0,1},{1,2},{4,5},{5,6},{8,9},{9,10},{12,13},{13,14},{16,17},{17,1... | collective-permute-start | bytes 1572872 | tf_op jit(solution)/shard_map/ppermute | solution.py:277
  445.5 21.0 %collective-permute-start.57 = (bf16[128,2048]{1,0:T(8,128)(2,1)S(1)}, bf16[128,2048]{1,0:T(8,128)(2,1)S(1)}, u32[]{:S(2)}, u32[]{:S(2)}) collective-permute-start(bf16[128,2048]{1,0:T(8,128)(2,1)S(1)} %get-tuple-element.201), channel_id=1, source_target_pairs={{2,1},{3,2},{6,5},{7,6},{10,9},{11,10},{14,13},{15,14},{18,17},{19... | collective-permute-start | bytes 1572872 | tf_op jit(solution)/shard_map/ppermute | solution.py:278
  446.2 20.4 %collective-permute-start.56 = (bf16[128,2048]{1,0:T(8,128)(2,1)S(1)}, bf16[128,2048]{1,0:T(8,128)(2,1)S(1)}, u32[]{:S(2)}, u32[]{:S(2)}) collective-permute-start(bf16[128,2048]{1,0:T(8,128)(2,1)S(1)} %get-tuple-element.200), channel_id=1, source_target_pairs={{0,1},{1,2},{4,5},{5,6},{8,9},{9,10},{12,13},{13,14},{16,17},{17,1... | collective-permute-start | bytes 1572872 | tf_op jit(solution)/shard_map/ppermute | solution.py:277
  451.7 16.6 %collective-permute-start.52 = (bf16[128,2048]{1,0:T(8,128)(2,1)S(1)}, bf16[128,2048]{1,0:T(8,128)(2,1)S(1)}, u32[]{:S(2)}, u32[]{:S(2)}) collective-permute-start(bf16[128,2048]{1,0:T(8,128)(2,1)S(1)} %get-tuple-element.195), channel_id=1, source_target_pairs={{0,1},{1,2},{2,3},{4,5},{5,6},{6,7},{8,9},{9,10},{10,11},{12,13},{... | collective-permute-start | bytes 1572872 | tf_op jit(solution)/shard_map/ppermute | solution.py:277
  469.8 23.8 %collective-permute-start.59 = (bf16[128,2048]{1,0:T(8,128)(2,1)S(1)}, bf16[128,2048]{1,0:T(8,128)(2,1)S(1)}, u32[]{:S(2)}, u32[]{:S(2)}) collective-permute-start(bf16[128,2048]{1,0:T(8,128)(2,1)S(1)} %get-tuple-element.203), channel_id=1, source_target_pairs={{1,0},{2,1},{3,2},{5,4},{6,5},{7,6},{9,8},{10,9},{11,10},{13,12},{... | collective-permute-start | bytes 1572872 | tf_op jit(solution)/shard_map/ppermute | solution.py:278
  471.1 22.5 %collective-permute-start.58 = (bf16[128,2048]{1,0:T(8,128)(2,1)S(1)}, bf16[128,2048]{1,0:T(8,128)(2,1)S(1)}, u32[]{:S(2)}, u32[]{:S(2)}) collective-permute-start(bf16[128,2048]{1,0:T(8,128)(2,1)S(1)} %get-tuple-element.202), channel_id=1, source_target_pairs={{0,1},{1,2},{2,3},{4,5},{5,6},{6,7},{8,9},{9,10},{10,11},{12,13},{... | collective-permute-start | bytes 1572872 | tf_op jit(solution)/shard_map/ppermute | solution.py:277
  501.8 171.8 %reduce-scatter.4.cloned.1.call-start = ((), (), s32[]{:S(2)}) async-start(), calls=%async_computation.6 | async-start | bytes 5242880 | tf_op jit(solution)/shard_map/reduce_scatter | solution.py:187
  507.2 16.3 %collective-permute-start.66 = (bf16[128,2048]{1,0:T(8,128)(2,1)S(1)}, bf16[128,2048]{1,0:T(8,128)(2,1)S(1)}, u32[]{:S(2)}, u32[]{:S(2)}) collective-permute-start(bf16[128,2048]{1,0:T(8,128)(2,1)S(1)} %get-tuple-element.334.in_ref), channel_id=1, source_target_pairs={{0,1},{1,2},{2,3},{4,5},{5,6},{6,7},{8,9},{9,10},{10,11},{12,13},{... | collective-permute-start | bytes 1572872 | tf_op jit(solution)/shard_map/ppermute | solution.py:166
  511.3 14.9 %collective-permute-start.67 = (bf16[128,2048]{1,0:T(8,128)(2,1)S(1)}, bf16[128,2048]{1,0:T(8,128)(2,1)S(1)}, u32[]{:S(2)}, u32[]{:S(2)}) collective-permute-start(bf16[128,2048]{1,0:T(8,128)(2,1)S(1)} %get-tuple-element.334.in_ref), channel_id=1, source_target_pairs={{1,0},{2,1},{3,2},{5,4},{6,5},{7,6},{9,8},{10,9},{11,10},{13,12},{... | collective-permute-start | bytes 1572872 | tf_op jit(solution)/shard_map/ppermute | solution.py:167
  516.8 24.1 %collective-permute-start.60 = (bf16[128,2048]{1,0:T(8,128)(2,1)S(1)}, bf16[128,2048]{1,0:T(8,128)(2,1)}, u32[]{:S(2)}, u32[]{:S(2)}) collective-permute-start(bf16[128,2048]{1,0:T(8,128)(2,1)S(1)} %get-tuple-element.332.in_ref), channel_id=1, source_target_pairs={{0,1},{1,2},{2,3},{4,5},{5,6},{6,7},{8,9},{9,10},{10,11},{12,13},{... | collective-permute-start | bytes 1572872 | tf_op jit(solution)/shard_map/ppermute | solution.py:166
  522.2 18.7 %collective-permute-start.61 = (bf16[128,2048]{1,0:T(8,128)(2,1)S(1)}, bf16[128,2048]{1,0:T(8,128)(2,1)}, u32[]{:S(2)}, u32[]{:S(2)}) collective-permute-start(bf16[128,2048]{1,0:T(8,128)(2,1)S(1)} %get-tuple-element.332.in_ref), channel_id=1, source_target_pairs={{1,0},{2,1},{3,2},{5,4},{6,5},{7,6},{9,8},{10,9},{11,10},{13,12},{... | collective-permute-start | bytes 1572872 | tf_op jit(solution)/shard_map/ppermute | solution.py:167
  526.2 17.5 %collective-permute-start.68 = (bf16[128,2048]{1,0:T(8,128)(2,1)S(1)}, bf16[128,2048]{1,0:T(8,128)(2,1)S(1)}, u32[]{:S(2)}, u32[]{:S(2)}) collective-permute-start(bf16[128,2048]{1,0:T(8,128)(2,1)S(1)} %collective-permute-done.66), channel_id=1, source_target_pairs={{1,2},{2,3},{5,6},{6,7},{9,10},{10,11},{13,14},{14,15},{17,18},{18... | collective-permute-start | bytes 1572872 | tf_op jit(solution)/shard_map/ppermute | solution.py:166
  526.9 16.8 %collective-permute-start.69 = (bf16[128,2048]{1,0:T(8,128)(2,1)S(1)}, bf16[128,2048]{1,0:T(8,128)(2,1)}, u32[]{:S(2)}, u32[]{:S(2)}) collective-permute-start(bf16[128,2048]{1,0:T(8,128)(2,1)S(1)} %collective-permute-done.67), channel_id=1, source_target_pairs={{1,0},{2,1},{5,4},{6,5},{9,8},{10,9},{13,12},{14,13},{17,16},{18,1... | collective-permute-start | bytes 1572872 | tf_op jit(solution)/shard_map/ppermute | solution.py:167
  542.4 19.9 %collective-permute-start.63 = (bf16[128,2048]{1,0:T(8,128)(2,1)}, bf16[128,2048]{1,0:T(8,128)(2,1)}, u32[]{:S(2)}, u32[]{:S(2)}) collective-permute-start(bf16[128,2048]{1,0:T(8,128)(2,1)} %collective-permute-done.61), channel_id=1, source_target_pairs={{1,0},{2,1},{5,4},{6,5},{9,8},{10,9},{13,12},{14,13},{17,16},{18,1... | collective-permute-start | bytes 1572872 | tf_op jit(solution)/shard_map/ppermute | solution.py:167
  543.7 24.2 %collective-permute-start.70 = (bf16[128,2048]{1,0:T(8,128)(2,1)}, bf16[128,2048]{1,0:T(8,128)(2,1)}, u32[]{:S(2)}, u32[]{:S(2)}) collective-permute-start(bf16[128,2048]{1,0:T(8,128)(2,1)} %collective-permute-done.69), channel_id=1, source_target_pairs={{1,0},{5,4},{9,8},{13,12},{17,16},{21,20},{25,24},{29,28}} | collective-permute-start | bytes 1572872 | tf_op jit(solution)/shard_map/ppermute | solution.py:167
  549.0 21.6 %collective-permute-start.71 = (bf16[128,2048]{1,0:T(8,128)(2,1)}, bf16[128,2048]{1,0:T(8,128)(2,1)S(1)}, u32[]{:S(2)}, u32[]{:S(2)}) collective-permute-start(bf16[128,2048]{1,0:T(8,128)(2,1)} %copy-done.84), channel_id=1, source_target_pairs={{2,3},{6,7},{10,11},{14,15},{18,19},{22,23},{26,27},{30,31}} | collective-permute-start | bytes 1572872 | tf_op jit(solution)/shard_map/ppermute | solution.py:166
  575.1 213.7 %reduce-scatter.8.cloned.1.call-start = ((), (), s32[]{:S(2)}) async-start(), calls=%async_computation.8 | async-start | bytes 17104896 | tf_op jit(solution)/shard_map/reduce_scatter | solution.py:1225
  687.5 30.7 %collective-permute-start.75 = (bf16[128,2048]{1,0:T(8,128)(2,1)}, bf16[128,2048]{1,0:T(8,128)(2,1)}, u32[]{:S(2)}, u32[]{:S(2)}) collective-permute-start(bf16[128,2048]{1,0:T(8,128)(2,1)} %get-tuple-element.238), channel_id=1, source_target_pairs={{0,1},{4,5},{8,9},{12,13},{16,17},{20,21},{24,25},{28,29}} | collective-permute-start | bytes 1572872 | tf_op jit(solution)/shard_map/ppermute | solution.py:277
  691.3 26.8 %collective-permute-start.76 = (bf16[128,2048]{1,0:T(8,128)(2,1)}, bf16[128,2048]{1,0:T(8,128)(2,1)}, u32[]{:S(2)}, u32[]{:S(2)}) collective-permute-start(bf16[128,2048]{1,0:T(8,128)(2,1)} %get-tuple-element.239), channel_id=1, source_target_pairs={{3,2},{7,6},{11,10},{15,14},{19,18},{23,22},{27,26},{31,30}} | collective-permute-start | bytes 1572872 | tf_op jit(solution)/shard_map/ppermute | solution.py:278
  719.0 14.0 %collective-permute-start.81 = (bf16[128,2048]{1,0:T(8,128)(2,1)}, bf16[128,2048]{1,0:T(8,128)(2,1)S(1)}, u32[]{:S(2)}, u32[]{:S(2)}) collective-permute-start(bf16[128,2048]{1,0:T(8,128)(2,1)} %get-tuple-element.245), channel_id=1, source_target_pairs={{0,1},{4,5},{8,9},{12,13},{16,17},{20,21},{24,25},{28,29}} | collective-permute-start | bytes 1572872 | tf_op jit(solution)/shard_map/ppermute | solution.py:277
  722.0 20.0 %collective-permute-start.77 = (bf16[128,2048]{1,0:T(8,128)(2,1)S(1)}, bf16[128,2048]{1,0:T(8,128)(2,1)S(1)}, u32[]{:S(2)}, u32[]{:S(2)}) collective-permute-start(bf16[128,2048]{1,0:T(8,128)(2,1)S(1)} %get-tuple-element.240), channel_id=1, source_target_pairs={{0,1},{1,2},{4,5},{5,6},{8,9},{9,10},{12,13},{13,14},{16,17},{17,1... | collective-permute-start | bytes 1572872 | tf_op jit(solution)/shard_map/ppermute | solution.py:277
  723.3 18.7 %collective-permute-start.78 = (bf16[128,2048]{1,0:T(8,128)(2,1)S(1)}, bf16[128,2048]{1,0:T(8,128)(2,1)S(1)}, u32[]{:S(2)}, u32[]{:S(2)}) collective-permute-start(bf16[128,2048]{1,0:T(8,128)(2,1)S(1)} %get-tuple-element.241), channel_id=1, source_target_pairs={{2,1},{3,2},{6,5},{7,6},{10,9},{11,10},{14,13},{15,14},{18,17},{19... | collective-permute-start | bytes 1572872 | tf_op jit(solution)/shard_map/ppermute | solution.py:278
  743.4 16.9 %collective-permute-start.83 = (bf16[128,2048]{1,0:T(8,128)(2,1)}, bf16[128,2048]{1,0:T(8,128)(2,1)}, u32[]{:S(2)}, u32[]{:S(2)}) collective-permute-start(bf16[128,2048]{1,0:T(8,128)(2,1)} %get-tuple-element.247), channel_id=1, source_target_pairs={{0,1},{1,2},{4,5},{5,6},{8,9},{9,10},{12,13},{13,14},{16,17},{17,1... | collective-permute-start | bytes 1572872 | tf_op jit(solution)/shard_map/ppermute | solution.py:277
  749.9 18.7 %collective-permute-start.79 = (bf16[128,2048]{1,0:T(8,128)(2,1)}, bf16[128,2048]{1,0:T(8,128)(2,1)S(1)}, u32[]{:S(2)}, u32[]{:S(2)}) collective-permute-start(bf16[128,2048]{1,0:T(8,128)(2,1)} %get-tuple-element.242), channel_id=1, source_target_pairs={{0,1},{1,2},{2,3},{4,5},{5,6},{6,7},{8,9},{9,10},{10,11},{12,13},{... | collective-permute-start | bytes 1572872 | tf_op jit(solution)/shard_map/ppermute | solution.py:277
  753.7 14.9 %collective-permute-start.80 = (bf16[128,2048]{1,0:T(8,128)(2,1)}, bf16[128,2048]{1,0:T(8,128)(2,1)S(1)}, u32[]{:S(2)}, u32[]{:S(2)}) collective-permute-start(bf16[128,2048]{1,0:T(8,128)(2,1)} %get-tuple-element.243), channel_id=1, source_target_pairs={{1,0},{2,1},{3,2},{5,4},{6,5},{7,6},{9,8},{10,9},{11,10},{13,12},{... | collective-permute-start | bytes 1572872 | tf_op jit(solution)/shard_map/ppermute | solution.py:278
  768.7 14.0 %collective-permute-start.86 = (bf16[128,2048]{1,0:T(8,128)(2,1)}, bf16[128,2048]{1,0:T(8,128)(2,1)}, u32[]{:S(2)}, u32[]{:S(2)}) collective-permute-start(bf16[128,2048]{1,0:T(8,128)(2,1)} %get-tuple-element.250), channel_id=1, source_target_pairs={{1,0},{2,1},{3,2},{5,4},{6,5},{7,6},{9,8},{10,9},{11,10},{13,12},{... | collective-permute-start | bytes 1572872 | tf_op jit(solution)/shard_map/ppermute | solution.py:278
  (141 other events, 1547.7 us)
Sparse Core Ops, SparseCore 0:
  51.8 67.6 all-gather.3
  121.4 36.7 all-gather.5
  160.0 72.1 all-gather.7
  502.0 92.7 reduce-scatter.5
  596.9 76.7 reduce-scatter.3
  677.5 108.0 reduce-scatter.7

commit v3 on v2

--- a/solution.py
+++ b/solution.py
@@ -149,7 +149,7 @@
     return [right, left]
 
 
-def z_gather_parts(parts, hooks=None, first=None):
+def z_gather_parts(parts, hooks=None, first=None, in_turn=False):
     size = lax.axis_size("tensor")
     hooks = hooks or {}
     moved = [[] for _ in parts]
@@ -161,6 +161,8 @@
                 moved[h].append(first)
                 continue
             earlier = list(hooks.get((h, s), []))
+            if h and in_turn:
+                earlier += moved[h - 1][s]
             if s or earlier:
                 right, left = ordered((right, left), *earlier)
             right = lax.ppermute(right, "tensor", [(i, i + 1) for i in range(s, size - 1)])
@@ -242,14 +244,21 @@
     return lax.dynamic_slice_in_dim(total, index * count, count, 0)
 
 
+def z_rotated(rows, moved):
+    size = lax.axis_size("tensor")
+    pieces = [moved[d - 1][0] + moved[size - d - 1][1] for d in range(1, size)]
+    return jnp.concatenate([rows] + pieces, axis=0)
+
+
 def z_scatter_first(parts):
     size = lax.axis_size("tensor")
-    right = lax.ppermute(block_of(parts[0], size - 1, size), "tensor", [(0, 1)])
-    left = lax.ppermute(block_of(parts[0], 0, size), "tensor", [(size - 1, size - 2)])
+    count = parts[0].shape[0] // size
+    right = lax.ppermute(parts[0][count : 2 * count], "tensor", [(0, 1)])
+    left = lax.ppermute(parts[0][(size - 1) * count :], "tensor", [(size - 1, size - 2)])
     return [right, left]
 
 
-def z_scatter_parts(parts, hooks=None, first=None):
+def z_scatter_parts(parts, hooks=None, first=None, rotated=False):
     size = lax.axis_size("tensor")
     me = lax.axis_index("tensor")
     hooks = hooks or {}
@@ -257,6 +266,10 @@
     for h, total in enumerate(parts):
 
         def part(offset, total=total):
+            if rotated:
+                count = total.shape[0] // size
+                at = (-offset) % size * count
+                return total[at : at + count]
             return block_of(total, jnp.clip(me + offset, 0, size - 1), size)
 
         right = left = None
@@ -281,12 +294,13 @@
     return sums, moved
 
 
+def z_sends(value):
+    size = lax.axis_size("tensor")
+    return [value] + [send_z(value, k) for k in range(1, size)]
+
+
 def z_sum(value):
-    size = lax.axis_size("tensor")
-    total = value
-    for k in range(1, size):
-        total = total + send_z(value, k)
-    return total
+    return sum(z_sends(value))
 
 
 def tile_of(width):
@@ -344,40 +358,51 @@
     )(x, gain, weights, *held)
 
 
-def gradient_kernel(parts, *refs):
-    out_ref = refs[-1]
-    count = len(parts)
-    lefts, rights = list(refs[: sum(parts)]), refs[sum(parts) : sum(parts) + count]
+def gradient_kernel(parts, uses, ranges, *refs):
+    out_ref, done_ref = refs[-2:]
+    done_ref[...] = jnp.zeros_like(done_ref)
+    lefts, rights = refs[: sum(parts)], refs[sum(parts) : sum(parts) + len(uses)]
+    turned, at = [], 0
+    for number in parts:
+        turned.append([left[...].T for left in lefts[at : at + number]])
+        at += number
     at = 0
-    for number, right in zip(parts, rights):
-        width = right.shape[1]
-        rows = right.shape[0] // number
+    for use, right, (first, stop) in zip(uses, rights, ranges):
+        width = stop - first
+        rows = right.shape[0] // parts[use]
         total = None
-        for h in range(number):
-            part = dot(lefts.pop(0)[...], right[h * rows : (h + 1) * rows, :], TN)
+        for h, left in enumerate(turned[use]):
+            part = dot(left, right[h * rows : (h + 1) * rows, first:stop])
             total = part if total is None else total + part
         out_ref[:, at : at + width] = total.astype(BF16)
         at += width
 
 
-def gradient(lefts, rights, held, piece, pieces):
+def gradient(lefts, rights, uses, held, piece, pieces, ranges=None):
     model = lefts[0][0].shape[1]
-    width = sum(right.shape[1] for right in rights)
+    ranges = ranges or [(0, right.shape[1]) for right in rights]
+    width = sum(stop - first for first, stop in ranges)
     tile = min(256, model // pieces)
     steps = model // pieces // tile
     parts = [len(left) for left in lefts]
     flat = [part for left in lefts for part in left]
     held = [] if held is None else [held]
     return pl.pallas_call(
-        partial(gradient_kernel, parts),
+        partial(gradient_kernel, parts, uses, ranges),
         grid=(steps,),
         in_specs=[
             pl.BlockSpec((part.shape[0], tile), lambda j: (0, piece * steps + j)) for part in flat
         ]
         + [pl.BlockSpec(right.shape, lambda j: (0, 0)) for right in rights]
         + [pl.BlockSpec(memory_space=pl.ANY)] * len(held),
-        out_specs=pl.BlockSpec((tile, width), lambda j: (piece * steps + j, 0)),
-        out_shape=jax.ShapeDtypeStruct((model, width), BF16),
+        out_specs=[
+            pl.BlockSpec((tile, width), lambda j: (piece * steps + j, 0)),
+            pl.BlockSpec((8, LANES), lambda j: (0, 0)),
+        ],
+        out_shape=[
+            jax.ShapeDtypeStruct((model, width), BF16),
+            jax.ShapeDtypeStruct((8, LANES), F32),
+        ],
         input_output_aliases={len(flat) + len(rights): 0} if held else {},
         compiler_params=pltpu.CompilerParams(vmem_limit_bytes=VMEM_LIMIT),
         cost_estimate=pl.CostEstimate(
@@ -480,15 +505,21 @@
     )(*d_branch, weights, gm)
 
 
+def put_parts(out, refs):
+    rows = out.shape[0] // len(refs)
+    for h, ref in enumerate(refs):
+        ref[...] = out[h * rows : (h + 1) * rows]
+
+
 def transposed_kernel(count, *refs):
     out = None
     for left, right in zip(refs[:count], refs[count : 2 * count]):
         part = dot(left[...], right[...], NT)
         out = part if out is None else out + part
-    refs[-1][...] = out.astype(BF16)
-
-
-def transposed_product(lefts, weights, first):
+    put_parts(out.astype(BF16), refs[2 * count :])
+
+
+def transposed_product(lefts, weights, first, parts):
     rows, width = lefts[0].shape
     model = weights.shape[0]
     tile = min(512, model)
@@ -502,8 +533,8 @@
         grid=(model // tile,),
         in_specs=[pl.BlockSpec((rows, width), lambda j: (0, 0))] * count
         + [columns(k) for k in range(count)],
-        out_specs=pl.BlockSpec((rows, tile), lambda j: (0, j)),
-        out_shape=jax.ShapeDtypeStruct((rows, model), BF16),
+        out_specs=[pl.BlockSpec((rows // parts, tile), lambda j: (0, j))] * parts,
+        out_shape=[jax.ShapeDtypeStruct((rows // parts, model), BF16)] * parts,
         compiler_params=pltpu.CompilerParams(vmem_limit_bytes=VMEM_LIMIT),
         cost_estimate=pl.CostEstimate(
             flops=2 * rows * model * width * count,
@@ -514,14 +545,14 @@
     )(*lefts, *([weights] * count))
 
 
-def branch_kernel(att_ref, gm_ref, rstd_ref, w_ref, out_ref):
+def branch_kernel(att_ref, gm_ref, rstd_ref, w_ref, *out_refs):
     split = att_ref.shape[1]
     out = dot(att_ref[...], w_ref[:, :split], NT)
     out = out + rstd_ref[...] * dot(gm_ref[...], w_ref[:, split:], NT)
-    out_ref[...] = out.astype(BF16)
-
-
-def branch_product(attended, gm, rstd, weights):
+    put_parts(out.astype(BF16), out_refs)
+
+
+def branch_product(attended, gm, rstd, weights, parts):
     rows = attended.shape[0]
     model, width = weights.shape
     tile = min(512, model)
@@ -538,8 +569,8 @@
             whole(rstd),
             pl.BlockSpec((tile, width), lambda j: (j, 0)),
         ],
-        out_specs=pl.BlockSpec((rows, tile), lambda j: (0, j)),
-        out_shape=jax.ShapeDtypeStruct((rows, model), BF16),
+        out_specs=[pl.BlockSpec((rows // parts, tile), lambda j: (0, j))] * parts,
+        out_shape=[jax.ShapeDtypeStruct((rows // parts, model), BF16)] * parts,
         compiler_params=pltpu.CompilerParams(vmem_limit_bytes=VMEM_LIMIT),
         cost_estimate=pl.CostEstimate(
             flops=2 * rows * model * width,
@@ -815,13 +846,13 @@
     parts = []
     for pair in range(width // LANES):
         pair_x = xs_low[:, pair * LANES : (pair + 1) * LANES]
-        sides = []
-        for e in range(2):
-            h = 2 * pair + e
+        both = []
+        for h in (2 * pair, 2 * pair + 1):
             gap = cum[:, h : h + 1] - cum_t[h : h + 1, :]
             decay = jnp.exp(jnp.where(mask, gap, MASK_FILL))
-            sides.append(dot((decay * c_dot_b).astype(BF16), pair_x))
-        parts.append(jnp.where(lane < P_SIZE, sides[0], sides[1]))
+            both.append((decay * c_dot_b).astype(BF16))
+        both = dot(jnp.concatenate(both, axis=0), pair_x)
+        parts.append(jnp.where(lane < P_SIZE, both[:rows], both[rows:]))
     y = jnp.concatenate(parts, axis=1) + carried + dskip_ref[0:1, :] * x_conv
     state[...] = held * enter_w[rows - 1 : rows, :] + dot(
         keys, (leave_w * xs).astype(BF16), TN
@@ -933,16 +964,17 @@
     for pair in range(width // LANES):
         pair_dy = dy_low[:, pair * LANES : (pair + 1) * LANES]
         pair_x = xs_low[:, pair * LANES : (pair + 1) * LANES]
-        sides = []
-        for e in range(2):
-            h = 2 * pair + e
+        none = jnp.zeros_like(pair_x)
+        only = [jnp.where(lane < P_SIZE, pair_x, none), jnp.where(lane < P_SIZE, none, pair_x)]
+        products = dot(jnp.concatenate(only, axis=0), pair_dy, NT)
+        both = []
+        for e, h in enumerate((2 * pair, 2 * pair + 1)):
             gap = cum_t[h : h + 1, :] - cum[:, h : h + 1]
             decay = jnp.exp(jnp.where(mask_t, gap, MASK_FILL))
-            sides.append(dot((decay * b_dot_c).astype(BF16), pair_dy))
-            inside = (lane < P_SIZE) if e == 0 else (lane >= P_SIZE)
-            only = jnp.where(inside, pair_x, jnp.zeros_like(pair_x))
-            d_gram = d_gram + decay * dot(only, pair_dy, NT)
-        parts.append(jnp.where(lane < P_SIZE, sides[0], sides[1]))
+            both.append((decay * b_dot_c).astype(BF16))
+            d_gram = d_gram + decay * products[e * rows : (e + 1) * rows]
+        both = dot(jnp.concatenate(both, axis=0), pair_dy)
+        parts.append(jnp.where(lane < P_SIZE, both[:rows], both[rows:]))
     d_xs_inner = jnp.concatenate(parts, axis=1)
     d_xs = d_xs_inner + from_next
     d_gram = d_gram.astype(BF16)
@@ -1230,7 +1262,6 @@
         return lax.all_gather(value, "dp", axis=0, tiled=True)
 
     x_parts = split(inputs[0])
-    x_first = z_gather_first(x_parts[0])
     shared = z_gather_direct(shared).reshape(size_z, 16 + owned, lane_rows)
     tiny = shared[:, :16]
     shared = shared[:, 16:].reshape(block, lane_rows)
@@ -1261,10 +1292,9 @@
     panel_rows = jnp.concatenate([w_zx[0].reshape(block, 2 * width), panel_rest], axis=1)
     all_width = panel_rows.shape[1]
     tiny = jnp.pad(tiny, ((0, 0), (0, all_width - block)))
-    panel_rows, tiny = ordered((panel_rows, tiny), *x_first)
     panel_rows = jnp.concatenate([panel_rows, tiny], axis=0)
     w_all = gather_dp(panel_rows)
-    x_moved = z_gather_parts(x_parts, None, x_first)
+    x_moved = z_gather_parts(x_parts, in_turn=True)
     tiny = w_all.reshape(members, block + 16, all_width)[:, block:, :block].astype(F32)
     gains = jnp.swapaxes(tiny[:, :2], 0, 1).reshape(2, model)
     convbc_all = jnp.swapaxes(tiny[:, 2:6, : size_z * taps], 0, 1).reshape(4, states2)
@@ -1288,18 +1318,20 @@
     held = ()
     d_moved = None
     for h in range(parts):
-        x_all = z_place(x_parts[h], x_moved[h])
+        pieces = x_moved[h]
+        if h:
+            pieces = pieces[:-1] + [ordered(pieces[-1], held[0])]
+        x_all = z_place(x_parts[h], pieces)
         held = norm_project(x_all, gain1, w_all, held, h, parts, members)
         if d_moved is None:
             d_moved = z_gather_parts([after(cotangent[0], held[0])])[0]
     normed1, panel = held
-    panel = after(panel, *d_moved[0])
     gm, squares, y_out, held = mamba_forward(cols, panel, *setup, chunk, parts, size_z)
-    squares = z_sum(squares[:, 0].reshape(-1, LANES)).reshape(length, 1)
+    squares = z_sends(squares[:, 0].reshape(-1, LANES))
     attended = attention_call(
         attention_forward_kernel,
         "attention_forward",
-        after(panel, y_out, *d_moved[min(1, size_z - 2)]),
+        after(panel, y_out, *d_moved[0]),
         2 * width + cols["q"],
         heads,
         tables,
@@ -1310,10 +1342,13 @@
         [],
         places,
     )
+    squares = sum(ordered(squares, attended)).reshape(length, 1)
     rstd = lax.rsqrt(squares / (HM * P_SIZE) + NORM_EPS)
-    branch = branch_product(attended, gm, rstd, w_b)
-    sums, moved = z_scatter_parts(by_part(branch), {(0, size_z - 2): d_moved[-1]})
-    x_own = after(inputs[0], branch).astype(F32)
+    branch = branch_product(attended, gm, rstd, w_b, parts)
+    sums, moved = z_scatter_parts(
+        branch, {(0, 1): d_moved[min(1, size_z - 2)], (late, size_z - 2): d_moved[-1]}
+    )
+    x_own = after(inputs[0], *branch).astype(F32)
     h_mid, normed2_own = [], []
     for h, x in enumerate(split(x_own)):
         total = sums[h]
@@ -1323,19 +1358,24 @@
         normed2_own.append((h_mid[h] * rms_factor(h_mid[h]) * gain2).astype(BF16))
     moved = z_gather_parts(normed2_own)
     d_out = [
-        z_place(own, [[split(right)[h], split(left)[h]] for right, left in d_moved])
+        z_rotated(own, [[split(right)[h], split(left)[h]] for right, left in d_moved])
         for h, own in enumerate(split(cotangent[0]))
     ]
-    normed2 = [z_place(own, m) for own, m in zip(normed2_own, moved)]
+    normed2 = [z_rotated(own, m) for own, m in zip(normed2_own, moved)]
     act, d_gate, d_up = feed_forward(normed2, d_out, w_cd, hidden_units)
-    d_norm2 = transposed_product([d_gate, d_up], w_cd, 0)
-    first = z_scatter_first(by_part(d_norm2))
-    sums, moved = z_scatter_parts(by_part(d_norm2), None, first)
-    g_cd, pieces = None, 4
-    steps = [first, moved[late][0], moved[0][-1], moved[late][-1]]
+    d_norm2 = transposed_product([d_gate, d_up], w_cd, 0, parts)
+    first = z_scatter_first(d_norm2)
+    hooks = {(0, 1): [], (late, 1): []}
+    given, g_cd, pieces = list(d_norm2), None, 2
+    places_of = [(0, 1), (late, 1)]
     for piece in range(pieces):
-        left, right = ordered((normed2, d_out), *steps[piece])
-        g_cd = gradient([left, left, right], [d_gate, d_up, act], g_cd, piece, pieces)
+        left, right = ordered((normed2, d_out), *given)
+        g_cd, token = gradient(
+            [left, right], [d_gate, d_up, act], [0, 0, 1], g_cd, piece, pieces
+        )
+        given = [*first, token]
+        hooks[places_of[piece]].append(token)
+    sums, moved = z_scatter_parts(d_norm2, hooks, first, True)
     g_cd = scatter_dp(g_cd)
     grad_mid, grad_low = [], []
     for h, part in enumerate(split(cotangent[0])):
@@ -1346,16 +1386,20 @@
         grad_mid.append(grad)
         grad_low.append(grad.astype(BF16))
     h_mid_all = jnp.concatenate(h_mid, axis=0)
-    ffn = transposed_product([after(act, *moved[0][-1])], w_cd, 2)
-    if parts > 1:
-        ffn = jnp.swapaxes(ffn.reshape(parts, size_z, sub, model), 0, 1).reshape(length, model)
-    moved = z_gather_parts(grad_low, {(late, 1): [ffn]})
+    moved = z_gather_parts(grad_low)
+    ffn = transposed_product([after(act, *moved[0][0])], w_cd, 2, parts)
+    ffn = [
+        lax.dynamic_slice_in_dim(part, lax.rem(me_z - b + size_z, size_z) * sub, sub, 0)
+        for b in range(size_z)
+        for part in ffn
+    ]
+    ffn = jnp.concatenate(ffn, axis=0)
     d_branch = [z_place(own, m) for own, m in zip(grad_low, moved)]
     ffn = line_scatter([ffn], *moved[late][-1])[0]
     g_c, g_d = g_cd[:, : 2 * hidden_units], g_cd[:, 2 * hidden_units :]
 
     d_b, inner = branch_back(d_branch, w_b, gm)
-    inner = z_sum(inner[:, 0].reshape(-1, LANES)).reshape(length, 1)
+    inner = z_sends(inner[:, 0].reshape(-1, LANES))
     d_qkv = attention_call(
         attention_backward_kernel,
         "attention_backward",
@@ -1370,6 +1414,7 @@
         [pltpu.VMEM((length, HEAD_SIZE), F32), pltpu.VMEM((length, HEAD_SIZE), F32)],
         places,
     )
+    inner = sum(ordered(inner, d_qkv)).reshape(length, 1)
     aux2 = jnp.pad(
         jnp.concatenate([rstd, rstd**3 * inner / (HM * P_SIZE)], axis=1),
         ((0, 0), (0, LANES - 2)),
@@ -1379,16 +1424,16 @@
     )
     mixed = (after(gm, aux2).astype(F32) * rstd).astype(BF16)
     mixed = jnp.concatenate([attended, mixed], axis=1)
-    g_all = gradient([[normed1], d_branch], [d_all, mixed], None, 0, 1)
+    g_all, _ = gradient([[normed1], d_branch], [d_all, mixed], [0, 1], None, 0, 1)
     d_norm1, low = [], g_all
     for h in range(parts):
         low = back_product(after(d_all, low), w_all, h, parts, members, model)
         d_norm1.append(low)
-    low = d_norm1[-1:]
     g_all = scatter_dp(g_all)
     g_zx = g_all[:, : 2 * width].astype(F32)
     g_rest = g_all[:, 2 * width : all_width]
     g_b = g_all[:, all_width:].astype(F32)
+
     by_dp = [
         g_cbc[:4].reshape(-1, LANES),
         g_heads[0:2],
@@ -1399,7 +1444,7 @@
     ends = np.cumsum([v.shape[0] for v in by_dp])
     by_dp = jnp.concatenate(by_dp, axis=0)
     by_dp = pad_rows(by_dp, -(-by_dp.shape[0] // 8) * 8)
-    by_dp = dp_sum(after(by_dp, *low))
+    by_dp = dp_sum(after(by_dp, *d_norm1))
     dp_taps = size_z * taps
     g_convbc = lax.dynamic_slice_in_dim(
         by_dp[: ends[0]].reshape(4, states2), lax.axis_index("dp") * dp_taps, dp_taps, 1
@@ -1443,13 +1488,13 @@
         ],
         axis=1,
     )
-    sums, moved = z_scatter_parts(d_norm1, {(late, 1): [ffn]})
     hidden_out = (h_mid_all + ffn).astype(BF16)
     shared_grad = z_scatter_direct(shared_grad.astype(BF16))
     small = shared_grad[:, kv_total + states2 :]
     shared_grad = shared_grad[:, : kv_total + states2]
     g_gains = small[:, :2].T[None]
     g_convbc = small[:taps, 2:6].T[None]
+    sums, moved = z_scatter_parts(d_norm1)
     norm_sum = jnp.concatenate(sums, axis=0)
     grad_in, _ = norm_backward(x_own, gain1, norm_sum, jnp.concatenate(grad_mid, axis=0))
     input_grad = grad_in

time: 832 us -> 792 us (0.952)
  waiting for transfers between devices: 214 us -> 192 us
  Pallas kernels: 239 us -> 222 us
  local copies, waits for them, and re-layouts: 74.3 us -> 62.6 us
  starting transfers between devices: 193 us -> 203 us
    ppermute x12, waiting for transfers between devices: 29 us -> 9.35 us  [send_z(): lax.ppermute(value, 'tensor', [(i, (i + shift) % size) for i in range(siz...]
    ppermute x17, waiting for transfers between devices: 6.86 us -> 25.8 us  [z_scatter_parts(): lax.ppermute(to_left, 'tensor', [(i, i - 1) for i in range(size - 1 - s,...]
    dynamic_update_slice x20 -> x12, other arithmetic: 32.9 us -> 18.6 us  [z_place(): out = lax.dynamic_update_slice_in_dim(out, piece, at, 0)]
    ppermute x17, waiting for transfers between devices: 72.5 us -> 59 us  [z_scatter_parts(): right = lax.ppermute(to_right, 'tensor', [(i, i + 1) for i in range(s + 1)])]
    ppermute x20 -> x21, waiting for transfers between devices: 82.9 us -> 92.3 us  [z_gather_parts(): lax.ppermute(left, 'tensor', [(i, i - 1) for i in range(1, size - s)])]
    pallas_call x5 -> x3, Pallas kernels: 55.6 us -> 47 us  [gradient(): pl.pallas_call(partial(gradient_kernel, parts, uses, ranges), grid=(steps...]
    ppermute x20 -> x21, starting transfers between devices: 41.9 us -> 50.3 us  [z_gather_parts(): lax.ppermute(right, 'tensor', [(i, i + 1) for i in range(s, size - 1)])]
    unnamed x226 -> x180, local copies, waits for them, and re-layouts: 34.2 us -> 36.5 us
  transfers between devices with their start and end apart: 100 -> 100, of which waited for: 42 -> 36; matrix products, arithmetic and copies ran while one was open for 15% -> 15% of each run, Pallas kernels for 24% -> 23%
where the time goes in v3:
time: 792 us; the launch traced here: 780 us
  Pallas kernels  222 us (28%)
  starting transfers between devices  203 us (26%)
  waiting for transfers between devices  192 us (24%)
  other arithmetic  84.6 us (11%)
  local copies, waits for them, and re-layouts  62.6 us (8%)
  between operations  16.9 us (2%)
    ppermute x21, waiting for transfers between devices, z_gather_parts(): lax.ppermute(left, 'tensor', [(i, i - 1) for i in range(1, size - s)])  92.3 us
    ppermute x17, starting transfers between devices, z_scatter_parts(): right = lax.ppermute(to_right, 'tensor', [(i, i + 1) for i in range(s + 1)])  72.2 us
    ppermute x17, waiting for transfers between devices, z_scatter_parts(): right = lax.ppermute(to_right, 'tensor', [(i, i + 1) for i in range(s + 1)])  59 us
    ppermute x21, starting transfers between devices, z_gather_parts(): lax.ppermute(right, 'tensor', [(i, i + 1) for i in range(s, size - 1)])  50.3 us
    pallas_call x3, Pallas kernels, gradient(): pl.pallas_call(partial(gradient_kernel, parts, uses, ranges), grid=(steps...  47 us
    unnamed x180, local copies, waits for them, and re-layouts  36.5 us
    pallas_call x1, Pallas kernels, mamba_backward(): pl.pallas_call(partial(mamba_backward_kernel, cols), grid=(chunks,), in_s...  31.6 us
    pallas_call x2, Pallas kernels, norm_project(): pl.pallas_call(partial(norm_project_kernel, members), grid=(width // tile...  28.3 us
  transfers between devices with their start and end apart: 100, of which 36 were waited for; matrix products, arithmetic and copies ran while one was open for 15% of the time, Pallas kernels for 23%

profile of v3, /device:TPU:0, one launch (start us, length us, event | category | flops | bytes accessed | tf_op | source)
XLA Modules:
  0.0 780.1 jit_solution(12232622501005488801)
XLA Ops:
  18.5 6.2 collective-permute-done.13
  32.0 6.6 collective-permute-start
  44.4 4.8 collective-permute-done
  49.2 5.0 collective-permute-done.1
  56.9 5.4 collective-permute-start.2
  63.8 8.9 %collective-permute-done.5 = bf16[128,2048]{1,0:T(8,128)(2,1)} collective-permute-done((bf16[128,2048]{1,0:T(8,128)(2,1)}, bf16[128,2048]{1,0:T(8,128)(2,1)}, u32[]{:S(2)}, u32[]{:S(2)}) %collective-permute-start.5) | collective-permute-done | bytes 524320 | tf_op jit(solution)/shard_map/ppermute | solution.py:169
  75.5 8.4 %collective-permute-done.3 = bf16[128,2048]{1,0:T(8,128)(2,1)} collective-permute-done((bf16[128,2048]{1,0:T(8,128)(2,1)S(1)}, bf16[128,2048]{1,0:T(8,128)(2,1)}, u32[]{:S(2)}, u32[]{:S(2)}) %collective-permute-start.3) | collective-permute-done | bytes 524320 | tf_op jit(solution)/shard_map/ppermute | solution.py:169
  87.4 7.8 collective-permute-done.9
  95.2 9.0 %collective-permute-done.7 = bf16[128,2048]{1,0:T(8,128)(2,1)} collective-permute-done((bf16[128,2048]{1,0:T(8,128)(2,1)}, bf16[128,2048]{1,0:T(8,128)(2,1)}, u32[]{:S(2)}, u32[]{:S(2)}) %collective-permute-start.7) | collective-permute-done | bytes 524320 | tf_op jit(solution)/shard_map/ppermute | solution.py:169
  114.3 14.1 %norm_project.2 = (bf16[1024,2048]{1,0:T(8,128)(2,1)}, f32[1024,2688]{1,0:T(8,128)}) custom-call(bf16[512,2048]{1,0:T(8,128)(2,1)S(1)} %copy-done.14, f32[1,2048]{1,0:T(1,128)S(1)} %bitcast.131, bf16[2176,2688]{1,0:T(8,128)(2,1)} %all-gather.4.cloned.1.call-done.w_ref), custom_call_target="tpu_custom_call" | custom-call | flops 5637144576 | bytes 18612224 | tf_op jit(solution)/shard_map/norm_project/pallas_call | solution.py:333
  128.4 6.2 collective-permute-start.15
  139.9 14.2 %norm_project.3 = (bf16[1024,2048]{1,0:T(8,128)(2,1)}, f32[1024,2688]{1,0:T(8,128)}) custom-call(bf16[512,2048]{1,0:T(8,128)(2,1)S(1)} %add_dynamic-update-slice_fusion.6.x_ref, f32[1,2048]{1,0:T(1,128)S(1)} %bitcast.132, bf16[2176,2688]{1,0:T(8,128)(2,1)} %all-gather.4.cloned.1.call-done.w_ref, ...), custom_call_target="tpu_custom_call", output_to_operand_aliasing={{0}: (3, {}), {1}: (4, {})} | custom-call | flops 5637144576 | bytes 18612224 | tf_op jit(solution)/shard_map/norm_project/pallas_call | solution.py:333
  154.1 13.6 %mamba_forward.1 = (bf16[1024,768]{1,0:T(8,128)(2,1)S(1)}, f32[1024,128]{1,0:T(8,128)S(1)}, f32[1024,768]{1,0:T(8,128)}, bf16[8,256,768]{2,1,0:T(8,128)(2,1)}) custom-call(f32[1024,2688]{1,0:T(8,128)} %get-tuple-element.250.p_ref.halo_ref.refs_0_.refs_1_.refs_2_.refs_3_, f32[1024,2688]{1,0:T(8,128)} %get-tuple-element.250.p_ref.halo_ref.refs_0_.refs_1_.refs_2_.refs_3_, ...), custom_call_target="tpu_custom_call" | custom-call | flops 15728640000 | bytes 20447232 | tf_op jit(solution)/shard_map/mamba_forward/pallas_call | solution.py:1066
  174.6 6.0 attention_forward.1.att_ref
  189.0 7.4 branch.1
  198.9 6.4 collective-permute-start.20
  206.6 5.3 collective-permute-done.20
  212.5 4.4 collective-permute-start.28
  222.2 6.5 collective-permute-done.28
  230.1 4.2 collective-permute-done.24
  238.7 6.3 collective-permute-start.30
  248.9 8.9 %collective-permute-start.26 = (bf16[128,2048]{1,0:T(8,128)(2,1)}, bf16[128,2048]{1,0:T(8,128)(2,1)}, u32[]{:S(2)}, u32[]{:S(2)}) collective-permute-start(bf16[128,2048]{1,0:T(8,128)(2,1)} %get-tuple-element.188), channel_id=1, source_target_pairs={{0,1},{1,2},{2,3},{4,5},{5,6},{6,7},{8,9},{9,10},{10,11},{12,13},{... | collective-permute-start | bytes 1572872 | tf_op jit(solution)/shard_map/ppermute | solution.py:290
  261.3 10.8 %collective-permute-done.27 = bf16[128,2048]{1,0:T(8,128)(2,1)} collective-permute-done((bf16[128,2048]{1,0:T(8,128)(2,1)}, bf16[128,2048]{1,0:T(8,128)(2,1)}, u32[]{:S(2)}, u32[]{:S(2)}) %collective-permute-start.27) | collective-permute-done | bytes 524320 | tf_op jit(solution)/shard_map/ppermute | solution.py:291
  273.5 4.6 collective-permute-start.34
  284.0 4.9 collective-permute-done.35
  291.1 4.4 collective-permute-start.42
  303.8 8.5 %collective-permute-done.43 = bf16[128,2048]{1,0:T(8,128)(2,1)S(1)} collective-permute-done((bf16[128,2048]{1,0:T(8,128)(2,1)S(1)}, bf16[128,2048]{1,0:T(8,128)(2,1)S(1)}, u32[]{:S(2)}, u32[]{:S(2)}) %collective-permute-start.43) | collective-permute-done | bytes 524320 | tf_op jit(solution)/shard_map/ppermute | solution.py:169
  315.9 7.6 collective-permute-done.39
  327.1 7.6 collective-permute-done.45
  339.9 3.8 collective-permute-done.40
  345.4 3.9 collective-permute-done.46
  350.9 20.3 %feed_forward.1 = (bf16[1024,1024]{1,0:T(8,128)(2,1)S(1)}, bf16[1024,1024]{1,0:T(8,128)(2,1)S(1)}, bf16[1024,1024]{1,0:T(8,128)(2,1)}) custom-call(bf16[512,2048]{1,0:T(8,128)(2,1)} %pad_maximum_fusion.refs_0_, bf16[512,2048]{1,0:T(8,128)(2,1)} %pad_maximum_fusion.1.refs_1_, bf16[512,2048]{1,0:T(8,128)(2,1)} %get-tuple-element.246.refs_2_, ...), custom_call_target="tpu_custom_call" | custom-call | flops 12884901888 | bytes 20971520 | tf_op jit(solution)/shard_map/feed_forward/pallas_call | solution.py:444
  373.8 12.8 %transposed_product.2 = (bf16[512,2048]{1,0:T(8,128)(2,1)S(1)}, bf16[512,2048]{1,0:T(8,128)(2,1)S(1)}) custom-call(bf16[1024,1024]{1,0:T(8,128)(2,1)} %copy-done.23, bf16[1024,1024]{1,0:T(8,128)(2,1)} %get-tuple-element.210.refs_1_.refs_5_, bf16[2048,3072]{1,0:T(8,128)(2,1)} %all-gather.8.cloned.1.call-done.refs_4_.refs_5_.refs_6_.refs_2_.refs_3_.refs_1_, ...), custom_call_target="tpu_custom_call" | custom-call | flops 8589934592 | bytes 16777216 | tf_op jit(solution)/shard_map/transposed_product/pallas_call | solution.py:531
  390.4 11.8 %gradient.3 = (bf16[2048,3072]{1,0:T(8,128)(2,1)}, f32[8,128]{1,0:T(8,128)}) custom-call(bf16[512,2048]{1,0:T(8,128)(2,1)S(1)} %copy-done.1, bf16[512,2048]{1,0:T(8,128)(2,1)S(1)} %copy-done.2, bf16[512,2048]{1,0:T(8,128)(2,1)} %get-tuple-element.246.refs_2_, bf16[512,2048]{1,0:T(8,128)(2,1)} %get-tuple-element.247.refs_3_, bf16[1024,1024]{1,0:T(8,128)(2,1)} %copy-done.23, ...), custom_call_target="tpu_custom_call" | custom-call | flops 6442450944 | bytes 11534336 | tf_op jit(solution)/shard_map/gradient/pallas_call | solution.py:390
  402.3 12.0 %gradient.4 = (bf16[2048,3072]{1,0:T(8,128)(2,1)}, f32[8,128]{1,0:T(8,128)}) custom-call(bf16[512,2048]{1,0:T(8,128)(2,1)S(1)} %copy-done.1, bf16[512,2048]{1,0:T(8,128)(2,1)S(1)} %copy-done.2, bf16[512,2048]{1,0:T(8,128)(2,1)} %get-tuple-element.246.refs_2_, bf16[512,2048]{1,0:T(8,128)(2,1)} %get-tuple-element.247.refs_3_, ...), custom_call_target="tpu_custom_call", output_to_operand_aliasing={{0}: (7, {})} | custom-call | flops 6442450944 | bytes 11534336 | tf_op jit(solution)/shard_map/gradient/pallas_call | solution.py:390
  420.7 6.4 collective-permute-done.56
  429.5 5.7 collective-permute-done.50
  436.7 5.0 collective-permute-start.58
  444.3 5.3 collective-permute-start.52
  452.7 4.8 collective-permute-done.53
  460.5 6.0 collective-permute-start.60
  468.0 3.1 fusion.34
  471.2 4.2 collective-permute-start.54
  482.8 5.3 collective-permute-start.62
  494.4 7.4 transposed_product.3
  519.7 9.0 %collective-permute-done.65 = bf16[128,2048]{1,0:T(8,128)(2,1)} collective-permute-done((bf16[128,2048]{1,0:T(8,128)(2,1)}, bf16[128,2048]{1,0:T(8,128)(2,1)}, u32[]{:S(2)}, u32[]{:S(2)}) %collective-permute-start.65) | collective-permute-done | bytes 524320 | tf_op jit(solution)/shard_map/ppermute | solution.py:169
  538.3 3.3 collective-permute-done.67
  548.4 9.3 %branch_back.1 = (f32[1024,1024]{1,0:T(8,128)}, f32[1024,128]{1,0:T(8,128)S(1)}) custom-call(bf16[512,2048]{1,0:T(8,128)(2,1)S(1)} %copy-done.17, bf16[512,2048]{1,0:T(8,128)(2,1)} %add_dynamic-update-slice_fusion.refs_1_.refs_2_, bf16[2048,1024]{1,0:T(8,128)(2,1)} %all-gather.6.cloned.1.call-done.w_ref.refs_2_, bf16[1024,768]{1,0:T(8,128)(2,1)S(1)} %copy-done.26), custom_call_target="tpu_custom_call" | custom-call | flops 4294967296 | bytes 8388608 | tf_op jit(solution)/shard_map/branch_back/pallas_call | solution.py:482
  561.7 9.2 %attention_backward.1.dqkv_ref = bf16[1024,512]{1,0:T(8,128)(2,1)S(1)} custom-call(f32[1024,2688]{1,0:T(8,128)} %get-tuple-element.250.p_ref.halo_ref.refs_0_.refs_1_.refs_2_.refs_3_, f32[1024,2688]{1,0:T(8,128)} %get-tuple-element.250.p_ref.halo_ref.refs_0_.refs_1_.refs_2_.refs_3_, ...), custom_call_target="tpu_custom_call" | custom-call | flops 10485760000 | bytes 6291456 | tf_op jit(solution)/shard_map/attention_backward/pallas_call | solution.py:732
  575.5 31.6 %mamba_backward.1 = (bf16[1024,2688]{1,0:T(8,128)(2,1)}, f32[8,768]{1,0:T(8,128)S(1)}, f32[8,768]{1,0:T(8,128)S(1)}, f32[8,512]{1,0:T(8,128)S(1)}, f32[8,128]{1,0:T(8,128)S(1)}) custom-call(f32[1024,2688]{1,0:T(8,128)} %get-tuple-element.250.p_ref.halo_ref.refs_0_.refs_1_.refs_2_.refs_3_, ...), custom_call_target="tpu_custom_call" | custom-call | flops 36962304000 | bytes 20447232 | tf_op jit(solution)/shard_map/mamba_backward/pallas_call | solution.py:1121
  607.1 23.2 %gradient.5 = (bf16[2048,3712]{1,0:T(8,128)(2,1)}, f32[8,128]{1,0:T(8,128)}) custom-call(bf16[1024,2048]{1,0:T(8,128)(2,1)} %get-tuple-element.256.refs_0_, bf16[512,2048]{1,0:T(8,128)(2,1)S(1)} %copy-done.18, bf16[512,2048]{1,0:T(8,128)(2,1)S(1)} %copy-done.19, bf16[1024,2688]{1,0:T(8,128)(2,1)} %get-tuple-element.266.refs_3_.d_ref, ...), custom_call_target="tpu_custom_call" | custom-call | flops 15569256448 | bytes 27000832 | tf_op jit(solution)/shard_map/gradient/pallas_call | solution.py:390
  634.3 11.1 %back_product.2 = bf16[512,2048]{1,0:T(8,128)(2,1)S(1)} custom-call(bf16[1024,2688]{1,0:T(8,128)(2,1)} %get-tuple-element.266.refs_3_.d_ref, bf16[2176,2688]{1,0:T(8,128)(2,1)} %all-gather.4.cloned.1.call-done.w_ref), custom_call_target="tpu_custom_call" | custom-call | flops 5637144576 | bytes 16547840 | tf_op jit(solution)/shard_map/back_product/pallas_call | solution.py:595
  650.9 10.0 %back_product.3 = bf16[512,2048]{1,0:T(8,128)(2,1)S(1)} custom-call(bf16[1024,2688]{1,0:T(8,128)(2,1)} %get-tuple-element.266.refs_3_.d_ref, bf16[2176,2688]{1,0:T(8,128)(2,1)} %all-gather.4.cloned.1.call-done.w_ref), custom_call_target="tpu_custom_call" | custom-call | flops 5637144576 | bytes 16547840 | tf_op jit(solution)/shard_map/back_product/pallas_call | solution.py:595
  665.6 6.2 collective-permute-start.90
  672.6 4.0 reshape.255
  683.9 9.0 %collective-permute-done.81 = bf16[128,2048]{1,0:T(8,128)(2,1)S(1)} collective-permute-done((bf16[128,2048]{1,0:T(8,128)(2,1)}, bf16[128,2048]{1,0:T(8,128)(2,1)S(1)}, u32[]{:S(2)}, u32[]{:S(2)}) %collective-permute-start.81) | collective-permute-done | bytes 524320 | tf_op jit(solution)/shard_map/ppermute | solution.py:290
  694.3 7.6 collective-permute-done.77
  703.4 5.0 collective-permute-start.83
  709.8 3.8 collective-permute-start.79
  715.7 4.6 collective-permute-done.83
  723.2 5.4 collective-permute-done.79
  729.9 5.7 collective-permute-start.85
  737.3 5.3 collective-permute-done.86
  754.0 6.0 collective-permute-start.93
  (522 shorter events, 262.0 us)
Async XLA Ops:
  7.2 104.6 %all-gather.4.cloned.1.call-start = ((), (), s32[]{:S(2)}) async-start(), calls=%async_computation.3 | async-start | bytes 13160448 | tf_op jit(solution)/shard_map/all_gather | solution.py:1262
  26.6 158.8 %all-gather.6.cloned.1.call-start = ((), (), s32[]{:S(2)}) async-start(), calls=%async_computation.4 | async-start | bytes 4718592 | tf_op jit(solution)/shard_map/all_gather | solution.py:1262
  27.8 323.1 %all-gather.8.cloned.1.call-start = ((), (), s32[]{:S(2)}) async-start(), calls=%async_computation.5 | async-start | bytes 14155776 | tf_op jit(solution)/shard_map/all_gather | solution.py:1262
  30.7 531.0 %reduce-scatter.6.cloned.1.call-start = ((), (), s32[]{:S(2)}) async-start(), calls=%async_computation.7 | async-start | bytes 14155776 | tf_op jit(solution)/shard_map/reduce_scatter | solution.py:1257
  32.0 17.2 %collective-permute-start = (bf16[128,2048]{1,0:T(8,128)(2,1)S(1)}, bf16[128,2048]{1,0:T(8,128)(2,1)}, u32[]{:S(2)}, u32[]{:S(2)}) collective-permute-start(bf16[128,2048]{1,0:T(8,128)(2,1)S(1)} %get-tuple-element.406.in_ref), channel_id=1, source_target_pairs={{0,1},{1,2},{2,3},{4,5},{5,6},{6,7},{8,9},{9,10},{10,11},{12,13},{... | collective-permute-start | bytes 1572872 | tf_op jit(solution)/shard_map/ppermute | solution.py:168
  38.7 15.6 %collective-permute-start.1 = (bf16[128,2048]{1,0:T(8,128)(2,1)S(1)}, bf16[128,2048]{1,0:T(8,128)(2,1)}, u32[]{:S(2)}, u32[]{:S(2)}) collective-permute-start(bf16[128,2048]{1,0:T(8,128)(2,1)S(1)} %get-tuple-element.406.in_ref), channel_id=1, source_target_pairs={{1,0},{2,1},{3,2},{5,4},{6,5},{7,6},{9,8},{10,9},{11,10},{13,12},{... | collective-permute-start | bytes 1572872 | tf_op jit(solution)/shard_map/ppermute | solution.py:169
  55.6 17.1 %collective-permute-start.5 = (bf16[128,2048]{1,0:T(8,128)(2,1)}, bf16[128,2048]{1,0:T(8,128)(2,1)}, u32[]{:S(2)}, u32[]{:S(2)}) collective-permute-start(bf16[128,2048]{1,0:T(8,128)(2,1)} %collective-permute-done.1), channel_id=1, source_target_pairs={{1,0},{2,1},{5,4},{6,5},{9,8},{10,9},{13,12},{14,13},{17,16},{18,1... | collective-permute-start | bytes 1572872 | tf_op jit(solution)/shard_map/ppermute | solution.py:169
  56.9 18.6 %collective-permute-start.2 = (bf16[128,2048]{1,0:T(8,128)(2,1)S(1)}, bf16[128,2048]{1,0:T(8,128)(2,1)}, u32[]{:S(2)}, u32[]{:S(2)}) collective-permute-start(bf16[128,2048]{1,0:T(8,128)(2,1)S(1)} %copy-done.57), channel_id=1, source_target_pairs={{0,1},{1,2},{2,3},{4,5},{5,6},{6,7},{8,9},{9,10},{10,11},{12,13},{... | collective-permute-start | bytes 1572872 | tf_op jit(solution)/shard_map/ppermute | solution.py:168
  62.3 21.6 %collective-permute-start.3 = (bf16[128,2048]{1,0:T(8,128)(2,1)S(1)}, bf16[128,2048]{1,0:T(8,128)(2,1)}, u32[]{:S(2)}, u32[]{:S(2)}) collective-permute-start(bf16[128,2048]{1,0:T(8,128)(2,1)S(1)} %copy-done.57), channel_id=1, source_target_pairs={{1,0},{2,1},{3,2},{5,4},{6,5},{7,6},{9,8},{10,9},{11,10},{13,12},{... | collective-permute-start | bytes 1572872 | tf_op jit(solution)/shard_map/ppermute | solution.py:169
  72.7 22.5 %collective-permute-start.9 = (bf16[128,2048]{1,0:T(8,128)(2,1)}, bf16[128,2048]{1,0:T(8,128)(2,1)}, u32[]{:S(2)}, u32[]{:S(2)}) collective-permute-start(bf16[128,2048]{1,0:T(8,128)(2,1)} %collective-permute-done.5), channel_id=1, source_target_pairs={{1,0},{5,4},{9,8},{13,12},{17,16},{21,20},{25,24},{29,28}} | collective-permute-start | bytes 1572872 | tf_op jit(solution)/shard_map/ppermute | solution.py:169
  74.0 21.2 %collective-permute-start.8 = (bf16[128,2048]{1,0:T(8,128)(2,1)}, bf16[128,2048]{1,0:T(8,128)(2,1)}, u32[]{:S(2)}, u32[]{:S(2)}) collective-permute-start(bf16[128,2048]{1,0:T(8,128)(2,1)} %collective-permute-done.4), channel_id=1, source_target_pairs={{2,3},{6,7},{10,11},{14,15},{18,19},{22,23},{26,27},{30,31}} | collective-permute-start | bytes 1572872 | tf_op jit(solution)/shard_map/ppermute | solution.py:168
  85.4 18.8 %collective-permute-start.7 = (bf16[128,2048]{1,0:T(8,128)(2,1)}, bf16[128,2048]{1,0:T(8,128)(2,1)}, u32[]{:S(2)}, u32[]{:S(2)}) collective-permute-start(bf16[128,2048]{1,0:T(8,128)(2,1)} %collective-permute-done.3), channel_id=1, source_target_pairs={{1,0},{2,1},{5,4},{6,5},{9,8},{10,9},{13,12},{14,13},{17,16},{18,1... | collective-permute-start | bytes 1572872 | tf_op jit(solution)/shard_map/ppermute | solution.py:169
  104.2 31.6 %collective-permute-start.10 = (bf16[128,2048]{1,0:T(8,128)(2,1)}, bf16[128,2048]{1,0:T(8,128)(2,1)S(1)}, u32[]{:S(2)}, u32[]{:S(2)}) collective-permute-start(bf16[128,2048]{1,0:T(8,128)(2,1)} %collective-permute-done.6), channel_id=1, source_target_pairs={{2,3},{6,7},{10,11},{14,15},{18,19},{22,23},{26,27},{30,31}} | collective-permute-start | bytes 1572872 | tf_op jit(solution)/shard_map/ppermute | solution.py:168
  104.9 30.9 %collective-permute-start.11 = (bf16[128,2048]{1,0:T(8,128)(2,1)}, bf16[128,2048]{1,0:T(8,128)(2,1)}, u32[]{:S(2)}, u32[]{:S(2)}) collective-permute-start(bf16[128,2048]{1,0:T(8,128)(2,1)} %collective-permute-done.7), channel_id=1, source_target_pairs={{1,0},{5,4},{9,8},{13,12},{17,16},{21,20},{25,24},{29,28}} | collective-permute-start | bytes 1572872 | tf_op jit(solution)/shard_map/ppermute | solution.py:169
  128.4 46.2 %collective-permute-start.15 = (bf16[256,2048]{1,0:T(8,128)(2,1)}, bf16[256,2048]{1,0:T(8,128)(2,1)}, u32[]{:S(2)}, u32[]{:S(2)}) collective-permute-start(bf16[256,2048]{1,0:T(8,128)(2,1)} %bitcast.39), channel_id=1, source_target_pairs={{0,1},{1,2},{2,3},{4,5},{5,6},{6,7},{8,9},{9,10},{10,11},{12,13},{... | collective-permute-start | bytes 3145736 | tf_op jit(solution)/shard_map/ppermute | solution.py:168
  134.6 40.0 %collective-permute-start.16 = (bf16[256,2048]{1,0:T(8,128)(2,1)}, bf16[256,2048]{1,0:T(8,128)(2,1)}, u32[]{:S(2)}, u32[]{:S(2)}) collective-permute-start(bf16[256,2048]{1,0:T(8,128)(2,1)} %bitcast.39), channel_id=1, source_target_pairs={{1,0},{2,1},{3,2},{5,4},{6,5},{7,6},{9,8},{10,9},{11,10},{13,12},{... | collective-permute-start | bytes 3145736 | tf_op jit(solution)/shard_map/ppermute | solution.py:169
  182.5 36.1 %collective-permute-start.22 = (bf16[256,2048]{1,0:T(8,128)(2,1)}, bf16[256,2048]{1,0:T(8,128)(2,1)}, u32[]{:S(2)}, u32[]{:S(2)}) collective-permute-start(bf16[256,2048]{1,0:T(8,128)(2,1)} %collective-permute-done.15), channel_id=1, source_target_pairs={{1,2},{2,3},{5,6},{6,7},{9,10},{10,11},{13,14},{14,15},{17,18},{18... | collective-permute-start | bytes 3145736 | tf_op jit(solution)/shard_map/ppermute | solution.py:168
  184.1 34.5 %collective-permute-start.23 = (bf16[256,2048]{1,0:T(8,128)(2,1)}, bf16[256,2048]{1,0:T(8,128)(2,1)}, u32[]{:S(2)}, u32[]{:S(2)}) collective-permute-start(bf16[256,2048]{1,0:T(8,128)(2,1)} %collective-permute-done.16), channel_id=1, source_target_pairs={{1,0},{2,1},{5,4},{6,5},{9,8},{10,9},{13,12},{14,13},{17,16},{18,1... | collective-permute-start | bytes 3145736 | tf_op jit(solution)/shard_map/ppermute | solution.py:169
  212.5 16.1 %collective-permute-start.28 = (bf16[128,2048]{1,0:T(8,128)(2,1)S(1)}, bf16[128,2048]{1,0:T(8,128)(2,1)S(1)}, u32[]{:S(2)}, u32[]{:S(2)}) collective-permute-start(bf16[128,2048]{1,0:T(8,128)(2,1)S(1)} %get-tuple-element.190), channel_id=1, source_target_pairs={{0,1},{4,5},{8,9},{12,13},{16,17},{20,21},{24,25},{28,29}} | collective-permute-start | bytes 1572872 | tf_op jit(solution)/shard_map/ppermute | solution.py:290
  220.1 14.2 %collective-permute-start.24 = (bf16[128,2048]{1,0:T(8,128)(2,1)S(1)}, bf16[128,2048]{1,0:T(8,128)(2,1)}, u32[]{:S(2)}, u32[]{:S(2)}) collective-permute-start(bf16[128,2048]{1,0:T(8,128)(2,1)S(1)} %get-tuple-element.186), channel_id=1, source_target_pairs={{0,1},{1,2},{4,5},{5,6},{8,9},{9,10},{12,13},{13,14},{16,17},{17,1... | collective-permute-start | bytes 1572872 | tf_op jit(solution)/shard_map/ppermute | solution.py:290
  234.3 14.6 %collective-permute-start.31 = (bf16[128,2048]{1,0:T(8,128)(2,1)}, bf16[128,2048]{1,0:T(8,128)(2,1)}, u32[]{:S(2)}, u32[]{:S(2)}) collective-permute-start(bf16[128,2048]{1,0:T(8,128)(2,1)} %get-tuple-element.193), channel_id=1, source_target_pairs={{2,1},{3,2},{6,5},{7,6},{10,9},{11,10},{14,13},{15,14},{18,17},{19... | collective-permute-start | bytes 1572872 | tf_op jit(solution)/shard_map/ppermute | solution.py:291
  235.8 36.4 %collective-permute-start.32 = (bf16[256,2048]{1,0:T(8,128)(2,1)}, bf16[256,2048]{1,0:T(8,128)(2,1)}, u32[]{:S(2)}, u32[]{:S(2)}) collective-permute-start(bf16[256,2048]{1,0:T(8,128)(2,1)} %collective-permute-done.22), channel_id=1, source_target_pairs={{2,3},{6,7},{10,11},{14,15},{18,19},{22,23},{26,27},{30,31}} | collective-permute-start | bytes 3145736 | tf_op jit(solution)/shard_map/ppermute | solution.py:168
  237.4 34.8 %collective-permute-start.33 = (bf16[256,2048]{1,0:T(8,128)(2,1)}, bf16[256,2048]{1,0:T(8,128)(2,1)}, u32[]{:S(2)}, u32[]{:S(2)}) collective-permute-start(bf16[256,2048]{1,0:T(8,128)(2,1)} %collective-permute-done.23), channel_id=1, source_target_pairs={{1,0},{5,4},{9,8},{13,12},{17,16},{21,20},{25,24},{29,28}} | collective-permute-start | bytes 3145736 | tf_op jit(solution)/shard_map/ppermute | solution.py:169
  238.7 20.8 %collective-permute-start.30 = (bf16[128,2048]{1,0:T(8,128)(2,1)}, bf16[128,2048]{1,0:T(8,128)(2,1)}, u32[]{:S(2)}, u32[]{:S(2)}) collective-permute-start(bf16[128,2048]{1,0:T(8,128)(2,1)} %get-tuple-element.192), channel_id=1, source_target_pairs={{0,1},{1,2},{4,5},{5,6},{8,9},{9,10},{12,13},{13,14},{16,17},{17,1... | collective-permute-start | bytes 1572872 | tf_op jit(solution)/shard_map/ppermute | solution.py:290
  247.6 24.5 %collective-permute-start.27 = (bf16[128,2048]{1,0:T(8,128)(2,1)}, bf16[128,2048]{1,0:T(8,128)(2,1)}, u32[]{:S(2)}, u32[]{:S(2)}) collective-permute-start(bf16[128,2048]{1,0:T(8,128)(2,1)} %get-tuple-element.189), channel_id=1, source_target_pairs={{1,0},{2,1},{3,2},{5,4},{6,5},{7,6},{9,8},{10,9},{11,10},{13,12},{... | collective-permute-start | bytes 1572872 | tf_op jit(solution)/shard_map/ppermute | solution.py:291
  248.9 23.2 %collective-permute-start.26 = (bf16[128,2048]{1,0:T(8,128)(2,1)}, bf16[128,2048]{1,0:T(8,128)(2,1)}, u32[]{:S(2)}, u32[]{:S(2)}) collective-permute-start(bf16[128,2048]{1,0:T(8,128)(2,1)} %get-tuple-element.188), channel_id=1, source_target_pairs={{0,1},{1,2},{2,3},{4,5},{5,6},{6,7},{8,9},{9,10},{10,11},{12,13},{... | collective-permute-start | bytes 1572872 | tf_op jit(solution)/shard_map/ppermute | solution.py:290
  272.2 16.7 %collective-permute-start.35 = (bf16[128,2048]{1,0:T(8,128)(2,1)S(1)}, bf16[128,2048]{1,0:T(8,128)(2,1)S(1)}, u32[]{:S(2)}, u32[]{:S(2)}) collective-permute-start(bf16[128,2048]{1,0:T(8,128)(2,1)S(1)} %get-tuple-element.197), channel_id=1, source_target_pairs={{1,0},{2,1},{3,2},{5,4},{6,5},{7,6},{9,8},{10,9},{11,10},{13,12},{... | collective-permute-start | bytes 1572872 | tf_op jit(solution)/shard_map/ppermute | solution.py:291
  273.5 16.9 %collective-permute-start.34 = (bf16[128,2048]{1,0:T(8,128)(2,1)S(1)}, bf16[128,2048]{1,0:T(8,128)(2,1)S(1)}, u32[]{:S(2)}, u32[]{:S(2)}) collective-permute-start(bf16[128,2048]{1,0:T(8,128)(2,1)S(1)} %get-tuple-element.196), channel_id=1, source_target_pairs={{0,1},{1,2},{2,3},{4,5},{5,6},{6,7},{8,9},{9,10},{10,11},{12,13},{... | collective-permute-start | bytes 1572872 | tf_op jit(solution)/shard_map/ppermute | solution.py:290
  279.8 18.2 %collective-permute-start.36 = (bf16[128,2048]{1,0:T(8,128)(2,1)S(1)}, bf16[128,2048]{1,0:T(8,128)(2,1)S(1)}, u32[]{:S(2)}, u32[]{:S(2)}) collective-permute-start(bf16[128,2048]{1,0:T(8,128)(2,1)S(1)} %multiply_convert_fusion.2), channel_id=1, source_target_pairs={{0,1},{1,2},{2,3},{4,5},{5,6},{6,7},{8,9},{9,10},{10,11},{12,13},{... | collective-permute-start | bytes 1572872 | tf_op jit(solution)/shard_map/ppermute | solution.py:168
  282.7 17.5 %collective-permute-start.37 = (bf16[128,2048]{1,0:T(8,128)(2,1)S(1)}, bf16[128,2048]{1,0:T(8,128)(2,1)S(1)}, u32[]{:S(2)}, u32[]{:S(2)}) collective-permute-start(bf16[128,2048]{1,0:T(8,128)(2,1)S(1)} %multiply_convert_fusion.2), channel_id=1, source_target_pairs={{1,0},{2,1},{3,2},{5,4},{6,5},{7,6},{9,8},{10,9},{11,10},{13,12},{... | collective-permute-start | bytes 1572872 | tf_op jit(solution)/shard_map/ppermute | solution.py:169
  295.5 16.8 %collective-permute-start.43 = (bf16[128,2048]{1,0:T(8,128)(2,1)S(1)}, bf16[128,2048]{1,0:T(8,128)(2,1)S(1)}, u32[]{:S(2)}, u32[]{:S(2)}) collective-permute-start(bf16[128,2048]{1,0:T(8,128)(2,1)S(1)} %multiply_convert_fusion.1), channel_id=1, source_target_pairs={{1,0},{2,1},{3,2},{5,4},{6,5},{7,6},{9,8},{10,9},{11,10},{13,12},{... | collective-permute-start | bytes 1572872 | tf_op jit(solution)/shard_map/ppermute | solution.py:169
  300.1 15.7 %collective-permute-start.38 = (bf16[128,2048]{1,0:T(8,128)(2,1)S(1)}, bf16[128,2048]{1,0:T(8,128)(2,1)S(1)}, u32[]{:S(2)}, u32[]{:S(2)}) collective-permute-start(bf16[128,2048]{1,0:T(8,128)(2,1)S(1)} %collective-permute-done.36), channel_id=1, source_target_pairs={{1,2},{2,3},{5,6},{6,7},{9,10},{10,11},{13,14},{14,15},{17,18},{18... | collective-permute-start | bytes 1572872 | tf_op jit(solution)/shard_map/ppermute | solution.py:168
  300.8 22.7 %collective-permute-start.39 = (bf16[128,2048]{1,0:T(8,128)(2,1)S(1)}, bf16[128,2048]{1,0:T(8,128)(2,1)S(1)}, u32[]{:S(2)}, u32[]{:S(2)}) collective-permute-start(bf16[128,2048]{1,0:T(8,128)(2,1)S(1)} %collective-permute-done.37), channel_id=1, source_target_pairs={{1,0},{2,1},{5,4},{6,5},{9,8},{10,9},{13,12},{14,13},{17,16},{18,1... | collective-permute-start | bytes 1572872 | tf_op jit(solution)/shard_map/ppermute | solution.py:169
  312.2 14.9 %collective-permute-start.44 = (bf16[128,2048]{1,0:T(8,128)(2,1)S(1)}, bf16[128,2048]{1,0:T(8,128)(2,1)S(1)}, u32[]{:S(2)}, u32[]{:S(2)}) collective-permute-start(bf16[128,2048]{1,0:T(8,128)(2,1)S(1)} %collective-permute-done.42), channel_id=1, source_target_pairs={{1,2},{2,3},{5,6},{6,7},{9,10},{10,11},{13,14},{14,15},{17,18},{18... | collective-permute-start | bytes 1572872 | tf_op jit(solution)/shard_map/ppermute | solution.py:168
  312.9 21.8 %collective-permute-start.45 = (bf16[128,2048]{1,0:T(8,128)(2,1)S(1)}, bf16[128,2048]{1,0:T(8,128)(2,1)S(1)}, u32[]{:S(2)}, u32[]{:S(2)}) collective-permute-start(bf16[128,2048]{1,0:T(8,128)(2,1)S(1)} %collective-permute-done.43), channel_id=1, source_target_pairs={{1,0},{2,1},{5,4},{6,5},{9,8},{10,9},{13,12},{14,13},{17,16},{18,1... | collective-permute-start | bytes 1572872 | tf_op jit(solution)/shard_map/ppermute | solution.py:169
  323.5 16.3 %collective-permute-start.41 = (bf16[128,2048]{1,0:T(8,128)(2,1)S(1)}, bf16[128,2048]{1,0:T(8,128)(2,1)S(1)}, u32[]{:S(2)}, u32[]{:S(2)}) collective-permute-start(bf16[128,2048]{1,0:T(8,128)(2,1)S(1)} %collective-permute-done.38), channel_id=1, source_target_pairs={{2,3},{6,7},{10,11},{14,15},{18,19},{22,23},{26,27},{30,31}} | collective-permute-start | bytes 1572872 | tf_op jit(solution)/shard_map/ppermute | solution.py:168
  324.2 19.5 %collective-permute-start.40 = (bf16[128,2048]{1,0:T(8,128)(2,1)S(1)}, bf16[128,2048]{1,0:T(8,128)(2,1)S(1)}, u32[]{:S(2)}, u32[]{:S(2)}) collective-permute-start(bf16[128,2048]{1,0:T(8,128)(2,1)S(1)} %collective-permute-done.39), channel_id=1, source_target_pairs={{1,0},{5,4},{9,8},{13,12},{17,16},{21,20},{25,24},{29,28}} | collective-permute-start | bytes 1572872 | tf_op jit(solution)/shard_map/ppermute | solution.py:169
  388.1 14.2 %collective-permute-start.49 = (bf16[128,2048]{1,0:T(8,128)(2,1)S(1)}, bf16[128,2048]{1,0:T(8,128)(2,1)S(1)}, u32[]{:S(2)}, u32[]{:S(2)}) collective-permute-start(bf16[128,2048]{1,0:T(8,128)(2,1)S(1)} %get-tuple-element.384), channel_id=1, source_target_pairs={{3,2},{7,6},{11,10},{15,14},{19,18},{23,22},{27,26},{31,30}} | collective-permute-start | bytes 1572872 | tf_op jit(solution)/shard_map/ppermute | solution.py:257
  414.3 216.0 %reduce-scatter.4.cloned.1.call-start = ((), (), s32[]{:S(2)}) async-start(), calls=%async_computation.6 | async-start | bytes 5242880 | tf_op jit(solution)/shard_map/reduce_scatter | solution.py:189
  418.8 16.4 %collective-permute-start.50 = (bf16[128,2048]{1,0:T(8,128)(2,1)S(1)}, bf16[128,2048]{1,0:T(8,128)(2,1)S(1)}, u32[]{:S(2)}, u32[]{:S(2)}) collective-permute-start(bf16[128,2048]{1,0:T(8,128)(2,1)S(1)} %get-tuple-element.218), channel_id=1, source_target_pairs={{0,1},{1,2},{4,5},{5,6},{8,9},{9,10},{12,13},{13,14},{16,17},{17,1... | collective-permute-start | bytes 1572872 | tf_op jit(solution)/shard_map/ppermute | solution.py:290
  435.2 14.5 %collective-permute-start.59 = (bf16[128,2048]{1,0:T(8,128)(2,1)}, bf16[128,2048]{1,0:T(8,128)(2,1)}, u32[]{:S(2)}, u32[]{:S(2)}) collective-permute-start(bf16[128,2048]{1,0:T(8,128)(2,1)} %get-tuple-element.228), channel_id=1, source_target_pairs={{2,1},{3,2},{6,5},{7,6},{10,9},{11,10},{14,13},{15,14},{18,17},{19... | collective-permute-start | bytes 1572872 | tf_op jit(solution)/shard_map/ppermute | solution.py:291
  443.1 14.4 %collective-permute-start.53 = (bf16[128,2048]{1,0:T(8,128)(2,1)}, bf16[128,2048]{1,0:T(8,128)(2,1)}, u32[]{:S(2)}, u32[]{:S(2)}) collective-permute-start(bf16[128,2048]{1,0:T(8,128)(2,1)} %get-tuple-element.221), channel_id=1, source_target_pairs={{1,0},{2,1},{3,2},{5,4},{6,5},{7,6},{9,8},{10,9},{11,10},{13,12},{... | collective-permute-start | bytes 1572872 | tf_op jit(solution)/shard_map/ppermute | solution.py:291
  444.3 14.8 %collective-permute-start.52 = (bf16[128,2048]{1,0:T(8,128)(2,1)}, bf16[128,2048]{1,0:T(8,128)(2,1)}, u32[]{:S(2)}, u32[]{:S(2)}) collective-permute-start(bf16[128,2048]{1,0:T(8,128)(2,1)} %get-tuple-element.220), channel_id=1, source_target_pairs={{0,1},{1,2},{2,3},{4,5},{5,6},{6,7},{8,9},{9,10},{10,11},{12,13},{... | collective-permute-start | bytes 1572872 | tf_op jit(solution)/shard_map/ppermute | solution.py:290
  459.2 19.4 %collective-permute-start.61 = (bf16[128,2048]{1,0:T(8,128)(2,1)}, bf16[128,2048]{1,0:T(8,128)(2,1)}, u32[]{:S(2)}, u32[]{:S(2)}) collective-permute-start(bf16[128,2048]{1,0:T(8,128)(2,1)} %get-tuple-element.230), channel_id=1, source_target_pairs={{1,0},{2,1},{3,2},{5,4},{6,5},{7,6},{9,8},{10,9},{11,10},{13,12},{... | collective-permute-start | bytes 1572872 | tf_op jit(solution)/shard_map/ppermute | solution.py:291
  460.5 18.1 %collective-permute-start.60 = (bf16[128,2048]{1,0:T(8,128)(2,1)}, bf16[128,2048]{1,0:T(8,128)(2,1)}, u32[]{:S(2)}, u32[]{:S(2)}) collective-permute-start(bf16[128,2048]{1,0:T(8,128)(2,1)} %get-tuple-element.229), channel_id=1, source_target_pairs={{0,1},{1,2},{2,3},{4,5},{5,6},{6,7},{8,9},{9,10},{10,11},{12,13},{... | collective-permute-start | bytes 1572872 | tf_op jit(solution)/shard_map/ppermute | solution.py:290
  471.2 18.2 %collective-permute-start.54 = (bf16[128,2048]{1,0:T(8,128)(2,1)}, bf16[128,2048]{1,0:T(8,128)(2,1)}, u32[]{:S(2)}, u32[]{:S(2)}) collective-permute-start(bf16[128,2048]{1,0:T(8,128)(2,1)} %get-tuple-element.356.in_ref), channel_id=1, source_target_pairs={{0,1},{1,2},{2,3},{4,5},{5,6},{6,7},{8,9},{9,10},{10,11},{12,13},{... | collective-permute-start | bytes 1572872 | tf_op jit(solution)/shard_map/ppermute | solution.py:168
  475.4 17.1 %collective-permute-start.55 = (bf16[128,2048]{1,0:T(8,128)(2,1)}, bf16[128,2048]{1,0:T(8,128)(2,1)}, u32[]{:S(2)}, u32[]{:S(2)}) collective-permute-start(bf16[128,2048]{1,0:T(8,128)(2,1)} %get-tuple-element.356.in_ref), channel_id=1, source_target_pairs={{1,0},{2,1},{3,2},{5,4},{6,5},{7,6},{9,8},{10,9},{11,10},{13,12},{... | collective-permute-start | bytes 1572872 | tf_op jit(solution)/shard_map/ppermute | solution.py:169
  482.8 24.0 %collective-permute-start.62 = (bf16[128,2048]{1,0:T(8,128)(2,1)S(1)}, bf16[128,2048]{1,0:T(8,128)(2,1)}, u32[]{:S(2)}, u32[]{:S(2)}) collective-permute-start(bf16[128,2048]{1,0:T(8,128)(2,1)S(1)} %get-tuple-element.354.in_ref), channel_id=1, source_target_pairs={{0,1},{1,2},{2,3},{4,5},{5,6},{6,7},{8,9},{9,10},{10,11},{12,13},{... | collective-permute-start | bytes 1572872 | tf_op jit(solution)/shard_map/ppermute | solution.py:168
  488.1 18.7 %collective-permute-start.63 = (bf16[128,2048]{1,0:T(8,128)(2,1)S(1)}, bf16[128,2048]{1,0:T(8,128)(2,1)}, u32[]{:S(2)}, u32[]{:S(2)}) collective-permute-start(bf16[128,2048]{1,0:T(8,128)(2,1)S(1)} %get-tuple-element.354.in_ref), channel_id=1, source_target_pairs={{1,0},{2,1},{3,2},{5,4},{6,5},{7,6},{9,8},{10,9},{11,10},{13,12},{... | collective-permute-start | bytes 1572872 | tf_op jit(solution)/shard_map/ppermute | solution.py:169
  492.4 17.1 %collective-permute-start.68 = (bf16[128,2048]{1,0:T(8,128)(2,1)}, bf16[128,2048]{1,0:T(8,128)(2,1)S(1)}, u32[]{:S(2)}, u32[]{:S(2)}) collective-permute-start(bf16[128,2048]{1,0:T(8,128)(2,1)} %collective-permute-done.54), channel_id=1, source_target_pairs={{1,2},{2,3},{5,6},{6,7},{9,10},{10,11},{13,14},{14,15},{17,18},{18... | collective-permute-start | bytes 1572872 | tf_op jit(solution)/shard_map/ppermute | solution.py:168
  493.1 17.9 %collective-permute-start.69 = (bf16[128,2048]{1,0:T(8,128)(2,1)}, bf16[128,2048]{1,0:T(8,128)(2,1)}, u32[]{:S(2)}, u32[]{:S(2)}) collective-permute-start(bf16[128,2048]{1,0:T(8,128)(2,1)} %collective-permute-done.55), channel_id=1, source_target_pairs={{1,0},{2,1},{5,4},{6,5},{9,8},{10,9},{13,12},{14,13},{17,16},{18,1... | collective-permute-start | bytes 1572872 | tf_op jit(solution)/shard_map/ppermute | solution.py:169
  508.3 20.5 %collective-permute-start.65 = (bf16[128,2048]{1,0:T(8,128)(2,1)}, bf16[128,2048]{1,0:T(8,128)(2,1)}, u32[]{:S(2)}, u32[]{:S(2)}) collective-permute-start(bf16[128,2048]{1,0:T(8,128)(2,1)} %collective-permute-done.63), channel_id=1, source_target_pairs={{1,0},{2,1},{5,4},{6,5},{9,8},{10,9},{13,12},{14,13},{17,16},{18,1... | collective-permute-start | bytes 1572872 | tf_op jit(solution)/shard_map/ppermute | solution.py:169
  511.1 23.3 %collective-permute-start.70 = (bf16[128,2048]{1,0:T(8,128)(2,1)}, bf16[128,2048]{1,0:T(8,128)(2,1)}, u32[]{:S(2)}, u32[]{:S(2)}) collective-permute-start(bf16[128,2048]{1,0:T(8,128)(2,1)} %collective-permute-done.69), channel_id=1, source_target_pairs={{1,0},{5,4},{9,8},{13,12},{17,16},{21,20},{25,24},{29,28}} | collective-permute-start | bytes 1572872 | tf_op jit(solution)/shard_map/ppermute | solution.py:169
  519.0 18.0 %collective-permute-start.71 = (bf16[128,2048]{1,0:T(8,128)(2,1)}, bf16[128,2048]{1,0:T(8,128)(2,1)S(1)}, u32[]{:S(2)}, u32[]{:S(2)}) collective-permute-start(bf16[128,2048]{1,0:T(8,128)(2,1)} %copy-done.67), channel_id=1, source_target_pairs={{2,3},{6,7},{10,11},{14,15},{18,19},{22,23},{26,27},{30,31}} | collective-permute-start | bytes 1572872 | tf_op jit(solution)/shard_map/ppermute | solution.py:168
  541.6 207.2 %reduce-scatter.8.cloned.1.call-start = ((), (), s32[]{:S(2)}) async-start(), calls=%async_computation.8 | async-start | bytes 17104896 | tf_op jit(solution)/shard_map/reduce_scatter | solution.py:1257
  557.8 14.1 %collective-permute-start.72 = (f32[8,128]{1,0:T(8,128)S(1)}, f32[8,128]{1,0:T(8,128)S(1)}, u32[]{:S(2)}, u32[]{:S(2)}) collective-permute-start(f32[8,128]{1,0:T(8,128)S(1)} %bitcast.171), channel_id=1, source_target_pairs={{0,1},{1,2},{2,3},{3,0},{4,5},{5,6},{6,7},{7,4},{8,9},{9,10},{10,1... | collective-permute-start | bytes 12296 | tf_op jit(solution)/shard_map/ppermute | solution.py:116
  646.5 31.4 %collective-permute-start.75 = (bf16[128,2048]{1,0:T(8,128)(2,1)}, bf16[128,2048]{1,0:T(8,128)(2,1)}, u32[]{:S(2)}, u32[]{:S(2)}) collective-permute-start(bf16[128,2048]{1,0:T(8,128)(2,1)} %get-tuple-element.260), channel_id=1, source_target_pairs={{0,1},{4,5},{8,9},{12,13},{16,17},{20,21},{24,25},{28,29}} | collective-permute-start | bytes 1572872 | tf_op jit(solution)/shard_map/ppermute | solution.py:290
  649.0 28.9 %collective-permute-start.76 = (bf16[128,2048]{1,0:T(8,128)(2,1)}, bf16[128,2048]{1,0:T(8,128)(2,1)}, u32[]{:S(2)}, u32[]{:S(2)}) collective-permute-start(bf16[128,2048]{1,0:T(8,128)(2,1)} %get-tuple-element.261), channel_id=1, source_target_pairs={{3,2},{7,6},{11,10},{15,14},{19,18},{23,22},{27,26},{31,30}} | collective-permute-start | bytes 1572872 | tf_op jit(solution)/shard_map/ppermute | solution.py:291
  678.8 14.1 %collective-permute-start.81 = (bf16[128,2048]{1,0:T(8,128)(2,1)}, bf16[128,2048]{1,0:T(8,128)(2,1)S(1)}, u32[]{:S(2)}, u32[]{:S(2)}) collective-permute-start(bf16[128,2048]{1,0:T(8,128)(2,1)} %get-tuple-element.267), channel_id=1, source_target_pairs={{0,1},{4,5},{8,9},{12,13},{16,17},{20,21},{24,25},{28,29}} | collective-permute-start | bytes 1572872 | tf_op jit(solution)/shard_map/ppermute | solution.py:290
  681.8 20.1 %collective-permute-start.77 = (bf16[128,2048]{1,0:T(8,128)(2,1)S(1)}, bf16[128,2048]{1,0:T(8,128)(2,1)S(1)}, u32[]{:S(2)}, u32[]{:S(2)}) collective-permute-start(bf16[128,2048]{1,0:T(8,128)(2,1)S(1)} %get-tuple-element.262), channel_id=1, source_target_pairs={{0,1},{1,2},{4,5},{5,6},{8,9},{9,10},{12,13},{13,14},{16,17},{17,1... | collective-permute-start | bytes 1572872 | tf_op jit(solution)/shard_map/ppermute | solution.py:290
  683.1 18.8 %collective-permute-start.78 = (bf16[128,2048]{1,0:T(8,128)(2,1)S(1)}, bf16[128,2048]{1,0:T(8,128)(2,1)S(1)}, u32[]{:S(2)}, u32[]{:S(2)}) collective-permute-start(bf16[128,2048]{1,0:T(8,128)(2,1)S(1)} %get-tuple-element.263), channel_id=1, source_target_pairs={{2,1},{3,2},{6,5},{7,6},{10,9},{11,10},{14,13},{15,14},{18,17},{19... | collective-permute-start | bytes 1572872 | tf_op jit(solution)/shard_map/ppermute | solution.py:291
  703.4 16.9 %collective-permute-start.83 = (bf16[128,2048]{1,0:T(8,128)(2,1)}, bf16[128,2048]{1,0:T(8,128)(2,1)}, u32[]{:S(2)}, u32[]{:S(2)}) collective-permute-start(bf16[128,2048]{1,0:T(8,128)(2,1)} %get-tuple-element.269), channel_id=1, source_target_pairs={{0,1},{1,2},{4,5},{5,6},{8,9},{9,10},{12,13},{13,14},{16,17},{17,1... | collective-permute-start | bytes 1572872 | tf_op jit(solution)/shard_map/ppermute | solution.py:290
  709.8 18.8 %collective-permute-start.79 = (bf16[128,2048]{1,0:T(8,128)(2,1)}, bf16[128,2048]{1,0:T(8,128)(2,1)S(1)}, u32[]{:S(2)}, u32[]{:S(2)}) collective-permute-start(bf16[128,2048]{1,0:T(8,128)(2,1)} %get-tuple-element.264), channel_id=1, source_target_pairs={{0,1},{1,2},{2,3},{4,5},{5,6},{6,7},{8,9},{9,10},{10,11},{12,13},{... | collective-permute-start | bytes 1572872 | tf_op jit(solution)/shard_map/ppermute | solution.py:290
  713.6 15.1 %collective-permute-start.80 = (bf16[128,2048]{1,0:T(8,128)(2,1)}, bf16[128,2048]{1,0:T(8,128)(2,1)S(1)}, u32[]{:S(2)}, u32[]{:S(2)}) collective-permute-start(bf16[128,2048]{1,0:T(8,128)(2,1)} %get-tuple-element.265), channel_id=1, source_target_pairs={{1,0},{2,1},{3,2},{5,4},{6,5},{7,6},{9,8},{10,9},{11,10},{13,12},{... | collective-permute-start | bytes 1572872 | tf_op jit(solution)/shard_map/ppermute | solution.py:291
  (115 other events, 1167.5 us)
Sparse Core Ops, SparseCore 0:
  26.7 71.0 all-gather.3
  99.7 36.7 all-gather.5
  138.3 72.1 all-gather.7
  414.5 92.9 reduce-scatter.5
  541.7 78.8 reduce-scatter.3
  630.4 108.2 reduce-scatter.7

commit v4 on v3

--- a/solution.py
+++ b/solution.py
@@ -382,7 +382,7 @@
     model = lefts[0][0].shape[1]
     ranges = ranges or [(0, right.shape[1]) for right in rights]
     width = sum(stop - first for first, stop in ranges)
-    tile = min(256, model // pieces)
+    tile = min(512, model // pieces)
     steps = model // pieces // tile
     parts = [len(left) for left in lefts]
     flat = [part for left in lefts for part in left]

time: 792 us -> 792 us (level)
  no operation moved by 1% of the time
where the time goes in v4:
time: 792 us; the launch traced here: 780 us
  Pallas kernels  221 us (28%)
  starting transfers between devices  203 us (26%)
  waiting for transfers between devices  191 us (24%)
  other arithmetic  84.6 us (11%)
  local copies, waits for them, and re-layouts  62.6 us (8%)
  between operations  16.9 us (2%)
    ppermute x21, waiting for transfers between devices, z_gather_parts(): lax.ppermute(left, 'tensor', [(i, i - 1) for i in range(1, size - s)])  92.3 us
    ppermute x17, starting transfers between devices, z_scatter_parts(): right = lax.ppermute(to_right, 'tensor', [(i, i + 1) for i in range(s + 1)])  73 us
    ppermute x17, waiting for transfers between devices, z_scatter_parts(): right = lax.ppermute(to_right, 'tensor', [(i, i + 1) for i in range(s + 1)])  58.9 us
    ppermute x21, starting transfers between devices, z_gather_parts(): lax.ppermute(right, 'tensor', [(i, i + 1) for i in range(s, size - 1)])  50.2 us
    pallas_call x3, Pallas kernels, gradient(): pl.pallas_call(partial(gradient_kernel, parts, uses, ranges), grid=(steps...  46.9 us
    unnamed x180, local copies, waits for them, and re-layouts  36.5 us
    pallas_call x1, Pallas kernels, mamba_backward(): pl.pallas_call(partial(mamba_backward_kernel, cols), grid=(chunks,), in_s...  31.6 us
    pallas_call x2, Pallas kernels, norm_project(): pl.pallas_call(partial(norm_project_kernel, members), grid=(width // tile...  28.3 us
  transfers between devices with their start and end apart: 100, of which 36 were waited for; matrix products, arithmetic and copies ran while one was open for 15% of the time, Pallas kernels for 23%

profile of v4, /device:TPU:0, one launch (start us, length us, event | category | flops | bytes accessed | tf_op | source)
XLA Modules:
  0.0 780.0 jit_solution(18060277552952619834)
XLA Ops:
  18.5 6.2 collective-permute-done.13
  32.0 6.6 collective-permute-start
  44.4 4.8 collective-permute-done
  49.2 5.0 collective-permute-done.1
  56.9 5.4 collective-permute-start.2
  63.8 8.9 %collective-permute-done.5 = bf16[128,2048]{1,0:T(8,128)(2,1)} collective-permute-done((bf16[128,2048]{1,0:T(8,128)(2,1)}, bf16[128,2048]{1,0:T(8,128)(2,1)}, u32[]{:S(2)}, u32[]{:S(2)}) %collective-permute-start.5) | collective-permute-done | bytes 524320 | tf_op jit(solution)/shard_map/ppermute | solution.py:169
  75.5 8.4 %collective-permute-done.3 = bf16[128,2048]{1,0:T(8,128)(2,1)} collective-permute-done((bf16[128,2048]{1,0:T(8,128)(2,1)S(1)}, bf16[128,2048]{1,0:T(8,128)(2,1)}, u32[]{:S(2)}, u32[]{:S(2)}) %collective-permute-start.3) | collective-permute-done | bytes 524320 | tf_op jit(solution)/shard_map/ppermute | solution.py:169
  87.4 7.8 collective-permute-done.9
  95.2 9.0 %collective-permute-done.7 = bf16[128,2048]{1,0:T(8,128)(2,1)} collective-permute-done((bf16[128,2048]{1,0:T(8,128)(2,1)}, bf16[128,2048]{1,0:T(8,128)(2,1)}, u32[]{:S(2)}, u32[]{:S(2)}) %collective-permute-start.7) | collective-permute-done | bytes 524320 | tf_op jit(solution)/shard_map/ppermute | solution.py:169
  114.3 14.1 %norm_project.2 = (bf16[1024,2048]{1,0:T(8,128)(2,1)}, f32[1024,2688]{1,0:T(8,128)}) custom-call(bf16[512,2048]{1,0:T(8,128)(2,1)S(1)} %copy-done.14, f32[1,2048]{1,0:T(1,128)S(1)} %bitcast.131, bf16[2176,2688]{1,0:T(8,128)(2,1)} %all-gather.4.cloned.1.call-done.w_ref), custom_call_target="tpu_custom_call" | custom-call | flops 5637144576 | bytes 18612224 | tf_op jit(solution)/shard_map/norm_project/pallas_call | solution.py:333
  128.4 6.2 collective-permute-start.15
  139.9 14.2 %norm_project.3 = (bf16[1024,2048]{1,0:T(8,128)(2,1)}, f32[1024,2688]{1,0:T(8,128)}) custom-call(bf16[512,2048]{1,0:T(8,128)(2,1)S(1)} %add_dynamic-update-slice_fusion.6.x_ref, f32[1,2048]{1,0:T(1,128)S(1)} %bitcast.132, bf16[2176,2688]{1,0:T(8,128)(2,1)} %all-gather.4.cloned.1.call-done.w_ref, ...), custom_call_target="tpu_custom_call", output_to_operand_aliasing={{0}: (3, {}), {1}: (4, {})} | custom-call | flops 5637144576 | bytes 18612224 | tf_op jit(solution)/shard_map/norm_project/pallas_call | solution.py:333
  154.1 13.6 %mamba_forward.1 = (bf16[1024,768]{1,0:T(8,128)(2,1)S(1)}, f32[1024,128]{1,0:T(8,128)S(1)}, f32[1024,768]{1,0:T(8,128)}, bf16[8,256,768]{2,1,0:T(8,128)(2,1)}) custom-call(f32[1024,2688]{1,0:T(8,128)} %get-tuple-element.250.p_ref.halo_ref.refs_0_.refs_1_.refs_2_.refs_3_, f32[1024,2688]{1,0:T(8,128)} %get-tuple-element.250.p_ref.halo_ref.refs_0_.refs_1_.refs_2_.refs_3_, ...), custom_call_target="tpu_custom_call" | custom-call | flops 15728640000 | bytes 20447232 | tf_op jit(solution)/shard_map/mamba_forward/pallas_call | solution.py:1066
  174.6 6.0 attention_forward.1.att_ref
  189.0 7.4 branch.1
  198.9 6.4 collective-permute-start.20
  206.6 5.3 collective-permute-done.20
  212.5 4.4 collective-permute-start.28
  222.2 6.5 collective-permute-done.28
  230.1 4.2 collective-permute-done.24
  238.7 6.3 collective-permute-start.30
  248.9 8.9 %collective-permute-start.26 = (bf16[128,2048]{1,0:T(8,128)(2,1)}, bf16[128,2048]{1,0:T(8,128)(2,1)}, u32[]{:S(2)}, u32[]{:S(2)}) collective-permute-start(bf16[128,2048]{1,0:T(8,128)(2,1)} %get-tuple-element.188), channel_id=1, source_target_pairs={{0,1},{1,2},{2,3},{4,5},{5,6},{6,7},{8,9},{9,10},{10,11},{12,13},{... | collective-permute-start | bytes 1572872 | tf_op jit(solution)/shard_map/ppermute | solution.py:290
  261.3 10.8 %collective-permute-done.27 = bf16[128,2048]{1,0:T(8,128)(2,1)} collective-permute-done((bf16[128,2048]{1,0:T(8,128)(2,1)}, bf16[128,2048]{1,0:T(8,128)(2,1)}, u32[]{:S(2)}, u32[]{:S(2)}) %collective-permute-start.27) | collective-permute-done | bytes 524320 | tf_op jit(solution)/shard_map/ppermute | solution.py:291
  273.5 4.6 collective-permute-start.34
  284.0 4.9 collective-permute-done.35
  291.1 4.4 collective-permute-start.42
  303.8 8.5 %collective-permute-done.43 = bf16[128,2048]{1,0:T(8,128)(2,1)S(1)} collective-permute-done((bf16[128,2048]{1,0:T(8,128)(2,1)S(1)}, bf16[128,2048]{1,0:T(8,128)(2,1)S(1)}, u32[]{:S(2)}, u32[]{:S(2)}) %collective-permute-start.43) | collective-permute-done | bytes 524320 | tf_op jit(solution)/shard_map/ppermute | solution.py:169
  315.9 7.6 collective-permute-done.39
  327.1 7.6 collective-permute-done.45
  339.9 3.8 collective-permute-done.40
  345.4 3.9 collective-permute-done.46
  350.9 20.3 %feed_forward.1 = (bf16[1024,1024]{1,0:T(8,128)(2,1)S(1)}, bf16[1024,1024]{1,0:T(8,128)(2,1)S(1)}, bf16[1024,1024]{1,0:T(8,128)(2,1)}) custom-call(bf16[512,2048]{1,0:T(8,128)(2,1)} %pad_maximum_fusion.refs_0_, bf16[512,2048]{1,0:T(8,128)(2,1)} %pad_maximum_fusion.1.refs_1_, bf16[512,2048]{1,0:T(8,128)(2,1)} %get-tuple-element.246.refs_2_, ...), custom_call_target="tpu_custom_call" | custom-call | flops 12884901888 | bytes 20971520 | tf_op jit(solution)/shard_map/feed_forward/pallas_call | solution.py:444
  373.8 12.8 %transposed_product.2 = (bf16[512,2048]{1,0:T(8,128)(2,1)S(1)}, bf16[512,2048]{1,0:T(8,128)(2,1)S(1)}) custom-call(bf16[1024,1024]{1,0:T(8,128)(2,1)} %copy-done.23, bf16[1024,1024]{1,0:T(8,128)(2,1)} %get-tuple-element.210.refs_1_.refs_5_, bf16[2048,3072]{1,0:T(8,128)(2,1)} %all-gather.8.cloned.1.call-done.refs_4_.refs_5_.refs_6_.refs_2_.refs_3_.refs_1_, ...), custom_call_target="tpu_custom_call" | custom-call | flops 8589934592 | bytes 16777216 | tf_op jit(solution)/shard_map/transposed_product/pallas_call | solution.py:531
  390.4 11.9 %gradient.3 = (bf16[2048,3072]{1,0:T(8,128)(2,1)}, f32[8,128]{1,0:T(8,128)}) custom-call(bf16[512,2048]{1,0:T(8,128)(2,1)S(1)} %copy-done.1, bf16[512,2048]{1,0:T(8,128)(2,1)S(1)} %copy-done.2, bf16[512,2048]{1,0:T(8,128)(2,1)} %get-tuple-element.246.refs_2_, bf16[512,2048]{1,0:T(8,128)(2,1)} %get-tuple-element.247.refs_3_, bf16[1024,1024]{1,0:T(8,128)(2,1)} %copy-done.23, ...), custom_call_target="tpu_custom_call" | custom-call | flops 6442450944 | bytes 11534336 | tf_op jit(solution)/shard_map/gradient/pallas_call | solution.py:390
  402.4 12.2 %gradient.4 = (bf16[2048,3072]{1,0:T(8,128)(2,1)}, f32[8,128]{1,0:T(8,128)}) custom-call(bf16[512,2048]{1,0:T(8,128)(2,1)S(1)} %copy-done.1, bf16[512,2048]{1,0:T(8,128)(2,1)S(1)} %copy-done.2, bf16[512,2048]{1,0:T(8,128)(2,1)} %get-tuple-element.246.refs_2_, bf16[512,2048]{1,0:T(8,128)(2,1)} %get-tuple-element.247.refs_3_, ...), custom_call_target="tpu_custom_call", output_to_operand_aliasing={{0}: (7, {})} | custom-call | flops 6442450944 | bytes 11534336 | tf_op jit(solution)/shard_map/gradient/pallas_call | solution.py:390
  421.1 6.2 collective-permute-done.56
  429.7 5.8 collective-permute-done.50
  436.9 5.0 collective-permute-start.58
  444.6 5.3 collective-permute-start.52
  452.9 4.8 collective-permute-done.53
  460.7 5.8 collective-permute-start.60
  468.1 3.1 fusion.34
  471.3 4.2 collective-permute-start.54
  482.9 5.3 collective-permute-start.62
  494.5 7.4 transposed_product.3
  519.8 9.0 %collective-permute-done.65 = bf16[128,2048]{1,0:T(8,128)(2,1)} collective-permute-done((bf16[128,2048]{1,0:T(8,128)(2,1)}, bf16[128,2048]{1,0:T(8,128)(2,1)}, u32[]{:S(2)}, u32[]{:S(2)}) %collective-permute-start.65) | collective-permute-done | bytes 524320 | tf_op jit(solution)/shard_map/ppermute | solution.py:169
  538.3 3.3 collective-permute-done.67
  548.4 9.1 %branch_back.1 = (f32[1024,1024]{1,0:T(8,128)}, f32[1024,128]{1,0:T(8,128)S(1)}) custom-call(bf16[512,2048]{1,0:T(8,128)(2,1)S(1)} %copy-done.17, bf16[512,2048]{1,0:T(8,128)(2,1)} %add_dynamic-update-slice_fusion.refs_1_.refs_2_, bf16[2048,1024]{1,0:T(8,128)(2,1)} %all-gather.6.cloned.1.call-done.w_ref.refs_2_, bf16[1024,768]{1,0:T(8,128)(2,1)S(1)} %copy-done.26), custom_call_target="tpu_custom_call" | custom-call | flops 4294967296 | bytes 8388608 | tf_op jit(solution)/shard_map/branch_back/pallas_call | solution.py:482
  561.6 9.2 %attention_backward.1.dqkv_ref = bf16[1024,512]{1,0:T(8,128)(2,1)S(1)} custom-call(f32[1024,2688]{1,0:T(8,128)} %get-tuple-element.250.p_ref.halo_ref.refs_0_.refs_1_.refs_2_.refs_3_, f32[1024,2688]{1,0:T(8,128)} %get-tuple-element.250.p_ref.halo_ref.refs_0_.refs_1_.refs_2_.refs_3_, ...), custom_call_target="tpu_custom_call" | custom-call | flops 10485760000 | bytes 6291456 | tf_op jit(solution)/shard_map/attention_backward/pallas_call | solution.py:732
  575.4 31.6 %mamba_backward.1 = (bf16[1024,2688]{1,0:T(8,128)(2,1)}, f32[8,768]{1,0:T(8,128)S(1)}, f32[8,768]{1,0:T(8,128)S(1)}, f32[8,512]{1,0:T(8,128)S(1)}, f32[8,128]{1,0:T(8,128)S(1)}) custom-call(f32[1024,2688]{1,0:T(8,128)} %get-tuple-element.250.p_ref.halo_ref.refs_0_.refs_1_.refs_2_.refs_3_, ...), custom_call_target="tpu_custom_call" | custom-call | flops 36962304000 | bytes 20447232 | tf_op jit(solution)/shard_map/mamba_backward/pallas_call | solution.py:1121
  607.0 22.9 %gradient.5 = (bf16[2048,3712]{1,0:T(8,128)(2,1)}, f32[8,128]{1,0:T(8,128)}) custom-call(bf16[1024,2048]{1,0:T(8,128)(2,1)} %get-tuple-element.256.refs_0_, bf16[512,2048]{1,0:T(8,128)(2,1)S(1)} %copy-done.18, bf16[512,2048]{1,0:T(8,128)(2,1)S(1)} %copy-done.19, bf16[1024,2688]{1,0:T(8,128)(2,1)} %get-tuple-element.266.refs_3_.d_ref, ...), custom_call_target="tpu_custom_call" | custom-call | flops 15569256448 | bytes 27000832 | tf_op jit(solution)/shard_map/gradient/pallas_call | solution.py:390
  633.9 10.7 %back_product.2 = bf16[512,2048]{1,0:T(8,128)(2,1)S(1)} custom-call(bf16[1024,2688]{1,0:T(8,128)(2,1)} %get-tuple-element.266.refs_3_.d_ref, bf16[2176,2688]{1,0:T(8,128)(2,1)} %all-gather.4.cloned.1.call-done.w_ref), custom_call_target="tpu_custom_call" | custom-call | flops 5637144576 | bytes 16547840 | tf_op jit(solution)/shard_map/back_product/pallas_call | solution.py:595
  650.6 10.1 %back_product.3 = bf16[512,2048]{1,0:T(8,128)(2,1)S(1)} custom-call(bf16[1024,2688]{1,0:T(8,128)(2,1)} %get-tuple-element.266.refs_3_.d_ref, bf16[2176,2688]{1,0:T(8,128)(2,1)} %all-gather.4.cloned.1.call-done.w_ref), custom_call_target="tpu_custom_call" | custom-call | flops 5637144576 | bytes 16547840 | tf_op jit(solution)/shard_map/back_product/pallas_call | solution.py:595
  665.4 6.3 collective-permute-start.90
  672.4 4.0 reshape.255
  684.0 8.7 %collective-permute-done.81 = bf16[128,2048]{1,0:T(8,128)(2,1)S(1)} collective-permute-done((bf16[128,2048]{1,0:T(8,128)(2,1)}, bf16[128,2048]{1,0:T(8,128)(2,1)S(1)}, u32[]{:S(2)}, u32[]{:S(2)}) %collective-permute-start.81) | collective-permute-done | bytes 524320 | tf_op jit(solution)/shard_map/ppermute | solution.py:290
  694.2 7.6 collective-permute-done.77
  703.3 5.0 collective-permute-start.83
  709.7 3.8 collective-permute-start.79
  715.3 4.9 collective-permute-done.83
  723.1 5.4 collective-permute-done.79
  729.8 5.7 collective-permute-start.85
  737.2 5.3 collective-permute-done.86
  753.9 6.0 collective-permute-start.93
  (522 shorter events, 262.7 us)
Async XLA Ops:
  7.2 104.6 %all-gather.4.cloned.1.call-start = ((), (), s32[]{:S(2)}) async-start(), calls=%async_computation.3 | async-start | bytes 13160448 | tf_op jit(solution)/shard_map/all_gather | solution.py:1262
  26.6 158.8 %all-gather.6.cloned.1.call-start = ((), (), s32[]{:S(2)}) async-start(), calls=%async_computation.4 | async-start | bytes 4718592 | tf_op jit(solution)/shard_map/all_gather | solution.py:1262
  27.8 323.1 %all-gather.8.cloned.1.call-start = ((), (), s32[]{:S(2)}) async-start(), calls=%async_computation.5 | async-start | bytes 14155776 | tf_op jit(solution)/shard_map/all_gather | solution.py:1262
  30.7 530.9 %reduce-scatter.6.cloned.1.call-start = ((), (), s32[]{:S(2)}) async-start(), calls=%async_computation.7 | async-start | bytes 14155776 | tf_op jit(solution)/shard_map/reduce_scatter | solution.py:1257
  32.0 17.2 %collective-permute-start = (bf16[128,2048]{1,0:T(8,128)(2,1)S(1)}, bf16[128,2048]{1,0:T(8,128)(2,1)}, u32[]{:S(2)}, u32[]{:S(2)}) collective-permute-start(bf16[128,2048]{1,0:T(8,128)(2,1)S(1)} %get-tuple-element.406.in_ref), channel_id=1, source_target_pairs={{0,1},{1,2},{2,3},{4,5},{5,6},{6,7},{8,9},{9,10},{10,11},{12,13},{... | collective-permute-start | bytes 1572872 | tf_op jit(solution)/shard_map/ppermute | solution.py:168
  38.7 15.6 %collective-permute-start.1 = (bf16[128,2048]{1,0:T(8,128)(2,1)S(1)}, bf16[128,2048]{1,0:T(8,128)(2,1)}, u32[]{:S(2)}, u32[]{:S(2)}) collective-permute-start(bf16[128,2048]{1,0:T(8,128)(2,1)S(1)} %get-tuple-element.406.in_ref), channel_id=1, source_target_pairs={{1,0},{2,1},{3,2},{5,4},{6,5},{7,6},{9,8},{10,9},{11,10},{13,12},{... | collective-permute-start | bytes 1572872 | tf_op jit(solution)/shard_map/ppermute | solution.py:169
  55.6 17.1 %collective-permute-start.5 = (bf16[128,2048]{1,0:T(8,128)(2,1)}, bf16[128,2048]{1,0:T(8,128)(2,1)}, u32[]{:S(2)}, u32[]{:S(2)}) collective-permute-start(bf16[128,2048]{1,0:T(8,128)(2,1)} %collective-permute-done.1), channel_id=1, source_target_pairs={{1,0},{2,1},{5,4},{6,5},{9,8},{10,9},{13,12},{14,13},{17,16},{18,1... | collective-permute-start | bytes 1572872 | tf_op jit(solution)/shard_map/ppermute | solution.py:169
  56.9 18.6 %collective-permute-start.2 = (bf16[128,2048]{1,0:T(8,128)(2,1)S(1)}, bf16[128,2048]{1,0:T(8,128)(2,1)}, u32[]{:S(2)}, u32[]{:S(2)}) collective-permute-start(bf16[128,2048]{1,0:T(8,128)(2,1)S(1)} %copy-done.57), channel_id=1, source_target_pairs={{0,1},{1,2},{2,3},{4,5},{5,6},{6,7},{8,9},{9,10},{10,11},{12,13},{... | collective-permute-start | bytes 1572872 | tf_op jit(solution)/shard_map/ppermute | solution.py:168
  62.3 21.6 %collective-permute-start.3 = (bf16[128,2048]{1,0:T(8,128)(2,1)S(1)}, bf16[128,2048]{1,0:T(8,128)(2,1)}, u32[]{:S(2)}, u32[]{:S(2)}) collective-permute-start(bf16[128,2048]{1,0:T(8,128)(2,1)S(1)} %copy-done.57), channel_id=1, source_target_pairs={{1,0},{2,1},{3,2},{5,4},{6,5},{7,6},{9,8},{10,9},{11,10},{13,12},{... | collective-permute-start | bytes 1572872 | tf_op jit(solution)/shard_map/ppermute | solution.py:169
  72.7 22.5 %collective-permute-start.9 = (bf16[128,2048]{1,0:T(8,128)(2,1)}, bf16[128,2048]{1,0:T(8,128)(2,1)}, u32[]{:S(2)}, u32[]{:S(2)}) collective-permute-start(bf16[128,2048]{1,0:T(8,128)(2,1)} %collective-permute-done.5), channel_id=1, source_target_pairs={{1,0},{5,4},{9,8},{13,12},{17,16},{21,20},{25,24},{29,28}} | collective-permute-start | bytes 1572872 | tf_op jit(solution)/shard_map/ppermute | solution.py:169
  74.0 21.2 %collective-permute-start.8 = (bf16[128,2048]{1,0:T(8,128)(2,1)}, bf16[128,2048]{1,0:T(8,128)(2,1)}, u32[]{:S(2)}, u32[]{:S(2)}) collective-permute-start(bf16[128,2048]{1,0:T(8,128)(2,1)} %collective-permute-done.4), channel_id=1, source_target_pairs={{2,3},{6,7},{10,11},{14,15},{18,19},{22,23},{26,27},{30,31}} | collective-permute-start | bytes 1572872 | tf_op jit(solution)/shard_map/ppermute | solution.py:168
  85.4 18.8 %collective-permute-start.7 = (bf16[128,2048]{1,0:T(8,128)(2,1)}, bf16[128,2048]{1,0:T(8,128)(2,1)}, u32[]{:S(2)}, u32[]{:S(2)}) collective-permute-start(bf16[128,2048]{1,0:T(8,128)(2,1)} %collective-permute-done.3), channel_id=1, source_target_pairs={{1,0},{2,1},{5,4},{6,5},{9,8},{10,9},{13,12},{14,13},{17,16},{18,1... | collective-permute-start | bytes 1572872 | tf_op jit(solution)/shard_map/ppermute | solution.py:169
  104.2 31.6 %collective-permute-start.10 = (bf16[128,2048]{1,0:T(8,128)(2,1)}, bf16[128,2048]{1,0:T(8,128)(2,1)S(1)}, u32[]{:S(2)}, u32[]{:S(2)}) collective-permute-start(bf16[128,2048]{1,0:T(8,128)(2,1)} %collective-permute-done.6), channel_id=1, source_target_pairs={{2,3},{6,7},{10,11},{14,15},{18,19},{22,23},{26,27},{30,31}} | collective-permute-start | bytes 1572872 | tf_op jit(solution)/shard_map/ppermute | solution.py:168
  104.9 30.9 %collective-permute-start.11 = (bf16[128,2048]{1,0:T(8,128)(2,1)}, bf16[128,2048]{1,0:T(8,128)(2,1)}, u32[]{:S(2)}, u32[]{:S(2)}) collective-permute-start(bf16[128,2048]{1,0:T(8,128)(2,1)} %collective-permute-done.7), channel_id=1, source_target_pairs={{1,0},{5,4},{9,8},{13,12},{17,16},{21,20},{25,24},{29,28}} | collective-permute-start | bytes 1572872 | tf_op jit(solution)/shard_map/ppermute | solution.py:169
  128.4 46.2 %collective-permute-start.15 = (bf16[256,2048]{1,0:T(8,128)(2,1)}, bf16[256,2048]{1,0:T(8,128)(2,1)}, u32[]{:S(2)}, u32[]{:S(2)}) collective-permute-start(bf16[256,2048]{1,0:T(8,128)(2,1)} %bitcast.39), channel_id=1, source_target_pairs={{0,1},{1,2},{2,3},{4,5},{5,6},{6,7},{8,9},{9,10},{10,11},{12,13},{... | collective-permute-start | bytes 3145736 | tf_op jit(solution)/shard_map/ppermute | solution.py:168
  134.6 40.0 %collective-permute-start.16 = (bf16[256,2048]{1,0:T(8,128)(2,1)}, bf16[256,2048]{1,0:T(8,128)(2,1)}, u32[]{:S(2)}, u32[]{:S(2)}) collective-permute-start(bf16[256,2048]{1,0:T(8,128)(2,1)} %bitcast.39), channel_id=1, source_target_pairs={{1,0},{2,1},{3,2},{5,4},{6,5},{7,6},{9,8},{10,9},{11,10},{13,12},{... | collective-permute-start | bytes 3145736 | tf_op jit(solution)/shard_map/ppermute | solution.py:169
  182.5 36.1 %collective-permute-start.22 = (bf16[256,2048]{1,0:T(8,128)(2,1)}, bf16[256,2048]{1,0:T(8,128)(2,1)}, u32[]{:S(2)}, u32[]{:S(2)}) collective-permute-start(bf16[256,2048]{1,0:T(8,128)(2,1)} %collective-permute-done.15), channel_id=1, source_target_pairs={{1,2},{2,3},{5,6},{6,7},{9,10},{10,11},{13,14},{14,15},{17,18},{18... | collective-permute-start | bytes 3145736 | tf_op jit(solution)/shard_map/ppermute | solution.py:168
  184.1 34.5 %collective-permute-start.23 = (bf16[256,2048]{1,0:T(8,128)(2,1)}, bf16[256,2048]{1,0:T(8,128)(2,1)}, u32[]{:S(2)}, u32[]{:S(2)}) collective-permute-start(bf16[256,2048]{1,0:T(8,128)(2,1)} %collective-permute-done.16), channel_id=1, source_target_pairs={{1,0},{2,1},{5,4},{6,5},{9,8},{10,9},{13,12},{14,13},{17,16},{18,1... | collective-permute-start | bytes 3145736 | tf_op jit(solution)/shard_map/ppermute | solution.py:169
  212.5 16.1 %collective-permute-start.28 = (bf16[128,2048]{1,0:T(8,128)(2,1)S(1)}, bf16[128,2048]{1,0:T(8,128)(2,1)S(1)}, u32[]{:S(2)}, u32[]{:S(2)}) collective-permute-start(bf16[128,2048]{1,0:T(8,128)(2,1)S(1)} %get-tuple-element.190), channel_id=1, source_target_pairs={{0,1},{4,5},{8,9},{12,13},{16,17},{20,21},{24,25},{28,29}} | collective-permute-start | bytes 1572872 | tf_op jit(solution)/shard_map/ppermute | solution.py:290
  220.1 14.2 %collective-permute-start.24 = (bf16[128,2048]{1,0:T(8,128)(2,1)S(1)}, bf16[128,2048]{1,0:T(8,128)(2,1)}, u32[]{:S(2)}, u32[]{:S(2)}) collective-permute-start(bf16[128,2048]{1,0:T(8,128)(2,1)S(1)} %get-tuple-element.186), channel_id=1, source_target_pairs={{0,1},{1,2},{4,5},{5,6},{8,9},{9,10},{12,13},{13,14},{16,17},{17,1... | collective-permute-start | bytes 1572872 | tf_op jit(solution)/shard_map/ppermute | solution.py:290
  234.3 14.6 %collective-permute-start.31 = (bf16[128,2048]{1,0:T(8,128)(2,1)}, bf16[128,2048]{1,0:T(8,128)(2,1)}, u32[]{:S(2)}, u32[]{:S(2)}) collective-permute-start(bf16[128,2048]{1,0:T(8,128)(2,1)} %get-tuple-element.193), channel_id=1, source_target_pairs={{2,1},{3,2},{6,5},{7,6},{10,9},{11,10},{14,13},{15,14},{18,17},{19... | collective-permute-start | bytes 1572872 | tf_op jit(solution)/shard_map/ppermute | solution.py:291
  235.8 36.4 %collective-permute-start.32 = (bf16[256,2048]{1,0:T(8,128)(2,1)}, bf16[256,2048]{1,0:T(8,128)(2,1)}, u32[]{:S(2)}, u32[]{:S(2)}) collective-permute-start(bf16[256,2048]{1,0:T(8,128)(2,1)} %collective-permute-done.22), channel_id=1, source_target_pairs={{2,3},{6,7},{10,11},{14,15},{18,19},{22,23},{26,27},{30,31}} | collective-permute-start | bytes 3145736 | tf_op jit(solution)/shard_map/ppermute | solution.py:168
  237.4 34.8 %collective-permute-start.33 = (bf16[256,2048]{1,0:T(8,128)(2,1)}, bf16[256,2048]{1,0:T(8,128)(2,1)}, u32[]{:S(2)}, u32[]{:S(2)}) collective-permute-start(bf16[256,2048]{1,0:T(8,128)(2,1)} %collective-permute-done.23), channel_id=1, source_target_pairs={{1,0},{5,4},{9,8},{13,12},{17,16},{21,20},{25,24},{29,28}} | collective-permute-start | bytes 3145736 | tf_op jit(solution)/shard_map/ppermute | solution.py:169
  238.7 20.8 %collective-permute-start.30 = (bf16[128,2048]{1,0:T(8,128)(2,1)}, bf16[128,2048]{1,0:T(8,128)(2,1)}, u32[]{:S(2)}, u32[]{:S(2)}) collective-permute-start(bf16[128,2048]{1,0:T(8,128)(2,1)} %get-tuple-element.192), channel_id=1, source_target_pairs={{0,1},{1,2},{4,5},{5,6},{8,9},{9,10},{12,13},{13,14},{16,17},{17,1... | collective-permute-start | bytes 1572872 | tf_op jit(solution)/shard_map/ppermute | solution.py:290
  247.6 24.5 %collective-permute-start.27 = (bf16[128,2048]{1,0:T(8,128)(2,1)}, bf16[128,2048]{1,0:T(8,128)(2,1)}, u32[]{:S(2)}, u32[]{:S(2)}) collective-permute-start(bf16[128,2048]{1,0:T(8,128)(2,1)} %get-tuple-element.189), channel_id=1, source_target_pairs={{1,0},{2,1},{3,2},{5,4},{6,5},{7,6},{9,8},{10,9},{11,10},{13,12},{... | collective-permute-start | bytes 1572872 | tf_op jit(solution)/shard_map/ppermute | solution.py:291
  248.9 23.2 %collective-permute-start.26 = (bf16[128,2048]{1,0:T(8,128)(2,1)}, bf16[128,2048]{1,0:T(8,128)(2,1)}, u32[]{:S(2)}, u32[]{:S(2)}) collective-permute-start(bf16[128,2048]{1,0:T(8,128)(2,1)} %get-tuple-element.188), channel_id=1, source_target_pairs={{0,1},{1,2},{2,3},{4,5},{5,6},{6,7},{8,9},{9,10},{10,11},{12,13},{... | collective-permute-start | bytes 1572872 | tf_op jit(solution)/shard_map/ppermute | solution.py:290
  272.2 16.7 %collective-permute-start.35 = (bf16[128,2048]{1,0:T(8,128)(2,1)S(1)}, bf16[128,2048]{1,0:T(8,128)(2,1)S(1)}, u32[]{:S(2)}, u32[]{:S(2)}) collective-permute-start(bf16[128,2048]{1,0:T(8,128)(2,1)S(1)} %get-tuple-element.197), channel_id=1, source_target_pairs={{1,0},{2,1},{3,2},{5,4},{6,5},{7,6},{9,8},{10,9},{11,10},{13,12},{... | collective-permute-start | bytes 1572872 | tf_op jit(solution)/shard_map/ppermute | solution.py:291
  273.5 16.9 %collective-permute-start.34 = (bf16[128,2048]{1,0:T(8,128)(2,1)S(1)}, bf16[128,2048]{1,0:T(8,128)(2,1)S(1)}, u32[]{:S(2)}, u32[]{:S(2)}) collective-permute-start(bf16[128,2048]{1,0:T(8,128)(2,1)S(1)} %get-tuple-element.196), channel_id=1, source_target_pairs={{0,1},{1,2},{2,3},{4,5},{5,6},{6,7},{8,9},{9,10},{10,11},{12,13},{... | collective-permute-start | bytes 1572872 | tf_op jit(solution)/shard_map/ppermute | solution.py:290
  279.8 18.2 %collective-permute-start.36 = (bf16[128,2048]{1,0:T(8,128)(2,1)S(1)}, bf16[128,2048]{1,0:T(8,128)(2,1)S(1)}, u32[]{:S(2)}, u32[]{:S(2)}) collective-permute-start(bf16[128,2048]{1,0:T(8,128)(2,1)S(1)} %multiply_convert_fusion.2), channel_id=1, source_target_pairs={{0,1},{1,2},{2,3},{4,5},{5,6},{6,7},{8,9},{9,10},{10,11},{12,13},{... | collective-permute-start | bytes 1572872 | tf_op jit(solution)/shard_map/ppermute | solution.py:168
  282.7 17.5 %collective-permute-start.37 = (bf16[128,2048]{1,0:T(8,128)(2,1)S(1)}, bf16[128,2048]{1,0:T(8,128)(2,1)S(1)}, u32[]{:S(2)}, u32[]{:S(2)}) collective-permute-start(bf16[128,2048]{1,0:T(8,128)(2,1)S(1)} %multiply_convert_fusion.2), channel_id=1, source_target_pairs={{1,0},{2,1},{3,2},{5,4},{6,5},{7,6},{9,8},{10,9},{11,10},{13,12},{... | collective-permute-start | bytes 1572872 | tf_op jit(solution)/shard_map/ppermute | solution.py:169
  295.5 16.8 %collective-permute-start.43 = (bf16[128,2048]{1,0:T(8,128)(2,1)S(1)}, bf16[128,2048]{1,0:T(8,128)(2,1)S(1)}, u32[]{:S(2)}, u32[]{:S(2)}) collective-permute-start(bf16[128,2048]{1,0:T(8,128)(2,1)S(1)} %multiply_convert_fusion.1), channel_id=1, source_target_pairs={{1,0},{2,1},{3,2},{5,4},{6,5},{7,6},{9,8},{10,9},{11,10},{13,12},{... | collective-permute-start | bytes 1572872 | tf_op jit(solution)/shard_map/ppermute | solution.py:169
  300.1 15.7 %collective-permute-start.38 = (bf16[128,2048]{1,0:T(8,128)(2,1)S(1)}, bf16[128,2048]{1,0:T(8,128)(2,1)S(1)}, u32[]{:S(2)}, u32[]{:S(2)}) collective-permute-start(bf16[128,2048]{1,0:T(8,128)(2,1)S(1)} %collective-permute-done.36), channel_id=1, source_target_pairs={{1,2},{2,3},{5,6},{6,7},{9,10},{10,11},{13,14},{14,15},{17,18},{18... | collective-permute-start | bytes 1572872 | tf_op jit(solution)/shard_map/ppermute | solution.py:168
  300.8 22.7 %collective-permute-start.39 = (bf16[128,2048]{1,0:T(8,128)(2,1)S(1)}, bf16[128,2048]{1,0:T(8,128)(2,1)S(1)}, u32[]{:S(2)}, u32[]{:S(2)}) collective-permute-start(bf16[128,2048]{1,0:T(8,128)(2,1)S(1)} %collective-permute-done.37), channel_id=1, source_target_pairs={{1,0},{2,1},{5,4},{6,5},{9,8},{10,9},{13,12},{14,13},{17,16},{18,1... | collective-permute-start | bytes 1572872 | tf_op jit(solution)/shard_map/ppermute | solution.py:169
  312.2 14.9 %collective-permute-start.44 = (bf16[128,2048]{1,0:T(8,128)(2,1)S(1)}, bf16[128,2048]{1,0:T(8,128)(2,1)S(1)}, u32[]{:S(2)}, u32[]{:S(2)}) collective-permute-start(bf16[128,2048]{1,0:T(8,128)(2,1)S(1)} %collective-permute-done.42), channel_id=1, source_target_pairs={{1,2},{2,3},{5,6},{6,7},{9,10},{10,11},{13,14},{14,15},{17,18},{18... | collective-permute-start | bytes 1572872 | tf_op jit(solution)/shard_map/ppermute | solution.py:168
  312.9 21.8 %collective-permute-start.45 = (bf16[128,2048]{1,0:T(8,128)(2,1)S(1)}, bf16[128,2048]{1,0:T(8,128)(2,1)S(1)}, u32[]{:S(2)}, u32[]{:S(2)}) collective-permute-start(bf16[128,2048]{1,0:T(8,128)(2,1)S(1)} %collective-permute-done.43), channel_id=1, source_target_pairs={{1,0},{2,1},{5,4},{6,5},{9,8},{10,9},{13,12},{14,13},{17,16},{18,1... | collective-permute-start | bytes 1572872 | tf_op jit(solution)/shard_map/ppermute | solution.py:169
  323.5 16.3 %collective-permute-start.41 = (bf16[128,2048]{1,0:T(8,128)(2,1)S(1)}, bf16[128,2048]{1,0:T(8,128)(2,1)S(1)}, u32[]{:S(2)}, u32[]{:S(2)}) collective-permute-start(bf16[128,2048]{1,0:T(8,128)(2,1)S(1)} %collective-permute-done.38), channel_id=1, source_target_pairs={{2,3},{6,7},{10,11},{14,15},{18,19},{22,23},{26,27},{30,31}} | collective-permute-start | bytes 1572872 | tf_op jit(solution)/shard_map/ppermute | solution.py:168
  324.2 19.5 %collective-permute-start.40 = (bf16[128,2048]{1,0:T(8,128)(2,1)S(1)}, bf16[128,2048]{1,0:T(8,128)(2,1)S(1)}, u32[]{:S(2)}, u32[]{:S(2)}) collective-permute-start(bf16[128,2048]{1,0:T(8,128)(2,1)S(1)} %collective-permute-done.39), channel_id=1, source_target_pairs={{1,0},{5,4},{9,8},{13,12},{17,16},{21,20},{25,24},{29,28}} | collective-permute-start | bytes 1572872 | tf_op jit(solution)/shard_map/ppermute | solution.py:169
  388.1 14.2 %collective-permute-start.49 = (bf16[128,2048]{1,0:T(8,128)(2,1)S(1)}, bf16[128,2048]{1,0:T(8,128)(2,1)S(1)}, u32[]{:S(2)}, u32[]{:S(2)}) collective-permute-start(bf16[128,2048]{1,0:T(8,128)(2,1)S(1)} %get-tuple-element.384), channel_id=1, source_target_pairs={{3,2},{7,6},{11,10},{15,14},{19,18},{23,22},{27,26},{31,30}} | collective-permute-start | bytes 1572872 | tf_op jit(solution)/shard_map/ppermute | solution.py:257
  414.6 215.3 %reduce-scatter.4.cloned.1.call-start = ((), (), s32[]{:S(2)}) async-start(), calls=%async_computation.6 | async-start | bytes 5242880 | tf_op jit(solution)/shard_map/reduce_scatter | solution.py:189
  419.1 16.4 %collective-permute-start.50 = (bf16[128,2048]{1,0:T(8,128)(2,1)S(1)}, bf16[128,2048]{1,0:T(8,128)(2,1)S(1)}, u32[]{:S(2)}, u32[]{:S(2)}) collective-permute-start(bf16[128,2048]{1,0:T(8,128)(2,1)S(1)} %get-tuple-element.218), channel_id=1, source_target_pairs={{0,1},{1,2},{4,5},{5,6},{8,9},{9,10},{12,13},{13,14},{16,17},{17,1... | collective-permute-start | bytes 1572872 | tf_op jit(solution)/shard_map/ppermute | solution.py:290
  435.5 14.5 %collective-permute-start.59 = (bf16[128,2048]{1,0:T(8,128)(2,1)}, bf16[128,2048]{1,0:T(8,128)(2,1)}, u32[]{:S(2)}, u32[]{:S(2)}) collective-permute-start(bf16[128,2048]{1,0:T(8,128)(2,1)} %get-tuple-element.228), channel_id=1, source_target_pairs={{2,1},{3,2},{6,5},{7,6},{10,9},{11,10},{14,13},{15,14},{18,17},{19... | collective-permute-start | bytes 1572872 | tf_op jit(solution)/shard_map/ppermute | solution.py:291
  443.3 14.4 %collective-permute-start.53 = (bf16[128,2048]{1,0:T(8,128)(2,1)}, bf16[128,2048]{1,0:T(8,128)(2,1)}, u32[]{:S(2)}, u32[]{:S(2)}) collective-permute-start(bf16[128,2048]{1,0:T(8,128)(2,1)} %get-tuple-element.221), channel_id=1, source_target_pairs={{1,0},{2,1},{3,2},{5,4},{6,5},{7,6},{9,8},{10,9},{11,10},{13,12},{... | collective-permute-start | bytes 1572872 | tf_op jit(solution)/shard_map/ppermute | solution.py:291
  444.6 14.8 %collective-permute-start.52 = (bf16[128,2048]{1,0:T(8,128)(2,1)}, bf16[128,2048]{1,0:T(8,128)(2,1)}, u32[]{:S(2)}, u32[]{:S(2)}) collective-permute-start(bf16[128,2048]{1,0:T(8,128)(2,1)} %get-tuple-element.220), channel_id=1, source_target_pairs={{0,1},{1,2},{2,3},{4,5},{5,6},{6,7},{8,9},{9,10},{10,11},{12,13},{... | collective-permute-start | bytes 1572872 | tf_op jit(solution)/shard_map/ppermute | solution.py:290
  459.4 19.2 %collective-permute-start.61 = (bf16[128,2048]{1,0:T(8,128)(2,1)}, bf16[128,2048]{1,0:T(8,128)(2,1)}, u32[]{:S(2)}, u32[]{:S(2)}) collective-permute-start(bf16[128,2048]{1,0:T(8,128)(2,1)} %get-tuple-element.230), channel_id=1, source_target_pairs={{1,0},{2,1},{3,2},{5,4},{6,5},{7,6},{9,8},{10,9},{11,10},{13,12},{... | collective-permute-start | bytes 1572872 | tf_op jit(solution)/shard_map/ppermute | solution.py:291
  460.7 17.9 %collective-permute-start.60 = (bf16[128,2048]{1,0:T(8,128)(2,1)}, bf16[128,2048]{1,0:T(8,128)(2,1)}, u32[]{:S(2)}, u32[]{:S(2)}) collective-permute-start(bf16[128,2048]{1,0:T(8,128)(2,1)} %get-tuple-element.229), channel_id=1, source_target_pairs={{0,1},{1,2},{2,3},{4,5},{5,6},{6,7},{8,9},{9,10},{10,11},{12,13},{... | collective-permute-start | bytes 1572872 | tf_op jit(solution)/shard_map/ppermute | solution.py:290
  471.3 18.2 %collective-permute-start.54 = (bf16[128,2048]{1,0:T(8,128)(2,1)}, bf16[128,2048]{1,0:T(8,128)(2,1)}, u32[]{:S(2)}, u32[]{:S(2)}) collective-permute-start(bf16[128,2048]{1,0:T(8,128)(2,1)} %get-tuple-element.356.in_ref), channel_id=1, source_target_pairs={{0,1},{1,2},{2,3},{4,5},{5,6},{6,7},{8,9},{9,10},{10,11},{12,13},{... | collective-permute-start | bytes 1572872 | tf_op jit(solution)/shard_map/ppermute | solution.py:168
  475.4 17.1 %collective-permute-start.55 = (bf16[128,2048]{1,0:T(8,128)(2,1)}, bf16[128,2048]{1,0:T(8,128)(2,1)}, u32[]{:S(2)}, u32[]{:S(2)}) collective-permute-start(bf16[128,2048]{1,0:T(8,128)(2,1)} %get-tuple-element.356.in_ref), channel_id=1, source_target_pairs={{1,0},{2,1},{3,2},{5,4},{6,5},{7,6},{9,8},{10,9},{11,10},{13,12},{... | collective-permute-start | bytes 1572872 | tf_op jit(solution)/shard_map/ppermute | solution.py:169
  482.9 24.0 %collective-permute-start.62 = (bf16[128,2048]{1,0:T(8,128)(2,1)S(1)}, bf16[128,2048]{1,0:T(8,128)(2,1)}, u32[]{:S(2)}, u32[]{:S(2)}) collective-permute-start(bf16[128,2048]{1,0:T(8,128)(2,1)S(1)} %get-tuple-element.354.in_ref), channel_id=1, source_target_pairs={{0,1},{1,2},{2,3},{4,5},{5,6},{6,7},{8,9},{9,10},{10,11},{12,13},{... | collective-permute-start | bytes 1572872 | tf_op jit(solution)/shard_map/ppermute | solution.py:168
  488.2 18.7 %collective-permute-start.63 = (bf16[128,2048]{1,0:T(8,128)(2,1)S(1)}, bf16[128,2048]{1,0:T(8,128)(2,1)}, u32[]{:S(2)}, u32[]{:S(2)}) collective-permute-start(bf16[128,2048]{1,0:T(8,128)(2,1)S(1)} %get-tuple-element.354.in_ref), channel_id=1, source_target_pairs={{1,0},{2,1},{3,2},{5,4},{6,5},{7,6},{9,8},{10,9},{11,10},{13,12},{... | collective-permute-start | bytes 1572872 | tf_op jit(solution)/shard_map/ppermute | solution.py:169
  492.5 17.1 %collective-permute-start.68 = (bf16[128,2048]{1,0:T(8,128)(2,1)}, bf16[128,2048]{1,0:T(8,128)(2,1)S(1)}, u32[]{:S(2)}, u32[]{:S(2)}) collective-permute-start(bf16[128,2048]{1,0:T(8,128)(2,1)} %collective-permute-done.54), channel_id=1, source_target_pairs={{1,2},{2,3},{5,6},{6,7},{9,10},{10,11},{13,14},{14,15},{17,18},{18... | collective-permute-start | bytes 1572872 | tf_op jit(solution)/shard_map/ppermute | solution.py:168
  493.2 18.0 %collective-permute-start.69 = (bf16[128,2048]{1,0:T(8,128)(2,1)}, bf16[128,2048]{1,0:T(8,128)(2,1)}, u32[]{:S(2)}, u32[]{:S(2)}) collective-permute-start(bf16[128,2048]{1,0:T(8,128)(2,1)} %collective-permute-done.55), channel_id=1, source_target_pairs={{1,0},{2,1},{5,4},{6,5},{9,8},{10,9},{13,12},{14,13},{17,16},{18,1... | collective-permute-start | bytes 1572872 | tf_op jit(solution)/shard_map/ppermute | solution.py:169
  508.3 20.5 %collective-permute-start.65 = (bf16[128,2048]{1,0:T(8,128)(2,1)}, bf16[128,2048]{1,0:T(8,128)(2,1)}, u32[]{:S(2)}, u32[]{:S(2)}) collective-permute-start(bf16[128,2048]{1,0:T(8,128)(2,1)} %collective-permute-done.63), channel_id=1, source_target_pairs={{1,0},{2,1},{5,4},{6,5},{9,8},{10,9},{13,12},{14,13},{17,16},{18,1... | collective-permute-start | bytes 1572872 | tf_op jit(solution)/shard_map/ppermute | solution.py:169
  511.2 23.3 %collective-permute-start.70 = (bf16[128,2048]{1,0:T(8,128)(2,1)}, bf16[128,2048]{1,0:T(8,128)(2,1)}, u32[]{:S(2)}, u32[]{:S(2)}) collective-permute-start(bf16[128,2048]{1,0:T(8,128)(2,1)} %collective-permute-done.69), channel_id=1, source_target_pairs={{1,0},{5,4},{9,8},{13,12},{17,16},{21,20},{25,24},{29,28}} | collective-permute-start | bytes 1572872 | tf_op jit(solution)/shard_map/ppermute | solution.py:169
  519.1 18.0 %collective-permute-start.71 = (bf16[128,2048]{1,0:T(8,128)(2,1)}, bf16[128,2048]{1,0:T(8,128)(2,1)S(1)}, u32[]{:S(2)}, u32[]{:S(2)}) collective-permute-start(bf16[128,2048]{1,0:T(8,128)(2,1)} %copy-done.67), channel_id=1, source_target_pairs={{2,3},{6,7},{10,11},{14,15},{18,19},{22,23},{26,27},{30,31}} | collective-permute-start | bytes 1572872 | tf_op jit(solution)/shard_map/ppermute | solution.py:168
  541.7 207.1 %reduce-scatter.8.cloned.1.call-start = ((), (), s32[]{:S(2)}) async-start(), calls=%async_computation.8 | async-start | bytes 17104896 | tf_op jit(solution)/shard_map/reduce_scatter | solution.py:1257
  557.7 14.1 %collective-permute-start.72 = (f32[8,128]{1,0:T(8,128)S(1)}, f32[8,128]{1,0:T(8,128)S(1)}, u32[]{:S(2)}, u32[]{:S(2)}) collective-permute-start(f32[8,128]{1,0:T(8,128)S(1)} %bitcast.171), channel_id=1, source_target_pairs={{0,1},{1,2},{2,3},{3,0},{4,5},{5,6},{6,7},{7,4},{8,9},{9,10},{10,1... | collective-permute-start | bytes 12296 | tf_op jit(solution)/shard_map/ppermute | solution.py:116
  645.6 32.2 %collective-permute-start.75 = (bf16[128,2048]{1,0:T(8,128)(2,1)}, bf16[128,2048]{1,0:T(8,128)(2,1)}, u32[]{:S(2)}, u32[]{:S(2)}) collective-permute-start(bf16[128,2048]{1,0:T(8,128)(2,1)} %get-tuple-element.260), channel_id=1, source_target_pairs={{0,1},{4,5},{8,9},{12,13},{16,17},{20,21},{24,25},{28,29}} | collective-permute-start | bytes 1572872 | tf_op jit(solution)/shard_map/ppermute | solution.py:290
  648.6 29.2 %collective-permute-start.76 = (bf16[128,2048]{1,0:T(8,128)(2,1)}, bf16[128,2048]{1,0:T(8,128)(2,1)}, u32[]{:S(2)}, u32[]{:S(2)}) collective-permute-start(bf16[128,2048]{1,0:T(8,128)(2,1)} %get-tuple-element.261), channel_id=1, source_target_pairs={{3,2},{7,6},{11,10},{15,14},{19,18},{23,22},{27,26},{31,30}} | collective-permute-start | bytes 1572872 | tf_op jit(solution)/shard_map/ppermute | solution.py:291
  678.7 14.1 %collective-permute-start.81 = (bf16[128,2048]{1,0:T(8,128)(2,1)}, bf16[128,2048]{1,0:T(8,128)(2,1)S(1)}, u32[]{:S(2)}, u32[]{:S(2)}) collective-permute-start(bf16[128,2048]{1,0:T(8,128)(2,1)} %get-tuple-element.267), channel_id=1, source_target_pairs={{0,1},{4,5},{8,9},{12,13},{16,17},{20,21},{24,25},{28,29}} | collective-permute-start | bytes 1572872 | tf_op jit(solution)/shard_map/ppermute | solution.py:290
  682.0 19.8 %collective-permute-start.77 = (bf16[128,2048]{1,0:T(8,128)(2,1)S(1)}, bf16[128,2048]{1,0:T(8,128)(2,1)S(1)}, u32[]{:S(2)}, u32[]{:S(2)}) collective-permute-start(bf16[128,2048]{1,0:T(8,128)(2,1)S(1)} %get-tuple-element.262), channel_id=1, source_target_pairs={{0,1},{1,2},{4,5},{5,6},{8,9},{9,10},{12,13},{13,14},{16,17},{17,1... | collective-permute-start | bytes 1572872 | tf_op jit(solution)/shard_map/ppermute | solution.py:290
  683.3 18.5 %collective-permute-start.78 = (bf16[128,2048]{1,0:T(8,128)(2,1)S(1)}, bf16[128,2048]{1,0:T(8,128)(2,1)S(1)}, u32[]{:S(2)}, u32[]{:S(2)}) collective-permute-start(bf16[128,2048]{1,0:T(8,128)(2,1)S(1)} %get-tuple-element.263), channel_id=1, source_target_pairs={{2,1},{3,2},{6,5},{7,6},{10,9},{11,10},{14,13},{15,14},{18,17},{19... | collective-permute-start | bytes 1572872 | tf_op jit(solution)/shard_map/ppermute | solution.py:291
  703.3 16.9 %collective-permute-start.83 = (bf16[128,2048]{1,0:T(8,128)(2,1)}, bf16[128,2048]{1,0:T(8,128)(2,1)}, u32[]{:S(2)}, u32[]{:S(2)}) collective-permute-start(bf16[128,2048]{1,0:T(8,128)(2,1)} %get-tuple-element.269), channel_id=1, source_target_pairs={{0,1},{1,2},{4,5},{5,6},{8,9},{9,10},{12,13},{13,14},{16,17},{17,1... | collective-permute-start | bytes 1572872 | tf_op jit(solution)/shard_map/ppermute | solution.py:290
  709.7 18.8 %collective-permute-start.79 = (bf16[128,2048]{1,0:T(8,128)(2,1)}, bf16[128,2048]{1,0:T(8,128)(2,1)S(1)}, u32[]{:S(2)}, u32[]{:S(2)}) collective-permute-start(bf16[128,2048]{1,0:T(8,128)(2,1)} %get-tuple-element.264), channel_id=1, source_target_pairs={{0,1},{1,2},{2,3},{4,5},{5,6},{6,7},{8,9},{9,10},{10,11},{12,13},{... | collective-permute-start | bytes 1572872 | tf_op jit(solution)/shard_map/ppermute | solution.py:290
  713.5 15.1 %collective-permute-start.80 = (bf16[128,2048]{1,0:T(8,128)(2,1)}, bf16[128,2048]{1,0:T(8,128)(2,1)S(1)}, u32[]{:S(2)}, u32[]{:S(2)}) collective-permute-start(bf16[128,2048]{1,0:T(8,128)(2,1)} %get-tuple-element.265), channel_id=1, source_target_pairs={{1,0},{2,1},{3,2},{5,4},{6,5},{7,6},{9,8},{10,9},{11,10},{13,12},{... | collective-permute-start | bytes 1572872 | tf_op jit(solution)/shard_map/ppermute | solution.py:291
  (115 other events, 1167.8 us)
Sparse Core Ops, SparseCore 0:
  26.7 71.0 all-gather.3
  99.7 36.7 all-gather.5
  138.3 72.1 all-gather.7
  414.7 92.9 reduce-scatter.5
  541.8 79.0 reduce-scatter.3
  630.0 108.5 reduce-scatter.7
